TPU v7x, 32 devices: a whole 2x2x4 slice. The times are simulated.
32 devices in a mesh: outer: 4 (over y, x), inner: 2 (over core), heads: 4 (over z).
Axes of the slice: x: 2, y: 2, z: 4, core: 2. Of those that a mesh axis runs over, the one named last changes fastest.
Arguments:
- queries: bfloat16 [4096, 4096], P(('outer', 'inner', 'heads')), may hold values from -6 to 6
- keys: bfloat16 [4096, 4096], P(('outer', 'inner', 'heads')), may hold values from -6 to 6
- values: bfloat16 [4096, 4096], P(('outer', 'inner', 'heads')), may hold values from -6 to 6
- out_grad: bfloat16 [4096, 4096], P(('outer', 'inner', 'heads')), may hold values from -6 to 6
- doc_ids: int32 [4096], P(('outer', 'inner')), may hold values from 0 to 3, never falling along the last dimension, each value on 1 to 2048 neighbouring positions
- carry_in: float32 [32, 128, 128], P('heads'), may hold values from -0.5 to 0.5
- carry_cot: float32 [32, 128, 128], P('heads'), may hold values from -256 to 256
Outputs:
- attended: bfloat16 [4096, 4096], P(('outer', 'inner', 'heads'))
- query_grad: bfloat16 [4096, 4096], P(('outer', 'inner', 'heads'))
- key_grad: bfloat16 [4096, 4096], P(('outer', 'inner', 'heads'))
- value_grad: bfloat16 [4096, 4096], P(('outer', 'inner', 'heads'))
Inputs may be any that keep to these rules, and one draw needn't show every extreme that they name: doc_ids never fall along the tokens; every document 0 to 3 has 1 to 2048 tokens and one has exactly 2048; document 0 continues the document whose state carry_in holds.
All inputs are finite; a program needn't handle non-finite values.
Results may differ from a plain program's by a relative error of at most 0.015.
Values may be sent and summed in bfloat16 or wider, within the bound.
No kernel may reach another device: no remote copies, remote signals or barrier semaphores. Data moves between devices by JAX's collectives and lax.ppermute only.
A program may use at most 192 MiB of HBM per device.

v0:
```python
import jax
import jax.numpy as jnp
from jax import lax
from jax.sharding import PartitionSpec as P

DH = 128
SPAN = 128


beyond_docs = 1000000000.0


def entering(part, axis, combine, identity, reverse):
    count = lax.axis_size(axis)
    place = lax.axis_index(axis)
    ahead = count - 1 - place if reverse else place
    gathered = jax.tree.map(lambda a: lax.all_gather(a, axis), part)
    state = jax.tree.map(lambda a, e: jnp.zeros_like(a) + jnp.asarray(e, a.dtype), part, identity)

    def one(turn, state):
        source = count - 1 - turn if reverse else turn
        return combine(
            state, jax.tree.map(lambda a: lax.dynamic_index_in_dim(a, source, 0, False), gathered)
        )

    return lax.fori_loop(0, ahead, one, state)


def broaden(matches):
    return matches.reshape(matches.shape + (1, 1, 1))


def join_forward(earlier, following):
    highest = jnp.maximum(earlier[0], following[0])
    memory = jnp.where(broaden(earlier[0] == highest), earlier[1], 0.0) + jnp.where(
        broaden(following[0] == highest), following[1], 0.0
    )
    return (highest, memory)


def join_backward(earlier, following):
    lowest = jnp.minimum(earlier[0], following[0])
    highest = jnp.maximum(earlier[1], following[1])
    memory = jnp.where(broaden(earlier[0] == lowest), earlier[2], 0.0) + jnp.where(
        broaden(following[0] == lowest), following[2], 0.0
    )
    return (lowest, highest, memory)


def forward_identity(memory):
    return (jnp.float32(-1.0), jnp.zeros_like(memory))


def backward_identity(memory):
    return (jnp.float32(beyond_docs), jnp.float32(-1.0), jnp.zeros_like(memory))


def forward_step(running, block_inputs):
    return (join_forward(running, block_inputs), running)


def backward_step(running, block_inputs):
    return (join_backward(running, block_inputs), running)


def joint_chain(forward_total, backward_total):
    forward_prefix = entering(
        (forward_total[0], forward_total[1]),
        ("outer", "inner"),
        join_forward,
        forward_identity(forward_total[1]),
        False,
    )
    backward_prefix = entering(
        (backward_total[0], backward_total[1], backward_total[2]),
        ("outer", "inner"),
        join_backward,
        backward_identity(backward_total[2]),
        True,
    )
    return (forward_prefix, backward_prefix)


def layer_pass(queries, keys, values, out_grad, doc_ids, carry_in, carry_cot, factor, connect):
    row_count = queries.shape[0]
    head_count = queries.shape[1] // DH
    blocks = row_count // SPAN
    block_shape = (blocks, SPAN, head_count, DH)
    query_blocks = queries.reshape(block_shape)
    key_blocks = keys.reshape(block_shape)
    value_blocks = values.reshape(block_shape)
    grad_blocks = out_grad.reshape(block_shape)
    doc_blocks = doc_ids.reshape(blocks, SPAN).astype(jnp.float32)
    first_docs = doc_blocks[:, 0]
    last_docs = doc_blocks[:, -1]
    in_first = (doc_blocks == first_docs[:, None])[:, :, None, None]
    in_last = (doc_blocks == last_docs[:, None])[:, :, None, None]
    positions = lax.iota(jnp.int32, SPAN)
    causal = positions[:, None] >= positions[None, :]
    allowed = (causal[None] & (doc_blocks[:, :, None] == doc_blocks[:, None, :]))[:, None]
    forward_terms = (
        jnp.einsum(
            "nuhd,nuhe->nhde",
            jnp.where(in_last, key_blocks, 0),
            value_blocks,
            preferred_element_type=jnp.float32,
        )
        * factor
    )
    backward_terms = (
        jnp.einsum(
            "nthd,nthe->nhde",
            jnp.where(in_first, query_blocks, 0),
            grad_blocks,
            preferred_element_type=jnp.float32,
        )
        * factor
    )
    empty_state = jnp.zeros((head_count, DH, DH), jnp.float32)
    forward_total, forward_before = lax.scan(
        forward_step, forward_identity(empty_state), (last_docs, forward_terms)
    )
    backward_total, backward_after = lax.scan(
        backward_step,
        backward_identity(empty_state),
        (first_docs, last_docs, backward_terms),
        reverse=True,
    )
    forward_prefix, backward_prefix = connect(forward_total, backward_total)
    forward_block = join_forward(forward_prefix, forward_before)
    backward_block = join_backward(backward_after, backward_prefix)
    state_before = jnp.where(
        broaden(forward_block[0] == first_docs), forward_block[1], 0.0
    ) + jnp.where(broaden(first_docs == 0.0), carry_in, 0.0)
    newest = jnp.maximum(backward_block[1], last_docs)
    state_after = jnp.where(
        broaden(backward_block[0] == last_docs), backward_block[2], 0.0
    ) + jnp.where(broaden(last_docs == newest), factor * carry_cot, 0.0)
    before_half = state_before.astype(jnp.bfloat16)
    after_half = state_after.astype(jnp.bfloat16)
    scores = jnp.where(
        allowed,
        jnp.einsum("nthd,nuhd->nhtu", query_blocks, key_blocks, preferred_element_type=jnp.float32)
        * factor,
        0.0,
    ).astype(jnp.bfloat16)
    grad_scores = jnp.where(
        allowed,
        jnp.einsum("nthe,nuhe->nhtu", grad_blocks, value_blocks, preferred_element_type=jnp.float32)
        * factor,
        0.0,
    ).astype(jnp.bfloat16)
    attended = jnp.einsum(
        "nhtu,nuhd->nthd", scores, value_blocks, preferred_element_type=jnp.float32
    ) + jnp.where(
        in_first,
        jnp.einsum(
            "nthd,nhde->nthe", query_blocks, before_half, preferred_element_type=jnp.float32
        ),
        0.0,
    )
    query_grad = jnp.einsum(
        "nhtu,nuhd->nthd", grad_scores, key_blocks, preferred_element_type=jnp.float32
    ) + jnp.where(
        in_first,
        jnp.einsum("nthe,nhde->nthd", grad_blocks, before_half, preferred_element_type=jnp.float32),
        0.0,
    )
    key_grad = jnp.einsum(
        "nhtu,nthd->nuhd", grad_scores, query_blocks, preferred_element_type=jnp.float32
    ) + jnp.where(
        in_last,
        jnp.einsum("nuhe,nhde->nuhd", value_blocks, after_half, preferred_element_type=jnp.float32),
        0.0,
    )
    value_grad = jnp.einsum(
        "nhtu,nthe->nuhe", scores, grad_blocks, preferred_element_type=jnp.float32
    ) + jnp.where(
        in_last,
        jnp.einsum("nuhd,nhde->nuhe", key_blocks, after_half, preferred_element_type=jnp.float32),
        0.0,
    )
    out_shape = (row_count, head_count * DH)
    return (
        attended.reshape(out_shape).astype(jnp.bfloat16),
        query_grad.reshape(out_shape).astype(jnp.bfloat16),
        key_grad.reshape(out_shape).astype(jnp.bfloat16),
        value_grad.reshape(out_shape).astype(jnp.bfloat16),
    )


def shards(queries, keys, values, out_grad, doc_ids, carry_in, carry_cot):
    tokens_all = doc_ids.shape[0] * lax.axis_size("outer") * lax.axis_size("inner")
    factor = float(DH * (tokens_all // 2)) ** (-0.5)
    local_arrays = (
        lax.all_to_all(queries, "heads", split_axis=1, concat_axis=0, tiled=True),
        lax.all_to_all(keys, "heads", split_axis=1, concat_axis=0, tiled=True),
        lax.all_to_all(values, "heads", split_axis=1, concat_axis=0, tiled=True),
        lax.all_to_all(out_grad, "heads", split_axis=1, concat_axis=0, tiled=True),
    )
    results = layer_pass(
        local_arrays[0],
        local_arrays[1],
        local_arrays[2],
        local_arrays[3],
        doc_ids,
        carry_in,
        carry_cot,
        factor,
        joint_chain,
    )
    return (
        lax.all_to_all(results[0], "heads", split_axis=0, concat_axis=1, tiled=True),
        lax.all_to_all(results[1], "heads", split_axis=0, concat_axis=1, tiled=True),
        lax.all_to_all(results[2], "heads", split_axis=0, concat_axis=1, tiled=True),
        lax.all_to_all(results[3], "heads", split_axis=0, concat_axis=1, tiled=True),
    )


def solution(mesh):
    placed = (
        P(("outer", "inner", "heads"), None),
        P(("outer", "inner", "heads"), None),
        P(("outer", "inner", "heads"), None),
        P(("outer", "inner", "heads"), None),
        P(("outer", "inner")),
        P("heads", None, None),
        P("heads", None, None),
    )
    return jax.shard_map(
        shards,
        mesh=mesh,
        in_specs=placed,
        out_specs=(
            P(("outer", "inner", "heads"), None),
            P(("outer", "inner", "heads"), None),
            P(("outer", "inner", "heads"), None),
            P(("outer", "inner", "heads"), None),
        ),
        check_vma=False,
    )
```

profile of v0, /device:TPU:6, one launch (start us, length us, event | category | flops | bytes accessed | tf_op | source)
XLA Modules:
  0.0 360.7 jit_solution(18276143913620379079)
XLA Ops:
  7.2 2.4 copy.81
  9.5 4.9 %all-to-all-start.4 = ((bf16[128,4,1024]{0,2,1:T(8,128)(2,1)}), bf16[128,4,1024]{0,2,1:T(8,128)(2,1)S(1)}, u32[]{:S(2)}, u32[]{:S(2)}) async-start(bf16[128,4,1024]{0,2,1:T(8,128)(2,1)} %bitcast.26), calls=%async_computation.4 | async-start | bytes 2097152 | tf_op jit(solution)/shard_map/all_to_all | solution.py:199
  14.4 1.3 copy.72
  15.7 24.4 %all-to-all-done.4 = bf16[128,4,1024]{0,2,1:T(8,128)(2,1)S(1)} async-done(((bf16[128,4,1024]{0,2,1:T(8,128)(2,1)}), bf16[128,4,1024]{0,2,1:T(8,128)(2,1)S(1)}, u32[]{:S(2)}, u32[]{:S(2)}) %all-to-all-start.4) | async-done | bytes 1048608 | tf_op jit(solution)/shard_map/all_to_all | solution.py:199
  40.1 3.5 all-to-all-start
  44.0 24.9 %all-to-all-done = bf16[128,4,1024]{0,2,1:T(8,128)(2,1)S(1)} async-done(((bf16[128,4,1024]{0,2,1:T(8,128)(2,1)}), bf16[128,4,1024]{0,2,1:T(8,128)(2,1)S(1)}, u32[]{:S(2)}, u32[]{:S(2)}) %all-to-all-start) | async-done | bytes 1048608 | tf_op jit(solution)/shard_map/all_to_all | solution.py:196
  69.8 2.4 convolution_multiply_fusion
  72.2 1.6 broadcast_in_dim.270.clone.1
  73.8 16.8 %while.73 = (s32[]{:T(128)}, f32[]{:T(128)}, f32[]{:T(128)}, f32[8,128,128]{2,1,0:T(8,128)S(1)}, f32[4]{0:T(128)S(1)}, /*index=5*/f32[4]{0:T(128)S(1)}, f32[4,8,...) while((s32[]{:T(128)}, f32[]{:T(128)}, f32[]{:T(128)}, ...), condition=%wide.region_5.6_spmd.clone, body=%wide.region_4.5_spmd.clone.sunk | while | flops 655368 | bytes 2621704 | solution.py:123
  91.5 2.4 copy.73
  93.8 3.5 all-to-all-start.1
  97.4 1.3 copy.104
  98.7 23.9 %all-to-all-done.1 = bf16[128,4,1024]{0,2,1:T(8,128)(2,1)S(1)} async-done(((bf16[128,4,1024]{0,2,1:T(8,128)(2,1)}), bf16[128,4,1024]{0,2,1:T(8,128)(2,1)S(1)}, u32[]{:S(2)}, u32[]{:S(2)}) %all-to-all-start.1) | async-done | bytes 1048608 | tf_op jit(solution)/shard_map/all_to_all | solution.py:197
  122.5 3.5 all-to-all-start.2
  126.1 25.1 %all-to-all-done.2 = bf16[128,4,1024]{0,2,1:T(8,128)(2,1)S(1)} async-done(((bf16[128,4,1024]{0,2,1:T(8,128)(2,1)}), bf16[128,4,1024]{0,2,1:T(8,128)(2,1)S(1)}, u32[]{:S(2)}, u32[]{:S(2)}) %all-to-all-start.2) | async-done | bytes 1048608 | tf_op jit(solution)/shard_map/all_to_all | solution.py:198
  151.2 2.2 convolution_multiply_fusion.1
  153.5 1.6 broadcast_in_dim.270.clone
  155.1 15.5 %while.72 = (s32[]{:T(128)}, f32[]{:T(128)}, f32[8,128,128]{2,1,0:T(8,128)S(1)}, f32[4]{0:T(128)S(1)}, f32[4,8,128,128]{3,2,1,0:T(8,128)}, /*index=5*/f32[4]{0:T...) while((s32[]{:T(128)}, f32[]{:T(128)}, f32[8,128,128]{2,1,0:T(8,128)S(1)}, f32[4]{0:T(128)S(1)}, ...), condition=%wide.region_1.2_spmd.clone, body=%wide.region_0.1_spmd.clone.sunk | while | flops 655366 | bytes 2622124 | solution.py:120
  175.3 10.5 %all-reduce.3 = (f32[8]{0:T(128)S(1)}, f32[8]{0:T(128)S(1)}, f32[8]{0:T(128)S(1)}) all-reduce(f32[8]{0:T(128)S(1)} %dynamic-update-slice, f32[8]{0:T(128)S(1)} %dynamic-update-slice.1, f32[8]{0:T(128)S(1)} %dynamic-update-slice.2), channel_id=1, replica_groups=mesh['outer'=4,'inner'=2,'heads'=4] {'outer','inner'}, use_global_device_ids=true, to_apply=%add | all-reduce | flops 24 | bytes 192
  185.8 2.7 select_convert_fusion.1
  188.6 4.7 %while.71 = (s32[]{:T(128)}, f32[]{:T(128)}, f32[]{:T(128)}, f32[8,128,128]{2,1,0:T(8,128)S(1)}, s32[]{:T(128)}, /*index=5*/f32[8]{0:T(128)S(1)}, f32[8]{0:T(128...) while((s32[]{:T(128)}, f32[]{:T(128)}, f32[]{:T(128)}, ...), condition=%wide.region_7.8_spmd, body=%wide.region_6.7_spmd.sunk | while | flops 393226 | bytes 1573107 | solution.py:26
  190.7 1.2 bitcast_add_fusion.13
  193.3 13.2 %all-gather.5.cloned.1.call-done = f32[64,128,128]{2,1,0:T(8,128)} async-done(((f32[8,128,128]{2,1,0:T(8,128)}), f32[64,128,128]{2,1,0:T(8,128)}) %all-gather.5.cloned.1.call-update) | async-done | bytes 4194320 | tf_op jit(solution)/shard_map/all_gather | solution.py:17
  206.6 18.8 %while.70 = (s32[]{:T(128)}, f32[]{:T(128)}, f32[8,128,128]{2,1,0:T(8,128)S(1)}, s32[]{:T(128)}, f32[8]{0:T(128)S(1)}, /*index=5*/f32[8,8,128,128]{3,2,1,0:T(8,128)}, s32[]{:T(128)}, s32[]{:T(128)}, s32[]{:T(128)}) while((s32[]{:T(128)}, f32[]{:T(128)}, f32[8,128,128]{2,1,0:T(8,128)S(1)}, s32[]{:T(128)}, f32[8]{0:T(128)S(1)}, ...), condition=%wide.region_3.4_spmd, body=%wide.region_2.3_spmd.sunk | while | flops 393224 | bytes 1573047 | solution.py:26
  208.5 1.2 bitcast_add_fusion.12
  211.6 1.2 bitcast_add_fusion.12
  214.7 1.2 bitcast_add_fusion.12
  217.9 1.2 bitcast_add_fusion.12
  225.4 2.2 add_convert_fusion
  229.6 1.5 fusion
  231.0 4.6 %all-to-all-start.7 = ((bf16[4,128,1024]{1,2,0:T(8,128)(2,1)}), bf16[4,128,1024]{1,2,0:T(8,128)(2,1)}, u32[]{:S(2)}, u32[]{:S(2)}) async-start(bf16[4,128,1024]{1,2,0:T(8,128)(2,1)} %bitcast.159), calls=%async_computation.7 | async-start | bytes 2097152 | tf_op jit(solution)/shard_map/all_to_all | solution.py:216
  235.6 1.9 select_convert_fusion
  239.1 1.5 fusion.1
  240.6 21.2 %all-to-all-done.7 = bf16[4,128,1024]{1,2,0:T(8,128)(2,1)} async-done(((bf16[4,128,1024]{1,2,0:T(8,128)(2,1)}), bf16[4,128,1024]{1,2,0:T(8,128)(2,1)}, u32[]{:S(2)}, u32[]{:S(2)}) %all-to-all-start.7) | async-done | bytes 1048608 | tf_op jit(solution)/shard_map/all_to_all | solution.py:216
  261.8 4.2 %all-to-all-start.6 = ((bf16[4,128,1024]{1,2,0:T(8,128)(2,1)}), bf16[4,128,1024]{1,2,0:T(8,128)(2,1)}, u32[]{:S(2)}, u32[]{:S(2)}) async-start(bf16[4,128,1024]{1,2,0:T(8,128)(2,1)} %bitcast.158), calls=%async_computation.6 | async-start | bytes 2097152 | tf_op jit(solution)/shard_map/all_to_all | solution.py:215
  266.1 2.2 fusion.13
  268.4 1.9 fusion.2
  270.2 22.9 %all-to-all-done.6 = bf16[4,128,1024]{1,2,0:T(8,128)(2,1)} async-done(((bf16[4,128,1024]{1,2,0:T(8,128)(2,1)}), bf16[4,128,1024]{1,2,0:T(8,128)(2,1)}, u32[]{:S(2)}, u32[]{:S(2)}) %all-to-all-start.6) | async-done | bytes 1048608 | tf_op jit(solution)/shard_map/all_to_all | solution.py:215
  293.2 4.4 %all-to-all-start.5 = ((bf16[4,128,1024]{1,2,0:T(8,128)(2,1)}), bf16[4,128,1024]{1,2,0:T(8,128)(2,1)}, u32[]{:S(2)}, u32[]{:S(2)}) async-start(bf16[4,128,1024]{1,2,0:T(8,128)(2,1)} %bitcast.32), calls=%async_computation.5 | async-start | bytes 2097152 | tf_op jit(solution)/shard_map/all_to_all | solution.py:214
  297.6 2.2 fusion.12
  299.9 1.9 fusion.3
  301.7 21.9 %all-to-all-done.5 = bf16[4,128,1024]{1,2,0:T(8,128)(2,1)} async-done(((bf16[4,128,1024]{1,2,0:T(8,128)(2,1)}), bf16[4,128,1024]{1,2,0:T(8,128)(2,1)}, u32[]{:S(2)}, u32[]{:S(2)}) %all-to-all-start.5) | async-done | bytes 1048608 | tf_op jit(solution)/shard_map/all_to_all | solution.py:214
  323.7 3.5 all-to-all-start.3
  327.2 2.3 copy.108
  329.5 2.3 copy.107
  331.7 2.3 copy.106
  334.0 18.5 %all-to-all-done.3 = bf16[4,128,1024]{1,2,0:T(8,128)(2,1)S(1)} async-done(((bf16[4,128,1024]{1,2,0:T(8,128)(2,1)}), bf16[4,128,1024]{1,2,0:T(8,128)(2,1)S(1)}, u32[]{:S(2)}, u32[]{:S(2)}) %all-to-all-start.3) | async-done | bytes 1048608 | tf_op jit(solution)/shard_map/all_to_all | solution.py:213
  352.5 1.3 copy.105
  (118 shorter events, 38.2 us)
Async XLA Ops:
  7.2 7.2 %copy-start.14 = (bf16[128,4096]{1,0:T(8,128)(2,1)S(1)}, bf16[128,4096]{1,0:T(8,128)(2,1)}, u32[]{:S(2)}) copy-start(bf16[128,4096]{1,0:T(8,128)(2,1)} %param.15) | copy-start | bytes 3145732
  9.5 30.6 %all-to-all-start.4 = ((bf16[128,4,1024]{0,2,1:T(8,128)(2,1)}), bf16[128,4,1024]{0,2,1:T(8,128)(2,1)S(1)}, u32[]{:S(2)}, u32[]{:S(2)}) async-start(bf16[128,4,1024]{0,2,1:T(8,128)(2,1)} %bitcast.26), calls=%async_computation.4 | async-start | bytes 2097152 | tf_op jit(solution)/shard_map/all_to_all | solution.py:199
  14.4 29.3 %copy-start.17 = (s32[512]{0:T(512)S(1)}, s32[512]{0:T(512)}, u32[]{:S(2)}) copy-start(s32[512]{0:T(512)} %param.19) | copy-start | bytes 6148
  40.1 28.7 %copy-start.5 = (bf16[128,4,1024]{0,2,1:T(8,128)(2,1)}, bf16[128,4,1024]{0,2,1:T(8,128)(2,1)S(1)}, u32[]{:S(2)}) copy-start(bf16[128,4,1024]{0,2,1:T(8,128)(2,1)S(1)} %all-to-all-done.4) | copy-start | bytes 3145732
  40.1 28.7 %all-to-all-start = ((bf16[128,4,1024]{0,2,1:T(8,128)(2,1)}), bf16[128,4,1024]{0,2,1:T(8,128)(2,1)S(1)}, u32[]{:S(2)}, u32[]{:S(2)}) async-start(bf16[128,4,1024]{0,2,1:T(8,128)(2,1)} %bitcast.155), calls=%async_computation | async-start | bytes 2097152 | tf_op jit(solution)/shard_map/all_to_all | solution.py:196
  43.6 144.9 %all-gather.7.cloned.1.call-start = ((), (), s32[]{:S(2)}) async-start(), calls=%async_computation.9 | async-start | bytes 4718592 | tf_op jit(solution)/shard_map/all_gather | solution.py:17
  68.8 1.0 copy-start.2
  90.6 0.8 copy-start
  91.5 5.9 %copy-start.15 = (bf16[128,4096]{1,0:T(8,128)(2,1)S(1)}, bf16[128,4096]{1,0:T(8,128)(2,1)}, u32[]{:S(2)}) copy-start(bf16[128,4096]{1,0:T(8,128)(2,1)} %param.17) | copy-start | bytes 3145732
  93.8 28.7 %all-to-all-start.1 = ((bf16[128,4,1024]{0,2,1:T(8,128)(2,1)}), bf16[128,4,1024]{0,2,1:T(8,128)(2,1)S(1)}, u32[]{:S(2)}, u32[]{:S(2)}) async-start(bf16[128,4,1024]{0,2,1:T(8,128)(2,1)} %bitcast.9), calls=%async_computation.1 | async-start | bytes 2097152 | tf_op jit(solution)/shard_map/all_to_all | solution.py:197
  122.5 28.7 %all-to-all-start.2 = ((bf16[128,4,1024]{0,2,1:T(8,128)(2,1)}), bf16[128,4,1024]{0,2,1:T(8,128)(2,1)S(1)}, u32[]{:S(2)}, u32[]{:S(2)}) async-start(bf16[128,4,1024]{0,2,1:T(8,128)(2,1)} %bitcast.157), calls=%async_computation.2 | async-start | bytes 2097152 | tf_op jit(solution)/shard_map/all_to_all | solution.py:198
  126.1 80.5 %all-gather.5.cloned.1.call-start = ((), (), s32[]{:S(2)}) async-start(), calls=%async_computation.8 | async-start | bytes 4718592 | tf_op jit(solution)/shard_map/all_gather | solution.py:17
  155.1 16.4 %copy-start.19 = (u32[32]{0:T(128)S(1)}, u32[32]{0:T(128)}, u32[]{:S(2)}) copy-start(u32[32]{0:T(128)} %constant.135) | copy-start | bytes 388
  155.1 17.1 %copy-start.16 = (f32[8,128,128]{2,1,0:T(8,128)S(1)}, f32[8,128,128]{2,1,0:T(8,128)}, u32[]{:S(2)}) copy-start(f32[8,128,128]{2,1,0:T(8,128)} %param.21) | copy-start | bytes 1572868
  170.6 0.8 copy-start.1
  227.6 1.0 copy-start.8
  227.6 1.6 copy-start.6
  227.7 1.9 copy-start.10
  231.0 30.8 %all-to-all-start.7 = ((bf16[4,128,1024]{1,2,0:T(8,128)(2,1)}), bf16[4,128,1024]{1,2,0:T(8,128)(2,1)}, u32[]{:S(2)}, u32[]{:S(2)}) async-start(bf16[4,128,1024]{1,2,0:T(8,128)(2,1)} %bitcast.159), calls=%async_computation.7 | async-start | bytes 2097152 | tf_op jit(solution)/shard_map/all_to_all | solution.py:216
  235.6 1.9 copy-start.9
  237.5 1.0 copy-start.11
  237.5 1.6 copy-start.3
  261.8 31.4 %all-to-all-start.6 = ((bf16[4,128,1024]{1,2,0:T(8,128)(2,1)}), bf16[4,128,1024]{1,2,0:T(8,128)(2,1)}, u32[]{:S(2)}, u32[]{:S(2)}) async-start(bf16[4,128,1024]{1,2,0:T(8,128)(2,1)} %bitcast.158), calls=%async_computation.6 | async-start | bytes 2097152 | tf_op jit(solution)/shard_map/all_to_all | solution.py:215
  266.0 2.3 copy-start.7
  266.1 2.3 copy-start.12
  266.1 2.3 copy-start.18
  293.2 30.5 %all-to-all-start.5 = ((bf16[4,128,1024]{1,2,0:T(8,128)(2,1)}), bf16[4,128,1024]{1,2,0:T(8,128)(2,1)}, u32[]{:S(2)}, u32[]{:S(2)}) async-start(bf16[4,128,1024]{1,2,0:T(8,128)(2,1)} %bitcast.32), calls=%async_computation.5 | async-start | bytes 2097152 | tf_op jit(solution)/shard_map/all_to_all | solution.py:214
  297.6 2.2 copy-start.4
  297.6 2.2 copy-start.13
  323.7 28.9 %all-to-all-start.3 = ((bf16[4,128,1024]{1,2,0:T(8,128)(2,1)}), bf16[4,128,1024]{1,2,0:T(8,128)(2,1)S(1)}, u32[]{:S(2)}, u32[]{:S(2)}) async-start(bf16[4,128,1024]{1,2,0:T(8,128)(2,1)} %bitcast.162), calls=%async_computation.3 | async-start | bytes 2097152 | tf_op jit(solution)/shard_map/all_to_all | solution.py:213
Sparse Core Ops, SparseCore 0:
  91.6 34.8 all-gather.6
  171.6 34.9 all-gather.4
where the time goes:
time: 363 us; the launch traced here: 361 us
  waiting for transfers between devices  196 us (54%)
  local copies, waits for them, and re-layouts  40.3 us (11%)
  starting transfers between devices  32.3 us (9%)
  other arithmetic  23.8 us (7%)
  loops' own time  22 us (6%)
  matrix products  21.3 us (6%)
  between operations  14.4 us (4%)
  blocking collectives  10.5 us (3%)
    all_to_all x1, waiting for transfers between devices, shards(): lax.all_to_all(values, 'heads', split_axis=1, concat_axis=0, tiled=True)  25.1 us
    all_to_all x1, waiting for transfers between devices, shards(): lax.all_to_all(queries, 'heads', split_axis=1, concat_axis=0, tiled=True)  24.9 us
    all_to_all x1, waiting for transfers between devices, shards(): lax.all_to_all(out_grad, 'heads', split_axis=1, concat_axis=0, tiled=True)  24.4 us
    all_to_all x1, waiting for transfers between devices, shards(): lax.all_to_all(keys, 'heads', split_axis=1, concat_axis=0, tiled=True)  23.9 us
    all_to_all x1, waiting for transfers between devices, shards(): lax.all_to_all(results[2], 'heads', split_axis=0, concat_axis=1, tiled=True)  22.9 us
    all_to_all x1, waiting for transfers between devices, shards(): lax.all_to_all(results[1], 'heads', split_axis=0, concat_axis=1, tiled=True)  21.9 us
    all_to_all x1, waiting for transfers between devices, shards(): lax.all_to_all(results[3], 'heads', split_axis=0, concat_axis=1, tiled=True)  21.2 us
    all_to_all x1, waiting for transfers between devices, shards(): lax.all_to_all(results[0], 'heads', split_axis=0, concat_axis=1, tiled=True)  18.5 us
  transfers between devices with their start and end apart: 10, of which 9 were waited for; matrix products, arithmetic and copies ran while one was open for 13% of the time, Pallas kernels for 0%

commit v1 on v0

v1 whole, which is shorter than its diff:
```python
import functools

import jax
import jax.numpy as jnp
from jax import lax
from jax.experimental import pallas as pl
from jax.experimental.pallas import tpu as pltpu
from jax.sharding import PartitionSpec as P

DH = 128
SPAN = 128
CHUNK = 4
STREAMS = 2
F32 = jnp.float32
BF16 = jnp.bfloat16


def flag(condition):
    return condition.astype(F32)


def both(a, b):
    return flag(jnp.logical_and(a, b))


def swap(array, axis, distance):
    count = lax.axis_size(axis)
    return lax.ppermute(array, axis, [(i, i ^ distance) for i in range(count)])


def shift(array, axis, step):
    count = lax.axis_size(axis)
    return lax.ppermute(
        array, axis, [(i, i + step) for i in range(count) if 0 <= i + step < count]
    )


def total(terms):
    out = None
    for weight, array in terms:
        piece = weight * array.astype(F32)
        out = piece if out is None else out + piece
    return out


def transposed_dot(a, b):
    return lax.dot_general(a, b, (((0,), (0,)), ((), ())), preferred_element_type=F32)


def dot_transposed(a, b):
    return lax.dot_general(a, b, (((1,), (1,)), ((), ())), preferred_element_type=F32)


def dot(a, b):
    return lax.dot_general(a, b, (((1,), (0,)), ((), ())), preferred_element_type=F32)


def term_kernel(factor, group, docs_ref, q_ref, k_ref, v_ref, g_ref, forward_ref, backward_ref):
    docs = docs_ref[...]
    in_first = docs == docs[0:1]
    in_last = docs == docs[SPAN - 1 : SPAN]
    for i in range(group):
        at = slice(i * DH, (i + 1) * DH)
        keys = jnp.where(in_last, k_ref[:, at], 0)
        queries = jnp.where(in_first, q_ref[:, at], 0)
        forward_ref[i] = (transposed_dot(keys, v_ref[:, at]) * factor).astype(BF16)
        backward_ref[i] = (transposed_dot(queries, g_ref[:, at]) * factor).astype(BF16)


def state_terms(docs_column, arrays, factor, head, heads):
    group = min(heads, 4)
    steps = heads // group
    first = head // group
    columns = pl.BlockSpec((SPAN, group * DH), lambda i: (0, first + i))
    states = pl.BlockSpec((group, DH, DH), lambda i: (i, 0, 0))
    shape = jax.ShapeDtypeStruct((heads, DH, DH), BF16)
    return pl.pallas_call(
        functools.partial(term_kernel, factor, group),
        grid=(steps,),
        in_specs=[pl.BlockSpec((SPAN, DH), lambda i: (0, 0))] + [columns] * 4,
        out_specs=[states, states],
        out_shape=[shape, shape],
        cost_estimate=pl.CostEstimate(
            flops=heads * 4 * SPAN * DH * DH, bytes_accessed=heads * 6 * SPAN * DH * 2, transcendentals=0
        ),
    )(docs_column, *arrays)


def output_kernel(factor, group, docs_ref, row_ref, q_ref, k_ref, v_ref, g_ref, before_ref, after_ref, *refs):
    attended_ref, query_grad_ref, key_grad_ref, value_grad_ref = refs[-4:]
    docs = docs_ref[...]
    in_first = docs == docs[0:1]
    in_last = docs == docs[SPAN - 1 : SPAN]
    places = lax.broadcasted_iota(jnp.int32, (SPAN, SPAN), 0)
    others = lax.broadcasted_iota(jnp.int32, (SPAN, SPAN), 1)
    allowed = jnp.logical_and(others <= places, docs == row_ref[0:1])
    for i in range(group):
        at = slice(i * DH, (i + 1) * DH)
        q, k, v, g = q_ref[:, at], k_ref[:, at], v_ref[:, at], g_ref[:, at]
        before, after = before_ref[i], after_ref[i]
        scores = jnp.where(allowed, dot_transposed(q, k) * factor, 0.0).astype(BF16)
        grad_scores = jnp.where(allowed, dot_transposed(g, v) * factor, 0.0).astype(BF16)
        attended_ref[:, at] = (dot(scores, v) + dot(jnp.where(in_first, q, 0), before)).astype(BF16)
        query_grad_ref[:, at] = (
            dot(grad_scores, k) + dot_transposed(jnp.where(in_first, g, 0), before)
        ).astype(BF16)
        key_grad_ref[:, at] = (
            transposed_dot(grad_scores, q) + dot_transposed(jnp.where(in_last, v, 0), after)
        ).astype(BF16)
        value_grad_ref[:, at] = (
            transposed_dot(scores, g) + dot(jnp.where(in_last, k, 0), after)
        ).astype(BF16)


def outputs_of(docs_column, docs_row, arrays, before, after, held, factor, head, heads):
    group = min(heads, 4)
    steps = heads // group
    first = head // group
    columns = pl.BlockSpec((SPAN, group * DH), lambda i: (0, first + i))
    states = pl.BlockSpec((group, DH, DH), lambda i: (i, 0, 0))
    whole = pl.BlockSpec((SPAN, DH), lambda i: (0, 0))
    row = pl.BlockSpec((8, SPAN), lambda i: (0, 0))
    shape = jax.ShapeDtypeStruct(arrays[0].shape, BF16)
    return pl.pallas_call(
        functools.partial(output_kernel, factor, group),
        grid=(steps,),
        in_specs=[whole, row] + [columns] * 4 + [states] * 2 + [pl.BlockSpec(memory_space=pl.ANY)] * len(held),
        out_specs=[columns] * 4,
        out_shape=[shape] * 4,
        input_output_aliases={8 + i: i for i in range(len(held))},
        cost_estimate=pl.CostEstimate(
            flops=heads * 20 * SPAN * DH * DH, bytes_accessed=heads * 10 * SPAN * DH * 2, transcendentals=0
        ),
    )(docs_column, docs_row, *arrays, before, after, *held)


def shards(queries, keys, values, out_grad, doc_ids, carry_in, carry_cot):
    outer_count, inner_count, depth = (lax.axis_size(a) for a in ("outer", "inner", "heads"))
    o, c, z = (lax.axis_index(a) for a in ("outer", "inner", "heads"))
    tokens_all = doc_ids.shape[0] * outer_count * inner_count
    factor = float(DH * (tokens_all // 2)) ** (-0.5)
    head_count = queries.shape[1] // DH
    held_heads = head_count // depth
    arrays = (queries, keys, values, out_grad)
    piece_heads = max(CHUNK * STREAMS, inner_count)
    part = piece_heads // inner_count
    pieces = head_count // piece_heads
    inner_turns, outer_turns = range(1, inner_count), range(1, outer_count)

    blocks = doc_ids.reshape(depth, SPAN)
    firsts, lasts = blocks[:, 0].astype(F32), blocks[:, -1].astype(F32)
    edges = jnp.concatenate([firsts, lasts])
    inner_edges = [edges] + [swap(edges, "inner", d) for d in inner_turns]
    group_first = [e[0] for e in inner_edges]
    group_last = [e[2 * depth - 1] for e in inner_edges]
    block_first = [lax.dynamic_index_in_dim(e, z, 0, False) for e in inner_edges]
    block_last = [lax.dynamic_index_in_dim(e, depth + z, 0, False) for e in inner_edges]
    outer_first = functools.reduce(jnp.minimum, group_first)
    outer_last = functools.reduce(jnp.maximum, group_last)
    outer_edge = jnp.stack([outer_first, outer_last])
    outer_edges = [swap(outer_edge, "outer", d) for d in outer_turns]
    newest = functools.reduce(jnp.maximum, [e[1] for e in outer_edges], outer_last)
    outer_prior = functools.reduce(
        jnp.maximum, [jnp.where((o ^ d) < o, e[1], 0.0) for d, e in zip(outer_turns, outer_edges)], F32(0.0)
    )
    outer_later = functools.reduce(
        jnp.minimum, [jnp.where((o ^ d) > o, e[0], newest) for d, e in zip(outer_turns, outer_edges)], newest
    )
    prior, later = [], []
    for t in range(inner_count):
        prior.append(functools.reduce(
            jnp.maximum, [jnp.where((c ^ d) < (c ^ t), group_last[d], 0.0) for d in range(inner_count)], outer_prior
        ))
        later.append(functools.reduce(
            jnp.minimum, [jnp.where((c ^ d) > (c ^ t), group_first[d], newest) for d in range(inner_count)], outer_later
        ))
    first, last = block_first[0], block_last[0]
    last_before = lax.dynamic_index_in_dim(lasts, jnp.maximum(z - 1, 0), 0, False)
    first_after = lax.dynamic_index_in_dim(firsts, jnp.minimum(z + 1, depth - 1), 0, False)

    docs_block = lax.dynamic_index_in_dim(blocks, z, 0, False)
    docs_column = jnp.broadcast_to(docs_block[:, None], (SPAN, DH))
    docs_row = jnp.broadcast_to(docs_block[None, :], (8, SPAN))

    chunks = head_count // CHUNK
    terms_f, terms_b, prefix_f, prefix_b = [], [], [], []
    for p in range(pieces):
        forward, backward = state_terms(docs_column, arrays, factor, p * piece_heads, piece_heads)
        shape = (inner_count, part, DH, DH)
        split_f, split_b = forward.reshape(shape), backward.reshape(shape)

        def sent(d):
            at = c ^ d
            return jnp.stack(
                [lax.dynamic_index_in_dim(split_f, at, 0, False), lax.dynamic_index_in_dim(split_b, at, 0, False)]
            )

        received = [sent(0)] + [swap(sent(d), "inner", d) for d in inner_turns]
        sum_f = total([(flag(block_last[d] == outer_last), received[d][0]) for d in range(inner_count)])
        sum_b = total([(flag(block_first[d] == outer_first), received[d][1]) for d in range(inner_count)])
        sum_f, sum_b = sum_f.astype(BF16), sum_b.astype(BF16)
        fans = [swap(jnp.where(o < (o ^ d), sum_f, sum_b), "outer", d) for d in outer_turns]
        own, given = None, []
        for t in range(inner_count):
            x_f = total(
                [(both((o ^ d) < o, e[1] == prior[t]), r) for d, e, r in zip(outer_turns, outer_edges, fans)]
                + [
                    (both((c ^ d) < (c ^ t), block_last[d] == prior[t]), received[d][0])
                    for d in range(inner_count) if d != t
                ]
            )
            x_b = total(
                [(both((o ^ d) > o, e[0] == later[t]), r) for d, e, r in zip(outer_turns, outer_edges, fans)]
                + [
                    (both((c ^ d) > (c ^ t), block_first[d] == later[t]), received[d][1])
                    for d in range(inner_count) if d != t
                ]
            )
            x = jnp.stack([x_f, x_b]).astype(BF16)
            given.append(x if t == 0 else swap(x, "inner", t))
        if inner_count == 2:
            x = jnp.where(
                c == 0, jnp.concatenate(given, axis=1), jnp.concatenate(given[::-1], axis=1)
            )
        else:
            x = jnp.take(jnp.stack(given), c ^ jnp.arange(inner_count), axis=0)
            x = x.transpose(1, 0, 2, 3, 4).reshape(2, piece_heads, DH, DH)
        for i in range(0, piece_heads, CHUNK):
            head = p * piece_heads + i
            owner, at = head // held_heads, head % held_heads
            mine = z == owner
            terms_f.append(forward[i : i + CHUNK])
            terms_b.append(backward[i : i + CHUNK])
            prefix_f.append((
                x[0, i : i + CHUNK].astype(F32) + both(mine, prior[0] == 0.0) * carry_in[at : at + CHUNK]
            ).astype(BF16))
            prefix_b.append((
                x[1, i : i + CHUNK].astype(F32)
                + both(mine, later[0] == newest) * (factor * carry_cot[at : at + CHUNK])
            ).astype(BF16))

    keep_f = both(z > 0, last_before == last)
    keep_b = both(z < depth - 1, first_after == first)
    join_f, join_b = flag(prior[0] == last), flag(later[0] == first)
    turns = chunks // STREAMS
    steps = turns + depth - 2

    def picked(lists, stream, turn_of):
        out = None
        for place in range(depth):
            turn = min(max(turn_of(place), 0), turns - 1)
            options = [l[turn * STREAMS + stream] for l in lists]
            if out is None:
                out = options
            else:
                out = [jnp.where(z == place, b, a) for a, b in zip(out, options)]
        return [a.astype(F32) for a in out]

    up = [[None] * steps for _ in range(STREAMS)]
    down = [[None] * steps for _ in range(STREAMS)]
    for s in range(steps):
        for stream in range(STREAMS):
            t_f, x_f, x_b = picked((terms_f, prefix_f, prefix_b), stream, lambda place: s - place)
            state, rest = t_f + join_f * x_f, x_b
            if s > 0:
                state = state + keep_f * up[stream][s - 1][0].astype(F32)
                rest = rest + up[stream][s - 1][1].astype(F32)
            up[stream][s] = shift(jnp.stack([state, rest]).astype(BF16), "heads", 1)
            t_b, x_f, x_b = picked((terms_b, prefix_f, prefix_b), stream, lambda place: s - (depth - 1 - place))
            state, rest = t_b + join_b * x_b, x_f
            if s > 0:
                state = state + keep_b * down[stream][s - 1][0].astype(F32)
                rest = rest + down[stream][s - 1][1].astype(F32)
            down[stream][s] = shift(jnp.stack([state, rest]).astype(BF16), "heads", -1)

    from_before, from_after = flag(last_before == first), flag(first_after == last)
    reach_f, reach_b = flag(prior[0] == first), flag(later[0] == last)
    held = ()
    for turn in range(turns):
        befores, afters = [], []
        for stream in range(STREAMS):
            j = turn * STREAMS + stream
            before = [(reach_f, prefix_f[j])]
            after = [(reach_b, prefix_b[j])]
            for place in range(depth):
                here = flag(z == place)
                if place > 0:
                    got = up[stream][turn + place - 1]
                    before.append((here * from_before, got[0]))
                    after.append((here * reach_b, got[1]))
                if place < depth - 1:
                    got = down[stream][turn + depth - 2 - place]
                    after.append((here * from_after, got[0]))
                    before.append((here * reach_f, got[1]))
            befores.append(total(before).astype(BF16))
            afters.append(total(after).astype(BF16))
        held = outputs_of(
            docs_column, docs_row, arrays, jnp.concatenate(befores), jnp.concatenate(afters),
            held, factor, turn * STREAMS * CHUNK, STREAMS * CHUNK,
        )
    return tuple(held)


def solution(mesh):
    tokens = P(("outer", "inner", "heads"), None)
    carry = P("heads", None, None)
    return jax.shard_map(
        shards,
        mesh=mesh,
        in_specs=(tokens,) * 4 + (P(("outer", "inner")), carry, carry),
        out_specs=(tokens,) * 4,
        check_vma=False,
    )
```

time: 363 us -> 235 us (0.65)
  the two profiles are of different devices: /device:TPU:6 before, /device:TPU:0 now
where the time goes in v1:
time: 235 us; the launch traced here: 233 us
  starting transfers between devices  87.4 us (37%)
  waiting for transfers between devices  39.7 us (17%)
  other arithmetic  36.7 us (16%)
  between operations  32.4 us (14%)
  Pallas kernels  26.3 us (11%)
  local copies, waits for them, and re-layouts  11 us (5%)
    ppermute x24, starting transfers between devices, shift(): lax.ppermute(array, axis, [(i, i + step) for i in range(count) if 0 <= i...  62.5 us
    ppermute x24, waiting for transfers between devices, shift(): lax.ppermute(array, axis, [(i, i + step) for i in range(count) if 0 <= i...  30 us
    ppermute x24, starting transfers between devices, swap(): return lax.ppermute(array, axis, [(i, i ^ distance) for i in range(count)])  24.8 us
    pallas_call x4, Pallas kernels, outputs_of(): pl.pallas_call(functools.partial(output_kernel, factor, group), grid=(ste...  16.5 us
    pallas_call x4, Pallas kernels, state_terms(): pl.pallas_call(functools.partial(term_kernel, factor, group), grid=(steps...  9.73 us
    ppermute x24, waiting for transfers between devices, swap(): return lax.ppermute(array, axis, [(i, i ^ distance) for i in range(count)])  9.7 us
    another operation x25, other arithmetic, shards(): down[stream][s] = shift(jnp.stack([state, rest]).astype(BF16), 'heads', -1)  7.42 us
    convert_element_type x8, other arithmetic, shards(): befores.append(total(before).astype(BF16))  6.68 us
  transfers between devices with their start and end apart: 48, of which 18 were waited for; matrix products, arithmetic and copies ran while one was open for 16% of the time, Pallas kernels for 9%

profile of v1, /device:TPU:0, one launch (start us, length us, event | category | flops | bytes accessed | tf_op | source)
XLA Modules:
  0.0 233.4 jit_solution(28197771174772979)
XLA Ops:
  3.5 2.5 %shard_map.105 = (bf16[8,128,128]{2,1,0:T(8,128)(2,1)}, bf16[8,128,128]{2,1,0:T(8,128)(2,1)}) custom-call(s32[128,128]{1,0:T(8,128)} %broadcast_in_dim.7.docs_ref, bf16[128,4096]{1,0:T(8,128)(2,1)} %q_ref.15, bf16[128,4096]{1,0:T(8,128)(2,1)} %k_ref.15, bf16[128,4096]{1,0:T(8,128)(2,1)} %v_ref.15, bf16[128,4096]{1,0:T(8,128)(2,1)} %g_ref.15), custom_call_target="tpu_custom_call" | custom-call | flops 67108864 | bytes 1572864 | tf_op jit(solution)/shard_map/pallas_call | solution.py:77
  7.1 2.4 %shard_map.104 = (bf16[8,128,128]{2,1,0:T(8,128)(2,1)}, bf16[8,128,128]{2,1,0:T(8,128)(2,1)}) custom-call(s32[128,128]{1,0:T(8,128)} %broadcast_in_dim.7.docs_ref, bf16[128,4096]{1,0:T(8,128)(2,1)} %q_ref.15, bf16[128,4096]{1,0:T(8,128)(2,1)} %k_ref.15, bf16[128,4096]{1,0:T(8,128)(2,1)} %v_ref.15, bf16[128,4096]{1,0:T(8,128)(2,1)} %g_ref.15), custom_call_target="tpu_custom_call" | custom-call | flops 67108864 | bytes 1572864 | tf_op jit(solution)/shard_map/pallas_call | solution.py:77
  11.1 2.4 %shard_map.103 = (bf16[8,128,128]{2,1,0:T(8,128)(2,1)}, bf16[8,128,128]{2,1,0:T(8,128)(2,1)}) custom-call(s32[128,128]{1,0:T(8,128)} %broadcast_in_dim.7.docs_ref, bf16[128,4096]{1,0:T(8,128)(2,1)} %q_ref.15, bf16[128,4096]{1,0:T(8,128)(2,1)} %k_ref.15, bf16[128,4096]{1,0:T(8,128)(2,1)} %v_ref.15, bf16[128,4096]{1,0:T(8,128)(2,1)} %g_ref.15), custom_call_target="tpu_custom_call" | custom-call | flops 67108864 | bytes 1572864 | tf_op jit(solution)/shard_map/pallas_call | solution.py:77
  14.7 2.4 %shard_map.102 = (bf16[8,128,128]{2,1,0:T(8,128)(2,1)}, bf16[8,128,128]{2,1,0:T(8,128)(2,1)}) custom-call(s32[128,128]{1,0:T(8,128)} %broadcast_in_dim.7.docs_ref, bf16[128,4096]{1,0:T(8,128)(2,1)} %q_ref.15, bf16[128,4096]{1,0:T(8,128)(2,1)} %k_ref.15, bf16[128,4096]{1,0:T(8,128)(2,1)} %v_ref.15, bf16[128,4096]{1,0:T(8,128)(2,1)} %g_ref.15), custom_call_target="tpu_custom_call" | custom-call | flops 67108864 | bytes 1572864 | tf_op jit(solution)/shard_map/pallas_call | solution.py:77
  31.9 2.6 %collective-permute-start.1 = (f32[2]{0:T(128)S(1)}, f32[2]{0:T(128)S(1)}, u32[]{:S(2)}, u32[]{:S(2)}) collective-permute-start(f32[2]{0:T(128)S(1)} %pad_maximum_fusion.41), channel_id=1, source_target_pairs={{0,8},{8,0},{16,24},{24,16},{1,9},{9,1},{17,25},{25,17},{2,10},{10... | collective-permute-start | bytes 32 | tf_op jit(solution)/shard_map/ppermute | solution.py:28
  34.4 1.5 collective-permute-done.1
  35.9 3.0 %collective-permute-start.3 = (f32[2]{0:T(128)S(1)}, f32[2]{0:T(128)S(1)}, u32[]{:S(2)}, u32[]{:S(2)}) collective-permute-start(f32[2]{0:T(128)S(1)} %pad_maximum_fusion.41), channel_id=1, source_target_pairs={{0,24},{8,16},{16,8},{24,0},{1,25},{9,17},{17,9},{25,1},{2,26},{10... | collective-permute-start | bytes 32 | tf_op jit(solution)/shard_map/ppermute | solution.py:28
  40.8 1.6 collective-permute-start.2
  62.7 1.6 collective-permute-start.20
  64.3 1.6 collective-permute-start.21
  66.6 1.6 collective-permute-start.15
  68.4 1.6 collective-permute-start.16
  70.1 1.3 collective-permute-start.17
  71.4 1.4 collective-permute-done.21
  74.1 1.4 collective-permute-start.11
  76.6 1.8 collective-permute-done.16
  78.4 1.3 collective-permute-start.5
  79.7 1.4 collective-permute-start.6
  82.8 1.5 collective-permute-done.12
  85.7 2.1 collective-permute-done.7
  89.8 3.5 %collective-permute-start.30 = (bf16[2,4,128,128]{3,2,1,0:T(8,128)(2,1)S(1)}, bf16[2,4,128,128]{3,2,1,0:T(8,128)(2,1)S(1)}, u32[]{:S(2)}, u32[]{:S(2)}) collective-permute-start(bf16[2,4,128,128]{3,2,1,0:T(8,128)(2,1)S(1)} %pad_maximum_fusion.14), channel_id=1, source_target_pairs={{0,1},{1,2},{2,3},{4,5},{5,6},{6,7},{8,9},{9,10},{10,11},{12,13},{... | collective-permute-start | bytes 786440 | tf_op jit(solution)/shard_map/ppermute | solution.py:33
  93.4 1.3 collective-permute-start.36
  96.1 5.2 %collective-permute-start.42 = (bf16[2,4,128,128]{3,2,1,0:T(8,128)(2,1)S(1)}, bf16[2,4,128,128]{3,2,1,0:T(8,128)(2,1)S(1)}, u32[]{:S(2)}, u32[]{:S(2)}) collective-permute-start(bf16[2,4,128,128]{3,2,1,0:T(8,128)(2,1)S(1)} %pad_maximum_fusion.26), channel_id=1, source_target_pairs={{0,1},{1,2},{2,3},{4,5},{5,6},{6,7},{8,9},{9,10},{10,11},{12,13},{... | collective-permute-start | bytes 786440 | tf_op jit(solution)/shard_map/ppermute | solution.py:33
  101.4 3.0 %collective-permute-done.36 = bf16[2,4,128,128]{3,2,1,0:T(8,128)(2,1)S(1)} collective-permute-done((bf16[2,4,128,128]{3,2,1,0:T(8,128)(2,1)S(1)}, bf16[2,4,128,128]{3,2,1,0:T(8,128)(2,1)S(1)}, u32[]{:S(2)}, u32[]{:S(2)}) %collective-permute-start.36) | collective-permute-done | bytes 262176 | tf_op jit(solution)/shard_map/ppermute | solution.py:33
  104.4 4.9 %collective-permute-done.24 = bf16[2,4,128,128]{3,2,1,0:T(8,128)(2,1)S(1)} collective-permute-done((bf16[2,4,128,128]{3,2,1,0:T(8,128)(2,1)S(1)}, bf16[2,4,128,128]{3,2,1,0:T(8,128)(2,1)S(1)}, u32[]{:S(2)}, u32[]{:S(2)}) %collective-permute-start.24) | collective-permute-done | bytes 262176 | tf_op jit(solution)/shard_map/ppermute | solution.py:33
  111.1 1.3 collective-permute-start.25
  112.8 5.2 %collective-permute-start.43 = (bf16[2,4,128,128]{3,2,1,0:T(8,128)(2,1)S(1)}, bf16[2,4,128,128]{3,2,1,0:T(8,128)(2,1)S(1)}, u32[]{:S(2)}, u32[]{:S(2)}) collective-permute-start(bf16[2,4,128,128]{3,2,1,0:T(8,128)(2,1)S(1)} %pad_maximum_fusion.27), channel_id=1, source_target_pairs={{0,1},{1,2},{2,3},{4,5},{5,6},{6,7},{8,9},{9,10},{10,11},{12,13},{... | collective-permute-start | bytes 786440 | tf_op jit(solution)/shard_map/ppermute | solution.py:33
  118.0 6.9 %collective-permute-done.25 = bf16[2,4,128,128]{3,2,1,0:T(8,128)(2,1)S(1)} collective-permute-done((bf16[2,4,128,128]{3,2,1,0:T(8,128)(2,1)S(1)}, bf16[2,4,128,128]{3,2,1,0:T(8,128)(2,1)S(1)}, u32[]{:S(2)}, u32[]{:S(2)}) %collective-permute-start.25) | collective-permute-done | bytes 262176 | tf_op jit(solution)/shard_map/ppermute | solution.py:33
  125.2 3.5 %collective-permute-start.31 = (bf16[2,4,128,128]{3,2,1,0:T(8,128)(2,1)S(1)}, bf16[2,4,128,128]{3,2,1,0:T(8,128)(2,1)S(1)}, u32[]{:S(2)}, u32[]{:S(2)}) collective-permute-start(bf16[2,4,128,128]{3,2,1,0:T(8,128)(2,1)S(1)} %pad_maximum_fusion.15), channel_id=1, source_target_pairs={{0,1},{1,2},{2,3},{4,5},{5,6},{6,7},{8,9},{9,10},{10,11},{12,13},{... | collective-permute-start | bytes 786440 | tf_op jit(solution)/shard_map/ppermute | solution.py:33
  132.8 7.2 %collective-permute-done.26 = bf16[2,4,128,128]{3,2,1,0:T(8,128)(2,1)S(1)} collective-permute-done((bf16[2,4,128,128]{3,2,1,0:T(8,128)(2,1)S(1)}, bf16[2,4,128,128]{3,2,1,0:T(8,128)(2,1)S(1)}, u32[]{:S(2)}, u32[]{:S(2)}) %collective-permute-start.26) | collective-permute-done | bytes 262176 | tf_op jit(solution)/shard_map/ppermute | solution.py:33
  140.6 3.5 %collective-permute-start.32 = (bf16[2,4,128,128]{3,2,1,0:T(8,128)(2,1)S(1)}, bf16[2,4,128,128]{3,2,1,0:T(8,128)(2,1)S(1)}, u32[]{:S(2)}, u32[]{:S(2)}) collective-permute-start(bf16[2,4,128,128]{3,2,1,0:T(8,128)(2,1)S(1)} %pad_maximum_fusion.16), channel_id=1, source_target_pairs={{0,1},{1,2},{2,3},{4,5},{5,6},{6,7},{8,9},{9,10},{10,11},{12,13},{... | collective-permute-start | bytes 786440 | tf_op jit(solution)/shard_map/ppermute | solution.py:33
  146.1 4.6 %collective-permute-start.44 = (bf16[2,4,128,128]{3,2,1,0:T(8,128)(2,1)S(1)}, bf16[2,4,128,128]{3,2,1,0:T(8,128)(2,1)S(1)}, u32[]{:S(2)}, u32[]{:S(2)}) collective-permute-start(bf16[2,4,128,128]{3,2,1,0:T(8,128)(2,1)S(1)} %pad_maximum_fusion.28), channel_id=1, source_target_pairs={{0,1},{1,2},{2,3},{4,5},{5,6},{6,7},{8,9},{9,10},{10,11},{12,13},{... | collective-permute-start | bytes 786440 | tf_op jit(solution)/shard_map/ppermute | solution.py:33
  152.0 3.0 %collective-permute-done.27 = bf16[2,4,128,128]{3,2,1,0:T(8,128)(2,1)S(1)} collective-permute-done((bf16[2,4,128,128]{3,2,1,0:T(8,128)(2,1)S(1)}, bf16[2,4,128,128]{3,2,1,0:T(8,128)(2,1)S(1)}, u32[]{:S(2)}, u32[]{:S(2)}) %collective-permute-start.27) | collective-permute-done | bytes 262176 | tf_op jit(solution)/shard_map/ppermute | solution.py:33
  156.1 2.4 %collective-permute-start.33 = (bf16[2,4,128,128]{3,2,1,0:T(8,128)(2,1)}, bf16[2,4,128,128]{3,2,1,0:T(8,128)(2,1)}, u32[]{:S(2)}, u32[]{:S(2)}) collective-permute-start(bf16[2,4,128,128]{3,2,1,0:T(8,128)(2,1)} %pad_maximum_fusion.17), channel_id=1, source_target_pairs={{0,1},{1,2},{2,3},{4,5},{5,6},{6,7},{8,9},{9,10},{10,11},{12,13},{... | collective-permute-start | bytes 786440 | tf_op jit(solution)/shard_map/ppermute | solution.py:33
  166.4 4.1 %shard_map.106 = (bf16[128,4096]{1,0:T(8,128)(2,1)}, bf16[128,4096]{1,0:T(8,128)(2,1)}, bf16[128,4096]{1,0:T(8,128)(2,1)}, bf16[128,4096]{1,0:T(8,128)(2,1)}) custom-call(s32[128,128]{1,0:T(8,128)} %broadcast_in_dim.7.docs_ref, s32[8,128]{1,0:T(8,128)} %broadcast_in_dim.16.row_ref, bf16[128,4096]{1,0:T(8,128)(2,1)} %q_ref.15, bf16[128,4096]{1,0:T(8,128)(2,1)} %k_ref.15, ...), custom_call_target="tpu_custom_call" | custom-call | flops 335544320 | bytes 2621440 | tf_op jit(solution)/shard_map/pallas_call | solution.py:124
  170.5 2.0 collective-permute-done.28
  172.5 2.2 fusion.409
  174.7 3.8 %collective-permute-start.45 = (bf16[2,4,128,128]{3,2,1,0:T(8,128)(2,1)S(1)}, bf16[2,4,128,128]{3,2,1,0:T(8,128)(2,1)S(1)}, u32[]{:S(2)}, u32[]{:S(2)}) collective-permute-start(bf16[2,4,128,128]{3,2,1,0:T(8,128)(2,1)S(1)} %pad_maximum_fusion.29), channel_id=1, source_target_pairs={{0,1},{1,2},{2,3},{4,5},{5,6},{6,7},{8,9},{9,10},{10,11},{12,13},{... | collective-permute-start | bytes 786440 | tf_op jit(solution)/shard_map/ppermute | solution.py:33
  180.8 1.5 collective-permute-done.45
  182.3 1.3 fusion.364
  184.7 5.1 %collective-permute-start.46 = (bf16[2,4,128,128]{3,2,1,0:T(8,128)(2,1)}, bf16[2,4,128,128]{3,2,1,0:T(8,128)(2,1)}, u32[]{:S(2)}, u32[]{:S(2)}) collective-permute-start(bf16[2,4,128,128]{3,2,1,0:T(8,128)(2,1)} %pad_maximum_fusion.30), channel_id=1, source_target_pairs={{0,1},{1,2},{2,3},{4,5},{5,6},{6,7},{8,9},{9,10},{10,11},{12,13},{... | collective-permute-start | bytes 786440 | tf_op jit(solution)/shard_map/ppermute | solution.py:33
  190.5 3.6 %collective-permute-start.34 = (bf16[2,4,128,128]{3,2,1,0:T(8,128)(2,1)}, bf16[2,4,128,128]{3,2,1,0:T(8,128)(2,1)}, u32[]{:S(2)}, u32[]{:S(2)}) collective-permute-start(bf16[2,4,128,128]{3,2,1,0:T(8,128)(2,1)} %pad_maximum_fusion.18), channel_id=1, source_target_pairs={{0,1},{1,2},{2,3},{4,5},{5,6},{6,7},{8,9},{9,10},{10,11},{12,13},{... | collective-permute-start | bytes 786440 | tf_op jit(solution)/shard_map/ppermute | solution.py:33
  195.7 4.2 %shard_map.107 = (bf16[128,4096]{1,0:T(8,128)(2,1)}, bf16[128,4096]{1,0:T(8,128)(2,1)}, bf16[128,4096]{1,0:T(8,128)(2,1)}, bf16[128,4096]{1,0:T(8,128)(2,1)}) custom-call(s32[128,128]{1,0:T(8,128)} %broadcast_in_dim.7.docs_ref, s32[8,128]{1,0:T(8,128)} %broadcast_in_dim.16.row_ref, ...), custom_call_target="tpu_custom_call", output_to_operand_aliasing={{0}: (8, {}), {1}: (9, {}), {2}: (10, {}), {3}: (11, {})} | custom-call | flops 335544320 | bytes 2621440 | tf_op jit(solution)/shard_map/pallas_call | solution.py:124
  199.9 1.3 fusion.213
  206.3 4.6 %collective-permute-start.47 = (bf16[2,4,128,128]{3,2,1,0:T(8,128)(2,1)}, bf16[2,4,128,128]{3,2,1,0:T(8,128)(2,1)S(1)}, u32[]{:S(2)}, u32[]{:S(2)}) collective-permute-start(bf16[2,4,128,128]{3,2,1,0:T(8,128)(2,1)} %pad_maximum_fusion.31), channel_id=1, source_target_pairs={{0,1},{1,2},{2,3},{4,5},{5,6},{6,7},{8,9},{9,10},{10,11},{12,13},{... | collective-permute-start | bytes 786440 | tf_op jit(solution)/shard_map/ppermute | solution.py:33
  212.2 2.3 collective-permute-start.35
  218.6 4.1 %shard_map.108 = (bf16[128,4096]{1,0:T(8,128)(2,1)}, bf16[128,4096]{1,0:T(8,128)(2,1)}, bf16[128,4096]{1,0:T(8,128)(2,1)}, bf16[128,4096]{1,0:T(8,128)(2,1)}) custom-call(s32[128,128]{1,0:T(8,128)} %broadcast_in_dim.7.docs_ref, s32[8,128]{1,0:T(8,128)} %broadcast_in_dim.16.row_ref, ...), custom_call_target="tpu_custom_call", output_to_operand_aliasing={{0}: (8, {}), {1}: (9, {}), {2}: (10, {}), {3}: (11, {})} | custom-call | flops 335544320 | bytes 2621440 | tf_op jit(solution)/shard_map/pallas_call | solution.py:124
  229.2 4.1 %shard_map.109 = (bf16[128,4096]{1,0:T(8,128)(2,1)}, bf16[128,4096]{1,0:T(8,128)(2,1)}, bf16[128,4096]{1,0:T(8,128)(2,1)}, bf16[128,4096]{1,0:T(8,128)(2,1)}) custom-call(s32[128,128]{1,0:T(8,128)} %broadcast_in_dim.7.docs_ref, s32[8,128]{1,0:T(8,128)} %broadcast_in_dim.16.row_ref, ...), custom_call_target="tpu_custom_call", output_to_operand_aliasing={{0}: (8, {}), {1}: (9, {}), {2}: (10, {}), {3}: (11, {})} | custom-call | flops 335544320 | bytes 2621440 | tf_op jit(solution)/shard_map/pallas_call | solution.py:124
  (241 shorter events, 64.8 us)
Async XLA Ops:
  1.7 23.9 %collective-permute-start = (f32[8]{0:T(128)S(1)}, f32[8]{0:T(128)S(1)}, u32[]{:S(2)}, u32[]{:S(2)}) collective-permute-start(f32[8]{0:T(128)S(1)} %pad_maximum_fusion.40), channel_id=1, source_target_pairs={{0,4},{4,0},{1,5},{5,1},{2,6},{6,2},{3,7},{7,3},{8,12},{12,8},{9,1... | collective-permute-start | bytes 104 | tf_op jit(solution)/shard_map/ppermute | solution.py:28
  7.0 55.5 %collective-permute-start.19 = (bf16[2,4,128,128]{3,2,1,0:T(8,128)(2,1)S(1)}, bf16[2,4,128,128]{3,2,1,0:T(8,128)(2,1)S(1)}, u32[]{:S(2)}, u32[]{:S(2)}) collective-permute-start(bf16[2,4,128,128]{3,2,1,0:T(8,128)(2,1)S(1)} %pad_maximum_fusion.6), channel_id=1, source_target_pairs={{0,4},{4,0},{1,5},{5,1},{2,6},{6,2},{3,7},{7,3},{8,12},{12,8},{9,1... | collective-permute-start | bytes 786440 | tf_op jit(solution)/shard_map/ppermute | solution.py:28
  10.6 55.4 %collective-permute-start.14 = (bf16[2,4,128,128]{3,2,1,0:T(8,128)(2,1)S(1)}, bf16[2,4,128,128]{3,2,1,0:T(8,128)(2,1)S(1)}, u32[]{:S(2)}, u32[]{:S(2)}) collective-permute-start(bf16[2,4,128,128]{3,2,1,0:T(8,128)(2,1)S(1)} %pad_maximum_fusion.4), channel_id=1, source_target_pairs={{0,4},{4,0},{1,5},{5,1},{2,6},{6,2},{3,7},{7,3},{8,12},{12,8},{9,1... | collective-permute-start | bytes 786440 | tf_op jit(solution)/shard_map/ppermute | solution.py:28
  14.6 52.0 %collective-permute-start.9 = (bf16[2,4,128,128]{3,2,1,0:T(8,128)(2,1)S(1)}, bf16[2,4,128,128]{3,2,1,0:T(8,128)(2,1)S(1)}, u32[]{:S(2)}, u32[]{:S(2)}) collective-permute-start(bf16[2,4,128,128]{3,2,1,0:T(8,128)(2,1)S(1)} %pad_maximum_fusion.2), channel_id=1, source_target_pairs={{0,4},{4,0},{1,5},{5,1},{2,6},{6,2},{3,7},{7,3},{8,12},{12,8},{9,1... | collective-permute-start | bytes 786440 | tf_op jit(solution)/shard_map/ppermute | solution.py:28
  18.1 50.2 %collective-permute-start.4 = (bf16[2,4,128,128]{3,2,1,0:T(8,128)(2,1)S(1)}, bf16[2,4,128,128]{3,2,1,0:T(8,128)(2,1)S(1)}, u32[]{:S(2)}, u32[]{:S(2)}) collective-permute-start(bf16[2,4,128,128]{3,2,1,0:T(8,128)(2,1)S(1)} %pad_maximum_fusion), channel_id=1, source_target_pairs={{0,4},{4,0},{1,5},{5,1},{2,6},{6,2},{3,7},{7,3},{8,12},{12,8},{9,1... | collective-permute-start | bytes 786440 | tf_op jit(solution)/shard_map/ppermute | solution.py:28
  31.9 4.1 %collective-permute-start.1 = (f32[2]{0:T(128)S(1)}, f32[2]{0:T(128)S(1)}, u32[]{:S(2)}, u32[]{:S(2)}) collective-permute-start(f32[2]{0:T(128)S(1)} %pad_maximum_fusion.41), channel_id=1, source_target_pairs={{0,8},{8,0},{16,24},{24,16},{1,9},{9,1},{17,25},{25,17},{2,10},{10... | collective-permute-start | bytes 32 | tf_op jit(solution)/shard_map/ppermute | solution.py:28
  35.9 4.9 %collective-permute-start.3 = (f32[2]{0:T(128)S(1)}, f32[2]{0:T(128)S(1)}, u32[]{:S(2)}, u32[]{:S(2)}) collective-permute-start(f32[2]{0:T(128)S(1)} %pad_maximum_fusion.41), channel_id=1, source_target_pairs={{0,24},{8,16},{16,8},{24,0},{1,25},{9,17},{17,9},{25,1},{2,26},{10... | collective-permute-start | bytes 32 | tf_op jit(solution)/shard_map/ppermute | solution.py:28
  40.8 3.6 %collective-permute-start.2 = (f32[2]{0:T(128)S(1)}, f32[2]{0:T(128)S(1)}, u32[]{:S(2)}, u32[]{:S(2)}) collective-permute-start(f32[2]{0:T(128)S(1)} %pad_maximum_fusion.41), channel_id=1, source_target_pairs={{0,16},{8,24},{16,0},{24,8},{1,17},{9,25},{17,1},{25,9},{2,18},{10... | collective-permute-start | bytes 32 | tf_op jit(solution)/shard_map/ppermute | solution.py:28
  62.7 7.4 %collective-permute-start.20 = (bf16[4,128,128]{2,1,0:T(8,128)(2,1)S(1)}, bf16[4,128,128]{2,1,0:T(8,128)(2,1)S(1)}, u32[]{:S(2)}, u32[]{:S(2)}) collective-permute-start(bf16[4,128,128]{2,1,0:T(8,128)(2,1)S(1)} %get-tuple-element.78), channel_id=1, source_target_pairs={{0,8},{8,0},{16,24},{24,16},{1,9},{9,1},{17,25},{25,17},{2,10},{10... | collective-permute-start | bytes 393224 | tf_op jit(solution)/shard_map/ppermute | solution.py:28
  64.3 8.5 %collective-permute-start.21 = (bf16[4,128,128]{2,1,0:T(8,128)(2,1)S(1)}, bf16[4,128,128]{2,1,0:T(8,128)(2,1)S(1)}, u32[]{:S(2)}, u32[]{:S(2)}) collective-permute-start(bf16[4,128,128]{2,1,0:T(8,128)(2,1)S(1)} %get-tuple-element.157), channel_id=1, source_target_pairs={{0,16},{8,24},{16,0},{24,8},{1,17},{9,25},{17,1},{25,9},{2,18},{10... | collective-permute-start | bytes 393224 | tf_op jit(solution)/shard_map/ppermute | solution.py:28
  65.9 8.2 %collective-permute-start.22 = (bf16[4,128,128]{2,1,0:T(8,128)(2,1)S(1)}, bf16[4,128,128]{2,1,0:T(8,128)(2,1)S(1)}, u32[]{:S(2)}, u32[]{:S(2)}) collective-permute-start(bf16[4,128,128]{2,1,0:T(8,128)(2,1)S(1)} %get-tuple-element.158), channel_id=1, source_target_pairs={{0,24},{8,16},{16,8},{24,0},{1,25},{9,17},{17,9},{25,1},{2,26},{10... | collective-permute-start | bytes 393224 | tf_op jit(solution)/shard_map/ppermute | solution.py:28
  66.6 9.0 %collective-permute-start.15 = (bf16[4,128,128]{2,1,0:T(8,128)(2,1)S(1)}, bf16[4,128,128]{2,1,0:T(8,128)(2,1)S(1)}, u32[]{:S(2)}, u32[]{:S(2)}) collective-permute-start(bf16[4,128,128]{2,1,0:T(8,128)(2,1)S(1)} %get-tuple-element.81), channel_id=1, source_target_pairs={{0,8},{8,0},{16,24},{24,16},{1,9},{9,1},{17,25},{25,17},{2,10},{10... | collective-permute-start | bytes 393224 | tf_op jit(solution)/shard_map/ppermute | solution.py:28
  68.4 10.0 %collective-permute-start.16 = (bf16[4,128,128]{2,1,0:T(8,128)(2,1)S(1)}, bf16[4,128,128]{2,1,0:T(8,128)(2,1)S(1)}, u32[]{:S(2)}, u32[]{:S(2)}) collective-permute-start(bf16[4,128,128]{2,1,0:T(8,128)(2,1)S(1)} %get-tuple-element.155), channel_id=1, source_target_pairs={{0,16},{8,24},{16,0},{24,8},{1,17},{9,25},{17,1},{25,9},{2,18},{10... | collective-permute-start | bytes 393224 | tf_op jit(solution)/shard_map/ppermute | solution.py:28
  70.1 9.6 %collective-permute-start.17 = (bf16[4,128,128]{2,1,0:T(8,128)(2,1)S(1)}, bf16[4,128,128]{2,1,0:T(8,128)(2,1)S(1)}, u32[]{:S(2)}, u32[]{:S(2)}) collective-permute-start(bf16[4,128,128]{2,1,0:T(8,128)(2,1)S(1)} %get-tuple-element.156), channel_id=1, source_target_pairs={{0,24},{8,16},{16,8},{24,0},{1,25},{9,17},{17,9},{25,1},{2,26},{10... | collective-permute-start | bytes 393224 | tf_op jit(solution)/shard_map/ppermute | solution.py:28
  72.8 9.0 %collective-permute-start.10 = (bf16[4,128,128]{2,1,0:T(8,128)(2,1)S(1)}, bf16[4,128,128]{2,1,0:T(8,128)(2,1)S(1)}, u32[]{:S(2)}, u32[]{:S(2)}) collective-permute-start(bf16[4,128,128]{2,1,0:T(8,128)(2,1)S(1)} %get-tuple-element.84), channel_id=1, source_target_pairs={{0,8},{8,0},{16,24},{24,16},{1,9},{9,1},{17,25},{25,17},{2,10},{10... | collective-permute-start | bytes 393224 | tf_op jit(solution)/shard_map/ppermute | solution.py:28
  74.1 8.7 %collective-permute-start.11 = (bf16[4,128,128]{2,1,0:T(8,128)(2,1)S(1)}, bf16[4,128,128]{2,1,0:T(8,128)(2,1)S(1)}, u32[]{:S(2)}, u32[]{:S(2)}) collective-permute-start(bf16[4,128,128]{2,1,0:T(8,128)(2,1)S(1)} %get-tuple-element.153), channel_id=1, source_target_pairs={{0,16},{8,24},{16,0},{24,8},{1,17},{9,25},{17,1},{25,9},{2,18},{10... | collective-permute-start | bytes 393224 | tf_op jit(solution)/shard_map/ppermute | solution.py:28
  75.6 8.7 %collective-permute-start.12 = (bf16[4,128,128]{2,1,0:T(8,128)(2,1)S(1)}, bf16[4,128,128]{2,1,0:T(8,128)(2,1)S(1)}, u32[]{:S(2)}, u32[]{:S(2)}) collective-permute-start(bf16[4,128,128]{2,1,0:T(8,128)(2,1)S(1)} %get-tuple-element.154), channel_id=1, source_target_pairs={{0,24},{8,16},{16,8},{24,0},{1,25},{9,17},{17,9},{25,1},{2,26},{10... | collective-permute-start | bytes 393224 | tf_op jit(solution)/shard_map/ppermute | solution.py:28
  78.4 6.4 %collective-permute-start.5 = (bf16[4,128,128]{2,1,0:T(8,128)(2,1)S(1)}, bf16[4,128,128]{2,1,0:T(8,128)(2,1)S(1)}, u32[]{:S(2)}, u32[]{:S(2)}) collective-permute-start(bf16[4,128,128]{2,1,0:T(8,128)(2,1)S(1)} %get-tuple-element.87), channel_id=1, source_target_pairs={{0,8},{8,0},{16,24},{24,16},{1,9},{9,1},{17,25},{25,17},{2,10},{10... | collective-permute-start | bytes 393224 | tf_op jit(solution)/shard_map/ppermute | solution.py:28
  79.7 6.0 %collective-permute-start.6 = (bf16[4,128,128]{2,1,0:T(8,128)(2,1)S(1)}, bf16[4,128,128]{2,1,0:T(8,128)(2,1)S(1)}, u32[]{:S(2)}, u32[]{:S(2)}) collective-permute-start(bf16[4,128,128]{2,1,0:T(8,128)(2,1)S(1)} %get-tuple-element.151), channel_id=1, source_target_pairs={{0,16},{8,24},{16,0},{24,8},{1,17},{9,25},{17,1},{25,9},{2,18},{10... | collective-permute-start | bytes 393224 | tf_op jit(solution)/shard_map/ppermute | solution.py:28
  81.8 5.9 %collective-permute-start.7 = (bf16[4,128,128]{2,1,0:T(8,128)(2,1)S(1)}, bf16[4,128,128]{2,1,0:T(8,128)(2,1)S(1)}, u32[]{:S(2)}, u32[]{:S(2)}) collective-permute-start(bf16[4,128,128]{2,1,0:T(8,128)(2,1)S(1)} %get-tuple-element.152), channel_id=1, source_target_pairs={{0,24},{8,16},{16,8},{24,0},{1,25},{9,17},{17,9},{25,1},{2,26},{10... | collective-permute-start | bytes 393224 | tf_op jit(solution)/shard_map/ppermute | solution.py:28
  82.8 5.5 %collective-permute-start.23 = (bf16[2,4,128,128]{3,2,1,0:T(8,128)(2,1)S(1)}, bf16[2,4,128,128]{3,2,1,0:T(8,128)(2,1)S(1)}, u32[]{:S(2)}, u32[]{:S(2)}) collective-permute-start(bf16[2,4,128,128]{3,2,1,0:T(8,128)(2,1)S(1)} %pad_maximum_fusion.7), channel_id=1, source_target_pairs={{0,4},{4,0},{1,5},{5,1},{2,6},{6,2},{3,7},{7,3},{8,12},{12,8},{9,1... | collective-permute-start | bytes 786440 | tf_op jit(solution)/shard_map/ppermute | solution.py:28
  84.3 10.4 %collective-permute-start.18 = (bf16[2,4,128,128]{3,2,1,0:T(8,128)(2,1)S(1)}, bf16[2,4,128,128]{3,2,1,0:T(8,128)(2,1)S(1)}, u32[]{:S(2)}, u32[]{:S(2)}) collective-permute-start(bf16[2,4,128,128]{3,2,1,0:T(8,128)(2,1)S(1)} %pad_maximum_fusion.5), channel_id=1, source_target_pairs={{0,4},{4,0},{1,5},{5,1},{2,6},{6,2},{3,7},{7,3},{8,12},{12,8},{9,1... | collective-permute-start | bytes 786440 | tf_op jit(solution)/shard_map/ppermute | solution.py:28
  84.7 11.4 %collective-permute-start.13 = (bf16[2,4,128,128]{3,2,1,0:T(8,128)(2,1)S(1)}, bf16[2,4,128,128]{3,2,1,0:T(8,128)(2,1)S(1)}, u32[]{:S(2)}, u32[]{:S(2)}) collective-permute-start(bf16[2,4,128,128]{3,2,1,0:T(8,128)(2,1)S(1)} %pad_maximum_fusion.3), channel_id=1, source_target_pairs={{0,4},{4,0},{1,5},{5,1},{2,6},{6,2},{3,7},{7,3},{8,12},{12,8},{9,1... | collective-permute-start | bytes 786440 | tf_op jit(solution)/shard_map/ppermute | solution.py:28
  88.2 13.2 %collective-permute-start.8 = (bf16[2,4,128,128]{3,2,1,0:T(8,128)(2,1)S(1)}, bf16[2,4,128,128]{3,2,1,0:T(8,128)(2,1)S(1)}, u32[]{:S(2)}, u32[]{:S(2)}) collective-permute-start(bf16[2,4,128,128]{3,2,1,0:T(8,128)(2,1)S(1)} %pad_maximum_fusion.1), channel_id=1, source_target_pairs={{0,4},{4,0},{1,5},{5,1},{2,6},{6,2},{3,7},{7,3},{8,12},{12,8},{9,1... | collective-permute-start | bytes 786440 | tf_op jit(solution)/shard_map/ppermute | solution.py:28
  89.8 22.6 %collective-permute-start.30 = (bf16[2,4,128,128]{3,2,1,0:T(8,128)(2,1)S(1)}, bf16[2,4,128,128]{3,2,1,0:T(8,128)(2,1)S(1)}, u32[]{:S(2)}, u32[]{:S(2)}) collective-permute-start(bf16[2,4,128,128]{3,2,1,0:T(8,128)(2,1)S(1)} %pad_maximum_fusion.14), channel_id=1, source_target_pairs={{0,1},{1,2},{2,3},{4,5},{5,6},{6,7},{8,9},{9,10},{10,11},{12,13},{... | collective-permute-start | bytes 786440 | tf_op jit(solution)/shard_map/ppermute | solution.py:33
  93.4 11.0 %collective-permute-start.36 = (bf16[2,4,128,128]{3,2,1,0:T(8,128)(2,1)S(1)}, bf16[2,4,128,128]{3,2,1,0:T(8,128)(2,1)S(1)}, u32[]{:S(2)}, u32[]{:S(2)}) collective-permute-start(bf16[2,4,128,128]{3,2,1,0:T(8,128)(2,1)S(1)} %pad_maximum_fusion.20), channel_id=1, source_target_pairs={{1,0},{2,1},{3,2},{5,4},{6,5},{7,6},{9,8},{10,9},{11,10},{13,12},{... | collective-permute-start | bytes 786440 | tf_op jit(solution)/shard_map/ppermute | solution.py:33
  94.7 14.6 %collective-permute-start.24 = (bf16[2,4,128,128]{3,2,1,0:T(8,128)(2,1)S(1)}, bf16[2,4,128,128]{3,2,1,0:T(8,128)(2,1)S(1)}, u32[]{:S(2)}, u32[]{:S(2)}) collective-permute-start(bf16[2,4,128,128]{3,2,1,0:T(8,128)(2,1)S(1)} %pad_maximum_fusion.8), channel_id=1, source_target_pairs={{1,0},{2,1},{3,2},{5,4},{6,5},{7,6},{9,8},{10,9},{11,10},{13,12},{... | collective-permute-start | bytes 786440 | tf_op jit(solution)/shard_map/ppermute | solution.py:33
  96.1 16.3 %collective-permute-start.42 = (bf16[2,4,128,128]{3,2,1,0:T(8,128)(2,1)S(1)}, bf16[2,4,128,128]{3,2,1,0:T(8,128)(2,1)S(1)}, u32[]{:S(2)}, u32[]{:S(2)}) collective-permute-start(bf16[2,4,128,128]{3,2,1,0:T(8,128)(2,1)S(1)} %pad_maximum_fusion.26), channel_id=1, source_target_pairs={{0,1},{1,2},{2,3},{4,5},{5,6},{6,7},{8,9},{9,10},{10,11},{12,13},{... | collective-permute-start | bytes 786440 | tf_op jit(solution)/shard_map/ppermute | solution.py:33
  109.8 18.9 %collective-permute-start.37 = (bf16[2,4,128,128]{3,2,1,0:T(8,128)(2,1)S(1)}, bf16[2,4,128,128]{3,2,1,0:T(8,128)(2,1)S(1)}, u32[]{:S(2)}, u32[]{:S(2)}) collective-permute-start(bf16[2,4,128,128]{3,2,1,0:T(8,128)(2,1)S(1)} %pad_maximum_fusion.21), channel_id=1, source_target_pairs={{1,0},{2,1},{3,2},{5,4},{6,5},{7,6},{9,8},{10,9},{11,10},{13,12},{... | collective-permute-start | bytes 786440 | tf_op jit(solution)/shard_map/ppermute | solution.py:33
  111.1 13.8 %collective-permute-start.25 = (bf16[2,4,128,128]{3,2,1,0:T(8,128)(2,1)S(1)}, bf16[2,4,128,128]{3,2,1,0:T(8,128)(2,1)S(1)}, u32[]{:S(2)}, u32[]{:S(2)}) collective-permute-start(bf16[2,4,128,128]{3,2,1,0:T(8,128)(2,1)S(1)} %pad_maximum_fusion.9), channel_id=1, source_target_pairs={{1,0},{2,1},{3,2},{5,4},{6,5},{7,6},{9,8},{10,9},{11,10},{13,12},{... | collective-permute-start | bytes 786440 | tf_op jit(solution)/shard_map/ppermute | solution.py:33
  112.8 27.4 %collective-permute-start.43 = (bf16[2,4,128,128]{3,2,1,0:T(8,128)(2,1)S(1)}, bf16[2,4,128,128]{3,2,1,0:T(8,128)(2,1)S(1)}, u32[]{:S(2)}, u32[]{:S(2)}) collective-permute-start(bf16[2,4,128,128]{3,2,1,0:T(8,128)(2,1)S(1)} %pad_maximum_fusion.27), channel_id=1, source_target_pairs={{0,1},{1,2},{2,3},{4,5},{5,6},{6,7},{8,9},{9,10},{10,11},{12,13},{... | collective-permute-start | bytes 786440 | tf_op jit(solution)/shard_map/ppermute | solution.py:33
  125.2 7.6 %collective-permute-start.31 = (bf16[2,4,128,128]{3,2,1,0:T(8,128)(2,1)S(1)}, bf16[2,4,128,128]{3,2,1,0:T(8,128)(2,1)S(1)}, u32[]{:S(2)}, u32[]{:S(2)}) collective-permute-start(bf16[2,4,128,128]{3,2,1,0:T(8,128)(2,1)S(1)} %pad_maximum_fusion.15), channel_id=1, source_target_pairs={{0,1},{1,2},{2,3},{4,5},{5,6},{6,7},{8,9},{9,10},{10,11},{12,13},{... | collective-permute-start | bytes 786440 | tf_op jit(solution)/shard_map/ppermute | solution.py:33
  128.9 11.1 %collective-permute-start.26 = (bf16[2,4,128,128]{3,2,1,0:T(8,128)(2,1)S(1)}, bf16[2,4,128,128]{3,2,1,0:T(8,128)(2,1)S(1)}, u32[]{:S(2)}, u32[]{:S(2)}) collective-permute-start(bf16[2,4,128,128]{3,2,1,0:T(8,128)(2,1)S(1)} %pad_maximum_fusion.10), channel_id=1, source_target_pairs={{1,0},{2,1},{3,2},{5,4},{6,5},{7,6},{9,8},{10,9},{11,10},{13,12},{... | collective-permute-start | bytes 786440 | tf_op jit(solution)/shard_map/ppermute | solution.py:33
  130.4 13.7 %collective-permute-start.38 = (bf16[2,4,128,128]{3,2,1,0:T(8,128)(2,1)S(1)}, bf16[2,4,128,128]{3,2,1,0:T(8,128)(2,1)S(1)}, u32[]{:S(2)}, u32[]{:S(2)}) collective-permute-start(bf16[2,4,128,128]{3,2,1,0:T(8,128)(2,1)S(1)} %pad_maximum_fusion.22), channel_id=1, source_target_pairs={{1,0},{2,1},{3,2},{5,4},{6,5},{7,6},{9,8},{10,9},{11,10},{13,12},{... | collective-permute-start | bytes 786440 | tf_op jit(solution)/shard_map/ppermute | solution.py:33
  140.6 11.3 %collective-permute-start.32 = (bf16[2,4,128,128]{3,2,1,0:T(8,128)(2,1)S(1)}, bf16[2,4,128,128]{3,2,1,0:T(8,128)(2,1)S(1)}, u32[]{:S(2)}, u32[]{:S(2)}) collective-permute-start(bf16[2,4,128,128]{3,2,1,0:T(8,128)(2,1)S(1)} %pad_maximum_fusion.16), channel_id=1, source_target_pairs={{0,1},{1,2},{2,3},{4,5},{5,6},{6,7},{8,9},{9,10},{10,11},{12,13},{... | collective-permute-start | bytes 786440 | tf_op jit(solution)/shard_map/ppermute | solution.py:33
  144.4 10.6 %collective-permute-start.27 = (bf16[2,4,128,128]{3,2,1,0:T(8,128)(2,1)S(1)}, bf16[2,4,128,128]{3,2,1,0:T(8,128)(2,1)S(1)}, u32[]{:S(2)}, u32[]{:S(2)}) collective-permute-start(bf16[2,4,128,128]{3,2,1,0:T(8,128)(2,1)S(1)} %pad_maximum_fusion.11), channel_id=1, source_target_pairs={{1,0},{2,1},{3,2},{5,4},{6,5},{7,6},{9,8},{10,9},{11,10},{13,12},{... | collective-permute-start | bytes 786440 | tf_op jit(solution)/shard_map/ppermute | solution.py:33
  146.1 13.2 %collective-permute-start.44 = (bf16[2,4,128,128]{3,2,1,0:T(8,128)(2,1)S(1)}, bf16[2,4,128,128]{3,2,1,0:T(8,128)(2,1)S(1)}, u32[]{:S(2)}, u32[]{:S(2)}) collective-permute-start(bf16[2,4,128,128]{3,2,1,0:T(8,128)(2,1)S(1)} %pad_maximum_fusion.28), channel_id=1, source_target_pairs={{0,1},{1,2},{2,3},{4,5},{5,6},{6,7},{8,9},{9,10},{10,11},{12,13},{... | collective-permute-start | bytes 786440 | tf_op jit(solution)/shard_map/ppermute | solution.py:33
  150.7 8.3 %collective-permute-start.39 = (bf16[2,4,128,128]{3,2,1,0:T(8,128)(2,1)S(1)}, bf16[2,4,128,128]{3,2,1,0:T(8,128)(2,1)S(1)}, u32[]{:S(2)}, u32[]{:S(2)}) collective-permute-start(bf16[2,4,128,128]{3,2,1,0:T(8,128)(2,1)S(1)} %pad_maximum_fusion.23), channel_id=1, source_target_pairs={{1,0},{2,1},{3,2},{5,4},{6,5},{7,6},{9,8},{10,9},{11,10},{13,12},{... | collective-permute-start | bytes 786440 | tf_op jit(solution)/shard_map/ppermute | solution.py:33
  156.1 22.4 %collective-permute-start.33 = (bf16[2,4,128,128]{3,2,1,0:T(8,128)(2,1)}, bf16[2,4,128,128]{3,2,1,0:T(8,128)(2,1)}, u32[]{:S(2)}, u32[]{:S(2)}) collective-permute-start(bf16[2,4,128,128]{3,2,1,0:T(8,128)(2,1)} %pad_maximum_fusion.17), channel_id=1, source_target_pairs={{0,1},{1,2},{2,3},{4,5},{5,6},{6,7},{8,9},{9,10},{10,11},{12,13},{... | collective-permute-start | bytes 786440 | tf_op jit(solution)/shard_map/ppermute | solution.py:33
  160.2 10.3 %collective-permute-start.40 = (bf16[2,4,128,128]{3,2,1,0:T(8,128)(2,1)S(1)}, bf16[2,4,128,128]{3,2,1,0:T(8,128)(2,1)}, u32[]{:S(2)}, u32[]{:S(2)}) collective-permute-start(bf16[2,4,128,128]{3,2,1,0:T(8,128)(2,1)S(1)} %pad_maximum_fusion.24), channel_id=1, source_target_pairs={{1,0},{2,1},{3,2},{5,4},{6,5},{7,6},{9,8},{10,9},{11,10},{13,12},{... | collective-permute-start | bytes 786440 | tf_op jit(solution)/shard_map/ppermute | solution.py:33
  162.2 10.3 %collective-permute-start.28 = (bf16[2,4,128,128]{3,2,1,0:T(8,128)(2,1)}, bf16[2,4,128,128]{3,2,1,0:T(8,128)(2,1)}, u32[]{:S(2)}, u32[]{:S(2)}) collective-permute-start(bf16[2,4,128,128]{3,2,1,0:T(8,128)(2,1)} %pad_maximum_fusion.12), channel_id=1, source_target_pairs={{1,0},{2,1},{3,2},{5,4},{6,5},{7,6},{9,8},{10,9},{11,10},{13,12},{... | collective-permute-start | bytes 786440 | tf_op jit(solution)/shard_map/ppermute | solution.py:33
  174.7 7.7 %collective-permute-start.45 = (bf16[2,4,128,128]{3,2,1,0:T(8,128)(2,1)S(1)}, bf16[2,4,128,128]{3,2,1,0:T(8,128)(2,1)S(1)}, u32[]{:S(2)}, u32[]{:S(2)}) collective-permute-start(bf16[2,4,128,128]{3,2,1,0:T(8,128)(2,1)S(1)} %pad_maximum_fusion.29), channel_id=1, source_target_pairs={{0,1},{1,2},{2,3},{4,5},{5,6},{6,7},{8,9},{9,10},{10,11},{12,13},{... | collective-permute-start | bytes 786440 | tf_op jit(solution)/shard_map/ppermute | solution.py:33
  184.7 15.2 %collective-permute-start.46 = (bf16[2,4,128,128]{3,2,1,0:T(8,128)(2,1)}, bf16[2,4,128,128]{3,2,1,0:T(8,128)(2,1)}, u32[]{:S(2)}, u32[]{:S(2)}) collective-permute-start(bf16[2,4,128,128]{3,2,1,0:T(8,128)(2,1)} %pad_maximum_fusion.30), channel_id=1, source_target_pairs={{0,1},{1,2},{2,3},{4,5},{5,6},{6,7},{8,9},{9,10},{10,11},{12,13},{... | collective-permute-start | bytes 786440 | tf_op jit(solution)/shard_map/ppermute | solution.py:33
  190.5 14.0 %collective-permute-start.34 = (bf16[2,4,128,128]{3,2,1,0:T(8,128)(2,1)}, bf16[2,4,128,128]{3,2,1,0:T(8,128)(2,1)}, u32[]{:S(2)}, u32[]{:S(2)}) collective-permute-start(bf16[2,4,128,128]{3,2,1,0:T(8,128)(2,1)} %pad_maximum_fusion.18), channel_id=1, source_target_pairs={{0,1},{1,2},{2,3},{4,5},{5,6},{6,7},{8,9},{9,10},{10,11},{12,13},{... | collective-permute-start | bytes 786440 | tf_op jit(solution)/shard_map/ppermute | solution.py:33
  201.9 20.8 %collective-permute-start.41 = (bf16[2,4,128,128]{3,2,1,0:T(8,128)(2,1)}, bf16[2,4,128,128]{3,2,1,0:T(8,128)(2,1)}, u32[]{:S(2)}, u32[]{:S(2)}) collective-permute-start(bf16[2,4,128,128]{3,2,1,0:T(8,128)(2,1)} %pad_maximum_fusion.25), channel_id=1, source_target_pairs={{1,0},{2,1},{3,2},{5,4},{6,5},{7,6},{9,8},{10,9},{11,10},{13,12},{... | collective-permute-start | bytes 786440 | tf_op jit(solution)/shard_map/ppermute | solution.py:33
  206.3 16.4 %collective-permute-start.47 = (bf16[2,4,128,128]{3,2,1,0:T(8,128)(2,1)}, bf16[2,4,128,128]{3,2,1,0:T(8,128)(2,1)S(1)}, u32[]{:S(2)}, u32[]{:S(2)}) collective-permute-start(bf16[2,4,128,128]{3,2,1,0:T(8,128)(2,1)} %pad_maximum_fusion.31), channel_id=1, source_target_pairs={{0,1},{1,2},{2,3},{4,5},{5,6},{6,7},{8,9},{9,10},{10,11},{12,13},{... | collective-permute-start | bytes 786440 | tf_op jit(solution)/shard_map/ppermute | solution.py:33
  212.2 11.8 %collective-permute-start.35 = (bf16[2,4,128,128]{3,2,1,0:T(8,128)(2,1)S(1)}, bf16[2,4,128,128]{3,2,1,0:T(8,128)(2,1)S(1)}, u32[]{:S(2)}, u32[]{:S(2)}) collective-permute-start(bf16[2,4,128,128]{3,2,1,0:T(8,128)(2,1)S(1)} %pad_maximum_fusion.19), channel_id=1, source_target_pairs={{0,1},{1,2},{2,3},{4,5},{5,6},{6,7},{8,9},{9,10},{10,11},{12,13},{... | collective-permute-start | bytes 786440 | tf_op jit(solution)/shard_map/ppermute | solution.py:33
  215.8 8.3 %collective-permute-start.29 = (bf16[2,4,128,128]{3,2,1,0:T(8,128)(2,1)S(1)}, bf16[2,4,128,128]{3,2,1,0:T(8,128)(2,1)S(1)}, u32[]{:S(2)}, u32[]{:S(2)}) collective-permute-start(bf16[2,4,128,128]{3,2,1,0:T(8,128)(2,1)S(1)} %pad_maximum_fusion.13), channel_id=1, source_target_pairs={{1,0},{2,1},{3,2},{5,4},{6,5},{7,6},{9,8},{10,9},{11,10},{13,12},{... | collective-permute-start | bytes 786440 | tf_op jit(solution)/shard_map/ppermute | solution.py:33
  (37 other events, 369.2 us)

commit v2 on v0

v2 whole, which is shorter than its diff:
```python
import functools

import jax
import jax.numpy as jnp
from jax import lax
from jax.experimental import pallas as pl
from jax.experimental.pallas import tpu as pltpu
from jax.sharding import PartitionSpec as P

DH = 128
SPAN = 128
LABELS = 16
DEPTH = 4
F32 = jnp.float32
BF16 = jnp.bfloat16
VMEM = pl.BlockSpec(memory_space=pltpu.VMEM)
SMEM = pl.BlockSpec(memory_space=pltpu.SMEM)
ANY = pl.BlockSpec(memory_space=pl.ANY)
LIMIT = 24 * 1024 * 1024


def pairs(array, axis, distance):
    count = lax.axis_size(axis)
    return lax.ppermute(array, axis, [(i, i ^ distance) for i in range(count)])


def transposed_dot(a, b):
    return lax.dot_general(a, b, (((0,), (0,)), ((), ())), preferred_element_type=F32)


def dot_transposed(a, b):
    return lax.dot_general(a, b, (((1,), (1,)), ((), ())), preferred_element_type=F32)


def dot(a, b):
    return lax.dot_general(a, b, (((1,), (0,)), ((), ())), preferred_element_type=F32)


def flag(row):
    return jnp.where(row, 1.0, 0.0).astype(F32)


def call(kernel, operands, out_shape, flops, scratch=(), aliases=None, specs=None, out_specs=None):
    size = sum(a.size * a.dtype.itemsize for a in operands) + sum(a.size * a.dtype.itemsize for a in out_shape)
    return pl.pallas_call(
        kernel,
        in_specs=specs,
        out_specs=out_specs or [VMEM] * len(out_shape),
        out_shape=out_shape,
        scratch_shapes=list(scratch),
        input_output_aliases=aliases or {},
        compiler_params=pltpu.CompilerParams(vmem_limit_bytes=LIMIT),
        cost_estimate=pl.CostEstimate(flops=flops, bytes_accessed=size, transcendentals=0),
    )(*operands)


def document_masks(docs):
    return docs == docs[0:1], docs == docs[SPAN - 1 : SPAN]


def term_kernel(factor, first, part, ids, docs_ref, q_ref, k_ref, v_ref, g_ref, *outs):
    c = ids[1]
    in_first, in_last = document_masks(docs_ref[...])
    for t, out in enumerate(outs):
        base = first + (c ^ t) * part
        for i in range(part):
            at = pl.ds(pl.multiple_of((base + i) * DH, DH), DH)
            keys = jnp.where(in_last, k_ref[:, at], 0)
            queries = jnp.where(in_first, q_ref[:, at], 0)
            out[0, i] = (transposed_dot(keys, v_ref[:, at]) * factor).astype(BF16)
            out[1, i] = (transposed_dot(queries, g_ref[:, at]) * factor).astype(BF16)


def own_row(ref, at):
    return ref[pl.ds(at, 1), :]


def sum_kernel(inner, part, levels, ids, *refs):
    labels, terms, outs = refs[:inner], refs[inner : 2 * inner], refs[2 * inner :]
    o, z = ids[0], ids[2]
    newest = functools.reduce(jnp.maximum, [l[2 * DEPTH - 1 : 2 * DEPTH, :] for l in labels])
    oldest = functools.reduce(jnp.minimum, [l[0:1, :] for l in labels])
    keep_f = [flag(own_row(l, DEPTH + z) == newest) for l in labels]
    keep_b = [flag(own_row(l, z) == oldest) for l in labels]
    low = [((o >> level) & 1) == 0 for level in range(levels)]
    for i in range(part):
        sum_f = sum(m * r[0, i].astype(F32) for m, r in zip(keep_f, terms)).astype(BF16)
        sum_b = sum(m * r[1, i].astype(F32) for m, r in zip(keep_b, terms)).astype(BF16)
        for chosen, out in zip(low, outs):
            out[i * DH : (i + 1) * DH, :] = jnp.where(chosen, sum_f, sum_b)
    rows = lax.broadcasted_iota(jnp.int32, (LABELS, DH), 0)
    marks = jnp.where(rows < LABELS // 2, jnp.broadcast_to(newest, (LABELS, DH)), jnp.broadcast_to(oldest, (LABELS, DH)))
    for out in outs:
        out[part * DH :, :] = marks.astype(BF16)


def prefix_kernel(factor, first, part, inner, outer, ids, carry_ref, cot_ref, *refs):
    labels, terms, fans = refs[:inner], refs[inner : 2 * inner], refs[2 * inner : 2 * inner + outer - 1]
    outs, edge_ref = refs[2 * inner + outer - 1 : -1], refs[-1]
    o, c, z = ids[0], ids[1], ids[2]
    held = carry_ref.shape[0]
    group_first = [l[0:1, :] for l in labels]
    group_last = [l[2 * DEPTH - 1 : 2 * DEPTH, :] for l in labels]
    block_first = [own_row(l, z) for l in labels]
    block_last = [own_row(l, DEPTH + z) for l in labels]
    marks = [r[part * DH : part * DH + LABELS, :].astype(F32) for r in fans]
    outer_last = [m[0:1] for m in marks]
    outer_first = [m[LABELS // 2 : LABELS // 2 + 1] for m in marks]
    newest = functools.reduce(jnp.maximum, group_last + outer_last)
    prior_base, later_base = jnp.zeros_like(newest), newest
    earlier = [(o ^ (d + 1)) < o for d in range(outer - 1)]
    for d in range(outer - 1):
        prior_base = jnp.maximum(prior_base, jnp.where(earlier[d], outer_last[d], 0.0))
        later_base = jnp.minimum(later_base, jnp.where(earlier[d], newest, outer_first[d]))
    head = first + c * part
    priors, laters, plans = [], [], []
    for t in range(inner):
        prior, later = prior_base, later_base
        for d in range(inner):
            if d != t:
                before = (c ^ d) < (c ^ t)
                prior = jnp.maximum(prior, jnp.where(before, group_last[d], 0.0))
                later = jnp.minimum(later, jnp.where(before, newest, group_first[d]))
        forward = [(flag(jnp.logical_and(earlier[d], outer_last[d] == prior)), fans[d], None) for d in range(outer - 1)]
        backward = [
            (flag(jnp.logical_and(jnp.logical_not(earlier[d]), outer_first[d] == later)), fans[d], None)
            for d in range(outer - 1)
        ]
        for d in range(inner):
            if d != t:
                before = (c ^ d) < (c ^ t)
                forward.append((flag(jnp.logical_and(before, block_last[d] == prior)), terms[d], 0))
                backward.append((flag(jnp.logical_and(jnp.logical_not(before), block_first[d] == later)), terms[d], 1))
        priors.append(prior)
        laters.append(later)
        plans.append((forward, backward, flag(prior == 0.0), flag(later == newest) * factor))
    for i in range(part):
        place = head + i - z * held
        mine = jnp.logical_and(place >= 0, place < held)
        place = jnp.clip(place, 0, held - 1)
        carries = (jnp.where(mine, carry_ref[place], 0.0), jnp.where(mine, cot_ref[place], 0.0))

        def value(ref, side):
            return (ref[i * DH : (i + 1) * DH, :] if side is None else ref[side, i]).astype(F32)

        for t, out in enumerate(outs):
            for side in range(2):
                total = plans[t][2 + side] * carries[side]
                for weight, ref, which in plans[t][side]:
                    total = total + weight * value(ref, which)
                out[side, i] = total.astype(BF16)
    edge_ref[0:1, :] = priors[0]
    edge_ref[1:2, :] = laters[0]
    edge_ref[2:8, :] = jnp.broadcast_to(newest, (6, DH))


def edge_rows(z, labels, edges):
    first, last = own_row(labels, z), own_row(labels, DEPTH + z)
    last_before = own_row(labels, DEPTH + jnp.maximum(z - 1, 0))
    first_after = own_row(labels, jnp.minimum(z + 1, DEPTH - 1))
    return (last, last_before, edges[0:1, :], first), (first, first_after, edges[1:2, :], last)


def hop(side, rows, part, term_ref, prefix_ref, got_ref, out):
    own, neighbour, prior, _ = [jnp.where(side == 0, a, b) for a, b in zip(*rows)]
    join, keep = flag(prior == own), flag(neighbour == own)
    for i in range(part):
        state = term_ref[side, i].astype(F32) + join * prefix_ref[side, i].astype(F32)
        rest = prefix_ref[1 - side, i].astype(F32)
        if got_ref is not None:
            state = state + keep * got_ref[0, i].astype(F32)
            rest = rest + got_ref[1, i].astype(F32)
        out[0, i] = state.astype(BF16)
        out[1, i] = rest.astype(BF16)


def end_kernel(part, near, far, ids, labels, edges, *refs):
    z = ids[2]
    out = refs[-1]
    rows = edge_rows(z, labels, edges)
    side = jnp.where(z >= DEPTH // 2, 1, 0)
    at_end = jnp.logical_or(z == 0, z == DEPTH - 1)
    if near:

        @pl.when(at_end)
        def _():
            hop(side, rows, part, refs[0], refs[1], None, out)

    if far:

        @pl.when(jnp.logical_not(at_end))
        def _():
            term, prefix, got = refs[-4:-1]
            hop(1 - side, rows, part, term, prefix, got, out)


def middle_kernel(part, ids, labels, edges, term, prefix, got, out):
    z = ids[2]
    rows = edge_rows(z, labels, edges)
    side = jnp.where(z >= DEPTH // 2, 1, 0)
    hop(side, rows, part, term, prefix, got, out)


def output_kernel(
    factor, first, part, turn, ids, labels, edges, docs_ref, row_ref, q_ref, k_ref, v_ref, g_ref,
    prefix, near, middle, far, *refs,
):
    outs, (states, held, sems) = refs[-7:-3], refs[-3:]
    c, z = ids[1], ids[2]
    side = jnp.where(z >= DEPTH // 2, 1, 0)
    at_end = jnp.logical_or(z == 0, z == DEPTH - 1)
    rows = edge_rows(z, labels, edges)

    def state(which, over, rest):
        _, neighbour, prior, target = [jnp.where(which == 0, a, b) for a, b in zip(*rows)]
        reach, come = flag(prior == target), flag(neighbour == target)
        for i in range(part):
            value = reach * prefix[which, i].astype(F32)
            if over is not None:
                value = value + come * over[0, i].astype(F32)
            if rest is not None:
                value = value + reach * rest[1, i].astype(F32)
            states[which, i] = value.astype(BF16)

    @pl.when(at_end)
    def _():
        state(side, None, far)
        state(1 - side, far, None)

    @pl.when(jnp.logical_not(at_end))
    def _():
        state(side, near, middle)
        state(1 - side, middle, near)

    docs = docs_ref[...]
    in_first, in_last = document_masks(docs)
    places = lax.broadcasted_iota(jnp.int32, (SPAN, SPAN), 0)
    others = lax.broadcasted_iota(jnp.int32, (SPAN, SPAN), 1)
    allowed = jnp.logical_and(others <= places, docs == row_ref[0:1])
    base = first + (c ^ turn) * part
    copies = []
    for i in range(part):
        at = pl.ds(pl.multiple_of((base + i) * DH, DH), DH)
        q, k, v, g = q_ref[:, at], k_ref[:, at], v_ref[:, at], g_ref[:, at]
        before, after = states[0, i], states[1, i]
        scores = jnp.where(allowed, dot_transposed(q, k) * factor, 0.0).astype(BF16)
        grad_scores = jnp.where(allowed, dot_transposed(g, v) * factor, 0.0).astype(BF16)
        results = (
            dot(scores, v) + dot(jnp.where(in_first, q, 0), before),
            dot(grad_scores, k) + dot_transposed(jnp.where(in_first, g, 0), before),
            transposed_dot(grad_scores, q) + dot_transposed(jnp.where(in_last, v, 0), after),
            transposed_dot(scores, g) + dot(jnp.where(in_last, k, 0), after),
        )
        for n, result in enumerate(results):
            held[n, i] = result.astype(BF16)
            copy = pltpu.make_async_copy(held.at[n, i], outs[n].at[:, at], sems.at[n, i])
            copy.start()
            copies.append(copy)
    for copy in copies:
        copy.wait()


def shards(queries, keys, values, out_grad, doc_ids, carry_in, carry_cot):
    outer, inner, depth = (lax.axis_size(a) for a in ("outer", "inner", "heads"))
    assert depth == DEPTH
    tokens_all = doc_ids.shape[0] * outer * inner
    factor = float(DH * (tokens_all // 2)) ** (-0.5)
    head_count = queries.shape[1] // DH
    arrays = (queries, keys, values, out_grad)
    part = min(4, head_count // inner)
    piece = part * inner
    chunks = head_count // part
    lag = 4

    ids = jnp.stack([lax.axis_index(a) for a in ("outer", "inner", "heads")]).astype(jnp.int32)
    blocks = doc_ids.reshape(depth, SPAN)
    edges = jnp.concatenate([blocks[:, 0], blocks[:, -1]]).astype(F32)
    own_labels = jnp.broadcast_to(edges[:, None], (2 * depth, DH))
    labels = [own_labels] + [pairs(own_labels, "inner", d) for d in range(1, inner)]
    docs = lax.dynamic_index_in_dim(blocks, ids[2], 0, False)
    docs_column = jnp.broadcast_to(docs[:, None], (SPAN, DH))
    docs_row = jnp.broadcast_to(docs[None, :], (8, SPAN))

    state_pair = jax.ShapeDtypeStruct((2, part, DH, DH), BF16)
    levels = (outer - 1).bit_length()
    fan_shape = jax.ShapeDtypeStruct((part * DH + LABELS, DH), BF16)
    edge_shape = jax.ShapeDtypeStruct((8, DH), F32)
    product = 2 * SPAN * DH * DH

    terms, prefixes, edge = [], [], None
    for first in range(0, head_count, piece):
        own = call(
            functools.partial(term_kernel, factor, first, part),
            (ids, docs_column) + arrays,
            [state_pair] * inner,
            2 * piece * product,
            specs=[SMEM] + [VMEM] * 5,
        )
        received = [own[0]] + [pairs(own[d], "inner", d) for d in range(1, inner)]
        sums = call(
            functools.partial(sum_kernel, inner, part, levels),
            (ids, *labels, *received),
            [fan_shape] * levels,
            part * DH * DH * 8,
            specs=[SMEM] + [VMEM] * (2 * inner),
        )
        fans = [pairs(sums[d.bit_length() - 1], "outer", d) for d in range(1, outer)]
        given = call(
            functools.partial(prefix_kernel, factor, first, part, inner, outer),
            (ids, carry_in, carry_cot, *labels, *received, *fans),
            [state_pair] * inner + [edge_shape],
            part * DH * DH * 16 * inner,
            specs=[SMEM] + [VMEM] * (2 + 2 * inner + outer - 1),
        )
        edge = given[-1] if edge is None else edge
        terms.extend(own)
        prefixes.extend([given[0]] + [pairs(given[d], "inner", d) for d in range(1, inner)])

    near, middle = [None] * (chunks + lag), [None] * chunks
    for k in range(chunks + lag):
        operands, perm = [ids, own_labels, edge], []
        if k < chunks:
            operands += [terms[k], prefixes[k]]
            perm += [(0, 1), (3, 2)]
        if k >= lag:
            operands += [terms[k - lag], prefixes[k - lag], middle[k - lag]]
            perm += [(1, 0), (2, 3)]
        sent = call(
            functools.partial(end_kernel, part, k < chunks, k >= lag),
            operands,
            [state_pair],
            part * DH * DH * 8,
            specs=[SMEM] + [VMEM] * (len(operands) - 1),
        )[0]
        near[k] = lax.ppermute(sent, "heads", perm)
        if k < chunks:
            sent = call(
                functools.partial(middle_kernel, part),
                (ids, own_labels, edge, terms[k], prefixes[k], near[k]),
                [state_pair],
                part * DH * DH * 8,
                specs=[SMEM] + [VMEM] * 5,
            )[0]
            middle[k] = lax.ppermute(sent, "heads", [(1, 2), (2, 1)])

    out_shape = jax.ShapeDtypeStruct(queries.shape, BF16)
    results = ()
    for k in range(chunks):
        operands = (ids, own_labels, edge, docs_column, docs_row) + arrays
        operands += (prefixes[k], near[k], middle[k], near[k + lag])
        results = call(
            functools.partial(output_kernel, factor, k // inner * piece, part, k % inner),
            operands + tuple(results),
            [out_shape] * 4,
            10 * part * product,
            scratch=[
                pltpu.VMEM((2, part, DH, DH), BF16),
                pltpu.VMEM((4, part, SPAN, DH), BF16),
                pltpu.SemaphoreType.DMA((4, part)),
            ],
            aliases={len(operands) + i: i for i in range(len(results))},
            specs=[SMEM] + [VMEM] * (len(operands) - 1) + [ANY] * len(results),
            out_specs=[ANY] * 4,
        )
    return tuple(results)


def solution(mesh):
    tokens = P(("outer", "inner", "heads"), None)
    carry = P("heads", None, None)
    return jax.shard_map(
        shards,
        mesh=mesh,
        in_specs=(tokens,) * 4 + (P(("outer", "inner")), carry, carry),
        out_specs=(tokens,) * 4,
        check_vma=False,
    )
```

time: 363 us -> 131 us (0.36)
  the two profiles are of different devices: /device:TPU:6 before, /device:TPU:0 now
where the time goes in v2:
time: 131 us; the launch traced here: 130 us
  starting transfers between devices  50.3 us (38%)
  Pallas kernels  43.2 us (33%)
  waiting for transfers between devices  29 us (22%)
  local copies, waits for them, and re-layouts  5.93 us (5%)
  between operations  1.42 us (1%)
    pallas_call x40, Pallas kernels, call(): pl.pallas_call(kernel, in_specs=specs, out_specs=out_specs or [VMEM] * le...  43.2 us
    ppermute x12, starting transfers between devices, shards(): near[k] = lax.ppermute(sent, 'heads', perm)  27.7 us
    ppermute x12, waiting for transfers between devices, shards(): near[k] = lax.ppermute(sent, 'heads', perm)  18.2 us
    ppermute x21, starting transfers between devices, pairs(): return lax.ppermute(array, axis, [(i, i ^ distance) for i in range(count)])  17.1 us
    ppermute x21, waiting for transfers between devices, pairs(): return lax.ppermute(array, axis, [(i, i ^ distance) for i in range(count)])  10.7 us
    unnamed x20, local copies, waits for them, and re-layouts  5.6 us
    ppermute x8, starting transfers between devices, shards(): middle[k] = lax.ppermute(sent, 'heads', [(1, 2), (2, 1)])  5.41 us
  transfers between devices with their start and end apart: 41, of which 13 were waited for; matrix products, arithmetic and copies ran while one was open for 0% of the time, Pallas kernels for 31%

profile of v2, /device:TPU:0, one launch (start us, length us, event | category | flops | bytes accessed | tf_op | source)
XLA Modules:
  0.0 129.9 jit_solution(14797114961459676829)
XLA Ops:
  1.5 1.2 copy-done
  2.7 1.2 copy-done.2
  3.9 1.2 copy-done.4
  5.2 1.2 copy-done.6
  7.9 1.0 shard_map.121
  10.9 1.1 collective-permute-done.refs_1_
  12.7 2.7 %collective-permute-start.2 = (bf16[528,128]{1,0:T(8,128)(2,1)S(1)}, bf16[528,128]{1,0:T(8,128)(2,1)S(1)}, u32[]{:S(2)}, u32[]{:S(2)}) collective-permute-start(bf16[528,128]{1,0:T(8,128)(2,1)S(1)} %get-tuple-element.59), channel_id=1, source_target_pairs={{0,8},{8,0},{16,24},{24,16},{1,9},{9,1},{17,25},{25,17},{2,10},{10... | collective-permute-start | bytes 405512 | tf_op jit(solution)/shard_map/ppermute | solution.py:24
  15.4 1.5 %collective-permute-start.3 = (bf16[528,128]{1,0:T(8,128)(2,1)S(1)}, bf16[528,128]{1,0:T(8,128)(2,1)S(1)}, u32[]{:S(2)}, u32[]{:S(2)}) collective-permute-start(bf16[528,128]{1,0:T(8,128)(2,1)S(1)} %get-tuple-element.60), channel_id=1, source_target_pairs={{0,16},{8,24},{16,0},{24,8},{1,17},{9,25},{17,1},{25,9},{2,18},{10... | collective-permute-start | bytes 405512 | tf_op jit(solution)/shard_map/ppermute | solution.py:24
  16.9 1.0 shard_map.105
  18.7 1.0 collective-permute-done.2.refs_4_
  19.7 2.1 %collective-permute-start.11 = (bf16[528,128]{1,0:T(8,128)(2,1)S(1)}, bf16[528,128]{1,0:T(8,128)(2,1)S(1)}, u32[]{:S(2)}, u32[]{:S(2)}) collective-permute-start(bf16[528,128]{1,0:T(8,128)(2,1)S(1)} %get-tuple-element.69), channel_id=1, source_target_pairs={{0,8},{8,0},{16,24},{24,16},{1,9},{9,1},{17,25},{25,17},{2,10},{10... | collective-permute-start | bytes 405512 | tf_op jit(solution)/shard_map/ppermute | solution.py:24
  21.8 2.0 %collective-permute-done.3.refs_5_ = bf16[528,128]{1,0:T(8,128)(2,1)S(1)} collective-permute-done((bf16[528,128]{1,0:T(8,128)(2,1)S(1)}, bf16[528,128]{1,0:T(8,128)(2,1)S(1)}, u32[]{:S(2)}, u32[]{:S(2)}) %collective-permute-start.3) | collective-permute-done | bytes 135200 | tf_op jit(solution)/shard_map/ppermute | solution.py:24
  23.7 1.6 %collective-permute-start.12 = (bf16[528,128]{1,0:T(8,128)(2,1)S(1)}, bf16[528,128]{1,0:T(8,128)(2,1)S(1)}, u32[]{:S(2)}, u32[]{:S(2)}) collective-permute-start(bf16[528,128]{1,0:T(8,128)(2,1)S(1)} %get-tuple-element.70), channel_id=1, source_target_pairs={{0,16},{8,24},{16,0},{24,8},{1,17},{9,25},{17,1},{25,9},{2,18},{10... | collective-permute-start | bytes 405512 | tf_op jit(solution)/shard_map/ppermute | solution.py:24
  25.4 1.0 shard_map.104
  27.2 1.9 %collective-permute-start.26 = (bf16[528,128]{1,0:T(8,128)(2,1)S(1)}, bf16[528,128]{1,0:T(8,128)(2,1)S(1)}, u32[]{:S(2)}, u32[]{:S(2)}) collective-permute-start(bf16[528,128]{1,0:T(8,128)(2,1)S(1)} %get-tuple-element.76), channel_id=1, source_target_pairs={{0,8},{8,0},{16,24},{24,16},{1,9},{9,1},{17,25},{25,17},{2,10},{10... | collective-permute-start | bytes 405512 | tf_op jit(solution)/shard_map/ppermute | solution.py:24
  29.1 2.5 %collective-permute-done.12.refs_5_ = bf16[528,128]{1,0:T(8,128)(2,1)S(1)} collective-permute-done((bf16[528,128]{1,0:T(8,128)(2,1)S(1)}, bf16[528,128]{1,0:T(8,128)(2,1)S(1)}, u32[]{:S(2)}, u32[]{:S(2)}) %collective-permute-start.12) | collective-permute-done | bytes 135200 | tf_op jit(solution)/shard_map/ppermute | solution.py:24
  31.6 1.2 shard_map.110
  33.5 3.5 %collective-permute-start.36 = (bf16[2,4,128,128]{3,2,1,0:T(8,128)(2,1)S(1)}, bf16[2,4,128,128]{3,2,1,0:T(8,128)(2,1)S(1)}, u32[]{:S(2)}, u32[]{:S(2)}) collective-permute-start(bf16[2,4,128,128]{3,2,1,0:T(8,128)(2,1)S(1)} %shard_map.129), channel_id=1, source_target_pairs={{0,1},{3,2},{4,5},{7,6},{8,9},{11,10},{12,13},{15,14},{16,17},{19,... | collective-permute-start | bytes 786440 | tf_op jit(solution)/shard_map/ppermute | solution.py:335
  36.9 1.4 %collective-permute-start.27 = (bf16[528,128]{1,0:T(8,128)(2,1)S(1)}, bf16[528,128]{1,0:T(8,128)(2,1)S(1)}, u32[]{:S(2)}, u32[]{:S(2)}) collective-permute-start(bf16[528,128]{1,0:T(8,128)(2,1)S(1)} %get-tuple-element.77), channel_id=1, source_target_pairs={{0,16},{8,24},{16,0},{24,8},{1,17},{9,25},{17,1},{25,9},{2,18},{10... | collective-permute-start | bytes 405512 | tf_op jit(solution)/shard_map/ppermute | solution.py:24
  39.4 1.9 %collective-permute-start.6 = (bf16[528,128]{1,0:T(8,128)(2,1)S(1)}, bf16[528,128]{1,0:T(8,128)(2,1)S(1)}, u32[]{:S(2)}, u32[]{:S(2)}) collective-permute-start(bf16[528,128]{1,0:T(8,128)(2,1)S(1)} %get-tuple-element.64), channel_id=1, source_target_pairs={{0,8},{8,0},{16,24},{24,16},{1,9},{9,1},{17,25},{25,17},{2,10},{10... | collective-permute-start | bytes 405512 | tf_op jit(solution)/shard_map/ppermute | solution.py:24
  41.8 3.7 %collective-permute-done.27.refs_5_ = bf16[528,128]{1,0:T(8,128)(2,1)S(1)} collective-permute-done((bf16[528,128]{1,0:T(8,128)(2,1)S(1)}, bf16[528,128]{1,0:T(8,128)(2,1)S(1)}, u32[]{:S(2)}, u32[]{:S(2)}) %collective-permute-start.27) | collective-permute-done | bytes 135200 | tf_op jit(solution)/shard_map/ppermute | solution.py:24
  45.5 1.6 %collective-permute-start.31 = (bf16[2,4,128,128]{3,2,1,0:T(8,128)(2,1)S(1)}, bf16[2,4,128,128]{3,2,1,0:T(8,128)(2,1)S(1)}, u32[]{:S(2)}, u32[]{:S(2)}) collective-permute-start(bf16[2,4,128,128]{3,2,1,0:T(8,128)(2,1)S(1)} %shard_map.124), channel_id=1, source_target_pairs={{0,1},{3,2},{4,5},{7,6},{8,9},{11,10},{12,13},{15,14},{16,17},{19,... | collective-permute-start | bytes 786440 | tf_op jit(solution)/shard_map/ppermute | solution.py:335
  47.8 1.3 %collective-permute-start.20 = (bf16[2,4,128,128]{3,2,1,0:T(8,128)(2,1)S(1)}, bf16[2,4,128,128]{3,2,1,0:T(8,128)(2,1)S(1)}, u32[]{:S(2)}, u32[]{:S(2)}) collective-permute-start(bf16[2,4,128,128]{3,2,1,0:T(8,128)(2,1)S(1)} %shard_map.116), channel_id=1, source_target_pairs={{0,1},{3,2},{4,5},{7,6},{8,9},{11,10},{12,13},{15,14},{16,17},{19,... | collective-permute-start | bytes 786440 | tf_op jit(solution)/shard_map/ppermute | solution.py:335
  49.1 1.4 %collective-permute-start.7 = (bf16[528,128]{1,0:T(8,128)(2,1)S(1)}, bf16[528,128]{1,0:T(8,128)(2,1)S(1)}, u32[]{:S(2)}, u32[]{:S(2)}) collective-permute-start(bf16[528,128]{1,0:T(8,128)(2,1)S(1)} %get-tuple-element.65), channel_id=1, source_target_pairs={{0,16},{8,24},{16,0},{24,8},{1,17},{9,25},{17,1},{25,9},{2,18},{10... | collective-permute-start | bytes 405512 | tf_op jit(solution)/shard_map/ppermute | solution.py:24
  51.1 1.3 %collective-permute-start.15 = (bf16[2,4,128,128]{3,2,1,0:T(8,128)(2,1)S(1)}, bf16[2,4,128,128]{3,2,1,0:T(8,128)(2,1)S(1)}, u32[]{:S(2)}, u32[]{:S(2)}) collective-permute-start(bf16[2,4,128,128]{3,2,1,0:T(8,128)(2,1)S(1)} %shard_map.111), channel_id=1, source_target_pairs={{0,1},{3,2},{4,5},{7,6},{8,9},{11,10},{12,13},{15,14},{16,17},{19,... | collective-permute-start | bytes 786440 | tf_op jit(solution)/shard_map/ppermute | solution.py:335
  55.0 1.2 shard_map.123
  56.9 2.7 %collective-permute-done.20.got.near = bf16[2,4,128,128]{3,2,1,0:T(8,128)(2,1)S(1)} collective-permute-done((bf16[2,4,128,128]{3,2,1,0:T(8,128)(2,1)S(1)}, bf16[2,4,128,128]{3,2,1,0:T(8,128)(2,1)S(1)}, u32[]{:S(2)}, u32[]{:S(2)}) %collective-permute-start.20) | collective-permute-done | bytes 262176 | tf_op jit(solution)/shard_map/ppermute | solution.py:335
  61.5 1.2 shard_map.107
  65.6 9.0 %collective-permute-start.38 = (bf16[2,4,128,128]{3,2,1,0:T(8,128)(2,1)S(1)}, bf16[2,4,128,128]{3,2,1,0:T(8,128)(2,1)S(1)}, u32[]{:S(2)}, u32[]{:S(2)}) collective-permute-start(bf16[2,4,128,128]{3,2,1,0:T(8,128)(2,1)S(1)} %shard_map.131), channel_id=1, source_target_pairs={{0,1},{3,2},{1,0},{2,3},{4,5},{7,6},{5,4},{6,7},{8,9},{11,10},{9,8... | collective-permute-start | bytes 786440 | tf_op jit(solution)/shard_map/ppermute | solution.py:335
  76.0 2.1 %collective-permute-start.22 = (bf16[2,4,128,128]{3,2,1,0:T(8,128)(2,1)S(1)}, bf16[2,4,128,128]{3,2,1,0:T(8,128)(2,1)S(1)}, u32[]{:S(2)}, u32[]{:S(2)}) collective-permute-start(bf16[2,4,128,128]{3,2,1,0:T(8,128)(2,1)S(1)} %shard_map.118), channel_id=1, source_target_pairs={{0,1},{3,2},{1,0},{2,3},{4,5},{7,6},{5,4},{6,7},{8,9},{11,10},{9,8... | collective-permute-start | bytes 786440 | tf_op jit(solution)/shard_map/ppermute | solution.py:335
  78.7 3.5 %collective-permute-start.17 = (bf16[2,4,128,128]{3,2,1,0:T(8,128)(2,1)S(1)}, bf16[2,4,128,128]{3,2,1,0:T(8,128)(2,1)S(1)}, u32[]{:S(2)}, u32[]{:S(2)}) collective-permute-start(bf16[2,4,128,128]{3,2,1,0:T(8,128)(2,1)S(1)} %shard_map.113), channel_id=1, source_target_pairs={{0,1},{3,2},{1,0},{2,3},{4,5},{7,6},{5,4},{6,7},{8,9},{11,10},{9,8... | collective-permute-start | bytes 786440 | tf_op jit(solution)/shard_map/ppermute | solution.py:335
  83.6 3.8 %collective-permute-done.33.got.far.near = bf16[2,4,128,128]{3,2,1,0:T(8,128)(2,1)S(1)} collective-permute-done((bf16[2,4,128,128]{3,2,1,0:T(8,128)(2,1)S(1)}, bf16[2,4,128,128]{3,2,1,0:T(8,128)(2,1)S(1)}, u32[]{:S(2)}, u32[]{:S(2)}) %collective-permute-start.33) | collective-permute-done | bytes 262176 | tf_op jit(solution)/shard_map/ppermute | solution.py:335
  88.7 4.3 %collective-permute-done.22.got.far.near = bf16[2,4,128,128]{3,2,1,0:T(8,128)(2,1)S(1)} collective-permute-done((bf16[2,4,128,128]{3,2,1,0:T(8,128)(2,1)S(1)}, bf16[2,4,128,128]{3,2,1,0:T(8,128)(2,1)S(1)}, u32[]{:S(2)}, u32[]{:S(2)}) %collective-permute-start.22) | collective-permute-done | bytes 262176 | tf_op jit(solution)/shard_map/ppermute | solution.py:335
  94.3 3.9 %collective-permute-done.17.got.far.near = bf16[2,4,128,128]{3,2,1,0:T(8,128)(2,1)S(1)} collective-permute-done((bf16[2,4,128,128]{3,2,1,0:T(8,128)(2,1)S(1)}, bf16[2,4,128,128]{3,2,1,0:T(8,128)(2,1)S(1)}, u32[]{:S(2)}, u32[]{:S(2)}) %collective-permute-start.17) | collective-permute-done | bytes 262176 | tf_op jit(solution)/shard_map/ppermute | solution.py:335
  100.1 1.3 collective-permute-start.40
  102.0 1.4 %collective-permute-start.35 = (bf16[2,4,128,128]{3,2,1,0:T(8,128)(2,1)S(1)}, bf16[2,4,128,128]{3,2,1,0:T(8,128)(2,1)S(1)}, u32[]{:S(2)}, u32[]{:S(2)}) collective-permute-start(bf16[2,4,128,128]{3,2,1,0:T(8,128)(2,1)S(1)} %shard_map.128), channel_id=1, source_target_pairs={{1,0},{2,3},{5,4},{6,7},{9,8},{10,11},{13,12},{14,15},{17,16},{18,... | collective-permute-start | bytes 786440 | tf_op jit(solution)/shard_map/ppermute | solution.py:335
  104.0 1.3 collective-permute-start.24
  105.9 1.3 collective-permute-start.19
  107.2 2.5 %shard_map.134 = (bf16[128,4096]{1,0:T(8,128)(2,1)}, bf16[128,4096]{1,0:T(8,128)(2,1)}, bf16[128,4096]{1,0:T(8,128)(2,1)}, bf16[128,4096]{1,0:T(8,128)(2,1)}) custom-call(s32[3]{0:T(128)S(1)} %pad_add_fusion.ids, f32[8,128]{1,0:T(8,128)S(1)} %broadcast_in_dim.8.refs_0_.labels, f32[8,128]{1,0:T(8,128)S(1)} %get-tuple-element.61.edges, ...), custom_call_target="tpu_custom_call" | custom-call | flops 167772160 | bytes 9515020 | tf_op jit(solution)/shard_map/pallas_call | solution.py:45
  109.7 2.6 %shard_map.135 = (bf16[128,4096]{1,0:T(8,128)(2,1)}, bf16[128,4096]{1,0:T(8,128)(2,1)}, bf16[128,4096]{1,0:T(8,128)(2,1)}, bf16[128,4096]{1,0:T(8,128)(2,1)}) custom-call(s32[3]{0:T(128)S(1)} %pad_add_fusion.ids, f32[8,128]{1,0:T(8,128)S(1)} %broadcast_in_dim.8.refs_0_.labels, ...), custom_call_target="tpu_custom_call", output_to_operand_aliasing={{0}: (13, {}), {1}: (14, {}), {2}: (15, {}), {3}: (16, {})} | custom-call | flops 167772160 | bytes 13709324 | tf_op jit(solution)/shard_map/pallas_call | solution.py:45
  112.3 2.5 %shard_map.136 = (bf16[128,4096]{1,0:T(8,128)(2,1)}, bf16[128,4096]{1,0:T(8,128)(2,1)}, bf16[128,4096]{1,0:T(8,128)(2,1)}, bf16[128,4096]{1,0:T(8,128)(2,1)}) custom-call(s32[3]{0:T(128)S(1)} %pad_add_fusion.ids, f32[8,128]{1,0:T(8,128)S(1)} %broadcast_in_dim.8.refs_0_.labels, ...), custom_call_target="tpu_custom_call", output_to_operand_aliasing={{0}: (13, {}), {1}: (14, {}), {2}: (15, {}), {3}: (16, {})} | custom-call | flops 167772160 | bytes 13709324 | tf_op jit(solution)/shard_map/pallas_call | solution.py:45
  114.8 2.5 %shard_map.137 = (bf16[128,4096]{1,0:T(8,128)(2,1)}, bf16[128,4096]{1,0:T(8,128)(2,1)}, bf16[128,4096]{1,0:T(8,128)(2,1)}, bf16[128,4096]{1,0:T(8,128)(2,1)}) custom-call(s32[3]{0:T(128)S(1)} %pad_add_fusion.ids, f32[8,128]{1,0:T(8,128)S(1)} %broadcast_in_dim.8.refs_0_.labels, ...), custom_call_target="tpu_custom_call", output_to_operand_aliasing={{0}: (13, {}), {1}: (14, {}), {2}: (15, {}), {3}: (16, {})} | custom-call | flops 167772160 | bytes 13709324 | tf_op jit(solution)/shard_map/pallas_call | solution.py:45
  117.3 2.5 %shard_map.138 = (bf16[128,4096]{1,0:T(8,128)(2,1)}, bf16[128,4096]{1,0:T(8,128)(2,1)}, bf16[128,4096]{1,0:T(8,128)(2,1)}, bf16[128,4096]{1,0:T(8,128)(2,1)}) custom-call(s32[3]{0:T(128)S(1)} %pad_add_fusion.ids, f32[8,128]{1,0:T(8,128)S(1)} %broadcast_in_dim.8.refs_0_.labels, ...), custom_call_target="tpu_custom_call", output_to_operand_aliasing={{0}: (13, {}), {1}: (14, {}), {2}: (15, {}), {3}: (16, {})} | custom-call | flops 167772160 | bytes 13709324 | tf_op jit(solution)/shard_map/pallas_call | solution.py:45
  119.7 2.5 %shard_map.139 = (bf16[128,4096]{1,0:T(8,128)(2,1)}, bf16[128,4096]{1,0:T(8,128)(2,1)}, bf16[128,4096]{1,0:T(8,128)(2,1)}, bf16[128,4096]{1,0:T(8,128)(2,1)}) custom-call(s32[3]{0:T(128)S(1)} %pad_add_fusion.ids, f32[8,128]{1,0:T(8,128)S(1)} %broadcast_in_dim.8.refs_0_.labels, ...), custom_call_target="tpu_custom_call", output_to_operand_aliasing={{0}: (13, {}), {1}: (14, {}), {2}: (15, {}), {3}: (16, {})} | custom-call | flops 167772160 | bytes 13709324 | tf_op jit(solution)/shard_map/pallas_call | solution.py:45
  122.2 1.1 collective-permute-done.24.far
  123.3 2.4 %shard_map.140 = (bf16[128,4096]{1,0:T(8,128)(2,1)}, bf16[128,4096]{1,0:T(8,128)(2,1)}, bf16[128,4096]{1,0:T(8,128)(2,1)}, bf16[128,4096]{1,0:T(8,128)(2,1)}) custom-call(s32[3]{0:T(128)S(1)} %pad_add_fusion.ids, f32[8,128]{1,0:T(8,128)S(1)} %broadcast_in_dim.8.refs_0_.labels, ...), custom_call_target="tpu_custom_call", output_to_operand_aliasing={{0}: (13, {}), {1}: (14, {}), {2}: (15, {}), {3}: (16, {})} | custom-call | flops 167772160 | bytes 13709324 | tf_op jit(solution)/shard_map/pallas_call | solution.py:45
  125.8 1.5 %collective-permute-done.19.far = bf16[2,4,128,128]{3,2,1,0:T(8,128)(2,1)S(1)} collective-permute-done((bf16[2,4,128,128]{3,2,1,0:T(8,128)(2,1)S(1)}, bf16[2,4,128,128]{3,2,1,0:T(8,128)(2,1)S(1)}, u32[]{:S(2)}, u32[]{:S(2)}) %collective-permute-start.19) | collective-permute-done | bytes 262176 | tf_op jit(solution)/shard_map/ppermute | solution.py:335
  127.3 2.4 %shard_map.141 = (bf16[128,4096]{1,0:T(8,128)(2,1)}, bf16[128,4096]{1,0:T(8,128)(2,1)}, bf16[128,4096]{1,0:T(8,128)(2,1)}, bf16[128,4096]{1,0:T(8,128)(2,1)}) custom-call(s32[3]{0:T(128)S(1)} %pad_add_fusion.ids, f32[8,128]{1,0:T(8,128)S(1)} %broadcast_in_dim.8.refs_0_.labels, ...), custom_call_target="tpu_custom_call", output_to_operand_aliasing={{0}: (13, {}), {1}: (14, {}), {2}: (15, {}), {3}: (16, {})} | custom-call | flops 167772160 | bytes 13709324 | tf_op jit(solution)/shard_map/pallas_call | solution.py:45
  (101 shorter events, 27.5 us)
Async XLA Ops:
  1.5 1.2 copy-start
  2.7 1.2 copy-start.2
  7.4 4.6 %collective-permute-start.1 = (bf16[2,4,128,128]{3,2,1,0:T(8,128)(2,1)S(1)}, bf16[2,4,128,128]{3,2,1,0:T(8,128)(2,1)S(1)}, u32[]{:S(2)}, u32[]{:S(2)}) collective-permute-start(bf16[2,4,128,128]{3,2,1,0:T(8,128)(2,1)S(1)} %get-tuple-element.58.refs_0_.term.refs_2_), channel_id=1, source_target_pairs={{0,4},{4,0},{1,5},{5,1},{2,6},{6,2},{3,7},{7,3},{8,12},{12,8},{9,1... | collective-permute-start | bytes 786440 | tf_op jit(solution)/shard_map/ppermute | solution.py:24
  8.9 17.6 %collective-permute-start.25 = (bf16[2,4,128,128]{3,2,1,0:T(8,128)(2,1)S(1)}, bf16[2,4,128,128]{3,2,1,0:T(8,128)(2,1)S(1)}, u32[]{:S(2)}, u32[]{:S(2)}) collective-permute-start(bf16[2,4,128,128]{3,2,1,0:T(8,128)(2,1)S(1)} %get-tuple-element.75.refs_0_.term), channel_id=1, source_target_pairs={{0,4},{4,0},{1,5},{5,1},{2,6},{6,2},{3,7},{7,3},{8,12},{12,8},{9,1... | collective-permute-start | bytes 786440 | tf_op jit(solution)/shard_map/ppermute | solution.py:24
  9.0 7.9 %copy-start.1 = (bf16[128,4096]{1,0:T(8,128)(2,1)S(1)}, bf16[128,4096]{1,0:T(8,128)(2,1)}, u32[]{:S(2)}) copy-start(bf16[128,4096]{1,0:T(8,128)(2,1)} %q_ref.23) | copy-start | bytes 3145732
  10.0 8.0 %collective-permute-start.10 = (bf16[2,4,128,128]{3,2,1,0:T(8,128)(2,1)S(1)}, bf16[2,4,128,128]{3,2,1,0:T(8,128)(2,1)S(1)}, u32[]{:S(2)}, u32[]{:S(2)}) collective-permute-start(bf16[2,4,128,128]{3,2,1,0:T(8,128)(2,1)S(1)} %get-tuple-element.67.refs_0_.term.refs_2_), channel_id=1, source_target_pairs={{0,4},{4,0},{1,5},{5,1},{2,6},{6,2},{3,7},{7,3},{8,12},{12,8},{9,1... | collective-permute-start | bytes 786440 | tf_op jit(solution)/shard_map/ppermute | solution.py:24
  10.8 1.2 collective-permute-start
  12.7 7.0 %collective-permute-start.2 = (bf16[528,128]{1,0:T(8,128)(2,1)S(1)}, bf16[528,128]{1,0:T(8,128)(2,1)S(1)}, u32[]{:S(2)}, u32[]{:S(2)}) collective-permute-start(bf16[528,128]{1,0:T(8,128)(2,1)S(1)} %get-tuple-element.59), channel_id=1, source_target_pairs={{0,8},{8,0},{16,24},{24,16},{1,9},{9,1},{17,25},{25,17},{2,10},{10... | collective-permute-start | bytes 405512 | tf_op jit(solution)/shard_map/ppermute | solution.py:24
  15.4 8.4 %collective-permute-start.3 = (bf16[528,128]{1,0:T(8,128)(2,1)S(1)}, bf16[528,128]{1,0:T(8,128)(2,1)S(1)}, u32[]{:S(2)}, u32[]{:S(2)}) collective-permute-start(bf16[528,128]{1,0:T(8,128)(2,1)S(1)} %get-tuple-element.60), channel_id=1, source_target_pairs={{0,16},{8,24},{16,0},{24,8},{1,17},{9,25},{17,1},{25,9},{2,18},{10... | collective-permute-start | bytes 405512 | tf_op jit(solution)/shard_map/ppermute | solution.py:24
  16.9 8.5 %collective-permute-start.4 = (bf16[528,128]{1,0:T(8,128)(2,1)S(1)}, bf16[528,128]{1,0:T(8,128)(2,1)S(1)}, u32[]{:S(2)}, u32[]{:S(2)}) collective-permute-start(bf16[528,128]{1,0:T(8,128)(2,1)S(1)} %get-tuple-element.60), channel_id=1, source_target_pairs={{0,24},{8,16},{16,8},{24,0},{1,25},{9,17},{17,9},{25,1},{2,26},{10... | collective-permute-start | bytes 405512 | tf_op jit(solution)/shard_map/ppermute | solution.py:24
  16.9 8.5 %copy-start.8 = (f32[8,128,128]{2,1,0:T(8,128)S(1)}, f32[8,128,128]{2,1,0:T(8,128)}, u32[]{:S(2)}) copy-start(f32[8,128,128]{2,1,0:T(8,128)} %cot_ref.7) | copy-start | bytes 1572868
  17.9 7.5 %copy-start.7 = (f32[8,128,128]{2,1,0:T(8,128)S(1)}, f32[8,128,128]{2,1,0:T(8,128)}, u32[]{:S(2)}) copy-start(f32[8,128,128]{2,1,0:T(8,128)} %carry_ref.7) | copy-start | bytes 1572868
  17.9 19.0 %collective-permute-start.5 = (bf16[2,4,128,128]{3,2,1,0:T(8,128)(2,1)S(1)}, bf16[2,4,128,128]{3,2,1,0:T(8,128)(2,1)S(1)}, u32[]{:S(2)}, u32[]{:S(2)}) collective-permute-start(bf16[2,4,128,128]{3,2,1,0:T(8,128)(2,1)S(1)} %get-tuple-element.63.refs_0_.term), channel_id=1, source_target_pairs={{0,4},{4,0},{1,5},{5,1},{2,6},{6,2},{3,7},{7,3},{8,12},{12,8},{9,1... | collective-permute-start | bytes 786440 | tf_op jit(solution)/shard_map/ppermute | solution.py:24
  19.7 7.6 %collective-permute-start.11 = (bf16[528,128]{1,0:T(8,128)(2,1)S(1)}, bf16[528,128]{1,0:T(8,128)(2,1)S(1)}, u32[]{:S(2)}, u32[]{:S(2)}) collective-permute-start(bf16[528,128]{1,0:T(8,128)(2,1)S(1)} %get-tuple-element.69), channel_id=1, source_target_pairs={{0,8},{8,0},{16,24},{24,16},{1,9},{9,1},{17,25},{25,17},{2,10},{10... | collective-permute-start | bytes 405512 | tf_op jit(solution)/shard_map/ppermute | solution.py:24
  23.7 7.9 %collective-permute-start.12 = (bf16[528,128]{1,0:T(8,128)(2,1)S(1)}, bf16[528,128]{1,0:T(8,128)(2,1)S(1)}, u32[]{:S(2)}, u32[]{:S(2)}) collective-permute-start(bf16[528,128]{1,0:T(8,128)(2,1)S(1)} %get-tuple-element.70), channel_id=1, source_target_pairs={{0,16},{8,24},{16,0},{24,8},{1,17},{9,25},{17,1},{25,9},{2,18},{10... | collective-permute-start | bytes 405512 | tf_op jit(solution)/shard_map/ppermute | solution.py:24
  25.3 6.3 %collective-permute-start.13 = (bf16[528,128]{1,0:T(8,128)(2,1)S(1)}, bf16[528,128]{1,0:T(8,128)(2,1)S(1)}, u32[]{:S(2)}, u32[]{:S(2)}) collective-permute-start(bf16[528,128]{1,0:T(8,128)(2,1)S(1)} %get-tuple-element.70), channel_id=1, source_target_pairs={{0,24},{8,16},{16,8},{24,0},{1,25},{9,17},{17,9},{25,1},{2,26},{10... | collective-permute-start | bytes 405512 | tf_op jit(solution)/shard_map/ppermute | solution.py:24
  26.5 12.9 %collective-permute-start.30 = (bf16[2,4,128,128]{3,2,1,0:T(8,128)(2,1)S(1)}, bf16[2,4,128,128]{3,2,1,0:T(8,128)(2,1)S(1)}, u32[]{:S(2)}, u32[]{:S(2)}) collective-permute-start(bf16[2,4,128,128]{3,2,1,0:T(8,128)(2,1)S(1)} %get-tuple-element.79), channel_id=1, source_target_pairs={{0,4},{4,0},{1,5},{5,1},{2,6},{6,2},{3,7},{7,3},{8,12},{12,8},{9,1... | collective-permute-start | bytes 786440 | tf_op jit(solution)/shard_map/ppermute | solution.py:24
  27.2 11.1 %collective-permute-start.26 = (bf16[528,128]{1,0:T(8,128)(2,1)S(1)}, bf16[528,128]{1,0:T(8,128)(2,1)S(1)}, u32[]{:S(2)}, u32[]{:S(2)}) collective-permute-start(bf16[528,128]{1,0:T(8,128)(2,1)S(1)} %get-tuple-element.76), channel_id=1, source_target_pairs={{0,8},{8,0},{16,24},{24,16},{1,9},{9,1},{17,25},{25,17},{2,10},{10... | collective-permute-start | bytes 405512 | tf_op jit(solution)/shard_map/ppermute | solution.py:24
  32.9 16.3 %collective-permute-start.14 = (bf16[2,4,128,128]{3,2,1,0:T(8,128)(2,1)S(1)}, bf16[2,4,128,128]{3,2,1,0:T(8,128)(2,1)S(1)}, u32[]{:S(2)}, u32[]{:S(2)}) collective-permute-start(bf16[2,4,128,128]{3,2,1,0:T(8,128)(2,1)S(1)} %get-tuple-element.71), channel_id=1, source_target_pairs={{0,4},{4,0},{1,5},{5,1},{2,6},{6,2},{3,7},{7,3},{8,12},{12,8},{9,1... | collective-permute-start | bytes 786440 | tf_op jit(solution)/shard_map/ppermute | solution.py:24
  33.5 17.6 %collective-permute-start.36 = (bf16[2,4,128,128]{3,2,1,0:T(8,128)(2,1)S(1)}, bf16[2,4,128,128]{3,2,1,0:T(8,128)(2,1)S(1)}, u32[]{:S(2)}, u32[]{:S(2)}) collective-permute-start(bf16[2,4,128,128]{3,2,1,0:T(8,128)(2,1)S(1)} %shard_map.129), channel_id=1, source_target_pairs={{0,1},{3,2},{4,5},{7,6},{8,9},{11,10},{12,13},{15,14},{16,17},{19,... | collective-permute-start | bytes 786440 | tf_op jit(solution)/shard_map/ppermute | solution.py:335
  36.9 8.6 %collective-permute-start.27 = (bf16[528,128]{1,0:T(8,128)(2,1)S(1)}, bf16[528,128]{1,0:T(8,128)(2,1)S(1)}, u32[]{:S(2)}, u32[]{:S(2)}) collective-permute-start(bf16[528,128]{1,0:T(8,128)(2,1)S(1)} %get-tuple-element.77), channel_id=1, source_target_pairs={{0,16},{8,24},{16,0},{24,8},{1,17},{9,25},{17,1},{25,9},{2,18},{10... | collective-permute-start | bytes 405512 | tf_op jit(solution)/shard_map/ppermute | solution.py:24
  38.3 9.5 %collective-permute-start.28 = (bf16[528,128]{1,0:T(8,128)(2,1)S(1)}, bf16[528,128]{1,0:T(8,128)(2,1)S(1)}, u32[]{:S(2)}, u32[]{:S(2)}) collective-permute-start(bf16[528,128]{1,0:T(8,128)(2,1)S(1)} %get-tuple-element.77), channel_id=1, source_target_pairs={{0,24},{8,16},{16,8},{24,0},{1,25},{9,17},{17,9},{25,1},{2,26},{10... | collective-permute-start | bytes 405512 | tf_op jit(solution)/shard_map/ppermute | solution.py:24
  39.4 13.7 %collective-permute-start.6 = (bf16[528,128]{1,0:T(8,128)(2,1)S(1)}, bf16[528,128]{1,0:T(8,128)(2,1)S(1)}, u32[]{:S(2)}, u32[]{:S(2)}) collective-permute-start(bf16[528,128]{1,0:T(8,128)(2,1)S(1)} %get-tuple-element.64), channel_id=1, source_target_pairs={{0,8},{8,0},{16,24},{24,16},{1,9},{9,1},{17,25},{25,17},{2,10},{10... | collective-permute-start | bytes 405512 | tf_op jit(solution)/shard_map/ppermute | solution.py:24
  45.5 10.6 %collective-permute-start.31 = (bf16[2,4,128,128]{3,2,1,0:T(8,128)(2,1)S(1)}, bf16[2,4,128,128]{3,2,1,0:T(8,128)(2,1)S(1)}, u32[]{:S(2)}, u32[]{:S(2)}) collective-permute-start(bf16[2,4,128,128]{3,2,1,0:T(8,128)(2,1)S(1)} %shard_map.124), channel_id=1, source_target_pairs={{0,1},{3,2},{4,5},{7,6},{8,9},{11,10},{12,13},{15,14},{16,17},{19,... | collective-permute-start | bytes 786440 | tf_op jit(solution)/shard_map/ppermute | solution.py:335
  47.8 11.7 %collective-permute-start.20 = (bf16[2,4,128,128]{3,2,1,0:T(8,128)(2,1)S(1)}, bf16[2,4,128,128]{3,2,1,0:T(8,128)(2,1)S(1)}, u32[]{:S(2)}, u32[]{:S(2)}) collective-permute-start(bf16[2,4,128,128]{3,2,1,0:T(8,128)(2,1)S(1)} %shard_map.116), channel_id=1, source_target_pairs={{0,1},{3,2},{4,5},{7,6},{8,9},{11,10},{12,13},{15,14},{16,17},{19,... | collective-permute-start | bytes 786440 | tf_op jit(solution)/shard_map/ppermute | solution.py:335
  49.1 5.1 %collective-permute-start.7 = (bf16[528,128]{1,0:T(8,128)(2,1)S(1)}, bf16[528,128]{1,0:T(8,128)(2,1)S(1)}, u32[]{:S(2)}, u32[]{:S(2)}) collective-permute-start(bf16[528,128]{1,0:T(8,128)(2,1)S(1)} %get-tuple-element.65), channel_id=1, source_target_pairs={{0,16},{8,24},{16,0},{24,8},{1,17},{9,25},{17,1},{25,9},{2,18},{10... | collective-permute-start | bytes 405512 | tf_op jit(solution)/shard_map/ppermute | solution.py:24
  51.1 12.6 %collective-permute-start.15 = (bf16[2,4,128,128]{3,2,1,0:T(8,128)(2,1)S(1)}, bf16[2,4,128,128]{3,2,1,0:T(8,128)(2,1)S(1)}, u32[]{:S(2)}, u32[]{:S(2)}) collective-permute-start(bf16[2,4,128,128]{3,2,1,0:T(8,128)(2,1)S(1)} %shard_map.111), channel_id=1, source_target_pairs={{0,1},{3,2},{4,5},{7,6},{8,9},{11,10},{12,13},{15,14},{16,17},{19,... | collective-permute-start | bytes 786440 | tf_op jit(solution)/shard_map/ppermute | solution.py:335
  53.1 11.2 %collective-permute-start.37 = (bf16[2,4,128,128]{3,2,1,0:T(8,128)(2,1)S(1)}, bf16[2,4,128,128]{3,2,1,0:T(8,128)(2,1)S(1)}, u32[]{:S(2)}, u32[]{:S(2)}) collective-permute-start(bf16[2,4,128,128]{3,2,1,0:T(8,128)(2,1)S(1)} %shard_map.130), channel_id=1, source_target_pairs={{1,2},{2,1},{5,6},{6,5},{9,10},{10,9},{13,14},{14,13},{17,18},{18,... | collective-permute-start | bytes 786440 | tf_op jit(solution)/shard_map/ppermute | solution.py:344
  54.2 6.7 %collective-permute-start.8 = (bf16[528,128]{1,0:T(8,128)(2,1)S(1)}, bf16[528,128]{1,0:T(8,128)(2,1)S(1)}, u32[]{:S(2)}, u32[]{:S(2)}) collective-permute-start(bf16[528,128]{1,0:T(8,128)(2,1)S(1)} %get-tuple-element.65), channel_id=1, source_target_pairs={{0,24},{8,16},{16,8},{24,0},{1,25},{9,17},{17,9},{25,1},{2,26},{10... | collective-permute-start | bytes 405512 | tf_op jit(solution)/shard_map/ppermute | solution.py:24
  56.2 9.4 %collective-permute-start.29 = (bf16[2,4,128,128]{3,2,1,0:T(8,128)(2,1)S(1)}, bf16[2,4,128,128]{3,2,1,0:T(8,128)(2,1)S(1)}, u32[]{:S(2)}, u32[]{:S(2)}) collective-permute-start(bf16[2,4,128,128]{3,2,1,0:T(8,128)(2,1)S(1)} %get-tuple-element.78), channel_id=1, source_target_pairs={{0,4},{4,0},{1,5},{5,1},{2,6},{6,2},{3,7},{7,3},{8,12},{12,8},{9,1... | collective-permute-start | bytes 786440 | tf_op jit(solution)/shard_map/ppermute | solution.py:24
  59.5 15.1 %collective-permute-start.32 = (bf16[2,4,128,128]{3,2,1,0:T(8,128)(2,1)S(1)}, bf16[2,4,128,128]{3,2,1,0:T(8,128)(2,1)S(1)}, u32[]{:S(2)}, u32[]{:S(2)}) collective-permute-start(bf16[2,4,128,128]{3,2,1,0:T(8,128)(2,1)S(1)} %shard_map.125), channel_id=1, source_target_pairs={{1,2},{2,1},{5,6},{6,5},{9,10},{10,9},{13,14},{14,13},{17,18},{18,... | collective-permute-start | bytes 786440 | tf_op jit(solution)/shard_map/ppermute | solution.py:344
  60.9 14.5 %collective-permute-start.21 = (bf16[2,4,128,128]{3,2,1,0:T(8,128)(2,1)S(1)}, bf16[2,4,128,128]{3,2,1,0:T(8,128)(2,1)S(1)}, u32[]{:S(2)}, u32[]{:S(2)}) collective-permute-start(bf16[2,4,128,128]{3,2,1,0:T(8,128)(2,1)S(1)} %shard_map.117), channel_id=1, source_target_pairs={{1,2},{2,1},{5,6},{6,5},{9,10},{10,9},{13,14},{14,13},{17,18},{18,... | collective-permute-start | bytes 786440 | tf_op jit(solution)/shard_map/ppermute | solution.py:344
  63.7 14.4 %collective-permute-start.9 = (bf16[2,4,128,128]{3,2,1,0:T(8,128)(2,1)S(1)}, bf16[2,4,128,128]{3,2,1,0:T(8,128)(2,1)S(1)}, u32[]{:S(2)}, u32[]{:S(2)}) collective-permute-start(bf16[2,4,128,128]{3,2,1,0:T(8,128)(2,1)S(1)} %get-tuple-element.66), channel_id=1, source_target_pairs={{0,4},{4,0},{1,5},{5,1},{2,6},{6,2},{3,7},{7,3},{8,12},{12,8},{9,1... | collective-permute-start | bytes 786440 | tf_op jit(solution)/shard_map/ppermute | solution.py:24
  64.3 13.7 %collective-permute-start.16 = (bf16[2,4,128,128]{3,2,1,0:T(8,128)(2,1)S(1)}, bf16[2,4,128,128]{3,2,1,0:T(8,128)(2,1)S(1)}, u32[]{:S(2)}, u32[]{:S(2)}) collective-permute-start(bf16[2,4,128,128]{3,2,1,0:T(8,128)(2,1)S(1)} %shard_map.112), channel_id=1, source_target_pairs={{1,2},{2,1},{5,6},{6,5},{9,10},{10,9},{13,14},{14,13},{17,18},{18,... | collective-permute-start | bytes 786440 | tf_op jit(solution)/shard_map/ppermute | solution.py:344
  65.6 16.6 %collective-permute-start.38 = (bf16[2,4,128,128]{3,2,1,0:T(8,128)(2,1)S(1)}, bf16[2,4,128,128]{3,2,1,0:T(8,128)(2,1)S(1)}, u32[]{:S(2)}, u32[]{:S(2)}) collective-permute-start(bf16[2,4,128,128]{3,2,1,0:T(8,128)(2,1)S(1)} %shard_map.131), channel_id=1, source_target_pairs={{0,1},{3,2},{1,0},{2,3},{4,5},{7,6},{5,4},{6,7},{8,9},{11,10},{9,8... | collective-permute-start | bytes 786440 | tf_op jit(solution)/shard_map/ppermute | solution.py:335
  75.2 12.1 %collective-permute-start.33 = (bf16[2,4,128,128]{3,2,1,0:T(8,128)(2,1)S(1)}, bf16[2,4,128,128]{3,2,1,0:T(8,128)(2,1)S(1)}, u32[]{:S(2)}, u32[]{:S(2)}) collective-permute-start(bf16[2,4,128,128]{3,2,1,0:T(8,128)(2,1)S(1)} %shard_map.126), channel_id=1, source_target_pairs={{0,1},{3,2},{1,0},{2,3},{4,5},{7,6},{5,4},{6,7},{8,9},{11,10},{9,8... | collective-permute-start | bytes 786440 | tf_op jit(solution)/shard_map/ppermute | solution.py:335
  76.0 17.0 %collective-permute-start.22 = (bf16[2,4,128,128]{3,2,1,0:T(8,128)(2,1)S(1)}, bf16[2,4,128,128]{3,2,1,0:T(8,128)(2,1)S(1)}, u32[]{:S(2)}, u32[]{:S(2)}) collective-permute-start(bf16[2,4,128,128]{3,2,1,0:T(8,128)(2,1)S(1)} %shard_map.118), channel_id=1, source_target_pairs={{0,1},{3,2},{1,0},{2,3},{4,5},{7,6},{5,4},{6,7},{8,9},{11,10},{9,8... | collective-permute-start | bytes 786440 | tf_op jit(solution)/shard_map/ppermute | solution.py:335
  78.7 19.5 %collective-permute-start.17 = (bf16[2,4,128,128]{3,2,1,0:T(8,128)(2,1)S(1)}, bf16[2,4,128,128]{3,2,1,0:T(8,128)(2,1)S(1)}, u32[]{:S(2)}, u32[]{:S(2)}) collective-permute-start(bf16[2,4,128,128]{3,2,1,0:T(8,128)(2,1)S(1)} %shard_map.113), channel_id=1, source_target_pairs={{0,1},{3,2},{1,0},{2,3},{4,5},{7,6},{5,4},{6,7},{8,9},{11,10},{9,8... | collective-permute-start | bytes 786440 | tf_op jit(solution)/shard_map/ppermute | solution.py:335
  82.9 16.7 %collective-permute-start.39 = (bf16[2,4,128,128]{3,2,1,0:T(8,128)(2,1)S(1)}, bf16[2,4,128,128]{3,2,1,0:T(8,128)(2,1)S(1)}, u32[]{:S(2)}, u32[]{:S(2)}) collective-permute-start(bf16[2,4,128,128]{3,2,1,0:T(8,128)(2,1)S(1)} %shard_map.132), channel_id=1, source_target_pairs={{1,2},{2,1},{5,6},{6,5},{9,10},{10,9},{13,14},{14,13},{17,18},{18,... | collective-permute-start | bytes 786440 | tf_op jit(solution)/shard_map/ppermute | solution.py:344
  88.0 13.4 %collective-permute-start.34 = (bf16[2,4,128,128]{3,2,1,0:T(8,128)(2,1)S(1)}, bf16[2,4,128,128]{3,2,1,0:T(8,128)(2,1)S(1)}, u32[]{:S(2)}, u32[]{:S(2)}) collective-permute-start(bf16[2,4,128,128]{3,2,1,0:T(8,128)(2,1)S(1)} %shard_map.127), channel_id=1, source_target_pairs={{1,2},{2,1},{5,6},{6,5},{9,10},{10,9},{13,14},{14,13},{17,18},{18,... | collective-permute-start | bytes 786440 | tf_op jit(solution)/shard_map/ppermute | solution.py:344
  93.6 9.8 %collective-permute-start.23 = (bf16[2,4,128,128]{3,2,1,0:T(8,128)(2,1)S(1)}, bf16[2,4,128,128]{3,2,1,0:T(8,128)(2,1)S(1)}, u32[]{:S(2)}, u32[]{:S(2)}) collective-permute-start(bf16[2,4,128,128]{3,2,1,0:T(8,128)(2,1)S(1)} %shard_map.119), channel_id=1, source_target_pairs={{1,2},{2,1},{5,6},{6,5},{9,10},{10,9},{13,14},{14,13},{17,18},{18,... | collective-permute-start | bytes 786440 | tf_op jit(solution)/shard_map/ppermute | solution.py:344
  98.8 6.5 %collective-permute-start.18 = (bf16[2,4,128,128]{3,2,1,0:T(8,128)(2,1)S(1)}, bf16[2,4,128,128]{3,2,1,0:T(8,128)(2,1)S(1)}, u32[]{:S(2)}, u32[]{:S(2)}) collective-permute-start(bf16[2,4,128,128]{3,2,1,0:T(8,128)(2,1)S(1)} %shard_map.114), channel_id=1, source_target_pairs={{1,2},{2,1},{5,6},{6,5},{9,10},{10,9},{13,14},{14,13},{17,18},{18,... | collective-permute-start | bytes 786440 | tf_op jit(solution)/shard_map/ppermute | solution.py:344
  100.1 17.2 %collective-permute-start.40 = (bf16[2,4,128,128]{3,2,1,0:T(8,128)(2,1)S(1)}, bf16[2,4,128,128]{3,2,1,0:T(8,128)(2,1)S(1)}, u32[]{:S(2)}, u32[]{:S(2)}) collective-permute-start(bf16[2,4,128,128]{3,2,1,0:T(8,128)(2,1)S(1)} %shard_map.133), channel_id=1, source_target_pairs={{1,0},{2,3},{5,4},{6,7},{9,8},{10,11},{13,12},{14,15},{17,16},{18,... | collective-permute-start | bytes 786440 | tf_op jit(solution)/shard_map/ppermute | solution.py:335
  102.0 5.2 %copy-start.3 = (bf16[128,4096]{1,0:T(8,128)(2,1)S(1)}, bf16[128,4096]{1,0:T(8,128)(2,1)}, u32[]{:S(2)}) copy-start(bf16[128,4096]{1,0:T(8,128)(2,1)} %k_ref.23) | copy-start | bytes 3145732
  102.0 5.2 %copy-start.5 = (bf16[128,4096]{1,0:T(8,128)(2,1)S(1)}, bf16[128,4096]{1,0:T(8,128)(2,1)}, u32[]{:S(2)}) copy-start(bf16[128,4096]{1,0:T(8,128)(2,1)} %v_ref.23) | copy-start | bytes 3145732
  102.0 17.8 %collective-permute-start.35 = (bf16[2,4,128,128]{3,2,1,0:T(8,128)(2,1)S(1)}, bf16[2,4,128,128]{3,2,1,0:T(8,128)(2,1)S(1)}, u32[]{:S(2)}, u32[]{:S(2)}) collective-permute-start(bf16[2,4,128,128]{3,2,1,0:T(8,128)(2,1)S(1)} %shard_map.128), channel_id=1, source_target_pairs={{1,0},{2,3},{5,4},{6,7},{9,8},{10,11},{13,12},{14,15},{17,16},{18,... | collective-permute-start | bytes 786440 | tf_op jit(solution)/shard_map/ppermute | solution.py:335
  104.0 19.3 %collective-permute-start.24 = (bf16[2,4,128,128]{3,2,1,0:T(8,128)(2,1)S(1)}, bf16[2,4,128,128]{3,2,1,0:T(8,128)(2,1)S(1)}, u32[]{:S(2)}, u32[]{:S(2)}) collective-permute-start(bf16[2,4,128,128]{3,2,1,0:T(8,128)(2,1)S(1)} %shard_map.120), channel_id=1, source_target_pairs={{1,0},{2,3},{5,4},{6,7},{9,8},{10,11},{13,12},{14,15},{17,16},{18,... | collective-permute-start | bytes 786440 | tf_op jit(solution)/shard_map/ppermute | solution.py:335
  105.9 21.5 %collective-permute-start.19 = (bf16[2,4,128,128]{3,2,1,0:T(8,128)(2,1)S(1)}, bf16[2,4,128,128]{3,2,1,0:T(8,128)(2,1)S(1)}, u32[]{:S(2)}, u32[]{:S(2)}) collective-permute-start(bf16[2,4,128,128]{3,2,1,0:T(8,128)(2,1)S(1)} %shard_map.115), channel_id=1, source_target_pairs={{1,0},{2,3},{5,4},{6,7},{9,8},{10,11},{13,12},{14,15},{17,16},{18,... | collective-permute-start | bytes 786440 | tf_op jit(solution)/shard_map/ppermute | solution.py:335
  (3 other events, 3.1 us)

commit v3 on v2

v3 whole, which is shorter than its diff:
```python
import functools

import jax
import jax.numpy as jnp
from jax import lax
from jax.experimental import pallas as pl
from jax.experimental.pallas import tpu as pltpu
from jax.sharding import PartitionSpec as P

DH = 128
SPAN = 128
LABELS = 16
DEPTH = 4
F32 = jnp.float32
BF16 = jnp.bfloat16
VMEM = pl.BlockSpec(memory_space=pltpu.VMEM)
SMEM = pl.BlockSpec(memory_space=pltpu.SMEM)
ANY = pl.BlockSpec(memory_space=pl.ANY)
LIMIT = 24 * 1024 * 1024


def pairs(array, axis, distance):
    count = lax.axis_size(axis)
    return lax.ppermute(array, axis, [(i, i ^ distance) for i in range(count)])


def transposed_dot(a, b):
    return lax.dot_general(a, b, (((0,), (0,)), ((), ())), preferred_element_type=F32)


def dot_transposed(a, b):
    return lax.dot_general(a, b, (((1,), (1,)), ((), ())), preferred_element_type=F32)


def dot(a, b):
    return lax.dot_general(a, b, (((1,), (0,)), ((), ())), preferred_element_type=F32)


def flag(row):
    return jnp.where(row, 1.0, 0.0).astype(F32)


def call(token, kernel, operands, out_shape, flops, scratch=(), aliases=None, specs=None, out_specs=None):
    count, results = len(operands), len(out_shape)

    def ordered(*refs):
        kernel(*refs[:count], *refs[count + 1 : count + 1 + results], *refs[count + 2 + results :])

    size = sum(a.size * a.dtype.itemsize for a in operands) + sum(a.size * a.dtype.itemsize for a in out_shape)
    *outs, token = pl.pallas_call(
        ordered,
        in_specs=list(specs or [SMEM] + [VMEM] * (count - 1)) + [VMEM],
        out_specs=list(out_specs or [VMEM] * results) + [VMEM],
        out_shape=list(out_shape) + [jax.ShapeDtypeStruct(token.shape, token.dtype)],
        scratch_shapes=list(scratch),
        input_output_aliases={**(aliases or {}), count: results},
        compiler_params=pltpu.CompilerParams(vmem_limit_bytes=LIMIT),
        cost_estimate=pl.CostEstimate(flops=flops, bytes_accessed=size, transcendentals=0),
    )(*operands, token)
    return token, outs


def document_masks(docs):
    return docs == docs[0:1], docs == docs[SPAN - 1 : SPAN]


def columns(head):
    return pl.ds(pl.multiple_of(head * DH, DH), DH)


def own_row(ref, at):
    return ref[pl.ds(at, 1), :]


def term_kernel(factor, groups, part, docs_ref, ids, heads, q_ref, k_ref, v_ref, g_ref, outs, extra=None):
    c = ids[1]
    in_first, in_last = document_masks(docs_ref[...])
    for t, out in enumerate(outs):
        for s in range(groups):
            head_f, head_b = heads(s, c ^ t)
            for i in range(part):
                at = columns(head_f + i)
                forward = transposed_dot(jnp.where(in_last, k_ref[:, at], 0), v_ref[:, at]) * factor
                at = columns(head_b + i)
                backward = transposed_dot(jnp.where(in_first, q_ref[:, at], 0), g_ref[:, at]) * factor
                if extra is not None:
                    add_f, add_b = extra((c ^ t) * part + i)
                    forward, backward = forward + add_f, backward + add_b
                out[0, s * part + i] = forward.astype(BF16)
                out[1, s * part + i] = backward.astype(BF16)


def rest_terms(factor, unit, part, places, shift, total, ids, docs_ref, q_ref, k_ref, v_ref, g_ref, *outs):
    def heads(s, inner_place):
        g = places[s]
        return g * unit + inner_place * part, (g + shift) % total * unit + inner_place * part

    term_kernel(factor, len(places), part, docs_ref, ids, heads, q_ref, k_ref, v_ref, g_ref, outs)


def lead_terms(
    factor, unit, part, shift, outer, inner, ids, docs_ref, labels, q_hbm, k_hbm, v_hbm, g_hbm, carry_hbm, cot_hbm, *refs,
):
    outs, (q_ref, k_ref, v_ref, g_ref, carry_ref, cot_ref, sems) = refs[:inner], refs[inner:]
    o, c, z = ids[0], ids[1], ids[2]
    held = carry_hbm.shape[0]
    forward, backward = pl.ds(0, unit * DH), pl.ds(shift * unit * DH, unit * DH)
    copies = [
        pltpu.make_async_copy(k_hbm.at[:, forward], k_ref, sems.at[0]),
        pltpu.make_async_copy(v_hbm.at[:, forward], v_ref, sems.at[1]),
        pltpu.make_async_copy(q_hbm.at[:, backward], q_ref, sems.at[2]),
        pltpu.make_async_copy(g_hbm.at[:, backward], g_ref, sems.at[3]),
        pltpu.make_async_copy(carry_hbm.at[pl.ds(0, unit)], carry_ref, sems.at[4]),
        pltpu.make_async_copy(cot_hbm.at[pl.ds(held - unit, unit)], cot_ref, sems.at[5]),
    ]
    for copy in copies:
        copy.start()
    for copy in copies:
        copy.wait()
    first, last = own_row(labels, z), own_row(labels, DEPTH + z)
    opens = jnp.logical_and(jnp.logical_and(o == 0, c == 0), z == 0)
    closes = jnp.logical_and(jnp.logical_and(o == outer - 1, c == inner - 1), z == DEPTH - 1)
    open_f = flag(jnp.logical_and(opens, last == 0.0))
    close_b = flag(jnp.logical_and(closes, first == last)) * factor

    def extra(place):
        return open_f * carry_ref[place], close_b * cot_ref[place]

    term_kernel(
        factor, 1, part, docs_ref, ids, lambda s, place: (place * part, place * part),
        q_ref, k_ref, v_ref, g_ref, outs, extra,
    )


def block_rows(labels, z, grouped):
    if grouped:
        return [l[0:1, :] for l in labels], [l[2 * DEPTH - 1 : 2 * DEPTH, :] for l in labels]
    return [own_row(l, z) for l in labels], [own_row(l, DEPTH + z) for l in labels]


def sum_kernel(inner, levels, grouped, ids, *refs):
    labels, terms, outs = refs[:inner], refs[inner : 2 * inner], refs[2 * inner :]
    o, z = ids[0], ids[2]
    count = terms[0].shape[1]
    newest = functools.reduce(jnp.maximum, [l[2 * DEPTH - 1 : 2 * DEPTH, :] for l in labels])
    oldest = functools.reduce(jnp.minimum, [l[0:1, :] for l in labels])
    firsts, lasts = block_rows(labels, z, grouped)
    keep_f = [flag(l == newest) for l in lasts]
    keep_b = [flag(l == oldest) for l in firsts]
    low = [((o >> level) & 1) == 0 for level in range(levels)]
    for i in range(count):
        sum_f = sum(m * r[0, i].astype(F32) for m, r in zip(keep_f, terms)).astype(BF16)
        sum_b = sum(m * r[1, i].astype(F32) for m, r in zip(keep_b, terms)).astype(BF16)
        for chosen, out in zip(low, outs):
            out[i * DH : (i + 1) * DH, :] = jnp.where(chosen, sum_f, sum_b)
    rows = lax.broadcasted_iota(jnp.int32, (LABELS, DH), 0)
    marks = jnp.where(rows < LABELS // 2, jnp.broadcast_to(newest, (LABELS, DH)), jnp.broadcast_to(oldest, (LABELS, DH)))
    for out in outs:
        out[count * DH :, :] = marks.astype(BF16)


def prefix_kernel(factor, unit, part, places, shift, total, inner, outer, grouped, ids, carry_ref, cot_ref, *refs):
    labels, terms, fans = refs[:inner], refs[inner : 2 * inner], refs[2 * inner : 2 * inner + outer - 1]
    outs, edge_ref = refs[2 * inner + outer - 1 : -1], refs[-1]
    o, c, z = ids[0], ids[1], ids[2]
    held = carry_ref.shape[0]
    count = terms[0].shape[1]
    group_first, group_last = block_rows(labels, z, True)
    block_first, block_last = block_rows(labels, z, grouped)
    marks = [r[count * DH : count * DH + LABELS, :].astype(F32) for r in fans]
    outer_last = [m[0:1] for m in marks]
    outer_first = [m[LABELS // 2 : LABELS // 2 + 1] for m in marks]
    newest = functools.reduce(jnp.maximum, group_last + outer_last)
    prior_base, later_base = jnp.zeros_like(newest), newest
    earlier = [(o ^ (d + 1)) < o for d in range(outer - 1)]
    for d in range(outer - 1):
        prior_base = jnp.maximum(prior_base, jnp.where(earlier[d], outer_last[d], 0.0))
        later_base = jnp.minimum(later_base, jnp.where(earlier[d], newest, outer_first[d]))
    priors, laters, plans = [], [], []
    for t in range(inner):
        prior, later = prior_base, later_base
        for d in range(inner):
            if d != t:
                before = (c ^ d) < (c ^ t)
                prior = jnp.maximum(prior, jnp.where(before, group_last[d], 0.0))
                later = jnp.minimum(later, jnp.where(before, newest, group_first[d]))
        forward = [(flag(jnp.logical_and(earlier[d], outer_last[d] == prior)), fans[d], None) for d in range(outer - 1)]
        backward = [
            (flag(jnp.logical_and(jnp.logical_not(earlier[d]), outer_first[d] == later)), fans[d], None)
            for d in range(outer - 1)
        ]
        for d in range(inner):
            if d != t:
                before = (c ^ d) < (c ^ t)
                forward.append((flag(jnp.logical_and(before, block_last[d] == prior)), terms[d], 0))
                backward.append((flag(jnp.logical_and(jnp.logical_not(before), block_first[d] == later)), terms[d], 1))
        take_f, take_b = prior == 0.0, later == newest
        if grouped:
            take_f = jnp.logical_and(take_f, jnp.logical_and(o == 0, (c ^ t) == 0))
            take_b = jnp.logical_and(take_b, jnp.logical_and(o == outer - 1, (c ^ t) == inner - 1))
        priors.append(prior)
        laters.append(later)
        plans.append((forward, backward, flag(take_f), flag(take_b) * factor))
    for s, g in enumerate(places):
        for i in range(part):
            at = s * part + i

            def carried(head, ref):
                place = head - z * held
                mine = jnp.logical_and(place >= 0, place < held)
                return jnp.where(mine, ref[jnp.clip(place, 0, held - 1)], 0.0)

            carries = (
                carried(g * unit + c * part + i, carry_ref),
                carried((g + shift) % total * unit + c * part + i, cot_ref),
            )

            def value(ref, side):
                return (ref[at * DH : (at + 1) * DH, :] if side is None else ref[side, at]).astype(F32)

            for t, out in enumerate(outs):
                for side in range(2):
                    amount = plans[t][2 + side] * carries[side]
                    for weight, ref, which in plans[t][side]:
                        amount = amount + weight * value(ref, which)
                    out[side, at] = amount.astype(BF16)
    edge_ref[0:1, :] = priors[0]
    edge_ref[1:2, :] = laters[0]
    edge_ref[2:8, :] = jnp.broadcast_to(newest, (6, DH))


def place_of(ids):
    z = ids[2]
    side = jnp.where(z >= DEPTH // 2, 1, 0)
    return z, side, jnp.logical_or(z == 0, z == DEPTH - 1)


def edge_rows(z, labels, edges):
    first, last = own_row(labels, z), own_row(labels, DEPTH + z)
    last_before = own_row(labels, DEPTH + jnp.maximum(z - 1, 0))
    first_after = own_row(labels, jnp.minimum(z + 1, DEPTH - 1))
    final_f, final_b = labels[2 * DEPTH - 1 : 2 * DEPTH, :], labels[0:1, :]
    prior = later = final_f
    if edges is not None:
        prior, later = edges[0:1, :], edges[1:2, :]
    return (last, last_before, final_f, first, prior), (first, first_after, final_b, last, later)


def pick(which, rows):
    return [jnp.where(which == 0, a, b) for a, b in zip(*rows)]


def hop(side, rows, lead, off, part, term_ref, prefix_ref, got_ref, out):
    own, neighbour, _, _, prior = pick(side, rows)
    other, _, final, _, _ = pick(1 - side, rows)
    join, keep, counts = flag(prior == own), flag(neighbour == own), flag(other == final)
    for i in range(part):
        state = term_ref[side, off + i].astype(F32)
        if lead:
            rest = counts * term_ref[1 - side, off + i].astype(F32)
        else:
            state = state + join * prefix_ref[side, off + i].astype(F32)
            rest = prefix_ref[1 - side, off + i].astype(F32)
        if got_ref is not None:
            state = state + keep * got_ref[0, i].astype(F32)
            rest = rest + got_ref[1, i].astype(F32)
        out[0, i] = state.astype(BF16)
        out[1, i] = rest.astype(BF16)


def hop_kernel(part, near, far, has_edges, ids, labels, *refs):
    z, side, at_end = place_of(ids)
    out, refs = refs[-1], list(refs[:-1])
    rows = edge_rows(z, labels, refs.pop(0) if has_edges else None)
    if near is not None:
        lead, off = near
        term = refs.pop(0)
        prefix = None if lead else refs.pop(0)

        @pl.when(at_end)
        def _():
            hop(side, rows, lead, off, part, term, prefix, None, out)

    if far is not None:
        lead, off, across = far
        term_far = refs.pop(0)
        prefix_far = None if lead else refs.pop(0)
        got = refs.pop(0)

        @pl.when(jnp.logical_not(at_end))
        def _():
            hop(side if across else 1 - side, rows, lead, off, part, term_far, prefix_far, got, out)


def lead_total_kernel(part, turns, ids, labels, *refs):
    z, side, at_end = place_of(ids)
    rows = edge_rows(z, labels, None)
    for t in range(turns):
        term, near, middle, far = refs[4 * t : 4 * t + 4]
        out = refs[4 * turns + t]

        def total(which, over, rest):
            own, neighbour, final, _, _ = pick(which, rows)
            counts, come = flag(own == final), flag(neighbour == final)
            for i in range(part):
                value = counts * term[which, i].astype(F32)
                if over is not None:
                    value = value + come * over[0, i].astype(F32)
                if rest is not None:
                    value = value + rest[1, i].astype(F32)
                out[which, i] = value.astype(BF16)

        @pl.when(at_end)
        def _():
            total(side, None, far)
            total(1 - side, far, None)

        @pl.when(jnp.logical_not(at_end))
        def _():
            total(side, near, middle)
            total(1 - side, middle, near)


def output_kernel(
    factor, base, part, turn, sides, ids, labels, edges, docs_ref, row_ref, q_ref, k_ref, v_ref, g_ref, *refs,
):
    sources = (refs[:4], refs[4:8])
    outs, (states, held, sems) = refs[-7:-3], refs[-3:]
    c = ids[1]
    z, side, at_end = place_of(ids)
    rows = edge_rows(z, labels, edges)

    for which in range(2):
        lead, off = sides[which]
        prefix, near, middle, far = sources[which]
        _, neighbour, _, target, prior = rows[which]
        reach, come = flag(prior == target), flag(neighbour == target)

        def state(over, rest):
            for i in range(part):
                value = reach * prefix[which, off + i].astype(F32)
                if over is not None:
                    value = value + come * over[0, i].astype(F32)
                if rest is not None and not lead:
                    value = value + reach * rest[1, i].astype(F32)
                states[which, i] = value.astype(BF16)

        near_side = side == which
        for condition, over, rest in (
            (jnp.logical_and(at_end, near_side), None, far),
            (jnp.logical_and(at_end, jnp.logical_not(near_side)), far, None),
            (jnp.logical_and(jnp.logical_not(at_end), near_side), near, middle),
            (jnp.logical_and(jnp.logical_not(at_end), jnp.logical_not(near_side)), middle, near),
        ):
            pl.when(condition)(functools.partial(state, over, rest))

    docs = docs_ref[...]
    in_first, in_last = document_masks(docs)
    places = lax.broadcasted_iota(jnp.int32, (SPAN, SPAN), 0)
    others = lax.broadcasted_iota(jnp.int32, (SPAN, SPAN), 1)
    allowed = jnp.logical_and(others <= places, docs == row_ref[0:1])
    head = base + (c ^ turn) * part
    copies = []
    for i in range(part):
        at = columns(head + i)
        q, k, v, g = q_ref[:, at], k_ref[:, at], v_ref[:, at], g_ref[:, at]
        before, after = states[0, i], states[1, i]
        scores = jnp.where(allowed, dot_transposed(q, k) * factor, 0.0).astype(BF16)
        grad_scores = jnp.where(allowed, dot_transposed(g, v) * factor, 0.0).astype(BF16)
        results = (
            dot(scores, v) + dot(jnp.where(in_first, q, 0), before),
            dot(grad_scores, k) + dot_transposed(jnp.where(in_first, g, 0), before),
            transposed_dot(grad_scores, q) + dot_transposed(jnp.where(in_last, v, 0), after),
            transposed_dot(scores, g) + dot(jnp.where(in_last, k, 0), after),
        )
        for n, result in enumerate(results):
            held[n, i] = result.astype(BF16)
            copy = pltpu.make_async_copy(held.at[n, i], outs[n].at[:, at], sems.at[n, i])
            copy.start()
            copies.append(copy)
    for copy in copies:
        copy.wait()


def shards(queries, keys, values, out_grad, doc_ids, carry_in, carry_cot):
    outer, inner, depth = (lax.axis_size(a) for a in ("outer", "inner", "heads"))
    assert depth == DEPTH
    tokens_all = doc_ids.shape[0] * outer * inner
    factor = float(DH * (tokens_all // 2)) ** (-0.5)
    head_count = queries.shape[1] // DH
    held = carry_in.shape[0]
    arrays = (queries, keys, values, out_grad)
    part = min(4, head_count // inner)
    unit = part * inner
    groups = head_count // unit
    leads = held % unit == 0
    shift = groups - 1 if leads else 0

    ids = jnp.stack([lax.axis_index(a) for a in ("outer", "inner", "heads")]).astype(jnp.int32)
    blocks = doc_ids.reshape(depth, SPAN)
    corners = jnp.concatenate([blocks[:, 0], blocks[:, -1]]).astype(F32)
    own_labels = jnp.broadcast_to(corners[:, None], (2 * depth, DH))
    labels = [own_labels] + [pairs(own_labels, "inner", d) for d in range(1, inner)]
    docs = lax.dynamic_index_in_dim(blocks, ids[2], 0, False)
    docs_column = jnp.broadcast_to(docs[:, None], (SPAN, DH))
    docs_row = jnp.broadcast_to(docs[None, :], (8, SPAN))

    levels = (outer - 1).bit_length()
    product = 2 * SPAN * DH * DH
    token = jnp.zeros((8, DH), F32) + 0.0 * own_labels[0, 0]

    def state_pair(count):
        return jax.ShapeDtypeStruct((2, count, DH, DH), BF16)

    terms, prefixes, near, middle, far = {}, {}, {}, {}, {}
    edge = None

    def exchange(own):
        return [own[0]] + [pairs(own[d], "inner", d) for d in range(1, inner)]

    def make_lead_terms():
        nonlocal token
        block = pltpu.VMEM((SPAN, unit * DH), BF16)
        carry = pltpu.VMEM((unit, DH, DH), F32)
        token, own = call(
            token,
            functools.partial(lead_terms, factor, unit, part, shift, outer, inner),
            (ids, docs_column, own_labels) + arrays + (carry_in, carry_cot),
            [state_pair(part)] * inner,
            2 * unit * product,
            scratch=[block] * 4 + [carry] * 2 + [pltpu.SemaphoreType.DMA((6,))],
            specs=[SMEM, VMEM, VMEM] + [ANY] * 6,
        )
        terms[0] = [(a, 0) for a in own]

    def make_terms(places):
        nonlocal token
        token, own = call(
            token,
            functools.partial(rest_terms, factor, unit, part, places, shift, groups),
            (ids, docs_column) + arrays,
            [state_pair(part * len(places))] * inner,
            2 * unit * len(places) * product,
        )
        for s, g in enumerate(places):
            terms[g] = [(a, s * part) for a in own]
        return exchange(own)

    def make_sums(received, grouped):
        nonlocal token
        count = received[0].shape[1]
        token, sums = call(
            token,
            functools.partial(sum_kernel, inner, levels, grouped),
            (ids, *labels, *received),
            [jax.ShapeDtypeStruct((count * DH + LABELS, DH), BF16)] * levels,
            count * DH * DH * 8,
        )
        return [pairs(sums[d.bit_length() - 1], "outer", d) for d in range(1, outer)]

    def make_prefixes(places, received, fans, grouped):
        nonlocal token, edge
        count = received[0].shape[1]
        token, given = call(
            token,
            functools.partial(
                prefix_kernel, factor, unit, part, places, shift, groups, inner, outer, grouped
            ),
            (ids, carry_in, carry_cot, *labels, *received, *fans),
            [state_pair(count)] * inner + [jax.ShapeDtypeStruct((8, DH), F32)],
            count * DH * DH * 16 * inner,
        )
        edge = given[-1] if edge is None else edge
        given = exchange(given[:-1])
        for s, g in enumerate(places):
            prefixes[g] = [(a, s * part) for a in given]

    def operands_of(chunk):
        g, t = chunk
        lead = leads and g == 0
        array, off = terms[g][t]
        return lead, off, [array] if lead else [array, prefixes[g][t][0]]

    def move(near_chunk, far_chunk, across, perm):
        nonlocal token
        use_edges = any(c is not None and not (leads and c[0] == 0) for c in (near_chunk, far_chunk))
        operands = [ids, own_labels] + ([edge] if use_edges else [])
        near_plan = far_plan = None
        if near_chunk is not None:
            lead, off, more = operands_of(near_chunk)
            near_plan = (lead, off)
            operands += more
        if far_chunk is not None:
            lead, off, more = operands_of(far_chunk)
            far_plan = (lead, off, across)
            operands += more + [near[far_chunk] if across else middle[far_chunk]]
        token, sent = call(
            token,
            functools.partial(hop_kernel, part, near_plan, far_plan, use_edges),
            operands,
            [state_pair(part)],
            part * DH * DH * 8,
        )
        return lax.ppermute(sent[0], "heads", perm)

    def ends(near_chunk, far_chunk):
        perm = ([(0, 1), (3, 2)] if near_chunk is not None else []) + ([(1, 0), (2, 3)] if far_chunk is not None else [])
        got = move(near_chunk, far_chunk, False, perm)
        if near_chunk is not None:
            near[near_chunk] = got
        if far_chunk is not None:
            far[far_chunk] = got

    def across(chunk):
        middle[chunk] = move(None, chunk, True, [(1, 2), (2, 1)])

    out_shape = jax.ShapeDtypeStruct(queries.shape, BF16)
    results = ()

    def make_outputs(g, t):
        nonlocal token, results
        operands = (ids, own_labels, edge, docs_column, docs_row) + arrays
        sides = []
        for chunk in ((g, t), ((g - shift) % groups, t)):
            lead = leads and chunk[0] == 0
            array, off = prefixes[chunk[0]][t]
            sides.append((lead, off))
            operands += (array, near[chunk], middle[chunk], far[chunk])
        token, results = call(
            token,
            functools.partial(output_kernel, factor, g * unit, part, t, tuple(sides)),
            operands + tuple(results),
            [out_shape] * 4,
            10 * part * product,
            scratch=[
                pltpu.VMEM((2, part, DH, DH), BF16),
                pltpu.VMEM((4, part, SPAN, DH), BF16),
                pltpu.SemaphoreType.DMA((4, part)),
            ],
            aliases={len(operands) + i: i for i in range(len(results))},
            specs=[SMEM] + [VMEM] * (len(operands) - 1) + [ANY] * len(results),
            out_specs=[ANY] * 4,
        )

    if leads and groups == 4 and inner == 2:
        make_lead_terms()
        ends((0, 0), None)
        ends((0, 1), None)
        got_a = make_terms((1,))
        got_b = make_terms((2, 3))
        fans_a = make_sums(got_a, False)
        across((0, 0))
        fans_b = make_sums(got_b, False)
        across((0, 1))
        make_prefixes((1,), got_a, fans_a, False)
        ends((1, 0), (0, 0))
        ends((1, 1), (0, 1))
        make_prefixes((2, 3), got_b, fans_b, False)
        across((1, 0))
        token, totals = call(
            token,
            functools.partial(lead_total_kernel, part, inner),
            [ids, own_labels]
            + [a for t in range(inner) for a in (terms[0][t][0], near[0, t], middle[0, t], far[0, t])],
            [state_pair(part)] * inner,
            unit * DH * DH * 8,
        )
        got_lead = exchange(totals)
        across((1, 1))
        ends((2, 0), None)
        fans_lead = make_sums(got_lead, True)
        ends((2, 1), (1, 0))
        across((2, 0))
        ends((3, 0), (1, 1))
        across((2, 1))
        make_prefixes((0,), got_lead, fans_lead, True)
        make_outputs(0, 0)
        ends((3, 1), (2, 0))
        across((3, 0))
        make_outputs(0, 1)
        ends(None, (2, 1))
        across((3, 1))
        make_outputs(1, 0)
        ends(None, (3, 0))
        make_outputs(1, 1)
        ends(None, (3, 1))
        make_outputs(2, 0)
        make_outputs(3, 0)
        make_outputs(2, 1)
        make_outputs(3, 1)
    else:
        assert not leads
        for g in range(groups):
            got = make_terms((g,))
            make_prefixes((g,), got, make_sums(got, False), False)
        chunks = [(g, t) for g in range(groups) for t in range(inner)]
        lag = 4
        for k in range(len(chunks) + lag):
            ends(chunks[k] if k < len(chunks) else None, chunks[k - lag] if k >= lag else None)
            if k < len(chunks):
                across(chunks[k])
        for g, t in chunks:
            make_outputs(g, t)
    return tuple(results)


def solution(mesh):
    tokens = P(("outer", "inner", "heads"), None)
    carry = P("heads", None, None)
    return jax.shard_map(
        shards,
        mesh=mesh,
        in_specs=(tokens,) * 4 + (P(("outer", "inner")), carry, carry),
        out_specs=(tokens,) * 4,
        check_vma=False,
    )
```

time: 131 us -> 134 us (1.023)
  starting transfers between devices: 50.3 us -> 63.5 us
  waiting for transfers between devices: 29 us -> 18.7 us
  local copies, waits for them, and re-layouts: 5.93 us -> 8.19 us
  Pallas kernels: 43.2 us -> 41.5 us
    ppermute x20 -> x19, starting transfers between devices: 33.2 us -> 51.1 us  [move(): return lax.ppermute(sent[0], 'heads', perm)]
    ppermute x21 -> x16, waiting for transfers between devices: 10.7 us -> 2.14 us  [pairs(): return lax.ppermute(array, axis, [(i, i ^ distance) for i in range(count)])]
    ppermute x21 -> x16, starting transfers between devices: 17.1 us -> 12.5 us  [pairs(): return lax.ppermute(array, axis, [(i, i ^ distance) for i in range(count)])]
    unnamed x20 -> x24, local copies, waits for them, and re-layouts: 5.6 us -> 7.68 us
    pallas_call x40 -> x37, Pallas kernels: 43.2 us -> 41.5 us  [call(): pl.pallas_call(ordered, in_specs=list(specs or [SMEM] + [VMEM] * (count -...]
    ppermute x20 -> x19, waiting for transfers between devices: 18.2 us -> 16.5 us  [move(): return lax.ppermute(sent[0], 'heads', perm)]
  transfers between devices with their start and end apart: 41 -> 35, of which waited for: 13 -> 9; matrix products, arithmetic and copies ran while one was open for 0% -> 0% of each run, Pallas kernels for 31% -> 24%
where the time goes in v3:
time: 134 us
  starting transfers between devices  63.5 us (47%)
  Pallas kernels  41.5 us (31%)
  waiting for transfers between devices  18.7 us (14%)
  local copies, waits for them, and re-layouts  8.19 us (6%)
  between operations  1.48 us (1%)
    ppermute x19, starting transfers between devices, move(): return lax.ppermute(sent[0], 'heads', perm)  51.1 us
    pallas_call x37, Pallas kernels, call(): pl.pallas_call(ordered, in_specs=list(specs or [SMEM] + [VMEM] * (count -...  41.5 us
    ppermute x19, waiting for transfers between devices, move(): return lax.ppermute(sent[0], 'heads', perm)  16.5 us
    ppermute x16, starting transfers between devices, pairs(): return lax.ppermute(array, axis, [(i, i ^ distance) for i in range(count)])  12.5 us
    unnamed x24, local copies, waits for them, and re-layouts  7.68 us
  transfers between devices with their start and end apart: 35, of which 9 were waited for; matrix products, arithmetic and copies ran while one was open for 0% of the time, Pallas kernels for 24%

profile of v3, /device:TPU:0, one launch (start us, length us, event | category | flops | bytes accessed | tf_op | source)
XLA Modules:
  0.0 133.6 jit_solution(12856488719688422716)
XLA Ops:
  2.1 1.2 copy-done
  3.4 1.2 copy-done.2
  4.6 1.2 copy-done.4
  5.8 1.2 copy-done.6
  7.0 1.0 copy-done.8
  8.1 1.0 copy-done.10
  9.1 1.2 shard_map.102
  11.5 1.0 shard_map.105
  12.5 1.2 shard_map.106
  14.4 4.9 %collective-permute-start.7 = (bf16[2,4,128,128]{3,2,1,0:T(8,128)(2,1)S(1)}, bf16[2,4,128,128]{3,2,1,0:T(8,128)(2,1)S(1)}, u32[]{:S(2)}, u32[]{:S(2)}) collective-permute-start(bf16[2,4,128,128]{3,2,1,0:T(8,128)(2,1)S(1)} %get-tuple-element.126), channel_id=1, source_target_pairs={{0,1},{3,2},{4,5},{7,6},{8,9},{11,10},{12,13},{15,14},{16,17},{19,... | collective-permute-start | bytes 786440 | tf_op jit(solution)/shard_map/ppermute | solution.py:504
  19.3 1.3 %collective-permute-start.5 = (bf16[2,4,128,128]{3,2,1,0:T(8,128)(2,1)S(1)}, bf16[2,4,128,128]{3,2,1,0:T(8,128)(2,1)S(1)}, u32[]{:S(2)}, u32[]{:S(2)}) collective-permute-start(bf16[2,4,128,128]{3,2,1,0:T(8,128)(2,1)S(1)} %get-tuple-element.123), channel_id=1, source_target_pairs={{0,1},{3,2},{4,5},{7,6},{8,9},{11,10},{12,13},{15,14},{16,17},{19,... | collective-permute-start | bytes 786440 | tf_op jit(solution)/shard_map/ppermute | solution.py:504
  21.3 4.5 %collective-permute-done.7.refs_3_.refs_10_.refs_14_ = bf16[2,4,128,128]{3,2,1,0:T(8,128)(2,1)S(1)} collective-permute-done((bf16[2,4,128,128]{3,2,1,0:T(8,128)(2,1)S(1)}, bf16[2,4,128,128]{3,2,1,0:T(8,128)(2,1)S(1)}, u32[]{:S(2)}, u32[]{:S(2)}) %collective-permute-start.7) | collective-permute-done | bytes 262176 | tf_op jit(solution)/shard_map/ppermute | solution.py:504
  27.1 1.6 %collective-permute-start.2 = (bf16[528,128]{1,0:T(8,128)(2,1)S(1)}, bf16[528,128]{1,0:T(8,128)(2,1)S(1)}, u32[]{:S(2)}, u32[]{:S(2)}) collective-permute-start(bf16[528,128]{1,0:T(8,128)(2,1)S(1)} %get-tuple-element.121), channel_id=1, source_target_pairs={{0,8},{8,0},{16,24},{24,16},{1,9},{9,1},{17,25},{25,17},{2,10},{10... | collective-permute-start | bytes 405512 | tf_op jit(solution)/shard_map/ppermute | solution.py:24
  28.7 1.5 %collective-permute-start.4 = (bf16[528,128]{1,0:T(8,128)(2,1)S(1)}, bf16[528,128]{1,0:T(8,128)(2,1)S(1)}, u32[]{:S(2)}, u32[]{:S(2)}) collective-permute-start(bf16[528,128]{1,0:T(8,128)(2,1)S(1)} %get-tuple-element.122), channel_id=1, source_target_pairs={{0,24},{8,16},{16,8},{24,0},{1,25},{9,17},{17,9},{25,1},{2,26},{10... | collective-permute-start | bytes 405512 | tf_op jit(solution)/shard_map/ppermute | solution.py:24
  30.7 0.8 shard_map.109
  31.5 1.6 %collective-permute-start.8 = (bf16[1040,128]{1,0:T(8,128)(2,1)S(1)}, bf16[1040,128]{1,0:T(8,128)(2,1)S(1)}, u32[]{:S(2)}, u32[]{:S(2)}) collective-permute-start(bf16[1040,128]{1,0:T(8,128)(2,1)S(1)} %get-tuple-element.132), channel_id=1, source_target_pairs={{0,8},{8,0},{16,24},{24,16},{1,9},{9,1},{17,25},{25,17},{2,10},{10... | collective-permute-start | bytes 798728 | tf_op jit(solution)/shard_map/ppermute | solution.py:24
  33.5 1.4 %collective-permute-start.10 = (bf16[1040,128]{1,0:T(8,128)(2,1)S(1)}, bf16[1040,128]{1,0:T(8,128)(2,1)S(1)}, u32[]{:S(2)}, u32[]{:S(2)}) collective-permute-start(bf16[1040,128]{1,0:T(8,128)(2,1)S(1)} %get-tuple-element.133), channel_id=1, source_target_pairs={{0,24},{8,16},{16,8},{24,0},{1,25},{9,17},{17,9},{25,1},{2,26},{10... | collective-permute-start | bytes 798728 | tf_op jit(solution)/shard_map/ppermute | solution.py:24
  34.9 1.4 %collective-permute-done.4.refs_9_ = bf16[528,128]{1,0:T(8,128)(2,1)S(1)} collective-permute-done((bf16[528,128]{1,0:T(8,128)(2,1)S(1)}, bf16[528,128]{1,0:T(8,128)(2,1)S(1)}, u32[]{:S(2)}, u32[]{:S(2)}) %collective-permute-start.4) | collective-permute-done | bytes 135200 | tf_op jit(solution)/shard_map/ppermute | solution.py:24
  36.3 1.6 %collective-permute-start.9 = (bf16[1040,128]{1,0:T(8,128)(2,1)S(1)}, bf16[1040,128]{1,0:T(8,128)(2,1)S(1)}, u32[]{:S(2)}, u32[]{:S(2)}) collective-permute-start(bf16[1040,128]{1,0:T(8,128)(2,1)S(1)} %get-tuple-element.133), channel_id=1, source_target_pairs={{0,16},{8,24},{16,0},{24,8},{1,17},{9,25},{17,1},{25,9},{2,18},{10... | collective-permute-start | bytes 798728 | tf_op jit(solution)/shard_map/ppermute | solution.py:24
  38.5 1.0 shard_map.111
  41.1 7.1 %collective-permute-start.16 = (bf16[2,4,128,128]{3,2,1,0:T(8,128)(2,1)S(1)}, bf16[2,4,128,128]{3,2,1,0:T(8,128)(2,1)S(1)}, u32[]{:S(2)}, u32[]{:S(2)}) collective-permute-start(bf16[2,4,128,128]{3,2,1,0:T(8,128)(2,1)S(1)} %get-tuple-element.144), channel_id=1, source_target_pairs={{0,1},{3,2},{1,0},{2,3},{4,5},{7,6},{5,4},{6,7},{8,9},{11,10},{9,8... | collective-permute-start | bytes 786440 | tf_op jit(solution)/shard_map/ppermute | solution.py:504
  48.8 7.6 %collective-permute-start.15 = (bf16[2,4,128,128]{3,2,1,0:T(8,128)(2,1)S(1)}, bf16[2,4,128,128]{3,2,1,0:T(8,128)(2,1)S(1)}, u32[]{:S(2)}, u32[]{:S(2)}) collective-permute-start(bf16[2,4,128,128]{3,2,1,0:T(8,128)(2,1)S(1)} %get-tuple-element.143), channel_id=1, source_target_pairs={{0,1},{3,2},{1,0},{2,3},{4,5},{7,6},{5,4},{6,7},{8,9},{11,10},{9,8... | collective-permute-start | bytes 786440 | tf_op jit(solution)/shard_map/ppermute | solution.py:504
  56.4 1.9 %shard_map.114 = (bf16[2,8,128,128]{3,2,1,0:T(8,128)(2,1)S(1)}, bf16[2,8,128,128]{3,2,1,0:T(8,128)(2,1)S(1)}, f32[8,128]{1,0:T(8,128)}, f32[8,128]{1,0:T(8,128)S(1)}) custom-call(s32[3]{0:T(128)S(1)} %pad_add_fusion.refs_0_, f32[8,128,128]{2,1,0:T(8,128)S(1)} %copy-done.9, f32[8,128,128]{2,1,0:T(8,128)S(1)} %copy-done.10, ...), custom_call_target="tpu_custom_call", output_to_operand_aliasing={{3}: (10, {})} | custom-call | flops 4194304 | bytes 3956748 | tf_op jit(solution)/shard_map/pallas_call | solution.py:50
  58.9 3.7 %collective-permute-done.15.refs_9_.refs_5_.refs_12_.refs_14_.refs_10_.refs_16_ = bf16[2,4,128,128]{3,2,1,0:T(8,128)(2,1)S(1)} collective-permute-done((bf16[2,4,128,128]{3,2,1,0:T(8,128)(2,1)S(1)}, bf16[2,4,128,128]{3,2,1,0:T(8,128)(2,1)S(1)}, u32[]{:S(2)}, u32[]{:S(2)}) %collective-permute-start.15) | collective-permute-done | bytes 262176 | tf_op jit(solution)/shard_map/ppermute | solution.py:504
  62.6 0.7 shard_map.116
  65.2 5.5 %collective-permute-start.17 = (bf16[2,4,128,128]{3,2,1,0:T(8,128)(2,1)S(1)}, bf16[2,4,128,128]{3,2,1,0:T(8,128)(2,1)S(1)}, u32[]{:S(2)}, u32[]{:S(2)}) collective-permute-start(bf16[2,4,128,128]{3,2,1,0:T(8,128)(2,1)S(1)} %get-tuple-element.149), channel_id=1, source_target_pairs={{0,1},{3,2},{4,5},{7,6},{8,9},{11,10},{12,13},{15,14},{16,17},{19,... | collective-permute-start | bytes 786440 | tf_op jit(solution)/shard_map/ppermute | solution.py:504
  72.7 4.2 %collective-permute-start.24 = (bf16[2,4,128,128]{3,2,1,0:T(8,128)(2,1)S(1)}, bf16[2,4,128,128]{3,2,1,0:T(8,128)(2,1)S(1)}, u32[]{:S(2)}, u32[]{:S(2)}) collective-permute-start(bf16[2,4,128,128]{3,2,1,0:T(8,128)(2,1)S(1)} %get-tuple-element.159), channel_id=1, source_target_pairs={{0,1},{3,2},{1,0},{2,3},{4,5},{7,6},{5,4},{6,7},{8,9},{11,10},{9,8... | collective-permute-start | bytes 786440 | tf_op jit(solution)/shard_map/ppermute | solution.py:504
  78.2 1.0 collective-permute-start.21
  79.2 1.5 %collective-permute-start.23 = (bf16[528,128]{1,0:T(8,128)(2,1)S(1)}, bf16[528,128]{1,0:T(8,128)(2,1)S(1)}, u32[]{:S(2)}, u32[]{:S(2)}) collective-permute-start(bf16[528,128]{1,0:T(8,128)(2,1)S(1)} %get-tuple-element.158), channel_id=1, source_target_pairs={{0,24},{8,16},{16,8},{24,0},{1,25},{9,17},{17,9},{25,1},{2,26},{10... | collective-permute-start | bytes 405512 | tf_op jit(solution)/shard_map/ppermute | solution.py:24
  80.7 1.0 collective-permute-start.22
  82.7 5.6 %collective-permute-start.29 = (bf16[2,4,128,128]{3,2,1,0:T(8,128)(2,1)S(1)}, bf16[2,4,128,128]{3,2,1,0:T(8,128)(2,1)S(1)}, u32[]{:S(2)}, u32[]{:S(2)}) collective-permute-start(bf16[2,4,128,128]{3,2,1,0:T(8,128)(2,1)S(1)} %get-tuple-element.170), channel_id=1, source_target_pairs={{0,1},{3,2},{1,0},{2,3},{4,5},{7,6},{5,4},{6,7},{8,9},{11,10},{9,8... | collective-permute-start | bytes 786440 | tf_op jit(solution)/shard_map/ppermute | solution.py:504
  88.9 1.5 %shard_map.124 = (bf16[2,4,128,128]{3,2,1,0:T(8,128)(2,1)S(1)}, bf16[2,4,128,128]{3,2,1,0:T(8,128)(2,1)S(1)}, f32[8,128]{1,0:T(8,128)}, f32[8,128]{1,0:T(8,128)S(1)}) custom-call(s32[3]{0:T(128)S(1)} %pad_add_fusion.refs_0_, f32[8,128,128]{2,1,0:T(8,128)S(1)} %copy-done.9, f32[8,128,128]{2,1,0:T(8,128)S(1)} %copy-done.10, ...), custom_call_target="tpu_custom_call", output_to_operand_aliasing={{3}: (10, {})} | custom-call | flops 2097152 | bytes 2514956 | tf_op jit(solution)/shard_map/pallas_call | solution.py:50
  91.0 2.5 %shard_map.125 = (bf16[128,4096]{1,0:T(8,128)(2,1)}, bf16[128,4096]{1,0:T(8,128)(2,1)}, bf16[128,4096]{1,0:T(8,128)(2,1)}, bf16[128,4096]{1,0:T(8,128)(2,1)}, f32[8,128]{1,0:T(8,128)S(1)}) custom-call(s32[3]{0:T(128)S(1)} %pad_add_fusion.refs_0_, f32[8,128]{1,0:T(8,128)S(1)} %broadcast_in_dim.8.refs_2_.refs_1_.refs_3_, ...), custom_call_target="tpu_custom_call", output_to_operand_aliasing={{4}: (17, {})} | custom-call | flops 167772160 | bytes 10563596 | tf_op jit(solution)/shard_map/pallas_call | solution.py:50
  94.1 5.7 %collective-permute-start.26 = (bf16[2,4,128,128]{3,2,1,0:T(8,128)(2,1)S(1)}, bf16[2,4,128,128]{3,2,1,0:T(8,128)(2,1)S(1)}, u32[]{:S(2)}, u32[]{:S(2)}) collective-permute-start(bf16[2,4,128,128]{3,2,1,0:T(8,128)(2,1)S(1)} %get-tuple-element.167), channel_id=1, source_target_pairs={{0,1},{3,2},{1,0},{2,3},{4,5},{7,6},{5,4},{6,7},{8,9},{11,10},{9,8... | collective-permute-start | bytes 786440 | tf_op jit(solution)/shard_map/ppermute | solution.py:504
  101.0 2.5 %shard_map.128 = (bf16[128,4096]{1,0:T(8,128)(2,1)}, bf16[128,4096]{1,0:T(8,128)(2,1)}, bf16[128,4096]{1,0:T(8,128)(2,1)}, bf16[128,4096]{1,0:T(8,128)(2,1)}, f32[8,128]{1,0:T(8,128)S(1)}) custom-call(s32[3]{0:T(128)S(1)} %pad_add_fusion.refs_0_, ...), custom_call_target="tpu_custom_call", output_to_operand_aliasing={{0}: (17, {}), {1}: (18, {}), {2}: (19, {}), {3}: (20, {}),... | custom-call | flops 167772160 | bytes 14757900 | tf_op jit(solution)/shard_map/pallas_call | solution.py:50
  103.5 0.7 shard_map.129
  104.2 1.3 collective-permute-start.31
  105.5 0.9 collective-permute-done.26.refs_5_.refs_16_.refs_12_.refs_14_.refs_10_
  107.7 2.5 %shard_map.131 = (bf16[128,4096]{1,0:T(8,128)(2,1)}, bf16[128,4096]{1,0:T(8,128)(2,1)}, bf16[128,4096]{1,0:T(8,128)(2,1)}, bf16[128,4096]{1,0:T(8,128)(2,1)}, f32[8,128]{1,0:T(8,128)S(1)}) custom-call(s32[3]{0:T(128)S(1)} %pad_add_fusion.refs_0_, ...), custom_call_target="tpu_custom_call", output_to_operand_aliasing={{0}: (17, {}), {1}: (18, {}), {2}: (19, {}), {3}: (20, {}),... | custom-call | flops 167772160 | bytes 15020044 | tf_op jit(solution)/shard_map/pallas_call | solution.py:50
  110.8 1.3 collective-permute-start.34
  112.1 2.9 %collective-permute-done.31.refs_16_.refs_12_ = bf16[2,4,128,128]{3,2,1,0:T(8,128)(2,1)S(1)} collective-permute-done((bf16[2,4,128,128]{3,2,1,0:T(8,128)(2,1)S(1)}, bf16[2,4,128,128]{3,2,1,0:T(8,128)(2,1)S(1)}, u32[]{:S(2)}, u32[]{:S(2)}) %collective-permute-start.31) | collective-permute-done | bytes 262176 | tf_op jit(solution)/shard_map/ppermute | solution.py:504
  115.0 2.5 %shard_map.133 = (bf16[128,4096]{1,0:T(8,128)(2,1)}, bf16[128,4096]{1,0:T(8,128)(2,1)}, bf16[128,4096]{1,0:T(8,128)(2,1)}, bf16[128,4096]{1,0:T(8,128)(2,1)}, f32[8,128]{1,0:T(8,128)S(1)}) custom-call(s32[3]{0:T(128)S(1)} %pad_add_fusion.refs_0_, ...), custom_call_target="tpu_custom_call", output_to_operand_aliasing={{0}: (17, {}), {1}: (18, {}), {2}: (19, {}), {3}: (20, {}),... | custom-call | flops 167772160 | bytes 15020044 | tf_op jit(solution)/shard_map/pallas_call | solution.py:50
  118.1 1.3 collective-permute-start.33
  119.4 4.1 %collective-permute-done.34.refs_16_.refs_12_ = bf16[2,4,128,128]{3,2,1,0:T(8,128)(2,1)S(1)} collective-permute-done((bf16[2,4,128,128]{3,2,1,0:T(8,128)(2,1)S(1)}, bf16[2,4,128,128]{3,2,1,0:T(8,128)(2,1)S(1)}, u32[]{:S(2)}, u32[]{:S(2)}) %collective-permute-start.34) | collective-permute-done | bytes 262176 | tf_op jit(solution)/shard_map/ppermute | solution.py:504
  123.4 2.5 %shard_map.135 = (bf16[128,4096]{1,0:T(8,128)(2,1)}, bf16[128,4096]{1,0:T(8,128)(2,1)}, bf16[128,4096]{1,0:T(8,128)(2,1)}, bf16[128,4096]{1,0:T(8,128)(2,1)}, f32[8,128]{1,0:T(8,128)S(1)}) custom-call(s32[3]{0:T(128)S(1)} %pad_add_fusion.refs_0_, ...), custom_call_target="tpu_custom_call", output_to_operand_aliasing={{0}: (17, {}), {1}: (18, {}), {2}: (19, {}), {3}: (20, {}),... | custom-call | flops 167772160 | bytes 15282188 | tf_op jit(solution)/shard_map/pallas_call | solution.py:50
  125.9 2.5 %shard_map.136 = (bf16[128,4096]{1,0:T(8,128)(2,1)}, bf16[128,4096]{1,0:T(8,128)(2,1)}, bf16[128,4096]{1,0:T(8,128)(2,1)}, bf16[128,4096]{1,0:T(8,128)(2,1)}, f32[8,128]{1,0:T(8,128)S(1)}) custom-call(s32[3]{0:T(128)S(1)} %pad_add_fusion.refs_0_, ...), custom_call_target="tpu_custom_call", output_to_operand_aliasing={{0}: (17, {}), {1}: (18, {}), {2}: (19, {}), {3}: (20, {}),... | custom-call | flops 167772160 | bytes 15020044 | tf_op jit(solution)/shard_map/pallas_call | solution.py:50
  128.4 2.5 %shard_map.137 = (bf16[128,4096]{1,0:T(8,128)(2,1)}, bf16[128,4096]{1,0:T(8,128)(2,1)}, bf16[128,4096]{1,0:T(8,128)(2,1)}, bf16[128,4096]{1,0:T(8,128)(2,1)}, f32[8,128]{1,0:T(8,128)S(1)}) custom-call(s32[3]{0:T(128)S(1)} %pad_add_fusion.refs_0_, ...), custom_call_target="tpu_custom_call", output_to_operand_aliasing={{0}: (17, {}), {1}: (18, {}), {2}: (19, {}), {3}: (20, {}),... | custom-call | flops 167772160 | bytes 15282188 | tf_op jit(solution)/shard_map/pallas_call | solution.py:50
  130.9 2.5 %shard_map.138 = (bf16[128,4096]{1,0:T(8,128)(2,1)}, bf16[128,4096]{1,0:T(8,128)(2,1)}, bf16[128,4096]{1,0:T(8,128)(2,1)}, bf16[128,4096]{1,0:T(8,128)(2,1)}, f32[8,128]{1,0:T(8,128)S(1)}) custom-call(s32[3]{0:T(128)S(1)} %pad_add_fusion.refs_0_, ...), custom_call_target="tpu_custom_call", output_to_operand_aliasing={{0}: (17, {}), {1}: (18, {}), {2}: (19, {}), {3}: (20, {}),... | custom-call | flops 167772160 | bytes 15020044 | tf_op jit(solution)/shard_map/pallas_call | solution.py:50
  (94 shorter events, 20.9 us)
Async XLA Ops:
  0.6 0.7 copy-start.11
  2.1 1.2 copy-start
  3.4 1.2 copy-start.2
  4.6 1.2 copy-start.4
  5.8 1.2 copy-start.6
  7.0 1.0 copy-start.8
  8.1 1.0 copy-start.10
  9.1 2.4 %copy-start.1 = (bf16[128,4096]{1,0:T(8,128)(2,1)S(1)}, bf16[128,4096]{1,0:T(8,128)(2,1)}, u32[]{:S(2)}) copy-start(bf16[128,4096]{1,0:T(8,128)(2,1)} %refs_5_.21) | copy-start | bytes 3145732
  9.1 2.4 %copy-start.3 = (bf16[128,4096]{1,0:T(8,128)(2,1)S(1)}, bf16[128,4096]{1,0:T(8,128)(2,1)}, u32[]{:S(2)}) copy-start(bf16[128,4096]{1,0:T(8,128)(2,1)} %refs_6_.17) | copy-start | bytes 3145732
  9.1 2.4 %copy-start.5 = (bf16[128,4096]{1,0:T(8,128)(2,1)S(1)}, bf16[128,4096]{1,0:T(8,128)(2,1)}, u32[]{:S(2)}) copy-start(bf16[128,4096]{1,0:T(8,128)(2,1)} %refs_7_.17) | copy-start | bytes 3145732
  9.1 2.4 %copy-start.7 = (bf16[128,4096]{1,0:T(8,128)(2,1)S(1)}, bf16[128,4096]{1,0:T(8,128)(2,1)}, u32[]{:S(2)}) copy-start(bf16[128,4096]{1,0:T(8,128)(2,1)} %refs_8_.17) | copy-start | bytes 3145732
  13.8 16.4 %collective-permute-start.6 = (bf16[2,8,128,128]{3,2,1,0:T(8,128)(2,1)S(1)}, bf16[2,8,128,128]{3,2,1,0:T(8,128)(2,1)S(1)}, u32[]{:S(2)}, u32[]{:S(2)}) collective-permute-start(bf16[2,8,128,128]{3,2,1,0:T(8,128)(2,1)S(1)} %get-tuple-element.125.refs_3_), channel_id=1, source_target_pairs={{0,4},{4,0},{1,5},{5,1},{2,6},{6,2},{3,7},{7,3},{8,12},{12,8},{9,1... | collective-permute-start | bytes 1572872 | tf_op jit(solution)/shard_map/ppermute | solution.py:24
  14.3 6.4 %collective-permute-start.1 = (bf16[2,4,128,128]{3,2,1,0:T(8,128)(2,1)S(1)}, bf16[2,4,128,128]{3,2,1,0:T(8,128)(2,1)S(1)}, u32[]{:S(2)}, u32[]{:S(2)}) collective-permute-start(bf16[2,4,128,128]{3,2,1,0:T(8,128)(2,1)S(1)} %get-tuple-element.118.refs_3_.refs_5_), channel_id=1, source_target_pairs={{0,4},{4,0},{1,5},{5,1},{2,6},{6,2},{3,7},{7,3},{8,12},{12,8},{9,1... | collective-permute-start | bytes 786440 | tf_op jit(solution)/shard_map/ppermute | solution.py:24
  14.4 11.5 %collective-permute-start.7 = (bf16[2,4,128,128]{3,2,1,0:T(8,128)(2,1)S(1)}, bf16[2,4,128,128]{3,2,1,0:T(8,128)(2,1)S(1)}, u32[]{:S(2)}, u32[]{:S(2)}) collective-permute-start(bf16[2,4,128,128]{3,2,1,0:T(8,128)(2,1)S(1)} %get-tuple-element.126), channel_id=1, source_target_pairs={{0,1},{3,2},{4,5},{7,6},{8,9},{11,10},{12,13},{15,14},{16,17},{19,... | collective-permute-start | bytes 786440 | tf_op jit(solution)/shard_map/ppermute | solution.py:504
  19.2 1.4 %collective-permute-start = (f32[8,128]{1,0:T(8,128)S(1)}, f32[8,128]{1,0:T(8,128)S(1)}, u32[]{:S(2)}, u32[]{:S(2)}) collective-permute-start(f32[8,128]{1,0:T(8,128)S(1)} %broadcast_in_dim.8.refs_2_.refs_1_.refs_3_), channel_id=1, source_target_pairs={{0,4},{4,0},{1,5},{5,1},{2,6},{6,2},{3,7},{7,3},{8,12},{12,8},{9,1... | collective-permute-start | bytes 12296 | tf_op jit(solution)/shard_map/ppermute | solution.py:24
  19.3 12.2 %collective-permute-start.5 = (bf16[2,4,128,128]{3,2,1,0:T(8,128)(2,1)S(1)}, bf16[2,4,128,128]{3,2,1,0:T(8,128)(2,1)S(1)}, u32[]{:S(2)}, u32[]{:S(2)}) collective-permute-start(bf16[2,4,128,128]{3,2,1,0:T(8,128)(2,1)S(1)} %get-tuple-element.123), channel_id=1, source_target_pairs={{0,1},{3,2},{4,5},{7,6},{8,9},{11,10},{12,13},{15,14},{16,17},{19,... | collective-permute-start | bytes 786440 | tf_op jit(solution)/shard_map/ppermute | solution.py:504
  26.4 13.2 %collective-permute-start.13 = (bf16[2,4,128,128]{3,2,1,0:T(8,128)(2,1)S(1)}, bf16[2,4,128,128]{3,2,1,0:T(8,128)(2,1)S(1)}, u32[]{:S(2)}, u32[]{:S(2)}) collective-permute-start(bf16[2,4,128,128]{3,2,1,0:T(8,128)(2,1)S(1)} %get-tuple-element.137), channel_id=1, source_target_pairs={{1,2},{2,1},{5,6},{6,5},{9,10},{10,9},{13,14},{14,13},{17,18},{18,... | collective-permute-start | bytes 786440 | tf_op jit(solution)/shard_map/ppermute | solution.py:504
  27.1 6.4 %collective-permute-start.2 = (bf16[528,128]{1,0:T(8,128)(2,1)S(1)}, bf16[528,128]{1,0:T(8,128)(2,1)S(1)}, u32[]{:S(2)}, u32[]{:S(2)}) collective-permute-start(bf16[528,128]{1,0:T(8,128)(2,1)S(1)} %get-tuple-element.121), channel_id=1, source_target_pairs={{0,8},{8,0},{16,24},{24,16},{1,9},{9,1},{17,25},{25,17},{2,10},{10... | collective-permute-start | bytes 405512 | tf_op jit(solution)/shard_map/ppermute | solution.py:24
  28.7 7.6 %collective-permute-start.4 = (bf16[528,128]{1,0:T(8,128)(2,1)S(1)}, bf16[528,128]{1,0:T(8,128)(2,1)S(1)}, u32[]{:S(2)}, u32[]{:S(2)}) collective-permute-start(bf16[528,128]{1,0:T(8,128)(2,1)S(1)} %get-tuple-element.122), channel_id=1, source_target_pairs={{0,24},{8,16},{16,8},{24,0},{1,25},{9,17},{17,9},{25,1},{2,26},{10... | collective-permute-start | bytes 405512 | tf_op jit(solution)/shard_map/ppermute | solution.py:24
  30.2 8.3 %collective-permute-start.3 = (bf16[528,128]{1,0:T(8,128)(2,1)S(1)}, bf16[528,128]{1,0:T(8,128)(2,1)S(1)}, u32[]{:S(2)}, u32[]{:S(2)}) collective-permute-start(bf16[528,128]{1,0:T(8,128)(2,1)S(1)} %get-tuple-element.122), channel_id=1, source_target_pairs={{0,16},{8,24},{16,0},{24,8},{1,17},{9,25},{17,1},{25,9},{2,18},{10... | collective-permute-start | bytes 405512 | tf_op jit(solution)/shard_map/ppermute | solution.py:24
  31.5 7.0 %copy-start.9 = (f32[8,128,128]{2,1,0:T(8,128)S(1)}, f32[8,128,128]{2,1,0:T(8,128)}, u32[]{:S(2)}) copy-start(f32[8,128,128]{2,1,0:T(8,128)} %refs_1_.5) | copy-start | bytes 1572868
  31.5 24.9 %collective-permute-start.8 = (bf16[1040,128]{1,0:T(8,128)(2,1)S(1)}, bf16[1040,128]{1,0:T(8,128)(2,1)S(1)}, u32[]{:S(2)}, u32[]{:S(2)}) collective-permute-start(bf16[1040,128]{1,0:T(8,128)(2,1)S(1)} %get-tuple-element.132), channel_id=1, source_target_pairs={{0,8},{8,0},{16,24},{24,16},{1,9},{9,1},{17,25},{25,17},{2,10},{10... | collective-permute-start | bytes 798728 | tf_op jit(solution)/shard_map/ppermute | solution.py:24
  33.5 22.9 %collective-permute-start.10 = (bf16[1040,128]{1,0:T(8,128)(2,1)S(1)}, bf16[1040,128]{1,0:T(8,128)(2,1)S(1)}, u32[]{:S(2)}, u32[]{:S(2)}) collective-permute-start(bf16[1040,128]{1,0:T(8,128)(2,1)S(1)} %get-tuple-element.133), channel_id=1, source_target_pairs={{0,24},{8,16},{16,8},{24,0},{1,25},{9,17},{17,9},{25,1},{2,26},{10... | collective-permute-start | bytes 798728 | tf_op jit(solution)/shard_map/ppermute | solution.py:24
  36.3 20.1 %collective-permute-start.9 = (bf16[1040,128]{1,0:T(8,128)(2,1)S(1)}, bf16[1040,128]{1,0:T(8,128)(2,1)S(1)}, u32[]{:S(2)}, u32[]{:S(2)}) collective-permute-start(bf16[1040,128]{1,0:T(8,128)(2,1)S(1)} %get-tuple-element.133), channel_id=1, source_target_pairs={{0,16},{8,24},{16,0},{24,8},{1,17},{9,25},{17,1},{25,9},{2,18},{10... | collective-permute-start | bytes 798728 | tf_op jit(solution)/shard_map/ppermute | solution.py:24
  39.5 1.6 %collective-permute-start.11 = (bf16[2,4,128,128]{3,2,1,0:T(8,128)(2,1)S(1)}, bf16[2,4,128,128]{3,2,1,0:T(8,128)(2,1)S(1)}, u32[]{:S(2)}, u32[]{:S(2)}) collective-permute-start(bf16[2,4,128,128]{3,2,1,0:T(8,128)(2,1)S(1)} %get-tuple-element.134), channel_id=1, source_target_pairs={{0,4},{4,0},{1,5},{5,1},{2,6},{6,2},{3,7},{7,3},{8,12},{12,8},{9,1... | collective-permute-start | bytes 786440 | tf_op jit(solution)/shard_map/ppermute | solution.py:24
  39.6 8.6 %collective-permute-start.12 = (bf16[2,4,128,128]{3,2,1,0:T(8,128)(2,1)S(1)}, bf16[2,4,128,128]{3,2,1,0:T(8,128)(2,1)S(1)}, u32[]{:S(2)}, u32[]{:S(2)}) collective-permute-start(bf16[2,4,128,128]{3,2,1,0:T(8,128)(2,1)S(1)} %get-tuple-element.135), channel_id=1, source_target_pairs={{1,2},{2,1},{5,6},{6,5},{9,10},{10,9},{13,14},{14,13},{17,18},{18,... | collective-permute-start | bytes 786440 | tf_op jit(solution)/shard_map/ppermute | solution.py:504
  41.1 17.2 %collective-permute-start.16 = (bf16[2,4,128,128]{3,2,1,0:T(8,128)(2,1)S(1)}, bf16[2,4,128,128]{3,2,1,0:T(8,128)(2,1)S(1)}, u32[]{:S(2)}, u32[]{:S(2)}) collective-permute-start(bf16[2,4,128,128]{3,2,1,0:T(8,128)(2,1)S(1)} %get-tuple-element.144), channel_id=1, source_target_pairs={{0,1},{3,2},{1,0},{2,3},{4,5},{7,6},{5,4},{6,7},{8,9},{11,10},{9,8... | collective-permute-start | bytes 786440 | tf_op jit(solution)/shard_map/ppermute | solution.py:504
  48.8 13.8 %collective-permute-start.15 = (bf16[2,4,128,128]{3,2,1,0:T(8,128)(2,1)S(1)}, bf16[2,4,128,128]{3,2,1,0:T(8,128)(2,1)S(1)}, u32[]{:S(2)}, u32[]{:S(2)}) collective-permute-start(bf16[2,4,128,128]{3,2,1,0:T(8,128)(2,1)S(1)} %get-tuple-element.143), channel_id=1, source_target_pairs={{0,1},{3,2},{1,0},{2,3},{4,5},{7,6},{5,4},{6,7},{8,9},{11,10},{9,8... | collective-permute-start | bytes 786440 | tf_op jit(solution)/shard_map/ppermute | solution.py:504
  58.3 13.8 %collective-permute-start.14 = (bf16[2,8,128,128]{3,2,1,0:T(8,128)(2,1)S(1)}, bf16[2,8,128,128]{3,2,1,0:T(8,128)(2,1)S(1)}, u32[]{:S(2)}, u32[]{:S(2)}) collective-permute-start(bf16[2,8,128,128]{3,2,1,0:T(8,128)(2,1)S(1)} %get-tuple-element.141), channel_id=1, source_target_pairs={{0,4},{4,0},{1,5},{5,1},{2,6},{6,2},{3,7},{7,3},{8,12},{12,8},{9,1... | collective-permute-start | bytes 1572872 | tf_op jit(solution)/shard_map/ppermute | solution.py:24
  63.3 8.1 %collective-permute-start.19 = (bf16[2,4,128,128]{3,2,1,0:T(8,128)(2,1)S(1)}, bf16[2,4,128,128]{3,2,1,0:T(8,128)(2,1)S(1)}, u32[]{:S(2)}, u32[]{:S(2)}) collective-permute-start(bf16[2,4,128,128]{3,2,1,0:T(8,128)(2,1)S(1)} %get-tuple-element.152), channel_id=1, source_target_pairs={{0,4},{4,0},{1,5},{5,1},{2,6},{6,2},{3,7},{7,3},{8,12},{12,8},{9,1... | collective-permute-start | bytes 786440 | tf_op jit(solution)/shard_map/ppermute | solution.py:24
  63.4 8.7 %collective-permute-start.18 = (bf16[2,4,128,128]{3,2,1,0:T(8,128)(2,1)S(1)}, bf16[2,4,128,128]{3,2,1,0:T(8,128)(2,1)S(1)}, u32[]{:S(2)}, u32[]{:S(2)}) collective-permute-start(bf16[2,4,128,128]{3,2,1,0:T(8,128)(2,1)S(1)} %get-tuple-element.150), channel_id=1, source_target_pairs={{1,2},{2,1},{5,6},{6,5},{9,10},{10,9},{13,14},{14,13},{17,18},{18,... | collective-permute-start | bytes 786440 | tf_op jit(solution)/shard_map/ppermute | solution.py:504
  65.2 11.7 %collective-permute-start.17 = (bf16[2,4,128,128]{3,2,1,0:T(8,128)(2,1)S(1)}, bf16[2,4,128,128]{3,2,1,0:T(8,128)(2,1)S(1)}, u32[]{:S(2)}, u32[]{:S(2)}) collective-permute-start(bf16[2,4,128,128]{3,2,1,0:T(8,128)(2,1)S(1)} %get-tuple-element.149), channel_id=1, source_target_pairs={{0,1},{3,2},{4,5},{7,6},{8,9},{11,10},{12,13},{15,14},{16,17},{19,... | collective-permute-start | bytes 786440 | tf_op jit(solution)/shard_map/ppermute | solution.py:504
  70.7 10.0 %collective-permute-start.25 = (bf16[2,4,128,128]{3,2,1,0:T(8,128)(2,1)S(1)}, bf16[2,4,128,128]{3,2,1,0:T(8,128)(2,1)S(1)}, u32[]{:S(2)}, u32[]{:S(2)}) collective-permute-start(bf16[2,4,128,128]{3,2,1,0:T(8,128)(2,1)S(1)} %get-tuple-element.160), channel_id=1, source_target_pairs={{1,2},{2,1},{5,6},{6,5},{9,10},{10,9},{13,14},{14,13},{17,18},{18,... | collective-permute-start | bytes 786440 | tf_op jit(solution)/shard_map/ppermute | solution.py:504
  72.7 10.0 %collective-permute-start.24 = (bf16[2,4,128,128]{3,2,1,0:T(8,128)(2,1)S(1)}, bf16[2,4,128,128]{3,2,1,0:T(8,128)(2,1)S(1)}, u32[]{:S(2)}, u32[]{:S(2)}) collective-permute-start(bf16[2,4,128,128]{3,2,1,0:T(8,128)(2,1)S(1)} %get-tuple-element.159), channel_id=1, source_target_pairs={{0,1},{3,2},{1,0},{2,3},{4,5},{7,6},{5,4},{6,7},{8,9},{11,10},{9,8... | collective-permute-start | bytes 786440 | tf_op jit(solution)/shard_map/ppermute | solution.py:504
  77.5 16.0 %collective-permute-start.20 = (bf16[2,4,128,128]{3,2,1,0:T(8,128)(2,1)S(1)}, bf16[2,4,128,128]{3,2,1,0:T(8,128)(2,1)S(1)}, u32[]{:S(2)}, u32[]{:S(2)}) collective-permute-start(bf16[2,4,128,128]{3,2,1,0:T(8,128)(2,1)S(1)} %get-tuple-element.156), channel_id=1, source_target_pairs={{1,2},{2,1},{5,6},{6,5},{9,10},{10,9},{13,14},{14,13},{17,18},{18,... | collective-permute-start | bytes 786440 | tf_op jit(solution)/shard_map/ppermute | solution.py:504
  78.2 10.7 %collective-permute-start.21 = (bf16[528,128]{1,0:T(8,128)(2,1)S(1)}, bf16[528,128]{1,0:T(8,128)(2,1)S(1)}, u32[]{:S(2)}, u32[]{:S(2)}) collective-permute-start(bf16[528,128]{1,0:T(8,128)(2,1)S(1)} %get-tuple-element.157), channel_id=1, source_target_pairs={{0,8},{8,0},{16,24},{24,16},{1,9},{9,1},{17,25},{25,17},{2,10},{10... | collective-permute-start | bytes 405512 | tf_op jit(solution)/shard_map/ppermute | solution.py:24
  79.2 9.6 %collective-permute-start.23 = (bf16[528,128]{1,0:T(8,128)(2,1)S(1)}, bf16[528,128]{1,0:T(8,128)(2,1)S(1)}, u32[]{:S(2)}, u32[]{:S(2)}) collective-permute-start(bf16[528,128]{1,0:T(8,128)(2,1)S(1)} %get-tuple-element.158), channel_id=1, source_target_pairs={{0,24},{8,16},{16,8},{24,0},{1,25},{9,17},{17,9},{25,1},{2,26},{10... | collective-permute-start | bytes 405512 | tf_op jit(solution)/shard_map/ppermute | solution.py:24
  80.7 8.2 %collective-permute-start.22 = (bf16[528,128]{1,0:T(8,128)(2,1)S(1)}, bf16[528,128]{1,0:T(8,128)(2,1)S(1)}, u32[]{:S(2)}, u32[]{:S(2)}) collective-permute-start(bf16[528,128]{1,0:T(8,128)(2,1)S(1)} %get-tuple-element.158), channel_id=1, source_target_pairs={{0,16},{8,24},{16,0},{24,8},{1,17},{9,25},{17,1},{25,9},{2,18},{10... | collective-permute-start | bytes 405512 | tf_op jit(solution)/shard_map/ppermute | solution.py:24
  82.7 17.1 %collective-permute-start.29 = (bf16[2,4,128,128]{3,2,1,0:T(8,128)(2,1)S(1)}, bf16[2,4,128,128]{3,2,1,0:T(8,128)(2,1)S(1)}, u32[]{:S(2)}, u32[]{:S(2)}) collective-permute-start(bf16[2,4,128,128]{3,2,1,0:T(8,128)(2,1)S(1)} %get-tuple-element.170), channel_id=1, source_target_pairs={{0,1},{3,2},{1,0},{2,3},{4,5},{7,6},{5,4},{6,7},{8,9},{11,10},{9,8... | collective-permute-start | bytes 786440 | tf_op jit(solution)/shard_map/ppermute | solution.py:504
  90.3 10.7 %collective-permute-start.28 = (bf16[2,4,128,128]{3,2,1,0:T(8,128)(2,1)S(1)}, bf16[2,4,128,128]{3,2,1,0:T(8,128)(2,1)S(1)}, u32[]{:S(2)}, u32[]{:S(2)}) collective-permute-start(bf16[2,4,128,128]{3,2,1,0:T(8,128)(2,1)S(1)} %get-tuple-element.169), channel_id=1, source_target_pairs={{0,4},{4,0},{1,5},{5,1},{2,6},{6,2},{3,7},{7,3},{8,12},{12,8},{9,1... | collective-permute-start | bytes 786440 | tf_op jit(solution)/shard_map/ppermute | solution.py:24
  90.3 13.2 %collective-permute-start.27 = (bf16[2,4,128,128]{3,2,1,0:T(8,128)(2,1)S(1)}, bf16[2,4,128,128]{3,2,1,0:T(8,128)(2,1)S(1)}, u32[]{:S(2)}, u32[]{:S(2)}) collective-permute-start(bf16[2,4,128,128]{3,2,1,0:T(8,128)(2,1)S(1)} %get-tuple-element.168), channel_id=1, source_target_pairs={{1,2},{2,1},{5,6},{6,5},{9,10},{10,9},{13,14},{14,13},{17,18},{18,... | collective-permute-start | bytes 786440 | tf_op jit(solution)/shard_map/ppermute | solution.py:504
  94.1 12.4 %collective-permute-start.26 = (bf16[2,4,128,128]{3,2,1,0:T(8,128)(2,1)S(1)}, bf16[2,4,128,128]{3,2,1,0:T(8,128)(2,1)S(1)}, u32[]{:S(2)}, u32[]{:S(2)}) collective-permute-start(bf16[2,4,128,128]{3,2,1,0:T(8,128)(2,1)S(1)} %get-tuple-element.167), channel_id=1, source_target_pairs={{0,1},{3,2},{1,0},{2,3},{4,5},{7,6},{5,4},{6,7},{8,9},{11,10},{9,8... | collective-permute-start | bytes 786440 | tf_op jit(solution)/shard_map/ppermute | solution.py:504
  100.3 9.9 %collective-permute-start.32 = (bf16[2,4,128,128]{3,2,1,0:T(8,128)(2,1)S(1)}, bf16[2,4,128,128]{3,2,1,0:T(8,128)(2,1)S(1)}, u32[]{:S(2)}, u32[]{:S(2)}) collective-permute-start(bf16[2,4,128,128]{3,2,1,0:T(8,128)(2,1)S(1)} %get-tuple-element.190), channel_id=1, source_target_pairs={{1,2},{2,1},{5,6},{6,5},{9,10},{10,9},{13,14},{14,13},{17,18},{18,... | collective-permute-start | bytes 786440 | tf_op jit(solution)/shard_map/ppermute | solution.py:504
  104.2 10.8 %collective-permute-start.31 = (bf16[2,4,128,128]{3,2,1,0:T(8,128)(2,1)S(1)}, bf16[2,4,128,128]{3,2,1,0:T(8,128)(2,1)S(1)}, u32[]{:S(2)}, u32[]{:S(2)}) collective-permute-start(bf16[2,4,128,128]{3,2,1,0:T(8,128)(2,1)S(1)} %get-tuple-element.180), channel_id=1, source_target_pairs={{1,0},{2,3},{5,4},{6,7},{9,8},{10,11},{13,12},{14,15},{17,16},{18,... | collective-permute-start | bytes 786440 | tf_op jit(solution)/shard_map/ppermute | solution.py:504
  107.0 10.5 %collective-permute-start.30 = (bf16[2,4,128,128]{3,2,1,0:T(8,128)(2,1)S(1)}, bf16[2,4,128,128]{3,2,1,0:T(8,128)(2,1)S(1)}, u32[]{:S(2)}, u32[]{:S(2)}) collective-permute-start(bf16[2,4,128,128]{3,2,1,0:T(8,128)(2,1)S(1)} %get-tuple-element.179), channel_id=1, source_target_pairs={{1,2},{2,1},{5,6},{6,5},{9,10},{10,9},{13,14},{14,13},{17,18},{18,... | collective-permute-start | bytes 786440 | tf_op jit(solution)/shard_map/ppermute | solution.py:504
  110.8 12.7 %collective-permute-start.34 = (bf16[2,4,128,128]{3,2,1,0:T(8,128)(2,1)S(1)}, bf16[2,4,128,128]{3,2,1,0:T(8,128)(2,1)S(1)}, u32[]{:S(2)}, u32[]{:S(2)}) collective-permute-start(bf16[2,4,128,128]{3,2,1,0:T(8,128)(2,1)S(1)} %get-tuple-element.195), channel_id=1, source_target_pairs={{1,0},{2,3},{5,4},{6,7},{9,8},{10,11},{13,12},{14,15},{17,16},{18,... | collective-permute-start | bytes 786440 | tf_op jit(solution)/shard_map/ppermute | solution.py:504
  118.1 10.4 %collective-permute-start.33 = (bf16[2,4,128,128]{3,2,1,0:T(8,128)(2,1)S(1)}, bf16[2,4,128,128]{3,2,1,0:T(8,128)(2,1)S(1)}, u32[]{:S(2)}, u32[]{:S(2)}) collective-permute-start(bf16[2,4,128,128]{3,2,1,0:T(8,128)(2,1)S(1)} %get-tuple-element.194), channel_id=1, source_target_pairs={{1,0},{2,3},{5,4},{6,7},{9,8},{10,11},{13,12},{14,15},{17,16},{18,... | collective-permute-start | bytes 786440 | tf_op jit(solution)/shard_map/ppermute | solution.py:504

commit v4 on v3

--- a/solution.py
+++ b/solution.py
@@ -15,7 +15,7 @@
 BF16 = jnp.bfloat16
 VMEM = pl.BlockSpec(memory_space=pltpu.VMEM)
 SMEM = pl.BlockSpec(memory_space=pltpu.SMEM)
-ANY = pl.BlockSpec(memory_space=pl.ANY)
+HBM = pl.BlockSpec(memory_space=pltpu.HBM)
 LIMIT = 24 * 1024 * 1024
 
 
@@ -40,13 +40,12 @@
     return jnp.where(row, 1.0, 0.0).astype(F32)
 
 
-def call(token, kernel, operands, out_shape, flops, scratch=(), aliases=None, specs=None, out_specs=None):
+def call(token, kernel, operands, out_shape, scratch=(), aliases=None, specs=None, out_specs=None):
     count, results = len(operands), len(out_shape)
 
     def ordered(*refs):
         kernel(*refs[:count], *refs[count + 1 : count + 1 + results], *refs[count + 2 + results :])
 
-    size = sum(a.size * a.dtype.itemsize for a in operands) + sum(a.size * a.dtype.itemsize for a in out_shape)
     *outs, token = pl.pallas_call(
         ordered,
         in_specs=list(specs or [SMEM] + [VMEM] * (count - 1)) + [VMEM],
@@ -55,7 +54,7 @@
         scratch_shapes=list(scratch),
         input_output_aliases={**(aliases or {}), count: results},
         compiler_params=pltpu.CompilerParams(vmem_limit_bytes=LIMIT),
-        cost_estimate=pl.CostEstimate(flops=flops, bytes_accessed=size, transcendentals=0),
+        cost_estimate=pl.CostEstimate(flops=0, bytes_accessed=0, transcendentals=0),
     )(*operands, token)
     return token, outs
 
@@ -72,30 +71,60 @@
     return ref[pl.ds(at, 1), :]
 
 
-def term_kernel(factor, groups, part, docs_ref, ids, heads, q_ref, k_ref, v_ref, g_ref, outs, extra=None):
-    c = ids[1]
+def label_kernel(ids, docs_ref, labels_ref, column_ref, row_ref):
+    docs = docs_ref[...]
+    for k in range(DEPTH):
+        row = docs[k : k + 1, :].astype(F32)
+        labels_ref[k : k + 1, :] = jnp.broadcast_to(row[:, 0:1], (1, DH))
+        labels_ref[DEPTH + k : DEPTH + k + 1, :] = jnp.broadcast_to(row[:, SPAN - 1 :], (1, DH))
+    own = own_row(docs_ref, ids[2]).astype(F32)
+    column_ref[...] = jnp.broadcast_to(own, (SPAN, SPAN)).T
+    row_ref[...] = jnp.broadcast_to(own, (8, SPAN))
+
+
+def fetch(pairs_of_refs, sems):
+    copies = [pltpu.make_async_copy(source, target, sems.at[n]) for n, (source, target) in enumerate(pairs_of_refs)]
+    for copy in copies:
+        copy.start()
+    return copies
+
+
+def add_terms(factor, part, docs_ref, c, q_ref, k_ref, v_ref, g_ref, outs, off, extra=None):
     in_first, in_last = document_masks(docs_ref[...])
     for t, out in enumerate(outs):
-        for s in range(groups):
-            head_f, head_b = heads(s, c ^ t)
-            for i in range(part):
-                at = columns(head_f + i)
-                forward = transposed_dot(jnp.where(in_last, k_ref[:, at], 0), v_ref[:, at]) * factor
-                at = columns(head_b + i)
-                backward = transposed_dot(jnp.where(in_first, q_ref[:, at], 0), g_ref[:, at]) * factor
-                if extra is not None:
-                    add_f, add_b = extra((c ^ t) * part + i)
-                    forward, backward = forward + add_f, backward + add_b
-                out[0, s * part + i] = forward.astype(BF16)
-                out[1, s * part + i] = backward.astype(BF16)
-
-
-def rest_terms(factor, unit, part, places, shift, total, ids, docs_ref, q_ref, k_ref, v_ref, g_ref, *outs):
-    def heads(s, inner_place):
-        g = places[s]
-        return g * unit + inner_place * part, (g + shift) % total * unit + inner_place * part
-
-    term_kernel(factor, len(places), part, docs_ref, ids, heads, q_ref, k_ref, v_ref, g_ref, outs)
+        for i in range(part):
+            at = columns((c ^ t) * part + i)
+            forward = transposed_dot(jnp.where(in_last, k_ref[:, at], 0), v_ref[:, at]) * factor
+            backward = transposed_dot(jnp.where(in_first, q_ref[:, at], 0), g_ref[:, at]) * factor
+            if extra is not None:
+                add_f, add_b = extra((c ^ t) * part + i)
+                forward, backward = forward + add_f, backward + add_b
+            out[0, off + i] = forward.astype(BF16)
+            out[1, off + i] = backward.astype(BF16)
+
+
+def group_columns(group, unit):
+    return pl.ds(group * unit * DH, unit * DH)
+
+
+def rest_terms(factor, unit, part, places, shift, total, ids, docs_ref, q_hbm, k_hbm, v_hbm, g_hbm, *refs):
+    outs, (q_ref, k_ref, v_ref, g_ref, sems) = refs[:-5], refs[-5:]
+    waiting = []
+    for s, g in enumerate(places):
+        forward, backward = group_columns(g, unit), group_columns((g + shift) % total, unit)
+        waiting.append(fetch(
+            [
+                (k_hbm.at[:, forward], k_ref.at[s]), (v_hbm.at[:, forward], v_ref.at[s]),
+                (q_hbm.at[:, backward], q_ref.at[s]), (g_hbm.at[:, backward], g_ref.at[s]),
+            ],
+            sems.at[s],
+        ))
+    for s in range(len(places)):
+        for copy in waiting[s]:
+            copy.wait()
+        add_terms(
+            factor, part, docs_ref, ids[1], q_ref.at[s], k_ref.at[s], v_ref.at[s], g_ref.at[s], outs, s * part
+        )
 
 
 def lead_terms(
@@ -104,17 +133,15 @@
     outs, (q_ref, k_ref, v_ref, g_ref, carry_ref, cot_ref, sems) = refs[:inner], refs[inner:]
     o, c, z = ids[0], ids[1], ids[2]
     held = carry_hbm.shape[0]
-    forward, backward = pl.ds(0, unit * DH), pl.ds(shift * unit * DH, unit * DH)
-    copies = [
-        pltpu.make_async_copy(k_hbm.at[:, forward], k_ref, sems.at[0]),
-        pltpu.make_async_copy(v_hbm.at[:, forward], v_ref, sems.at[1]),
-        pltpu.make_async_copy(q_hbm.at[:, backward], q_ref, sems.at[2]),
-        pltpu.make_async_copy(g_hbm.at[:, backward], g_ref, sems.at[3]),
-        pltpu.make_async_copy(carry_hbm.at[pl.ds(0, unit)], carry_ref, sems.at[4]),
-        pltpu.make_async_copy(cot_hbm.at[pl.ds(held - unit, unit)], cot_ref, sems.at[5]),
-    ]
-    for copy in copies:
-        copy.start()
+    forward, backward = group_columns(0, unit), group_columns(shift, unit)
+    copies = fetch(
+        [
+            (k_hbm.at[:, forward], k_ref), (v_hbm.at[:, forward], v_ref),
+            (q_hbm.at[:, backward], q_ref), (g_hbm.at[:, backward], g_ref),
+            (carry_hbm.at[pl.ds(0, unit)], carry_ref), (cot_hbm.at[pl.ds(held - unit, unit)], cot_ref),
+        ],
+        sems,
+    )
     for copy in copies:
         copy.wait()
     first, last = own_row(labels, z), own_row(labels, DEPTH + z)
@@ -126,10 +153,7 @@
     def extra(place):
         return open_f * carry_ref[place], close_b * cot_ref[place]
 
-    term_kernel(
-        factor, 1, part, docs_ref, ids, lambda s, place: (place * part, place * part),
-        q_ref, k_ref, v_ref, g_ref, outs, extra,
-    )
+    add_terms(factor, part, docs_ref, c, q_ref, k_ref, v_ref, g_ref, outs, 0, extra)
 
 
 def block_rows(labels, z, grouped):
@@ -322,11 +346,20 @@
 
 
 def output_kernel(
-    factor, base, part, turn, sides, ids, labels, edges, docs_ref, row_ref, q_ref, k_ref, v_ref, g_ref, *refs,
+    factor, base, part, turn, sides, ids, labels, edges, docs_ref, row_ref, q_hbm, k_hbm, v_hbm, g_hbm, *refs,
 ):
     sources = (refs[:4], refs[4:8])
-    outs, (states, held, sems) = refs[-7:-3], refs[-3:]
+    outs, (q_ref, k_ref, v_ref, g_ref, states, held, sems, in_sems) = refs[-12:-8], refs[-8:]
     c = ids[1]
+    head = base + (c ^ turn) * part
+    own = pl.ds(pl.multiple_of(head * DH, part * DH), part * DH)
+    waiting = fetch(
+        [
+            (q_hbm.at[:, own], q_ref), (k_hbm.at[:, own], k_ref),
+            (v_hbm.at[:, own], v_ref), (g_hbm.at[:, own], g_ref),
+        ],
+        in_sems,
+    )
     z, side, at_end = place_of(ids)
     rows = edge_rows(z, labels, edges)
 
@@ -359,10 +392,11 @@
     places = lax.broadcasted_iota(jnp.int32, (SPAN, SPAN), 0)
     others = lax.broadcasted_iota(jnp.int32, (SPAN, SPAN), 1)
     allowed = jnp.logical_and(others <= places, docs == row_ref[0:1])
-    head = base + (c ^ turn) * part
+    for copy in waiting:
+        copy.wait()
     copies = []
     for i in range(part):
-        at = columns(head + i)
+        at, to = slice(i * DH, (i + 1) * DH), columns(head + i)
         q, k, v, g = q_ref[:, at], k_ref[:, at], v_ref[:, at], g_ref[:, at]
         before, after = states[0, i], states[1, i]
         scores = jnp.where(allowed, dot_transposed(q, k) * factor, 0.0).astype(BF16)
@@ -375,7 +409,7 @@
         )
         for n, result in enumerate(results):
             held[n, i] = result.astype(BF16)
-            copy = pltpu.make_async_copy(held.at[n, i], outs[n].at[:, at], sems.at[n, i])
+            copy = pltpu.make_async_copy(held.at[n, i], outs[n].at[:, to], sems.at[n, i])
             copy.start()
             copies.append(copy)
     for copy in copies:
@@ -397,17 +431,19 @@
     shift = groups - 1 if leads else 0
 
     ids = jnp.stack([lax.axis_index(a) for a in ("outer", "inner", "heads")]).astype(jnp.int32)
-    blocks = doc_ids.reshape(depth, SPAN)
-    corners = jnp.concatenate([blocks[:, 0], blocks[:, -1]]).astype(F32)
-    own_labels = jnp.broadcast_to(corners[:, None], (2 * depth, DH))
+    token, (own_labels, docs_column, docs_row) = call(
+        jnp.zeros((8, DH), F32),
+        label_kernel,
+        (ids, doc_ids.reshape(depth, SPAN)),
+        [
+            jax.ShapeDtypeStruct((2 * depth, DH), F32),
+            jax.ShapeDtypeStruct((SPAN, SPAN), F32),
+            jax.ShapeDtypeStruct((8, SPAN), F32),
+        ],
+    )
     labels = [own_labels] + [pairs(own_labels, "inner", d) for d in range(1, inner)]
-    docs = lax.dynamic_index_in_dim(blocks, ids[2], 0, False)
-    docs_column = jnp.broadcast_to(docs[:, None], (SPAN, DH))
-    docs_row = jnp.broadcast_to(docs[None, :], (8, SPAN))
 
     levels = (outer - 1).bit_length()
-    product = 2 * SPAN * DH * DH
-    token = jnp.zeros((8, DH), F32) + 0.0 * own_labels[0, 0]
 
     def state_pair(count):
         return jax.ShapeDtypeStruct((2, count, DH, DH), BF16)
@@ -427,9 +463,8 @@
             functools.partial(lead_terms, factor, unit, part, shift, outer, inner),
             (ids, docs_column, own_labels) + arrays + (carry_in, carry_cot),
             [state_pair(part)] * inner,
-            2 * unit * product,
             scratch=[block] * 4 + [carry] * 2 + [pltpu.SemaphoreType.DMA((6,))],
-            specs=[SMEM, VMEM, VMEM] + [ANY] * 6,
+            specs=[SMEM, VMEM, VMEM] + [HBM] * 6,
         )
         terms[0] = [(a, 0) for a in own]
 
@@ -440,7 +475,9 @@
             functools.partial(rest_terms, factor, unit, part, places, shift, groups),
             (ids, docs_column) + arrays,
             [state_pair(part * len(places))] * inner,
-            2 * unit * len(places) * product,
+            scratch=[pltpu.VMEM((len(places), SPAN, unit * DH), BF16)] * 4
+            + [pltpu.SemaphoreType.DMA((len(places), 4))],
+            specs=[SMEM, VMEM] + [HBM] * 4,
         )
         for s, g in enumerate(places):
             terms[g] = [(a, s * part) for a in own]
@@ -454,7 +491,6 @@
             functools.partial(sum_kernel, inner, levels, grouped),
             (ids, *labels, *received),
             [jax.ShapeDtypeStruct((count * DH + LABELS, DH), BF16)] * levels,
-            count * DH * DH * 8,
         )
         return [pairs(sums[d.bit_length() - 1], "outer", d) for d in range(1, outer)]
 
@@ -468,7 +504,6 @@
             ),
             (ids, carry_in, carry_cot, *labels, *received, *fans),
             [state_pair(count)] * inner + [jax.ShapeDtypeStruct((8, DH), F32)],
-            count * DH * DH * 16 * inner,
         )
         edge = given[-1] if edge is None else edge
         given = exchange(given[:-1])
@@ -499,7 +534,6 @@
             functools.partial(hop_kernel, part, near_plan, far_plan, use_edges),
             operands,
             [state_pair(part)],
-            part * DH * DH * 8,
         )
         return lax.ppermute(sent[0], "heads", perm)
 
@@ -531,61 +565,61 @@
             functools.partial(output_kernel, factor, g * unit, part, t, tuple(sides)),
             operands + tuple(results),
             [out_shape] * 4,
-            10 * part * product,
-            scratch=[
+            scratch=[pltpu.VMEM((SPAN, part * DH), BF16)] * 4
+            + [
                 pltpu.VMEM((2, part, DH, DH), BF16),
                 pltpu.VMEM((4, part, SPAN, DH), BF16),
                 pltpu.SemaphoreType.DMA((4, part)),
+                pltpu.SemaphoreType.DMA((4,)),
             ],
             aliases={len(operands) + i: i for i in range(len(results))},
-            specs=[SMEM] + [VMEM] * (len(operands) - 1) + [ANY] * len(results),
-            out_specs=[ANY] * 4,
+            specs=[SMEM] + [VMEM] * 4 + [HBM] * 4 + [VMEM] * 8 + [HBM] * len(results),
+            out_specs=[HBM] * 4,
         )
 
     if leads and groups == 4 and inner == 2:
         make_lead_terms()
         ends((0, 0), None)
         ends((0, 1), None)
-        got_a = make_terms((1,))
-        got_b = make_terms((2, 3))
-        fans_a = make_sums(got_a, False)
+        rest = tuple(range(1, groups))
+        got_rest = make_terms(rest)
+        fans_rest = make_sums(got_rest, False)
         across((0, 0))
-        fans_b = make_sums(got_b, False)
         across((0, 1))
-        make_prefixes((1,), got_a, fans_a, False)
-        ends((1, 0), (0, 0))
-        ends((1, 1), (0, 1))
-        make_prefixes((2, 3), got_b, fans_b, False)
-        across((1, 0))
+        ends(None, (0, 0))
+        ends(None, (0, 1))
+        make_prefixes(rest, got_rest, fans_rest, False)
+        ends((1, 0), None)
+        ends((2, 0), None)
         token, totals = call(
             token,
             functools.partial(lead_total_kernel, part, inner),
             [ids, own_labels]
             + [a for t in range(inner) for a in (terms[0][t][0], near[0, t], middle[0, t], far[0, t])],
             [state_pair(part)] * inner,
-            unit * DH * DH * 8,
         )
         got_lead = exchange(totals)
+        across((1, 0))
+        ends((3, 0), None)
+        across((2, 0))
+        fans_lead = make_sums(got_lead, True)
+        ends((1, 1), (1, 0))
+        across((3, 0))
+        make_prefixes((0,), got_lead, fans_lead, True)
+        ends((2, 1), (2, 0))
         across((1, 1))
-        ends((2, 0), None)
-        fans_lead = make_sums(got_lead, True)
-        ends((2, 1), (1, 0))
-        across((2, 0))
-        ends((3, 0), (1, 1))
+        make_outputs(0, 0)
+        ends((3, 1), (3, 0))
         across((2, 1))
-        make_prefixes((0,), got_lead, fans_lead, True)
-        make_outputs(0, 0)
-        ends((3, 1), (2, 0))
-        across((3, 0))
-        make_outputs(0, 1)
-        ends(None, (2, 1))
+        make_outputs(1, 0)
+        ends(None, (1, 1))
         across((3, 1))
-        make_outputs(1, 0)
-        ends(None, (3, 0))
-        make_outputs(1, 1)
-        ends(None, (3, 1))
         make_outputs(2, 0)
         make_outputs(3, 0)
+        ends(None, (2, 1))
+        ends(None, (3, 1))
+        make_outputs(0, 1)
+        make_outputs(1, 1)
         make_outputs(2, 1)
         make_outputs(3, 1)
     else:

time: 134 us -> 137 us (1.022)
  waiting for transfers between devices: 18.7 us -> 38.7 us
  starting transfers between devices: 63.5 us -> 45.9 us
    ppermute x16 -> x11, waiting for transfers between devices: 2.14 us -> 17.1 us  [pairs(): return lax.ppermute(array, axis, [(i, i ^ distance) for i in range(count)])]
    ppermute x19 -> x21, starting transfers between devices: 51.1 us -> 36.5 us  [move(): return lax.ppermute(sent[0], 'heads', perm)]
    ppermute x19 -> x21, waiting for transfers between devices: 16.5 us -> 21.6 us  [move(): return lax.ppermute(sent[0], 'heads', perm)]
    ppermute x16 -> x11, starting transfers between devices: 12.5 us -> 9.39 us  [pairs(): return lax.ppermute(array, axis, [(i, i ^ distance) for i in range(count)])]
    unnamed x24 -> x26, local copies, waits for them, and re-layouts: 7.68 us -> 7.69 us
  transfers between devices with their start and end apart: 35 -> 32, of which waited for: 9 -> 14; matrix products, arithmetic and copies ran while one was open for 0% -> 0% of each run, Pallas kernels for 24% -> 22%
where the time goes in v4:
time: 137 us; the launch traced here: 136 us
  starting transfers between devices  45.9 us (34%)
  Pallas kernels  42.7 us (31%)
  waiting for transfers between devices  38.7 us (28%)
  local copies, waits for them, and re-layouts  7.69 us (6%)
  between operations  1.41 us (1%)
    pallas_call x37, Pallas kernels, call(): pl.pallas_call(ordered, in_specs=list(specs or [SMEM] + [VMEM] * (count -...  42.7 us
    ppermute x21, starting transfers between devices, move(): return lax.ppermute(sent[0], 'heads', perm)  36.5 us
    ppermute x21, waiting for transfers between devices, move(): return lax.ppermute(sent[0], 'heads', perm)  21.6 us
    ppermute x11, waiting for transfers between devices, pairs(): return lax.ppermute(array, axis, [(i, i ^ distance) for i in range(count)])  17.1 us
    ppermute x11, starting transfers between devices, pairs(): return lax.ppermute(array, axis, [(i, i ^ distance) for i in range(count)])  9.39 us
    unnamed x26, local copies, waits for them, and re-layouts  7.69 us
  transfers between devices with their start and end apart: 32, of which 14 were waited for; matrix products, arithmetic and copies ran while one was open for 0% of the time, Pallas kernels for 22%

profile of v4, /device:TPU:0, one launch (start us, length us, event | category | flops | bytes accessed | tf_op | source)
XLA Modules:
  0.0 136.5 jit_solution(13232923243387014750)
XLA Ops:
  2.0 1.2 copy-done
  3.3 1.2 copy-done.2
  4.5 1.2 copy-done.4
  5.7 1.2 copy-done.6
  6.9 1.0 copy-done.8
  8.0 1.0 copy-done.10
  9.0 1.2 shard_map.103
  11.5 2.2 %shard_map.106 = (bf16[2,12,128,128]{3,2,1,0:T(8,128)(2,1)S(1)}, bf16[2,12,128,128]{3,2,1,0:T(8,128)(2,1)S(1)}, f32[8,128]{1,0:T(8,128)S(1)}) custom-call(s32[3]{0:T(128)S(1)} %pad_add_fusion.refs_0_, f32[128,128]{1,0:T(8,128)S(1)} %get-tuple-element.112.refs_1_.refs_3_, bf16[128,4096]{1,0:T(8,128)(2,1)S(1)} %copy-done.1, ...), custom_call_target="tpu_custom_call", output_to_operand_aliasing={{2}: (6, {})} | custom-call | tf_op jit(solution)/shard_map/pallas_call | solution.py:49
  14.2 4.4 %collective-permute-start.6 = (bf16[2,4,128,128]{3,2,1,0:T(8,128)(2,1)S(1)}, bf16[2,4,128,128]{3,2,1,0:T(8,128)(2,1)S(1)}, u32[]{:S(2)}, u32[]{:S(2)}) collective-permute-start(bf16[2,4,128,128]{3,2,1,0:T(8,128)(2,1)S(1)} %get-tuple-element.125), channel_id=1, source_target_pairs={{0,1},{3,2},{4,5},{7,6},{8,9},{11,10},{12,13},{15,14},{16,17},{19,... | collective-permute-start | bytes 786440 | tf_op jit(solution)/shard_map/ppermute | solution.py:538
  18.6 1.3 collective-permute-start.5
  22.1 1.6 %collective-permute-start.2 = (bf16[1552,128]{1,0:T(8,128)(2,1)S(1)}, bf16[1552,128]{1,0:T(8,128)(2,1)S(1)}, u32[]{:S(2)}, u32[]{:S(2)}) collective-permute-start(bf16[1552,128]{1,0:T(8,128)(2,1)S(1)} %get-tuple-element.122), channel_id=1, source_target_pairs={{0,8},{8,0},{16,24},{24,16},{1,9},{9,1},{17,25},{25,17},{2,10},{10... | collective-permute-start | bytes 1191944 | tf_op jit(solution)/shard_map/ppermute | solution.py:24
  23.6 1.5 %collective-permute-start.4 = (bf16[1552,128]{1,0:T(8,128)(2,1)S(1)}, bf16[1552,128]{1,0:T(8,128)(2,1)S(1)}, u32[]{:S(2)}, u32[]{:S(2)}) collective-permute-start(bf16[1552,128]{1,0:T(8,128)(2,1)S(1)} %get-tuple-element.123), channel_id=1, source_target_pairs={{0,24},{8,16},{16,8},{24,0},{1,25},{9,17},{17,9},{25,1},{2,26},{10... | collective-permute-start | bytes 1191944 | tf_op jit(solution)/shard_map/ppermute | solution.py:24
  26.9 3.5 %collective-permute-done.5.refs_3_.refs_7_.refs_10_.refs_14_ = bf16[2,4,128,128]{3,2,1,0:T(8,128)(2,1)S(1)} collective-permute-done((bf16[2,4,128,128]{3,2,1,0:T(8,128)(2,1)S(1)}, bf16[2,4,128,128]{3,2,1,0:T(8,128)(2,1)S(1)}, u32[]{:S(2)}, u32[]{:S(2)}) %collective-permute-start.5) | collective-permute-done | bytes 262176 | tf_op jit(solution)/shard_map/ppermute | solution.py:538
  32.8 1.4 collective-permute-done.2.refs_7_
  34.2 8.8 %collective-permute-done.4.refs_9_ = bf16[1552,128]{1,0:T(8,128)(2,1)S(1)} collective-permute-done((bf16[1552,128]{1,0:T(8,128)(2,1)S(1)}, bf16[1552,128]{1,0:T(8,128)(2,1)S(1)}, u32[]{:S(2)}, u32[]{:S(2)}) %collective-permute-start.4) | collective-permute-done | bytes 397344 | tf_op jit(solution)/shard_map/ppermute | solution.py:24
  43.0 1.4 collective-permute-done.3.refs_8_
  44.4 1.9 %shard_map.112 = (bf16[2,12,128,128]{3,2,1,0:T(8,128)(2,1)S(1)}, bf16[2,12,128,128]{3,2,1,0:T(8,128)(2,1)S(1)}, f32[8,128]{1,0:T(8,128)S(1)}, f32[8,128]{1,0:T(8,128)S(1)}) custom-call(s32[3]{0:T(128)S(1)} %pad_add_fusion.refs_0_, f32[8,128,128]{2,1,0:T(8,128)S(1)} %copy-done.9, f32[8,128,128]{2,1,0:T(8,128)S(1)} %copy-done.11, ...), custom_call_target="tpu_custom_call", output_to_operand_aliasing={{3}: (10, {})} | custom-call | tf_op jit(solution)/shard_map/pallas_call | solution.py:49
  46.4 1.3 collective-permute-start.12
  47.7 1.3 collective-permute-start.11
  49.6 4.5 %collective-permute-start.10 = (bf16[2,4,128,128]{3,2,1,0:T(8,128)(2,1)S(1)}, bf16[2,4,128,128]{3,2,1,0:T(8,128)(2,1)S(1)}, u32[]{:S(2)}, u32[]{:S(2)}) collective-permute-start(bf16[2,4,128,128]{3,2,1,0:T(8,128)(2,1)S(1)} %get-tuple-element.138), channel_id=1, source_target_pairs={{0,1},{3,2},{4,5},{7,6},{8,9},{11,10},{12,13},{15,14},{16,17},{19,... | collective-permute-start | bytes 786440 | tf_op jit(solution)/shard_map/ppermute | solution.py:538
  54.8 1.3 collective-permute-start.16
  56.1 1.3 collective-permute-done.12.refs_9_.refs_12_.refs_16_
  57.4 5.2 %collective-permute-done.11.refs_5_.refs_12_.refs_16_ = bf16[2,4,128,128]{3,2,1,0:T(8,128)(2,1)S(1)} collective-permute-done((bf16[2,4,128,128]{3,2,1,0:T(8,128)(2,1)S(1)}, bf16[2,4,128,128]{3,2,1,0:T(8,128)(2,1)S(1)}, u32[]{:S(2)}, u32[]{:S(2)}) %collective-permute-start.11) | collective-permute-done | bytes 262176 | tf_op jit(solution)/shard_map/ppermute | solution.py:538
  65.3 4.6 %collective-permute-start.13 = (bf16[2,4,128,128]{3,2,1,0:T(8,128)(2,1)S(1)}, bf16[2,4,128,128]{3,2,1,0:T(8,128)(2,1)S(1)}, u32[]{:S(2)}, u32[]{:S(2)}) collective-permute-start(bf16[2,4,128,128]{3,2,1,0:T(8,128)(2,1)S(1)} %get-tuple-element.145), channel_id=1, source_target_pairs={{0,1},{3,2},{4,5},{7,6},{8,9},{11,10},{12,13},{15,14},{16,17},{19,... | collective-permute-start | bytes 786440 | tf_op jit(solution)/shard_map/ppermute | solution.py:538
  71.2 1.6 %collective-permute-start.18 = (bf16[528,128]{1,0:T(8,128)(2,1)S(1)}, bf16[528,128]{1,0:T(8,128)(2,1)S(1)}, u32[]{:S(2)}, u32[]{:S(2)}) collective-permute-start(bf16[528,128]{1,0:T(8,128)(2,1)S(1)} %get-tuple-element.155), channel_id=1, source_target_pairs={{0,8},{8,0},{16,24},{24,16},{1,9},{9,1},{17,25},{25,17},{2,10},{10... | collective-permute-start | bytes 405512 | tf_op jit(solution)/shard_map/ppermute | solution.py:24
  74.0 1.3 collective-permute-start.21
  75.3 1.0 collective-permute-done.13.refs_5_.refs_14_.refs_10_
  77.6 1.8 %collective-permute-start.20 = (bf16[528,128]{1,0:T(8,128)(2,1)S(1)}, bf16[528,128]{1,0:T(8,128)(2,1)S(1)}, u32[]{:S(2)}, u32[]{:S(2)}) collective-permute-start(bf16[528,128]{1,0:T(8,128)(2,1)S(1)} %get-tuple-element.156), channel_id=1, source_target_pairs={{0,24},{8,16},{16,8},{24,0},{1,25},{9,17},{17,9},{25,1},{2,26},{10... | collective-permute-start | bytes 405512 | tf_op jit(solution)/shard_map/ppermute | solution.py:24
  79.3 1.5 %collective-permute-start.19 = (bf16[528,128]{1,0:T(8,128)(2,1)S(1)}, bf16[528,128]{1,0:T(8,128)(2,1)S(1)}, u32[]{:S(2)}, u32[]{:S(2)}) collective-permute-start(bf16[528,128]{1,0:T(8,128)(2,1)S(1)} %get-tuple-element.156), channel_id=1, source_target_pairs={{0,16},{8,24},{16,0},{24,8},{1,17},{9,25},{17,1},{25,9},{2,18},{10... | collective-permute-start | bytes 405512 | tf_op jit(solution)/shard_map/ppermute | solution.py:24
  80.8 2.8 %collective-permute-done.20.refs_9_ = bf16[528,128]{1,0:T(8,128)(2,1)S(1)} collective-permute-done((bf16[528,128]{1,0:T(8,128)(2,1)S(1)}, bf16[528,128]{1,0:T(8,128)(2,1)S(1)}, u32[]{:S(2)}, u32[]{:S(2)}) %collective-permute-start.20) | collective-permute-done | bytes 135200 | tf_op jit(solution)/shard_map/ppermute | solution.py:24
  83.6 1.7 %collective-permute-done.19.refs_8_ = bf16[528,128]{1,0:T(8,128)(2,1)S(1)} collective-permute-done((bf16[528,128]{1,0:T(8,128)(2,1)S(1)}, bf16[528,128]{1,0:T(8,128)(2,1)S(1)}, u32[]{:S(2)}, u32[]{:S(2)}) %collective-permute-start.19) | collective-permute-done | bytes 135200 | tf_op jit(solution)/shard_map/ppermute | solution.py:24
  85.4 1.5 %shard_map.122 = (bf16[2,4,128,128]{3,2,1,0:T(8,128)(2,1)S(1)}, bf16[2,4,128,128]{3,2,1,0:T(8,128)(2,1)S(1)}, f32[8,128]{1,0:T(8,128)}, f32[8,128]{1,0:T(8,128)S(1)}) custom-call(s32[3]{0:T(128)S(1)} %pad_add_fusion.refs_0_, f32[8,128,128]{2,1,0:T(8,128)S(1)} %copy-done.9, f32[8,128,128]{2,1,0:T(8,128)S(1)} %copy-done.11, ...), custom_call_target="tpu_custom_call", output_to_operand_aliasing={{3}: (10, {})} | custom-call | tf_op jit(solution)/shard_map/pallas_call | solution.py:49
  87.5 4.1 %collective-permute-start.25 = (bf16[2,4,128,128]{3,2,1,0:T(8,128)(2,1)S(1)}, bf16[2,4,128,128]{3,2,1,0:T(8,128)(2,1)S(1)}, u32[]{:S(2)}, u32[]{:S(2)}) collective-permute-start(bf16[2,4,128,128]{3,2,1,0:T(8,128)(2,1)S(1)} %get-tuple-element.167), channel_id=1, source_target_pairs={{0,1},{3,2},{1,0},{2,3},{4,5},{7,6},{5,4},{6,7},{8,9},{11,10},{9,8... | collective-permute-start | bytes 786440 | tf_op jit(solution)/shard_map/ppermute | solution.py:538
  92.8 2.6 %shard_map.125 = (bf16[128,4096]{1,0:T(8,128)(2,1)}, bf16[128,4096]{1,0:T(8,128)(2,1)}, bf16[128,4096]{1,0:T(8,128)(2,1)}, bf16[128,4096]{1,0:T(8,128)(2,1)}, f32[8,128]{1,0:T(8,128)S(1)}) custom-call(s32[3]{0:T(128)S(1)} %pad_add_fusion.refs_0_, f32[8,128]{1,0:T(8,128)S(1)} %get-tuple-element.111.refs_2_.refs_1_.refs_3_, ...), custom_call_target="tpu_custom_call", output_to_operand_aliasing={{4}: (17, {})} | custom-call | tf_op jit(solution)/shard_map/pallas_call | solution.py:49
  96.0 3.1 %collective-permute-start.23 = (bf16[2,4,128,128]{3,2,1,0:T(8,128)(2,1)S(1)}, bf16[2,4,128,128]{3,2,1,0:T(8,128)(2,1)S(1)}, u32[]{:S(2)}, u32[]{:S(2)}) collective-permute-start(bf16[2,4,128,128]{3,2,1,0:T(8,128)(2,1)S(1)} %get-tuple-element.165), channel_id=1, source_target_pairs={{0,1},{3,2},{1,0},{2,3},{4,5},{7,6},{5,4},{6,7},{8,9},{11,10},{9,8... | collective-permute-start | bytes 786440 | tf_op jit(solution)/shard_map/ppermute | solution.py:538
  100.3 2.8 %shard_map.128 = (bf16[128,4096]{1,0:T(8,128)(2,1)}, bf16[128,4096]{1,0:T(8,128)(2,1)}, bf16[128,4096]{1,0:T(8,128)(2,1)}, bf16[128,4096]{1,0:T(8,128)(2,1)}, f32[8,128]{1,0:T(8,128)S(1)}) custom-call(s32[3]{0:T(128)S(1)} %pad_add_fusion.refs_0_, ...), custom_call_target="tpu_custom_call", output_to_operand_aliasing={{0}: (17, {}), {1}: (18, {}), {2}: (19, {}), {3}: (20, {}),... | custom-call | tf_op jit(solution)/shard_map/pallas_call | solution.py:49
  105.2 1.3 collective-permute-start.31
  106.5 2.6 %shard_map.131 = (bf16[128,4096]{1,0:T(8,128)(2,1)}, bf16[128,4096]{1,0:T(8,128)(2,1)}, bf16[128,4096]{1,0:T(8,128)(2,1)}, bf16[128,4096]{1,0:T(8,128)(2,1)}, f32[8,128]{1,0:T(8,128)S(1)}) custom-call(s32[3]{0:T(128)S(1)} %pad_add_fusion.refs_0_, ...), custom_call_target="tpu_custom_call", output_to_operand_aliasing={{0}: (17, {}), {1}: (18, {}), {2}: (19, {}), {3}: (20, {}),... | custom-call | tf_op jit(solution)/shard_map/pallas_call | solution.py:49
  109.1 2.6 %shard_map.132 = (bf16[128,4096]{1,0:T(8,128)(2,1)}, bf16[128,4096]{1,0:T(8,128)(2,1)}, bf16[128,4096]{1,0:T(8,128)(2,1)}, bf16[128,4096]{1,0:T(8,128)(2,1)}, f32[8,128]{1,0:T(8,128)S(1)}) custom-call(s32[3]{0:T(128)S(1)} %pad_add_fusion.refs_0_, ...), custom_call_target="tpu_custom_call", output_to_operand_aliasing={{0}: (17, {}), {1}: (18, {}), {2}: (19, {}), {3}: (20, {}),... | custom-call | tf_op jit(solution)/shard_map/pallas_call | solution.py:49
  112.4 1.3 collective-permute-start.30
  114.2 1.3 collective-permute-start.28
  115.5 2.6 %collective-permute-done.31.refs_16_.refs_12_ = bf16[2,4,128,128]{3,2,1,0:T(8,128)(2,1)S(1)} collective-permute-done((bf16[2,4,128,128]{3,2,1,0:T(8,128)(2,1)S(1)}, bf16[2,4,128,128]{3,2,1,0:T(8,128)(2,1)S(1)}, u32[]{:S(2)}, u32[]{:S(2)}) %collective-permute-start.31) | collective-permute-done | bytes 262176 | tf_op jit(solution)/shard_map/ppermute | solution.py:538
  118.1 2.6 %shard_map.135 = (bf16[128,4096]{1,0:T(8,128)(2,1)}, bf16[128,4096]{1,0:T(8,128)(2,1)}, bf16[128,4096]{1,0:T(8,128)(2,1)}, bf16[128,4096]{1,0:T(8,128)(2,1)}, f32[8,128]{1,0:T(8,128)S(1)}) custom-call(s32[3]{0:T(128)S(1)} %pad_add_fusion.refs_0_, ...), custom_call_target="tpu_custom_call", output_to_operand_aliasing={{0}: (17, {}), {1}: (18, {}), {2}: (19, {}), {3}: (20, {}),... | custom-call | tf_op jit(solution)/shard_map/pallas_call | solution.py:49
  120.7 4.9 %collective-permute-done.30.refs_16_.refs_12_ = bf16[2,4,128,128]{3,2,1,0:T(8,128)(2,1)S(1)} collective-permute-done((bf16[2,4,128,128]{3,2,1,0:T(8,128)(2,1)S(1)}, bf16[2,4,128,128]{3,2,1,0:T(8,128)(2,1)S(1)}, u32[]{:S(2)}, u32[]{:S(2)}) %collective-permute-start.30) | collective-permute-done | bytes 262176 | tf_op jit(solution)/shard_map/ppermute | solution.py:538
  125.7 2.6 %shard_map.136 = (bf16[128,4096]{1,0:T(8,128)(2,1)}, bf16[128,4096]{1,0:T(8,128)(2,1)}, bf16[128,4096]{1,0:T(8,128)(2,1)}, bf16[128,4096]{1,0:T(8,128)(2,1)}, f32[8,128]{1,0:T(8,128)S(1)}) custom-call(s32[3]{0:T(128)S(1)} %pad_add_fusion.refs_0_, ...), custom_call_target="tpu_custom_call", output_to_operand_aliasing={{0}: (17, {}), {1}: (18, {}), {2}: (19, {}), {3}: (20, {}),... | custom-call | tf_op jit(solution)/shard_map/pallas_call | solution.py:49
  128.3 2.8 %collective-permute-done.28.refs_16_.refs_12_ = bf16[2,4,128,128]{3,2,1,0:T(8,128)(2,1)S(1)} collective-permute-done((bf16[2,4,128,128]{3,2,1,0:T(8,128)(2,1)S(1)}, bf16[2,4,128,128]{3,2,1,0:T(8,128)(2,1)S(1)}, u32[]{:S(2)}, u32[]{:S(2)}) %collective-permute-start.28) | collective-permute-done | bytes 262176 | tf_op jit(solution)/shard_map/ppermute | solution.py:538
  131.1 2.6 %shard_map.137 = (bf16[128,4096]{1,0:T(8,128)(2,1)}, bf16[128,4096]{1,0:T(8,128)(2,1)}, bf16[128,4096]{1,0:T(8,128)(2,1)}, bf16[128,4096]{1,0:T(8,128)(2,1)}, f32[8,128]{1,0:T(8,128)S(1)}) custom-call(s32[3]{0:T(128)S(1)} %pad_add_fusion.refs_0_, ...), custom_call_target="tpu_custom_call", output_to_operand_aliasing={{0}: (17, {}), {1}: (18, {}), {2}: (19, {}), {3}: (20, {}),... | custom-call | tf_op jit(solution)/shard_map/pallas_call | solution.py:49
  133.7 2.6 %shard_map.138 = (bf16[128,4096]{1,0:T(8,128)(2,1)}, bf16[128,4096]{1,0:T(8,128)(2,1)}, bf16[128,4096]{1,0:T(8,128)(2,1)}, bf16[128,4096]{1,0:T(8,128)(2,1)}, f32[8,128]{1,0:T(8,128)S(1)}) custom-call(s32[3]{0:T(128)S(1)} %pad_add_fusion.refs_0_, ...), custom_call_target="tpu_custom_call", output_to_operand_aliasing={{0}: (17, {}), {1}: (18, {}), {2}: (19, {}), {3}: (20, {}),... | custom-call | tf_op jit(solution)/shard_map/pallas_call | solution.py:49
  (81 shorter events, 23.7 us)
Async XLA Ops:
  0.7 0.7 copy-start.12
  2.0 1.2 copy-start
  3.3 1.2 copy-start.2
  4.5 1.2 copy-start.4
  5.7 1.2 copy-start.6
  6.9 1.0 copy-start.8
  8.0 1.0 copy-start.10
  9.0 2.4 %copy-start.1 = (bf16[128,4096]{1,0:T(8,128)(2,1)S(1)}, bf16[128,4096]{1,0:T(8,128)(2,1)}, u32[]{:S(2)}) copy-start(bf16[128,4096]{1,0:T(8,128)(2,1)} %refs_5_.19) | copy-start | bytes 3145732
  9.0 2.4 %copy-start.3 = (bf16[128,4096]{1,0:T(8,128)(2,1)S(1)}, bf16[128,4096]{1,0:T(8,128)(2,1)}, u32[]{:S(2)}) copy-start(bf16[128,4096]{1,0:T(8,128)(2,1)} %refs_6_.17) | copy-start | bytes 3145732
  9.0 2.4 %copy-start.5 = (bf16[128,4096]{1,0:T(8,128)(2,1)S(1)}, bf16[128,4096]{1,0:T(8,128)(2,1)}, u32[]{:S(2)}) copy-start(bf16[128,4096]{1,0:T(8,128)(2,1)} %refs_7_.17) | copy-start | bytes 3145732
  9.0 2.4 %copy-start.7 = (bf16[128,4096]{1,0:T(8,128)(2,1)S(1)}, bf16[128,4096]{1,0:T(8,128)(2,1)}, u32[]{:S(2)}) copy-start(bf16[128,4096]{1,0:T(8,128)(2,1)} %refs_8_.17) | copy-start | bytes 3145732
  13.6 7.5 %collective-permute-start.1 = (bf16[2,12,128,128]{3,2,1,0:T(8,128)(2,1)S(1)}, bf16[2,12,128,128]{3,2,1,0:T(8,128)(2,1)S(1)}, u32[]{:S(2)}, u32[]{:S(2)}) collective-permute-start(bf16[2,12,128,128]{3,2,1,0:T(8,128)(2,1)S(1)} %get-tuple-element.120.refs_3_), channel_id=1, source_target_pairs={{0,4},{4,0},{1,5},{5,1},{2,6},{6,2},{3,7},{7,3},{8,12},{12,8},{9,1... | collective-permute-start | bytes 2359304 | tf_op jit(solution)/shard_map/ppermute | solution.py:24
  14.2 11.5 %collective-permute-start.6 = (bf16[2,4,128,128]{3,2,1,0:T(8,128)(2,1)S(1)}, bf16[2,4,128,128]{3,2,1,0:T(8,128)(2,1)S(1)}, u32[]{:S(2)}, u32[]{:S(2)}) collective-permute-start(bf16[2,4,128,128]{3,2,1,0:T(8,128)(2,1)S(1)} %get-tuple-element.125), channel_id=1, source_target_pairs={{0,1},{3,2},{4,5},{7,6},{8,9},{11,10},{12,13},{15,14},{16,17},{19,... | collective-permute-start | bytes 786440 | tf_op jit(solution)/shard_map/ppermute | solution.py:538
  18.6 11.8 %collective-permute-start.5 = (bf16[2,4,128,128]{3,2,1,0:T(8,128)(2,1)S(1)}, bf16[2,4,128,128]{3,2,1,0:T(8,128)(2,1)S(1)}, u32[]{:S(2)}, u32[]{:S(2)}) collective-permute-start(bf16[2,4,128,128]{3,2,1,0:T(8,128)(2,1)S(1)} %get-tuple-element.124), channel_id=1, source_target_pairs={{0,1},{3,2},{4,5},{7,6},{8,9},{11,10},{12,13},{15,14},{16,17},{19,... | collective-permute-start | bytes 786440 | tf_op jit(solution)/shard_map/ppermute | solution.py:538
  19.9 1.2 collective-permute-start
  22.1 12.1 %collective-permute-start.2 = (bf16[1552,128]{1,0:T(8,128)(2,1)S(1)}, bf16[1552,128]{1,0:T(8,128)(2,1)S(1)}, u32[]{:S(2)}, u32[]{:S(2)}) collective-permute-start(bf16[1552,128]{1,0:T(8,128)(2,1)S(1)} %get-tuple-element.122), channel_id=1, source_target_pairs={{0,8},{8,0},{16,24},{24,16},{1,9},{9,1},{17,25},{25,17},{2,10},{10... | collective-permute-start | bytes 1191944 | tf_op jit(solution)/shard_map/ppermute | solution.py:24
  23.6 19.4 %collective-permute-start.4 = (bf16[1552,128]{1,0:T(8,128)(2,1)S(1)}, bf16[1552,128]{1,0:T(8,128)(2,1)S(1)}, u32[]{:S(2)}, u32[]{:S(2)}) collective-permute-start(bf16[1552,128]{1,0:T(8,128)(2,1)S(1)} %get-tuple-element.123), channel_id=1, source_target_pairs={{0,24},{8,16},{16,8},{24,0},{1,25},{9,17},{17,9},{25,1},{2,26},{10... | collective-permute-start | bytes 1191944 | tf_op jit(solution)/shard_map/ppermute | solution.py:24
  25.1 19.3 %collective-permute-start.3 = (bf16[1552,128]{1,0:T(8,128)(2,1)S(1)}, bf16[1552,128]{1,0:T(8,128)(2,1)S(1)}, u32[]{:S(2)}, u32[]{:S(2)}) collective-permute-start(bf16[1552,128]{1,0:T(8,128)(2,1)S(1)} %get-tuple-element.123), channel_id=1, source_target_pairs={{0,16},{8,24},{16,0},{24,8},{1,17},{9,25},{17,1},{25,9},{2,18},{10... | collective-permute-start | bytes 1191944 | tf_op jit(solution)/shard_map/ppermute | solution.py:24
  26.2 5.5 %collective-permute-start.8 = (bf16[2,4,128,128]{3,2,1,0:T(8,128)(2,1)S(1)}, bf16[2,4,128,128]{3,2,1,0:T(8,128)(2,1)S(1)}, u32[]{:S(2)}, u32[]{:S(2)}) collective-permute-start(bf16[2,4,128,128]{3,2,1,0:T(8,128)(2,1)S(1)} %get-tuple-element.129), channel_id=1, source_target_pairs={{1,2},{2,1},{5,6},{6,5},{9,10},{10,9},{13,14},{14,13},{17,18},{18,... | collective-permute-start | bytes 786440 | tf_op jit(solution)/shard_map/ppermute | solution.py:538
  31.0 1.3 collective-permute-start.7
  31.7 12.7 %copy-start.9 = (f32[8,128,128]{2,1,0:T(8,128)S(1)}, f32[8,128,128]{2,1,0:T(8,128)}, u32[]{:S(2)}) copy-start(f32[8,128,128]{2,1,0:T(8,128)} %refs_1_.3) | copy-start | bytes 1572868
  31.7 12.7 %copy-start.11 = (f32[8,128,128]{2,1,0:T(8,128)S(1)}, f32[8,128,128]{2,1,0:T(8,128)}, u32[]{:S(2)}) copy-start(f32[8,128,128]{2,1,0:T(8,128)} %refs_2_.5) | copy-start | bytes 1572868
  46.3 27.1 %collective-permute-start.9 = (bf16[2,12,128,128]{3,2,1,0:T(8,128)(2,1)S(1)}, bf16[2,12,128,128]{3,2,1,0:T(8,128)(2,1)S(1)}, u32[]{:S(2)}, u32[]{:S(2)}) collective-permute-start(bf16[2,12,128,128]{3,2,1,0:T(8,128)(2,1)S(1)} %get-tuple-element.135), channel_id=1, source_target_pairs={{0,4},{4,0},{1,5},{5,1},{2,6},{6,2},{3,7},{7,3},{8,12},{12,8},{9,1... | collective-permute-start | bytes 2359304 | tf_op jit(solution)/shard_map/ppermute | solution.py:24
  46.4 11.0 %collective-permute-start.12 = (bf16[2,4,128,128]{3,2,1,0:T(8,128)(2,1)S(1)}, bf16[2,4,128,128]{3,2,1,0:T(8,128)(2,1)S(1)}, u32[]{:S(2)}, u32[]{:S(2)}) collective-permute-start(bf16[2,4,128,128]{3,2,1,0:T(8,128)(2,1)S(1)} %get-tuple-element.140), channel_id=1, source_target_pairs={{1,0},{2,3},{5,4},{6,7},{9,8},{10,11},{13,12},{14,15},{17,16},{18,... | collective-permute-start | bytes 786440 | tf_op jit(solution)/shard_map/ppermute | solution.py:538
  47.7 14.9 %collective-permute-start.11 = (bf16[2,4,128,128]{3,2,1,0:T(8,128)(2,1)S(1)}, bf16[2,4,128,128]{3,2,1,0:T(8,128)(2,1)S(1)}, u32[]{:S(2)}, u32[]{:S(2)}) collective-permute-start(bf16[2,4,128,128]{3,2,1,0:T(8,128)(2,1)S(1)} %get-tuple-element.139), channel_id=1, source_target_pairs={{1,0},{2,3},{5,4},{6,7},{9,8},{10,11},{13,12},{14,15},{17,16},{18,... | collective-permute-start | bytes 786440 | tf_op jit(solution)/shard_map/ppermute | solution.py:538
  49.6 13.8 %collective-permute-start.10 = (bf16[2,4,128,128]{3,2,1,0:T(8,128)(2,1)S(1)}, bf16[2,4,128,128]{3,2,1,0:T(8,128)(2,1)S(1)}, u32[]{:S(2)}, u32[]{:S(2)}) collective-permute-start(bf16[2,4,128,128]{3,2,1,0:T(8,128)(2,1)S(1)} %get-tuple-element.138), channel_id=1, source_target_pairs={{0,1},{3,2},{4,5},{7,6},{8,9},{11,10},{12,13},{15,14},{16,17},{19,... | collective-permute-start | bytes 786440 | tf_op jit(solution)/shard_map/ppermute | solution.py:538
  54.8 15.1 %collective-permute-start.16 = (bf16[2,4,128,128]{3,2,1,0:T(8,128)(2,1)S(1)}, bf16[2,4,128,128]{3,2,1,0:T(8,128)(2,1)S(1)}, u32[]{:S(2)}, u32[]{:S(2)}) collective-permute-start(bf16[2,4,128,128]{3,2,1,0:T(8,128)(2,1)S(1)} %get-tuple-element.149), channel_id=1, source_target_pairs={{0,1},{3,2},{4,5},{7,6},{8,9},{11,10},{12,13},{15,14},{16,17},{19,... | collective-permute-start | bytes 786440 | tf_op jit(solution)/shard_map/ppermute | solution.py:538
  63.4 7.1 %collective-permute-start.15 = (bf16[2,4,128,128]{3,2,1,0:T(8,128)(2,1)S(1)}, bf16[2,4,128,128]{3,2,1,0:T(8,128)(2,1)S(1)}, u32[]{:S(2)}, u32[]{:S(2)}) collective-permute-start(bf16[2,4,128,128]{3,2,1,0:T(8,128)(2,1)S(1)} %get-tuple-element.148), channel_id=1, source_target_pairs={{0,4},{4,0},{1,5},{5,1},{2,6},{6,2},{3,7},{7,3},{8,12},{12,8},{9,1... | collective-permute-start | bytes 786440 | tf_op jit(solution)/shard_map/ppermute | solution.py:24
  64.0 9.4 %collective-permute-start.14 = (bf16[2,4,128,128]{3,2,1,0:T(8,128)(2,1)S(1)}, bf16[2,4,128,128]{3,2,1,0:T(8,128)(2,1)S(1)}, u32[]{:S(2)}, u32[]{:S(2)}) collective-permute-start(bf16[2,4,128,128]{3,2,1,0:T(8,128)(2,1)S(1)} %get-tuple-element.146), channel_id=1, source_target_pairs={{1,2},{2,1},{5,6},{6,5},{9,10},{10,9},{13,14},{14,13},{17,18},{18,... | collective-permute-start | bytes 786440 | tf_op jit(solution)/shard_map/ppermute | solution.py:538
  65.3 11.0 %collective-permute-start.13 = (bf16[2,4,128,128]{3,2,1,0:T(8,128)(2,1)S(1)}, bf16[2,4,128,128]{3,2,1,0:T(8,128)(2,1)S(1)}, u32[]{:S(2)}, u32[]{:S(2)}) collective-permute-start(bf16[2,4,128,128]{3,2,1,0:T(8,128)(2,1)S(1)} %get-tuple-element.145), channel_id=1, source_target_pairs={{0,1},{3,2},{4,5},{7,6},{8,9},{11,10},{12,13},{15,14},{16,17},{19,... | collective-permute-start | bytes 786440 | tf_op jit(solution)/shard_map/ppermute | solution.py:538
  71.2 8.1 %collective-permute-start.18 = (bf16[528,128]{1,0:T(8,128)(2,1)S(1)}, bf16[528,128]{1,0:T(8,128)(2,1)S(1)}, u32[]{:S(2)}, u32[]{:S(2)}) collective-permute-start(bf16[528,128]{1,0:T(8,128)(2,1)S(1)} %get-tuple-element.155), channel_id=1, source_target_pairs={{0,8},{8,0},{16,24},{24,16},{1,9},{9,1},{17,25},{25,17},{2,10},{10... | collective-permute-start | bytes 405512 | tf_op jit(solution)/shard_map/ppermute | solution.py:24
  72.7 14.1 %collective-permute-start.22 = (bf16[2,4,128,128]{3,2,1,0:T(8,128)(2,1)S(1)}, bf16[2,4,128,128]{3,2,1,0:T(8,128)(2,1)S(1)}, u32[]{:S(2)}, u32[]{:S(2)}) collective-permute-start(bf16[2,4,128,128]{3,2,1,0:T(8,128)(2,1)S(1)} %get-tuple-element.160), channel_id=1, source_target_pairs={{1,2},{2,1},{5,6},{6,5},{9,10},{10,9},{13,14},{14,13},{17,18},{18,... | collective-permute-start | bytes 786440 | tf_op jit(solution)/shard_map/ppermute | solution.py:538
  74.0 17.5 %collective-permute-start.21 = (bf16[2,4,128,128]{3,2,1,0:T(8,128)(2,1)S(1)}, bf16[2,4,128,128]{3,2,1,0:T(8,128)(2,1)S(1)}, u32[]{:S(2)}, u32[]{:S(2)}) collective-permute-start(bf16[2,4,128,128]{3,2,1,0:T(8,128)(2,1)S(1)} %get-tuple-element.159), channel_id=1, source_target_pairs={{0,1},{3,2},{1,0},{2,3},{4,5},{7,6},{5,4},{6,7},{8,9},{11,10},{9,8... | collective-permute-start | bytes 786440 | tf_op jit(solution)/shard_map/ppermute | solution.py:538
  76.9 18.5 %collective-permute-start.17 = (bf16[2,4,128,128]{3,2,1,0:T(8,128)(2,1)S(1)}, bf16[2,4,128,128]{3,2,1,0:T(8,128)(2,1)S(1)}, u32[]{:S(2)}, u32[]{:S(2)}) collective-permute-start(bf16[2,4,128,128]{3,2,1,0:T(8,128)(2,1)S(1)} %get-tuple-element.154), channel_id=1, source_target_pairs={{1,2},{2,1},{5,6},{6,5},{9,10},{10,9},{13,14},{14,13},{17,18},{18,... | collective-permute-start | bytes 786440 | tf_op jit(solution)/shard_map/ppermute | solution.py:538
  77.6 6.1 %collective-permute-start.20 = (bf16[528,128]{1,0:T(8,128)(2,1)S(1)}, bf16[528,128]{1,0:T(8,128)(2,1)S(1)}, u32[]{:S(2)}, u32[]{:S(2)}) collective-permute-start(bf16[528,128]{1,0:T(8,128)(2,1)S(1)} %get-tuple-element.156), channel_id=1, source_target_pairs={{0,24},{8,16},{16,8},{24,0},{1,25},{9,17},{17,9},{25,1},{2,26},{10... | collective-permute-start | bytes 405512 | tf_op jit(solution)/shard_map/ppermute | solution.py:24
  79.3 6.1 %collective-permute-start.19 = (bf16[528,128]{1,0:T(8,128)(2,1)S(1)}, bf16[528,128]{1,0:T(8,128)(2,1)S(1)}, u32[]{:S(2)}, u32[]{:S(2)}) collective-permute-start(bf16[528,128]{1,0:T(8,128)(2,1)S(1)} %get-tuple-element.156), channel_id=1, source_target_pairs={{0,16},{8,24},{16,0},{24,8},{1,17},{9,25},{17,1},{25,9},{2,18},{10... | collective-permute-start | bytes 405512 | tf_op jit(solution)/shard_map/ppermute | solution.py:24
  87.5 11.7 %collective-permute-start.25 = (bf16[2,4,128,128]{3,2,1,0:T(8,128)(2,1)S(1)}, bf16[2,4,128,128]{3,2,1,0:T(8,128)(2,1)S(1)}, u32[]{:S(2)}, u32[]{:S(2)}) collective-permute-start(bf16[2,4,128,128]{3,2,1,0:T(8,128)(2,1)S(1)} %get-tuple-element.167), channel_id=1, source_target_pairs={{0,1},{3,2},{1,0},{2,3},{4,5},{7,6},{5,4},{6,7},{8,9},{11,10},{9,8... | collective-permute-start | bytes 786440 | tf_op jit(solution)/shard_map/ppermute | solution.py:538
  92.1 11.1 %collective-permute-start.24 = (bf16[2,4,128,128]{3,2,1,0:T(8,128)(2,1)S(1)}, bf16[2,4,128,128]{3,2,1,0:T(8,128)(2,1)S(1)}, u32[]{:S(2)}, u32[]{:S(2)}) collective-permute-start(bf16[2,4,128,128]{3,2,1,0:T(8,128)(2,1)S(1)} %get-tuple-element.166), channel_id=1, source_target_pairs={{1,2},{2,1},{5,6},{6,5},{9,10},{10,9},{13,14},{14,13},{17,18},{18,... | collective-permute-start | bytes 786440 | tf_op jit(solution)/shard_map/ppermute | solution.py:538
  96.0 7.9 %collective-permute-start.23 = (bf16[2,4,128,128]{3,2,1,0:T(8,128)(2,1)S(1)}, bf16[2,4,128,128]{3,2,1,0:T(8,128)(2,1)S(1)}, u32[]{:S(2)}, u32[]{:S(2)}) collective-permute-start(bf16[2,4,128,128]{3,2,1,0:T(8,128)(2,1)S(1)} %get-tuple-element.165), channel_id=1, source_target_pairs={{0,1},{3,2},{1,0},{2,3},{4,5},{7,6},{5,4},{6,7},{8,9},{11,10},{9,8... | collective-permute-start | bytes 786440 | tf_op jit(solution)/shard_map/ppermute | solution.py:538
  99.7 12.1 %collective-permute-start.27 = (bf16[2,4,128,128]{3,2,1,0:T(8,128)(2,1)S(1)}, bf16[2,4,128,128]{3,2,1,0:T(8,128)(2,1)S(1)}, u32[]{:S(2)}, u32[]{:S(2)}) collective-permute-start(bf16[2,4,128,128]{3,2,1,0:T(8,128)(2,1)S(1)} %get-tuple-element.177), channel_id=1, source_target_pairs={{1,2},{2,1},{5,6},{6,5},{9,10},{10,9},{13,14},{14,13},{17,18},{18,... | collective-permute-start | bytes 786440 | tf_op jit(solution)/shard_map/ppermute | solution.py:538
  104.5 9.2 %collective-permute-start.26 = (bf16[2,4,128,128]{3,2,1,0:T(8,128)(2,1)S(1)}, bf16[2,4,128,128]{3,2,1,0:T(8,128)(2,1)S(1)}, u32[]{:S(2)}, u32[]{:S(2)}) collective-permute-start(bf16[2,4,128,128]{3,2,1,0:T(8,128)(2,1)S(1)} %get-tuple-element.176), channel_id=1, source_target_pairs={{1,2},{2,1},{5,6},{6,5},{9,10},{10,9},{13,14},{14,13},{17,18},{18,... | collective-permute-start | bytes 786440 | tf_op jit(solution)/shard_map/ppermute | solution.py:538
  105.1 10.4 %collective-permute-start.29 = (bf16[2,4,128,128]{3,2,1,0:T(8,128)(2,1)S(1)}, bf16[2,4,128,128]{3,2,1,0:T(8,128)(2,1)S(1)}, u32[]{:S(2)}, u32[]{:S(2)}) collective-permute-start(bf16[2,4,128,128]{3,2,1,0:T(8,128)(2,1)S(1)} %get-tuple-element.191), channel_id=1, source_target_pairs={{0,4},{4,0},{1,5},{5,1},{2,6},{6,2},{3,7},{7,3},{8,12},{12,8},{9,1... | collective-permute-start | bytes 786440 | tf_op jit(solution)/shard_map/ppermute | solution.py:24
  105.2 12.9 %collective-permute-start.31 = (bf16[2,4,128,128]{3,2,1,0:T(8,128)(2,1)S(1)}, bf16[2,4,128,128]{3,2,1,0:T(8,128)(2,1)S(1)}, u32[]{:S(2)}, u32[]{:S(2)}) collective-permute-start(bf16[2,4,128,128]{3,2,1,0:T(8,128)(2,1)S(1)} %get-tuple-element.193), channel_id=1, source_target_pairs={{1,0},{2,3},{5,4},{6,7},{9,8},{10,11},{13,12},{14,15},{17,16},{18,... | collective-permute-start | bytes 786440 | tf_op jit(solution)/shard_map/ppermute | solution.py:538
  112.4 13.3 %collective-permute-start.30 = (bf16[2,4,128,128]{3,2,1,0:T(8,128)(2,1)S(1)}, bf16[2,4,128,128]{3,2,1,0:T(8,128)(2,1)S(1)}, u32[]{:S(2)}, u32[]{:S(2)}) collective-permute-start(bf16[2,4,128,128]{3,2,1,0:T(8,128)(2,1)S(1)} %get-tuple-element.192), channel_id=1, source_target_pairs={{1,0},{2,3},{5,4},{6,7},{9,8},{10,11},{13,12},{14,15},{17,16},{18,... | collective-permute-start | bytes 786440 | tf_op jit(solution)/shard_map/ppermute | solution.py:538
  114.2 16.9 %collective-permute-start.28 = (bf16[2,4,128,128]{3,2,1,0:T(8,128)(2,1)S(1)}, bf16[2,4,128,128]{3,2,1,0:T(8,128)(2,1)S(1)}, u32[]{:S(2)}, u32[]{:S(2)}) collective-permute-start(bf16[2,4,128,128]{3,2,1,0:T(8,128)(2,1)S(1)} %get-tuple-element.190), channel_id=1, source_target_pairs={{1,0},{2,3},{5,4},{6,7},{9,8},{10,11},{13,12},{14,15},{17,16},{18,... | collective-permute-start | bytes 786440 | tf_op jit(solution)/shard_map/ppermute | solution.py:538

commit v5 on v4

--- a/solution.py
+++ b/solution.py
@@ -130,7 +130,7 @@
 def lead_terms(
     factor, unit, part, shift, outer, inner, ids, docs_ref, labels, q_hbm, k_hbm, v_hbm, g_hbm, carry_hbm, cot_hbm, *refs,
 ):
-    outs, (q_ref, k_ref, v_ref, g_ref, carry_ref, cot_ref, sems) = refs[:inner], refs[inner:]
+    outs, sents, (q_ref, k_ref, v_ref, g_ref, carry_ref, cot_ref, sems) = refs[:inner], refs[inner : 2 * inner], refs[2 * inner :]
     o, c, z = ids[0], ids[1], ids[2]
     held = carry_hbm.shape[0]
     forward, backward = group_columns(0, unit), group_columns(shift, unit)
@@ -154,6 +154,12 @@
         return open_f * carry_ref[place], close_b * cot_ref[place]
 
     add_terms(factor, part, docs_ref, c, q_ref, k_ref, v_ref, g_ref, outs, 0, extra)
+    _, side, at_end = place_of(ids)
+
+    @pl.when(at_end)
+    def _():
+        for term, out in zip(outs, sents):
+            hop(side, edge_rows(z, labels, None), True, 0, part, term, None, None, 0, out, 0)
 
 
 def block_rows(labels, z, grouped):
@@ -274,7 +280,7 @@
     return [jnp.where(which == 0, a, b) for a, b in zip(*rows)]
 
 
-def hop(side, rows, lead, off, part, term_ref, prefix_ref, got_ref, out):
+def hop(side, rows, lead, off, part, term_ref, prefix_ref, got_ref, got_off, out, out_off):
     own, neighbour, _, _, prior = pick(side, rows)
     other, _, final, _, _ = pick(1 - side, rows)
     join, keep, counts = flag(prior == own), flag(neighbour == own), flag(other == final)
@@ -286,34 +292,30 @@
             state = state + join * prefix_ref[side, off + i].astype(F32)
             rest = prefix_ref[1 - side, off + i].astype(F32)
         if got_ref is not None:
-            state = state + keep * got_ref[0, i].astype(F32)
-            rest = rest + got_ref[1, i].astype(F32)
-        out[0, i] = state.astype(BF16)
-        out[1, i] = rest.astype(BF16)
-
-
-def hop_kernel(part, near, far, has_edges, ids, labels, *refs):
+            state = state + keep * got_ref[0, got_off + i].astype(F32)
+            rest = rest + got_ref[1, got_off + i].astype(F32)
+        out[0, out_off + i] = state.astype(BF16)
+        out[1, out_off + i] = rest.astype(BF16)
+
+
+def hop_kernel(part, near, far, across, has_edges, ids, labels, *refs):
     z, side, at_end = place_of(ids)
     out, refs = refs[-1], list(refs[:-1])
     rows = edge_rows(z, labels, refs.pop(0) if has_edges else None)
-    if near is not None:
-        lead, off = near
-        term = refs.pop(0)
-        prefix = None if lead else refs.pop(0)
-
-        @pl.when(at_end)
-        def _():
-            hop(side, rows, lead, off, part, term, prefix, None, out)
-
-    if far is not None:
-        lead, off, across = far
-        term_far = refs.pop(0)
-        prefix_far = None if lead else refs.pop(0)
-        got = refs.pop(0)
-
-        @pl.when(jnp.logical_not(at_end))
-        def _():
-            hop(side if across else 1 - side, rows, lead, off, part, term_far, prefix_far, got, out)
+
+    def take(plans):
+        return [(plan, refs.pop(0), None if plan[0] else refs.pop(0), refs.pop(0) if plan[2] is not None else None) for plan in plans]
+
+    near, far = take(near), take(far)
+
+    def write(side, entries):
+        for n, ((lead, off, got_off), term, prefix, got) in enumerate(entries):
+            hop(side, rows, lead, off, part, term, prefix, got, got_off, out, n * part)
+
+    if near:
+        pl.when(at_end)(lambda: write(side, near))
+    if far:
+        pl.when(jnp.logical_not(at_end))(lambda: write(side if across else 1 - side, far))
 
 
 def lead_total_kernel(part, turns, ids, labels, *refs):
@@ -345,73 +347,74 @@
             total(1 - side, middle, near)
 
 
-def output_kernel(
-    factor, base, part, turn, sides, ids, labels, edges, docs_ref, row_ref, q_hbm, k_hbm, v_hbm, g_hbm, *refs,
-):
-    sources = (refs[:4], refs[4:8])
-    outs, (q_ref, k_ref, v_ref, g_ref, states, held, sems, in_sems) = refs[-12:-8], refs[-8:]
-    c = ids[1]
-    head = base + (c ^ turn) * part
-    own = pl.ds(pl.multiple_of(head * DH, part * DH), part * DH)
-    waiting = fetch(
-        [
-            (q_hbm.at[:, own], q_ref), (k_hbm.at[:, own], k_ref),
-            (v_hbm.at[:, own], v_ref), (g_hbm.at[:, own], g_ref),
-        ],
-        in_sems,
-    )
-    z, side, at_end = place_of(ids)
-    rows = edge_rows(z, labels, edges)
-
-    for which in range(2):
-        lead, off = sides[which]
-        prefix, near, middle, far = sources[which]
-        _, neighbour, _, target, prior = rows[which]
-        reach, come = flag(prior == target), flag(neighbour == target)
-
-        def state(over, rest):
-            for i in range(part):
-                value = reach * prefix[which, off + i].astype(F32)
-                if over is not None:
-                    value = value + come * over[0, i].astype(F32)
-                if rest is not None and not lead:
-                    value = value + reach * rest[1, i].astype(F32)
-                states[which, i] = value.astype(BF16)
-
-        near_side = side == which
-        for condition, over, rest in (
-            (jnp.logical_and(at_end, near_side), None, far),
-            (jnp.logical_and(at_end, jnp.logical_not(near_side)), far, None),
-            (jnp.logical_and(jnp.logical_not(at_end), near_side), near, middle),
-            (jnp.logical_and(jnp.logical_not(at_end), jnp.logical_not(near_side)), middle, near),
-        ):
-            pl.when(condition)(functools.partial(state, over, rest))
-
+def local_kernel(factor, base, count, docs_ref, row_ref, q_ref, k_ref, v_ref, g_ref, out):
     docs = docs_ref[...]
-    in_first, in_last = document_masks(docs)
     places = lax.broadcasted_iota(jnp.int32, (SPAN, SPAN), 0)
     others = lax.broadcasted_iota(jnp.int32, (SPAN, SPAN), 1)
     allowed = jnp.logical_and(others <= places, docs == row_ref[0:1])
-    for copy in waiting:
-        copy.wait()
-    copies = []
-    for i in range(part):
-        at, to = slice(i * DH, (i + 1) * DH), columns(head + i)
+    for i in range(count):
+        at = slice((base + i) * DH, (base + i + 1) * DH)
         q, k, v, g = q_ref[:, at], k_ref[:, at], v_ref[:, at], g_ref[:, at]
-        before, after = states[0, i], states[1, i]
         scores = jnp.where(allowed, dot_transposed(q, k) * factor, 0.0).astype(BF16)
         grad_scores = jnp.where(allowed, dot_transposed(g, v) * factor, 0.0).astype(BF16)
-        results = (
-            dot(scores, v) + dot(jnp.where(in_first, q, 0), before),
-            dot(grad_scores, k) + dot_transposed(jnp.where(in_first, g, 0), before),
-            transposed_dot(grad_scores, q) + dot_transposed(jnp.where(in_last, v, 0), after),
-            transposed_dot(scores, g) + dot(jnp.where(in_last, k, 0), after),
-        )
-        for n, result in enumerate(results):
-            held[n, i] = result.astype(BF16)
-            copy = pltpu.make_async_copy(held.at[n, i], outs[n].at[:, to], sems.at[n, i])
-            copy.start()
-            copies.append(copy)
+        out[0, i] = dot(scores, v)
+        out[1, i] = dot(grad_scores, k)
+        out[2, i] = transposed_dot(grad_scores, q)
+        out[3, i] = transposed_dot(scores, g)
+
+
+def output_kernel(unit, part, plans, ids, labels, edges, docs_ref, q_ref, k_ref, v_ref, g_ref, *refs):
+    count = len(plans)
+    sources, locals_ = refs[: 8 * count], refs[8 * count : 9 * count]
+    outs, (states, held, sems) = refs[-7:-3], refs[-3:]
+    c = ids[1]
+    z, side, at_end = place_of(ids)
+    rows = edge_rows(z, labels, edges)
+
+    def make_states(ends, side):
+        for n, (_, _, both) in enumerate(plans):
+            for which in range(2):
+                lead, off, near_off, middle_off, far_off = both[which]
+                prefix, near, middle, far = sources[8 * n + 4 * which : 8 * n + 4 * which + 4]
+                _, neighbour, _, target, prior = rows[which]
+                reach, come = flag(prior == target), flag(neighbour == target)
+                if ends:
+                    over, rest = (None, (far, far_off)) if side == which else ((far, far_off), None)
+                elif side == which:
+                    over, rest = (near, near_off), (middle, middle_off)
+                else:
+                    over, rest = (middle, middle_off), (near, near_off)
+                for i in range(part):
+                    value = reach * prefix[which, off + i].astype(F32)
+                    if over is not None:
+                        value = value + come * over[0][0, over[1] + i].astype(F32)
+                    if rest is not None and not lead:
+                        value = value + reach * rest[0][1, rest[1] + i].astype(F32)
+                    states[n, which, i] = value.astype(BF16)
+
+    for ends in (True, False):
+        for which in range(2):
+            here = jnp.logical_and(at_end if ends else jnp.logical_not(at_end), side == which)
+            pl.when(here)(functools.partial(make_states, ends, which))
+
+    in_first, in_last = document_masks(docs_ref[...])
+    copies = []
+    for n, (group, turn, _) in enumerate(plans):
+        place = (c ^ turn) * part
+        for i in range(part):
+            at = columns(group * unit + place + i)
+            before, after = states[n, 0, i], states[n, 1, i]
+            results = (
+                dot(jnp.where(in_first, q_ref[:, at], 0), before),
+                dot_transposed(jnp.where(in_first, g_ref[:, at], 0), before),
+                dot_transposed(jnp.where(in_last, v_ref[:, at], 0), after),
+                dot(jnp.where(in_last, k_ref[:, at], 0), after),
+            )
+            for m, result in enumerate(results):
+                held[n, m, i] = (locals_[n][m, place + i] + result).astype(BF16)
+                copy = pltpu.make_async_copy(held.at[n, m, i], outs[m].at[:, at], sems.at[n, m, i])
+                copy.start()
+                copies.append(copy)
     for copy in copies:
         copy.wait()
 
@@ -423,7 +426,6 @@
     factor = float(DH * (tokens_all // 2)) ** (-0.5)
     head_count = queries.shape[1] // DH
     held = carry_in.shape[0]
-    arrays = (queries, keys, values, out_grad)
     part = min(4, head_count // inner)
     unit = part * inner
     groups = head_count // unit
@@ -448,11 +450,20 @@
     def state_pair(count):
         return jax.ShapeDtypeStruct((2, count, DH, DH), BF16)
 
-    terms, prefixes, near, middle, far = {}, {}, {}, {}, {}
-    edge = None
+    terms, prefixes, near, middle, far, local = {}, {}, {}, {}, {}, {}
+    edge, arrays, carries = None, (queries, keys, values, out_grad), (carry_in, carry_cot)
+    far_arrays, far_carries = (
+        tuple(pltpu.with_memory_space_constraint(a, pltpu.HBM) for a in group) for group in (arrays, carries)
+    )
 
     def exchange(own):
         return [own[0]] + [pairs(own[d], "inner", d) for d in range(1, inner)]
+
+    def receive(units, kind, sent, perm):
+        got = lax.ppermute(sent, "heads", perm)
+        for n, u in enumerate(units):
+            kind[u] = (got, n * part)
+        return got
 
     def make_lead_terms():
         nonlocal token
@@ -461,19 +472,21 @@
         token, own = call(
             token,
             functools.partial(lead_terms, factor, unit, part, shift, outer, inner),
-            (ids, docs_column, own_labels) + arrays + (carry_in, carry_cot),
-            [state_pair(part)] * inner,
+            (ids, docs_column, own_labels) + far_arrays + far_carries,
+            [state_pair(part)] * (2 * inner),
             scratch=[block] * 4 + [carry] * 2 + [pltpu.SemaphoreType.DMA((6,))],
             specs=[SMEM, VMEM, VMEM] + [HBM] * 6,
         )
-        terms[0] = [(a, 0) for a in own]
+        terms[0] = [(a, 0) for a in own[:inner]]
+        for t in range(inner):
+            receive([(0, t)], near, own[inner + t], [(0, 1), (3, 2)])
 
     def make_terms(places):
         nonlocal token
         token, own = call(
             token,
             functools.partial(rest_terms, factor, unit, part, places, shift, groups),
-            (ids, docs_column) + arrays,
+            (ids, docs_column) + far_arrays,
             [state_pair(part * len(places))] * inner,
             scratch=[pltpu.VMEM((len(places), SPAN, unit * DH), BF16)] * 4
             + [pltpu.SemaphoreType.DMA((len(places), 4))],
@@ -502,7 +515,7 @@
             functools.partial(
                 prefix_kernel, factor, unit, part, places, shift, groups, inner, outer, grouped
             ),
-            (ids, carry_in, carry_cot, *labels, *received, *fans),
+            (ids, *carries, *labels, *received, *fans),
             [state_pair(count)] * inner + [jax.ShapeDtypeStruct((8, DH), F32)],
         )
         edge = given[-1] if edge is None else edge
@@ -510,131 +523,141 @@
         for s, g in enumerate(places):
             prefixes[g] = [(a, s * part) for a in given]
 
-    def operands_of(chunk):
-        g, t = chunk
-        lead = leads and g == 0
-        array, off = terms[g][t]
-        return lead, off, [array] if lead else [array, prefixes[g][t][0]]
-
-    def move(near_chunk, far_chunk, across, perm):
+    def move(near_units, far_units, across, perm):
         nonlocal token
-        use_edges = any(c is not None and not (leads and c[0] == 0) for c in (near_chunk, far_chunk))
+        units = list(near_units) + list(far_units)
+        use_edges = not all(leads and g == 0 for g, _ in units)
         operands = [ids, own_labels] + ([edge] if use_edges else [])
-        near_plan = far_plan = None
-        if near_chunk is not None:
-            lead, off, more = operands_of(near_chunk)
-            near_plan = (lead, off)
-            operands += more
-        if far_chunk is not None:
-            lead, off, more = operands_of(far_chunk)
-            far_plan = (lead, off, across)
-            operands += more + [near[far_chunk] if across else middle[far_chunk]]
+
+        def plans_of(chosen, got):
+            plans = []
+            for u in chosen:
+                g, t = u
+                lead = leads and g == 0
+                array, off = terms[g][t]
+                operands.append(array)
+                if not lead:
+                    operands.append(prefixes[g][t][0])
+                if got is not None:
+                    operands.append(got[u][0])
+                plans.append((lead, off, None if got is None else got[u][1]))
+            return plans
+
+        near_plans = plans_of(near_units, None)
+        far_plans = plans_of(far_units, near if across else middle)
         token, sent = call(
             token,
-            functools.partial(hop_kernel, part, near_plan, far_plan, use_edges),
+            functools.partial(hop_kernel, part, near_plans, far_plans, across, use_edges),
             operands,
-            [state_pair(part)],
-        )
-        return lax.ppermute(sent[0], "heads", perm)
-
-    def ends(near_chunk, far_chunk):
-        perm = ([(0, 1), (3, 2)] if near_chunk is not None else []) + ([(1, 0), (2, 3)] if far_chunk is not None else [])
-        got = move(near_chunk, far_chunk, False, perm)
-        if near_chunk is not None:
-            near[near_chunk] = got
-        if far_chunk is not None:
-            far[far_chunk] = got
-
-    def across(chunk):
-        middle[chunk] = move(None, chunk, True, [(1, 2), (2, 1)])
+            [state_pair(part * max(len(near_units), len(far_units)))],
+        )
+        return sent[0]
+
+    def ends(near_units, far_units):
+        perm = ([(0, 1), (3, 2)] if near_units else []) + ([(1, 0), (2, 3)] if far_units else [])
+        got = receive(near_units, near, move(near_units, far_units, False, perm), perm)
+        for n, u in enumerate(far_units):
+            far[u] = (got, n * part)
+
+    def across(units):
+        receive(units, middle, move([], units, True, None), [(1, 2), (2, 1)])
+
+    def make_local(g):
+        nonlocal token
+        token, out = call(
+            token,
+            functools.partial(local_kernel, factor, g * unit, unit),
+            (docs_column, docs_row) + arrays,
+            [jax.ShapeDtypeStruct((4, unit, SPAN, DH), F32)],
+            specs=[VMEM] * 6,
+        )
+        local[g] = out[0]
 
     out_shape = jax.ShapeDtypeStruct(queries.shape, BF16)
     results = ()
 
-    def make_outputs(g, t):
+    def make_outputs(units):
         nonlocal token, results
-        operands = (ids, own_labels, edge, docs_column, docs_row) + arrays
-        sides = []
-        for chunk in ((g, t), ((g - shift) % groups, t)):
-            lead = leads and chunk[0] == 0
-            array, off = prefixes[chunk[0]][t]
-            sides.append((lead, off))
-            operands += (array, near[chunk], middle[chunk], far[chunk])
+        operands, plans = (ids, own_labels, edge, docs_column) + arrays, []
+        for g, t in units:
+            both = []
+            for u in ((g, t), ((g - shift) % groups, t)):
+                lead = leads and u[0] == 0
+                array, off = prefixes[u[0]][t]
+                both.append((lead, off, near[u][1], middle[u][1], far[u][1]))
+                operands += (array, near[u][0], middle[u][0], far[u][0])
+            plans.append((g, t, both))
+        operands += tuple(local[g] for g, _ in units)
+        count = len(units)
         token, results = call(
             token,
-            functools.partial(output_kernel, factor, g * unit, part, t, tuple(sides)),
+            functools.partial(output_kernel, unit, part, plans),
             operands + tuple(results),
             [out_shape] * 4,
-            scratch=[pltpu.VMEM((SPAN, part * DH), BF16)] * 4
-            + [
-                pltpu.VMEM((2, part, DH, DH), BF16),
-                pltpu.VMEM((4, part, SPAN, DH), BF16),
-                pltpu.SemaphoreType.DMA((4, part)),
-                pltpu.SemaphoreType.DMA((4,)),
+            scratch=[
+                pltpu.VMEM((count, 2, part, DH, DH), BF16),
+                pltpu.VMEM((count, 4, part, SPAN, DH), BF16),
+                pltpu.SemaphoreType.DMA((count, 4, part)),
             ],
             aliases={len(operands) + i: i for i in range(len(results))},
-            specs=[SMEM] + [VMEM] * 4 + [HBM] * 4 + [VMEM] * 8 + [HBM] * len(results),
+            specs=[SMEM] + [VMEM] * (len(operands) - 1) + [HBM] * len(results),
             out_specs=[HBM] * 4,
         )
 
     if leads and groups == 4 and inner == 2:
         make_lead_terms()
-        ends((0, 0), None)
-        ends((0, 1), None)
         rest = tuple(range(1, groups))
         got_rest = make_terms(rest)
+        across([(0, 0)])
         fans_rest = make_sums(got_rest, False)
-        across((0, 0))
-        across((0, 1))
-        ends(None, (0, 0))
-        ends(None, (0, 1))
+        across([(0, 1)])
+        make_local(0)
+        ends([], [(0, 0)])
+        make_local(1)
+        ends([], [(0, 1)])
         make_prefixes(rest, got_rest, fans_rest, False)
-        ends((1, 0), None)
-        ends((2, 0), None)
+        ends([(1, 0), (2, 0)], [])
         token, totals = call(
             token,
             functools.partial(lead_total_kernel, part, inner),
             [ids, own_labels]
-            + [a for t in range(inner) for a in (terms[0][t][0], near[0, t], middle[0, t], far[0, t])],
+            + [a for t in range(inner) for a in (terms[0][t][0], near[0, t][0], middle[0, t][0], far[0, t][0])],
             [state_pair(part)] * inner,
         )
         got_lead = exchange(totals)
-        across((1, 0))
-        ends((3, 0), None)
-        across((2, 0))
+        ends([(3, 0), (1, 1)], [])
         fans_lead = make_sums(got_lead, True)
-        ends((1, 1), (1, 0))
-        across((3, 0))
+        across([(1, 0), (2, 0)])
+        make_local(2)
+        ends([(2, 1)], [(1, 0)])
+        across([(3, 0), (1, 1)])
         make_prefixes((0,), got_lead, fans_lead, True)
-        ends((2, 1), (2, 0))
-        across((1, 1))
-        make_outputs(0, 0)
-        ends((3, 1), (3, 0))
-        across((2, 1))
-        make_outputs(1, 0)
-        ends(None, (1, 1))
-        across((3, 1))
-        make_outputs(2, 0)
-        make_outputs(3, 0)
-        ends(None, (2, 1))
-        ends(None, (3, 1))
-        make_outputs(0, 1)
-        make_outputs(1, 1)
-        make_outputs(2, 1)
-        make_outputs(3, 1)
+        ends([(3, 1)], [(2, 0)])
+        across([(2, 1)])
+        make_local(3)
+        ends([], [(3, 0), (1, 1)])
+        across([(3, 1)])
+        make_outputs([(1, 0), (0, 0)])
+        ends([], [(2, 1)])
+        make_outputs([(2, 0), (3, 0), (0, 1)])
+        ends([], [(3, 1)])
+        make_outputs([(1, 1)])
+        make_outputs([(2, 1), (3, 1)])
     else:
         assert not leads
+        places = tuple(range(groups))
+        got = make_terms(places)
+        make_prefixes(places, got, make_sums(got, False), False)
+        units = [(g, t) for g in range(groups) for t in range(inner)]
+        lag = 4
+        for k in range(len(units) + lag):
+            ends(units[k : k + 1], units[k - lag : k - lag + 1] if k >= lag else [])
+            if k < len(units):
+                across([units[k]])
         for g in range(groups):
-            got = make_terms((g,))
-            make_prefixes((g,), got, make_sums(got, False), False)
-        chunks = [(g, t) for g in range(groups) for t in range(inner)]
-        lag = 4
-        for k in range(len(chunks) + lag):
-            ends(chunks[k] if k < len(chunks) else None, chunks[k - lag] if k >= lag else None)
-            if k < len(chunks):
-                across(chunks[k])
-        for g, t in chunks:
-            make_outputs(g, t)
+            make_local(g)
+        for u in units:
+            make_outputs([u])
     return tuple(results)
 
 

time: 137 us -> 139 us (1.015)
  waiting for transfers between devices: 38.7 us -> 54.7 us
  local copies, waits for them, and re-layouts: 7.69 us -> 0.72 us
  Pallas kernels: 42.7 us -> 37.9 us
  starting transfers between devices: 45.9 us -> 43.4 us
    ppermute x21 -> x17, waiting for transfers between devices: 21.6 us -> 40.1 us  [receive(): got = lax.ppermute(sent, 'heads', perm)]
    unnamed x26 -> x14, local copies, waits for them, and re-layouts: 7.69 us -> 0.72 us
    pallas_call x37 -> x31, Pallas kernels: 42.7 us -> 37.9 us  [call(): pl.pallas_call(ordered, in_specs=list(specs or [SMEM] + [VMEM] * (count -...]
    ppermute x11, waiting for transfers between devices: 17.1 us -> 14.6 us  [pairs(): return lax.ppermute(array, axis, [(i, i ^ distance) for i in range(count)])]
    ppermute x11, starting transfers between devices: 9.39 us -> 7.92 us  [pairs(): return lax.ppermute(array, axis, [(i, i ^ distance) for i in range(count)])]
    ppermute x21 -> x17, starting transfers between devices: 36.5 us -> 35.5 us  [receive(): got = lax.ppermute(sent, 'heads', perm)]
  transfers between devices with their start and end apart: 32 -> 28, of which waited for: 14 -> 14; matrix products, arithmetic and copies ran while one was open for 0% -> 0% of each run, Pallas kernels for 22% -> 19%
where the time goes in v5:
time: 139 us; the launch traced here: 138 us
  waiting for transfers between devices  54.7 us (39%)
  starting transfers between devices  43.4 us (31%)
  Pallas kernels  37.9 us (27%)
    ppermute x17, waiting for transfers between devices, receive(): got = lax.ppermute(sent, 'heads', perm)  40.1 us
    pallas_call x31, Pallas kernels, call(): pl.pallas_call(ordered, in_specs=list(specs or [SMEM] + [VMEM] * (count -...  37.9 us
    ppermute x17, starting transfers between devices, receive(): got = lax.ppermute(sent, 'heads', perm)  35.5 us
    ppermute x11, waiting for transfers between devices, pairs(): return lax.ppermute(array, axis, [(i, i ^ distance) for i in range(count)])  14.6 us
    ppermute x11, starting transfers between devices, pairs(): return lax.ppermute(array, axis, [(i, i ^ distance) for i in range(count)])  7.92 us
  transfers between devices with their start and end apart: 28, of which 14 were waited for; matrix products, arithmetic and copies ran while one was open for 0% of the time, Pallas kernels for 19%

profile of v5, /device:TPU:0, one launch (start us, length us, event | category | flops | bytes accessed | tf_op | source)
XLA Modules:
  0.0 138.1 jit_solution(4123171612096604277)
XLA Ops:
  0.7 0.7 copy-done.6
  2.0 2.6 %shard_map.103 = (bf16[2,4,128,128]{3,2,1,0:T(8,128)(2,1)S(1)}, bf16[2,4,128,128]{3,2,1,0:T(8,128)(2,1)S(1)}, bf16[2,4,128,128]{3,2,1,0:T(8,128)(2,1)S(1)}, bf16...) custom-call(s32[3]{0:T(128)S(1)} %pad_add_fusion.refs_0_, ...), custom_call_target="tpu_custom_call", output_to_operand_aliasing={{4}: (9, {})} | custom-call | tf_op jit(solution)/shard_map/pallas_call | solution.py:49
  4.7 3.2 %shard_map.104 = (bf16[2,12,128,128]{3,2,1,0:T(8,128)(2,1)S(1)}, bf16[2,12,128,128]{3,2,1,0:T(8,128)(2,1)S(1)}, f32[8,128]{1,0:T(8,128)S(1)}) custom-call(s32[3]{0:T(128)S(1)} %pad_add_fusion.refs_0_, f32[128,128]{1,0:T(8,128)S(1)} %get-tuple-element.90.refs_1_.refs_0_.refs_3_, bf16[128,4096]{1,0:T(8,128)(2,1)} %refs_4_.19, ...), custom_call_target="tpu_custom_call", output_to_operand_aliasing={{2}: (6, {})} | custom-call | tf_op jit(solution)/shard_map/pallas_call | solution.py:49
  8.4 4.6 %collective-permute-start.2 = (bf16[2,4,128,128]{3,2,1,0:T(8,128)(2,1)S(1)}, bf16[2,4,128,128]{3,2,1,0:T(8,128)(2,1)S(1)}, u32[]{:S(2)}, u32[]{:S(2)}) collective-permute-start(bf16[2,4,128,128]{3,2,1,0:T(8,128)(2,1)S(1)} %get-tuple-element.96), channel_id=1, source_target_pairs={{0,1},{3,2},{4,5},{7,6},{8,9},{11,10},{12,13},{15,14},{16,17},{19,... | collective-permute-start | bytes 786440 | tf_op jit(solution)/shard_map/ppermute | solution.py:463
  13.0 1.3 collective-permute-start.6
  14.5 5.2 %collective-permute-done.2.refs_3_.refs_17_.refs_21_ = bf16[2,4,128,128]{3,2,1,0:T(8,128)(2,1)S(1)} collective-permute-done((bf16[2,4,128,128]{3,2,1,0:T(8,128)(2,1)S(1)}, bf16[2,4,128,128]{3,2,1,0:T(8,128)(2,1)S(1)}, u32[]{:S(2)}, u32[]{:S(2)}) %collective-permute-start.2) | collective-permute-done | bytes 262176 | tf_op jit(solution)/shard_map/ppermute | solution.py:463
  20.2 0.9 shard_map.106
  21.1 1.6 %collective-permute-start.3 = (bf16[1552,128]{1,0:T(8,128)(2,1)S(1)}, bf16[1552,128]{1,0:T(8,128)(2,1)S(1)}, u32[]{:S(2)}, u32[]{:S(2)}) collective-permute-start(bf16[1552,128]{1,0:T(8,128)(2,1)S(1)} %get-tuple-element.99), channel_id=1, source_target_pairs={{0,8},{8,0},{16,24},{24,16},{1,9},{9,1},{17,25},{25,17},{2,10},{10... | collective-permute-start | bytes 1191944 | tf_op jit(solution)/shard_map/ppermute | solution.py:24
  22.7 1.5 %collective-permute-start.4 = (bf16[1552,128]{1,0:T(8,128)(2,1)S(1)}, bf16[1552,128]{1,0:T(8,128)(2,1)S(1)}, u32[]{:S(2)}, u32[]{:S(2)}) collective-permute-start(bf16[1552,128]{1,0:T(8,128)(2,1)S(1)} %get-tuple-element.100), channel_id=1, source_target_pairs={{0,16},{8,24},{16,0},{24,8},{1,17},{9,25},{17,1},{25,9},{2,18},{10... | collective-permute-start | bytes 1191944 | tf_op jit(solution)/shard_map/ppermute | solution.py:24
  26.7 2.0 %shard_map.108 = (f32[4,8,128,128]{3,2,1,0:T(8,128)S(1)}, f32[8,128]{1,0:T(8,128)S(1)}) custom-call(f32[128,128]{1,0:T(8,128)S(1)} %get-tuple-element.90.refs_1_.refs_0_.refs_3_, f32[8,128]{1,0:T(8,128)S(1)} %get-tuple-element.105.refs_1_, bf16[128,4096]{1,0:T(8,128)(2,1)S(1)} %copy-done, ...), custom_call_target="tpu_custom_call", output_to_operand_aliasing={{1}: (6, {})} | custom-call | tf_op jit(solution)/shard_map/pallas_call | solution.py:49
  29.2 2.0 %shard_map.110 = (f32[4,8,128,128]{3,2,1,0:T(8,128)S(1)}, f32[8,128]{1,0:T(8,128)S(1)}) custom-call(f32[128,128]{1,0:T(8,128)S(1)} %get-tuple-element.90.refs_1_.refs_0_.refs_3_, f32[8,128]{1,0:T(8,128)S(1)} %get-tuple-element.105.refs_1_, bf16[128,4096]{1,0:T(8,128)(2,1)S(1)} %copy-done, ...), custom_call_target="tpu_custom_call", output_to_operand_aliasing={{1}: (6, {})} | custom-call | tf_op jit(solution)/shard_map/pallas_call | solution.py:49
  31.8 1.6 %collective-permute-done.3.refs_7_ = bf16[1552,128]{1,0:T(8,128)(2,1)S(1)} collective-permute-done((bf16[1552,128]{1,0:T(8,128)(2,1)S(1)}, bf16[1552,128]{1,0:T(8,128)(2,1)S(1)}, u32[]{:S(2)}, u32[]{:S(2)}) %collective-permute-start.3) | collective-permute-done | bytes 397344 | tf_op jit(solution)/shard_map/ppermute | solution.py:24
  33.3 7.7 %collective-permute-done.4.refs_8_ = bf16[1552,128]{1,0:T(8,128)(2,1)S(1)} collective-permute-done((bf16[1552,128]{1,0:T(8,128)(2,1)S(1)}, bf16[1552,128]{1,0:T(8,128)(2,1)S(1)}, u32[]{:S(2)}, u32[]{:S(2)}) %collective-permute-start.4) | collective-permute-done | bytes 397344 | tf_op jit(solution)/shard_map/ppermute | solution.py:24
  41.0 1.9 %shard_map.112 = (bf16[2,12,128,128]{3,2,1,0:T(8,128)(2,1)S(1)}, bf16[2,12,128,128]{3,2,1,0:T(8,128)(2,1)S(1)}, f32[8,128]{1,0:T(8,128)S(1)}, f32[8,128]{1,0:T(8,128)S(1)}) custom-call(s32[3]{0:T(128)S(1)} %pad_add_fusion.refs_0_, f32[8,128,128]{2,1,0:T(8,128)S(1)} %copy-done.4, f32[8,128,128]{2,1,0:T(8,128)S(1)} %copy-done.5, ...), custom_call_target="tpu_custom_call", output_to_operand_aliasing={{3}: (10, {})} | custom-call | tf_op jit(solution)/shard_map/pallas_call | solution.py:49
  43.1 1.3 collective-permute-start.11
  44.4 1.3 collective-permute-start.12
  46.3 4.5 %collective-permute-start.10 = (bf16[2,8,128,128]{3,2,1,0:T(8,128)(2,1)S(1)}, bf16[2,8,128,128]{3,2,1,0:T(8,128)(2,1)S(1)}, u32[]{:S(2)}, u32[]{:S(2)}) collective-permute-start(bf16[2,8,128,128]{3,2,1,0:T(8,128)(2,1)S(1)} %get-tuple-element.116), channel_id=1, source_target_pairs={{0,1},{3,2},{4,5},{7,6},{8,9},{11,10},{12,13},{15,14},{16,17},{19,... | collective-permute-start | bytes 1572872 | tf_op jit(solution)/shard_map/ppermute | solution.py:463
  50.8 3.3 %collective-permute-done.11.refs_5_.refs_19_.refs_23_ = bf16[2,4,128,128]{3,2,1,0:T(8,128)(2,1)S(1)} collective-permute-done((bf16[2,4,128,128]{3,2,1,0:T(8,128)(2,1)S(1)}, bf16[2,4,128,128]{3,2,1,0:T(8,128)(2,1)S(1)}, u32[]{:S(2)}, u32[]{:S(2)}) %collective-permute-start.11) | collective-permute-done | bytes 262176 | tf_op jit(solution)/shard_map/ppermute | solution.py:463
  54.1 5.3 %collective-permute-done.12.refs_9_.refs_27_.refs_23_ = bf16[2,4,128,128]{3,2,1,0:T(8,128)(2,1)S(1)} collective-permute-done((bf16[2,4,128,128]{3,2,1,0:T(8,128)(2,1)S(1)}, bf16[2,4,128,128]{3,2,1,0:T(8,128)(2,1)S(1)}, u32[]{:S(2)}, u32[]{:S(2)}) %collective-permute-start.12) | collective-permute-done | bytes 262176 | tf_op jit(solution)/shard_map/ppermute | solution.py:463
  59.5 0.7 shard_map.114
  60.9 0.9 collective-permute-done.13.refs_4_.refs_6_
  63.1 0.7 collective-permute-start.14
  63.8 7.4 %collective-permute-start.19 = (bf16[2,8,128,128]{3,2,1,0:T(8,128)(2,1)S(1)}, bf16[2,8,128,128]{3,2,1,0:T(8,128)(2,1)S(1)}, u32[]{:S(2)}, u32[]{:S(2)}) collective-permute-start(bf16[2,8,128,128]{3,2,1,0:T(8,128)(2,1)S(1)} %get-tuple-element.131), channel_id=1, source_target_pairs={{0,1},{3,2},{4,5},{7,6},{8,9},{11,10},{12,13},{15,14},{16,17},{19,... | collective-permute-start | bytes 1572872 | tf_op jit(solution)/shard_map/ppermute | solution.py:463
  71.2 2.0 %shard_map.118 = (f32[4,8,128,128]{3,2,1,0:T(8,128)S(1)}, f32[8,128]{1,0:T(8,128)S(1)}) custom-call(f32[128,128]{1,0:T(8,128)S(1)} %get-tuple-element.90.refs_1_.refs_0_.refs_3_, f32[8,128]{1,0:T(8,128)S(1)} %get-tuple-element.105.refs_1_, bf16[128,4096]{1,0:T(8,128)(2,1)S(1)} %copy-done, ...), custom_call_target="tpu_custom_call", output_to_operand_aliasing={{1}: (6, {})} | custom-call | tf_op jit(solution)/shard_map/pallas_call | solution.py:49
  73.8 8.1 %collective-permute-done.19.refs_5_.refs_8_.refs_13_.refs_17_.refs_29_.refs_9_ = bf16[2,8,128,128]{3,2,1,0:T(8,128)(2,1)S(1)} collective-permute-done((bf16[2,8,128,128]{3,2,1,0:T(8,128)(2,1)S(1)}, bf16[2,8,128,128]{3,2,1,0:T(8,128)(2,1)S(1)}, u32[]{:S(2)}, u32[]{:S(2)}) %collective-permute-start.19) | collective-permute-done | bytes 524320 | tf_op jit(solution)/shard_map/ppermute | solution.py:463
  82.4 0.7 collective-permute-start.22
  83.1 4.4 %collective-permute-start.15 = (bf16[2,4,128,128]{3,2,1,0:T(8,128)(2,1)S(1)}, bf16[2,4,128,128]{3,2,1,0:T(8,128)(2,1)S(1)}, u32[]{:S(2)}, u32[]{:S(2)}) collective-permute-start(bf16[2,4,128,128]{3,2,1,0:T(8,128)(2,1)S(1)} %get-tuple-element.128), channel_id=1, source_target_pairs={{0,1},{3,2},{1,0},{2,3},{4,5},{7,6},{5,4},{6,7},{8,9},{11,10},{9,8... | collective-permute-start | bytes 786440 | tf_op jit(solution)/shard_map/ppermute | solution.py:463
  87.5 1.2 collective-permute-start.16
  88.8 0.8 collective-permute-start.17
  89.6 1.4 %collective-permute-start.18 = (bf16[528,128]{1,0:T(8,128)(2,1)S(1)}, bf16[528,128]{1,0:T(8,128)(2,1)S(1)}, u32[]{:S(2)}, u32[]{:S(2)}) collective-permute-start(bf16[528,128]{1,0:T(8,128)(2,1)S(1)} %get-tuple-element.130), channel_id=1, source_target_pairs={{0,24},{8,16},{16,8},{24,0},{1,25},{9,17},{17,9},{25,1},{2,26},{10... | collective-permute-start | bytes 405512 | tf_op jit(solution)/shard_map/ppermute | solution.py:24
  91.0 2.0 %collective-permute-done.16.refs_7_ = bf16[528,128]{1,0:T(8,128)(2,1)S(1)} collective-permute-done((bf16[528,128]{1,0:T(8,128)(2,1)S(1)}, bf16[528,128]{1,0:T(8,128)(2,1)S(1)}, u32[]{:S(2)}, u32[]{:S(2)}) %collective-permute-start.16) | collective-permute-done | bytes 135200 | tf_op jit(solution)/shard_map/ppermute | solution.py:24
  93.0 0.7 collective-permute-done.17.refs_8_
  93.8 1.7 %collective-permute-done.18.refs_9_ = bf16[528,128]{1,0:T(8,128)(2,1)S(1)} collective-permute-done((bf16[528,128]{1,0:T(8,128)(2,1)S(1)}, bf16[528,128]{1,0:T(8,128)(2,1)S(1)}, u32[]{:S(2)}, u32[]{:S(2)}) %collective-permute-start.18) | collective-permute-done | bytes 135200 | tf_op jit(solution)/shard_map/ppermute | solution.py:24
  95.5 1.5 %shard_map.121 = (bf16[2,4,128,128]{3,2,1,0:T(8,128)(2,1)S(1)}, bf16[2,4,128,128]{3,2,1,0:T(8,128)(2,1)S(1)}, f32[8,128]{1,0:T(8,128)}, f32[8,128]{1,0:T(8,128)S(1)}) custom-call(s32[3]{0:T(128)S(1)} %pad_add_fusion.refs_0_, f32[8,128,128]{2,1,0:T(8,128)S(1)} %copy-done.4, f32[8,128,128]{2,1,0:T(8,128)S(1)} %copy-done.5, ...), custom_call_target="tpu_custom_call", output_to_operand_aliasing={{3}: (10, {})} | custom-call | tf_op jit(solution)/shard_map/pallas_call | solution.py:49
  97.6 0.7 shard_map.123
  98.3 2.0 %shard_map.124 = (f32[4,8,128,128]{3,2,1,0:T(8,128)S(1)}, f32[8,128]{1,0:T(8,128)S(1)}) custom-call(f32[128,128]{1,0:T(8,128)S(1)} %get-tuple-element.90.refs_1_.refs_0_.refs_3_, f32[8,128]{1,0:T(8,128)S(1)} %get-tuple-element.105.refs_1_, bf16[128,4096]{1,0:T(8,128)(2,1)S(1)} %copy-done, ...), custom_call_target="tpu_custom_call", output_to_operand_aliasing={{1}: (6, {})} | custom-call | tf_op jit(solution)/shard_map/pallas_call | solution.py:49
  100.9 1.3 collective-permute-start.25
  102.2 2.7 %collective-permute-start.21 = (bf16[2,4,128,128]{3,2,1,0:T(8,128)(2,1)S(1)}, bf16[2,4,128,128]{3,2,1,0:T(8,128)(2,1)S(1)}, u32[]{:S(2)}, u32[]{:S(2)}) collective-permute-start(bf16[2,4,128,128]{3,2,1,0:T(8,128)(2,1)S(1)} %get-tuple-element.137), channel_id=1, source_target_pairs={{0,1},{3,2},{1,0},{2,3},{4,5},{7,6},{5,4},{6,7},{8,9},{11,10},{9,8... | collective-permute-start | bytes 786440 | tf_op jit(solution)/shard_map/ppermute | solution.py:463
  105.7 12.7 %collective-permute-done.21.refs_5_.refs_15_.refs_11_.refs_13_.refs_17_ = bf16[2,4,128,128]{3,2,1,0:T(8,128)(2,1)S(1)} collective-permute-done((bf16[2,4,128,128]{3,2,1,0:T(8,128)(2,1)S(1)}, bf16[2,4,128,128]{3,2,1,0:T(8,128)(2,1)S(1)}, u32[]{:S(2)}, u32[]{:S(2)}) %collective-permute-start.21) | collective-permute-done | bytes 262176 | tf_op jit(solution)/shard_map/ppermute | solution.py:463
  118.9 0.7 collective-permute-start.24
  119.6 2.3 %shard_map.127 = (bf16[128,4096]{1,0:T(8,128)(2,1)}, bf16[128,4096]{1,0:T(8,128)(2,1)}, bf16[128,4096]{1,0:T(8,128)(2,1)}, bf16[128,4096]{1,0:T(8,128)(2,1)}, f32[8,128]{1,0:T(8,128)S(1)}) custom-call(s32[3]{0:T(128)S(1)} %pad_add_fusion.refs_0_, f32[8,128]{1,0:T(8,128)S(1)} %get-tuple-element.89.refs_2_.refs_1_.refs_3_, ...), custom_call_target="tpu_custom_call", output_to_operand_aliasing={{4}: (26, {})} | custom-call | tf_op jit(solution)/shard_map/pallas_call | solution.py:49
  122.5 1.3 collective-permute-start.23
  123.8 2.8 %shard_map.129 = (bf16[128,4096]{1,0:T(8,128)(2,1)}, bf16[128,4096]{1,0:T(8,128)(2,1)}, bf16[128,4096]{1,0:T(8,128)(2,1)}, bf16[128,4096]{1,0:T(8,128)(2,1)}, f32[8,128]{1,0:T(8,128)S(1)}) custom-call(s32[3]{0:T(128)S(1)} %pad_add_fusion.refs_0_, ...), custom_call_target="tpu_custom_call", output_to_operand_aliasing={{0}: (35, {}), {1}: (36, {}), {2}: (37, {}), {3}: (38, {}),... | custom-call | tf_op jit(solution)/shard_map/pallas_call | solution.py:49
  127.2 1.3 collective-permute-start.27
  128.5 4.3 %collective-permute-done.23.refs_15_.refs_11_ = bf16[2,4,128,128]{3,2,1,0:T(8,128)(2,1)S(1)} collective-permute-done((bf16[2,4,128,128]{3,2,1,0:T(8,128)(2,1)S(1)}, bf16[2,4,128,128]{3,2,1,0:T(8,128)(2,1)S(1)}, u32[]{:S(2)}, u32[]{:S(2)}) %collective-permute-start.23) | collective-permute-done | bytes 262176 | tf_op jit(solution)/shard_map/ppermute | solution.py:463
  132.8 1.8 %shard_map.131 = (bf16[128,4096]{1,0:T(8,128)(2,1)}, bf16[128,4096]{1,0:T(8,128)(2,1)}, bf16[128,4096]{1,0:T(8,128)(2,1)}, bf16[128,4096]{1,0:T(8,128)(2,1)}, f32[8,128]{1,0:T(8,128)S(1)}) custom-call(s32[3]{0:T(128)S(1)} %pad_add_fusion.refs_0_, ...), custom_call_target="tpu_custom_call", output_to_operand_aliasing={{0}: (17, {}), {1}: (18, {}), {2}: (19, {}), {3}: (20, {}),... | custom-call | tf_op jit(solution)/shard_map/pallas_call | solution.py:49
  134.6 1.1 collective-permute-done.27.refs_15_.refs_19_
  135.7 2.3 %shard_map.132 = (bf16[128,4096]{1,0:T(8,128)(2,1)}, bf16[128,4096]{1,0:T(8,128)(2,1)}, bf16[128,4096]{1,0:T(8,128)(2,1)}, bf16[128,4096]{1,0:T(8,128)(2,1)}, f32[8,128]{1,0:T(8,128)S(1)}) custom-call(s32[3]{0:T(128)S(1)} %pad_add_fusion.refs_0_, ...), custom_call_target="tpu_custom_call", output_to_operand_aliasing={{0}: (26, {}), {1}: (27, {}), {2}: (28, {}), {3}: (29, {}),... | custom-call | tf_op jit(solution)/shard_map/pallas_call | solution.py:49
  (55 shorter events, 12.9 us)
Async XLA Ops:
  0.7 0.7 copy-start.6
  4.7 22.0 %copy-start.2 = (bf16[128,4096]{1,0:T(8,128)(2,1)S(1)}, bf16[128,4096]{1,0:T(8,128)(2,1)}, u32[]{:S(2)}) copy-start(bf16[128,4096]{1,0:T(8,128)(2,1)} %refs_6_.9) | copy-start | bytes 3145732
  4.7 22.0 %copy-start.3 = (bf16[128,4096]{1,0:T(8,128)(2,1)S(1)}, bf16[128,4096]{1,0:T(8,128)(2,1)}, u32[]{:S(2)}) copy-start(bf16[128,4096]{1,0:T(8,128)(2,1)} %refs_7_.9) | copy-start | bytes 3145732
  7.9 18.7 %copy-start = (bf16[128,4096]{1,0:T(8,128)(2,1)S(1)}, bf16[128,4096]{1,0:T(8,128)(2,1)}, u32[]{:S(2)}) copy-start(bf16[128,4096]{1,0:T(8,128)(2,1)} %refs_4_.19) | copy-start | bytes 3145732
  7.9 18.7 %copy-start.1 = (bf16[128,4096]{1,0:T(8,128)(2,1)S(1)}, bf16[128,4096]{1,0:T(8,128)(2,1)}, u32[]{:S(2)}) copy-start(bf16[128,4096]{1,0:T(8,128)(2,1)} %refs_5_.19) | copy-start | bytes 3145732
  7.9 12.3 %collective-permute-start.1 = (bf16[2,12,128,128]{3,2,1,0:T(8,128)(2,1)S(1)}, bf16[2,12,128,128]{3,2,1,0:T(8,128)(2,1)S(1)}, u32[]{:S(2)}, u32[]{:S(2)}) collective-permute-start(bf16[2,12,128,128]{3,2,1,0:T(8,128)(2,1)S(1)} %get-tuple-element.94.refs_5_.refs_3_.refs_6_), channel_id=1, source_target_pairs={{0,4},{4,0},{1,5},{5,1},{2,6},{6,2},{3,7},{7,3},{8,12},{12,8},{9,1... | collective-permute-start | bytes 2359304 | tf_op jit(solution)/shard_map/ppermute | solution.py:24
  8.4 11.2 %collective-permute-start.2 = (bf16[2,4,128,128]{3,2,1,0:T(8,128)(2,1)S(1)}, bf16[2,4,128,128]{3,2,1,0:T(8,128)(2,1)S(1)}, u32[]{:S(2)}, u32[]{:S(2)}) collective-permute-start(bf16[2,4,128,128]{3,2,1,0:T(8,128)(2,1)S(1)} %get-tuple-element.96), channel_id=1, source_target_pairs={{0,1},{3,2},{4,5},{7,6},{8,9},{11,10},{12,13},{15,14},{16,17},{19,... | collective-permute-start | bytes 786440 | tf_op jit(solution)/shard_map/ppermute | solution.py:463
  13.0 12.3 %collective-permute-start.6 = (bf16[2,4,128,128]{3,2,1,0:T(8,128)(2,1)S(1)}, bf16[2,4,128,128]{3,2,1,0:T(8,128)(2,1)S(1)}, u32[]{:S(2)}, u32[]{:S(2)}) collective-permute-start(bf16[2,4,128,128]{3,2,1,0:T(8,128)(2,1)S(1)} %get-tuple-element.102), channel_id=1, source_target_pairs={{0,1},{3,2},{4,5},{7,6},{8,9},{11,10},{12,13},{15,14},{16,17},{19,... | collective-permute-start | bytes 786440 | tf_op jit(solution)/shard_map/ppermute | solution.py:463
  14.3 5.9 %collective-permute-start = (f32[8,128]{1,0:T(8,128)S(1)}, f32[8,128]{1,0:T(8,128)S(1)}, u32[]{:S(2)}, u32[]{:S(2)}) collective-permute-start(f32[8,128]{1,0:T(8,128)S(1)} %get-tuple-element.89.refs_2_.refs_1_.refs_3_), channel_id=1, source_target_pairs={{0,4},{4,0},{1,5},{5,1},{2,6},{6,2},{3,7},{7,3},{8,12},{12,8},{9,1... | collective-permute-start | bytes 12296 | tf_op jit(solution)/shard_map/ppermute | solution.py:24
  21.1 12.2 %collective-permute-start.3 = (bf16[1552,128]{1,0:T(8,128)(2,1)S(1)}, bf16[1552,128]{1,0:T(8,128)(2,1)S(1)}, u32[]{:S(2)}, u32[]{:S(2)}) collective-permute-start(bf16[1552,128]{1,0:T(8,128)(2,1)S(1)} %get-tuple-element.99), channel_id=1, source_target_pairs={{0,8},{8,0},{16,24},{24,16},{1,9},{9,1},{17,25},{25,17},{2,10},{10... | collective-permute-start | bytes 1191944 | tf_op jit(solution)/shard_map/ppermute | solution.py:24
  22.7 18.3 %collective-permute-start.4 = (bf16[1552,128]{1,0:T(8,128)(2,1)S(1)}, bf16[1552,128]{1,0:T(8,128)(2,1)S(1)}, u32[]{:S(2)}, u32[]{:S(2)}) collective-permute-start(bf16[1552,128]{1,0:T(8,128)(2,1)S(1)} %get-tuple-element.100), channel_id=1, source_target_pairs={{0,16},{8,24},{16,0},{24,8},{1,17},{9,25},{17,1},{25,9},{2,18},{10... | collective-permute-start | bytes 1191944 | tf_op jit(solution)/shard_map/ppermute | solution.py:24
  24.2 16.8 %collective-permute-start.5 = (bf16[1552,128]{1,0:T(8,128)(2,1)S(1)}, bf16[1552,128]{1,0:T(8,128)(2,1)S(1)}, u32[]{:S(2)}, u32[]{:S(2)}) collective-permute-start(bf16[1552,128]{1,0:T(8,128)(2,1)S(1)} %get-tuple-element.100), channel_id=1, source_target_pairs={{0,24},{8,16},{16,8},{24,0},{1,25},{9,17},{17,9},{25,1},{2,26},{10... | collective-permute-start | bytes 1191944 | tf_op jit(solution)/shard_map/ppermute | solution.py:24
  24.7 4.0 %collective-permute-start.8 = (bf16[2,4,128,128]{3,2,1,0:T(8,128)(2,1)S(1)}, bf16[2,4,128,128]{3,2,1,0:T(8,128)(2,1)S(1)}, u32[]{:S(2)}, u32[]{:S(2)}) collective-permute-start(bf16[2,4,128,128]{3,2,1,0:T(8,128)(2,1)S(1)} %get-tuple-element.106), channel_id=1, source_target_pairs={{1,2},{2,1},{5,6},{6,5},{9,10},{10,9},{13,14},{14,13},{17,18},{18,... | collective-permute-start | bytes 786440 | tf_op jit(solution)/shard_map/ppermute | solution.py:463
  25.9 5.3 %collective-permute-start.7 = (bf16[2,4,128,128]{3,2,1,0:T(8,128)(2,1)S(1)}, bf16[2,4,128,128]{3,2,1,0:T(8,128)(2,1)S(1)}, u32[]{:S(2)}, u32[]{:S(2)}) collective-permute-start(bf16[2,4,128,128]{3,2,1,0:T(8,128)(2,1)S(1)} %get-tuple-element.104), channel_id=1, source_target_pairs={{1,2},{2,1},{5,6},{6,5},{9,10},{10,9},{13,14},{14,13},{17,18},{18,... | collective-permute-start | bytes 786440 | tf_op jit(solution)/shard_map/ppermute | solution.py:463
  29.2 11.8 %copy-start.4 = (f32[8,128,128]{2,1,0:T(8,128)S(1)}, f32[8,128,128]{2,1,0:T(8,128)}, u32[]{:S(2)}) copy-start(f32[8,128,128]{2,1,0:T(8,128)} %refs_1_.3) | copy-start | bytes 1572868
  29.2 11.8 %copy-start.5 = (f32[8,128,128]{2,1,0:T(8,128)S(1)}, f32[8,128,128]{2,1,0:T(8,128)}, u32[]{:S(2)}) copy-start(f32[8,128,128]{2,1,0:T(8,128)} %refs_2_.12) | copy-start | bytes 1572868
  43.0 17.3 %collective-permute-start.9 = (bf16[2,12,128,128]{3,2,1,0:T(8,128)(2,1)S(1)}, bf16[2,12,128,128]{3,2,1,0:T(8,128)(2,1)S(1)}, u32[]{:S(2)}, u32[]{:S(2)}) collective-permute-start(bf16[2,12,128,128]{3,2,1,0:T(8,128)(2,1)S(1)} %get-tuple-element.113), channel_id=1, source_target_pairs={{0,4},{4,0},{1,5},{5,1},{2,6},{6,2},{3,7},{7,3},{8,12},{12,8},{9,1... | collective-permute-start | bytes 2359304 | tf_op jit(solution)/shard_map/ppermute | solution.py:24
  43.1 11.1 %collective-permute-start.11 = (bf16[2,4,128,128]{3,2,1,0:T(8,128)(2,1)S(1)}, bf16[2,4,128,128]{3,2,1,0:T(8,128)(2,1)S(1)}, u32[]{:S(2)}, u32[]{:S(2)}) collective-permute-start(bf16[2,4,128,128]{3,2,1,0:T(8,128)(2,1)S(1)} %get-tuple-element.117), channel_id=1, source_target_pairs={{1,0},{2,3},{5,4},{6,7},{9,8},{10,11},{13,12},{14,15},{17,16},{18,... | collective-permute-start | bytes 786440 | tf_op jit(solution)/shard_map/ppermute | solution.py:463
  44.4 15.1 %collective-permute-start.12 = (bf16[2,4,128,128]{3,2,1,0:T(8,128)(2,1)S(1)}, bf16[2,4,128,128]{3,2,1,0:T(8,128)(2,1)S(1)}, u32[]{:S(2)}, u32[]{:S(2)}) collective-permute-start(bf16[2,4,128,128]{3,2,1,0:T(8,128)(2,1)S(1)} %get-tuple-element.118), channel_id=1, source_target_pairs={{1,0},{2,3},{5,4},{6,7},{9,8},{10,11},{13,12},{14,15},{17,16},{18,... | collective-permute-start | bytes 786440 | tf_op jit(solution)/shard_map/ppermute | solution.py:463
  46.3 16.3 %collective-permute-start.10 = (bf16[2,8,128,128]{3,2,1,0:T(8,128)(2,1)S(1)}, bf16[2,8,128,128]{3,2,1,0:T(8,128)(2,1)S(1)}, u32[]{:S(2)}, u32[]{:S(2)}) collective-permute-start(bf16[2,8,128,128]{3,2,1,0:T(8,128)(2,1)S(1)} %get-tuple-element.116), channel_id=1, source_target_pairs={{0,1},{3,2},{4,5},{7,6},{8,9},{11,10},{12,13},{15,14},{16,17},{19,... | collective-permute-start | bytes 1572872 | tf_op jit(solution)/shard_map/ppermute | solution.py:463
  60.2 1.6 %collective-permute-start.13 = (bf16[2,4,128,128]{3,2,1,0:T(8,128)(2,1)S(1)}, bf16[2,4,128,128]{3,2,1,0:T(8,128)(2,1)S(1)}, u32[]{:S(2)}, u32[]{:S(2)}) collective-permute-start(bf16[2,4,128,128]{3,2,1,0:T(8,128)(2,1)S(1)} %get-tuple-element.121), channel_id=1, source_target_pairs={{0,4},{4,0},{1,5},{5,1},{2,6},{6,2},{3,7},{7,3},{8,12},{12,8},{9,1... | collective-permute-start | bytes 786440 | tf_op jit(solution)/shard_map/ppermute | solution.py:24
  63.1 10.1 %collective-permute-start.14 = (bf16[2,8,128,128]{3,2,1,0:T(8,128)(2,1)S(1)}, bf16[2,8,128,128]{3,2,1,0:T(8,128)(2,1)S(1)}, u32[]{:S(2)}, u32[]{:S(2)}) collective-permute-start(bf16[2,8,128,128]{3,2,1,0:T(8,128)(2,1)S(1)} %get-tuple-element.125), channel_id=1, source_target_pairs={{1,2},{2,1},{5,6},{6,5},{9,10},{10,9},{13,14},{14,13},{17,18},{18,... | collective-permute-start | bytes 1572872 | tf_op jit(solution)/shard_map/ppermute | solution.py:463
  63.8 18.1 %collective-permute-start.19 = (bf16[2,8,128,128]{3,2,1,0:T(8,128)(2,1)S(1)}, bf16[2,8,128,128]{3,2,1,0:T(8,128)(2,1)S(1)}, u32[]{:S(2)}, u32[]{:S(2)}) collective-permute-start(bf16[2,8,128,128]{3,2,1,0:T(8,128)(2,1)S(1)} %get-tuple-element.131), channel_id=1, source_target_pairs={{0,1},{3,2},{4,5},{7,6},{8,9},{11,10},{12,13},{15,14},{16,17},{19,... | collective-permute-start | bytes 1572872 | tf_op jit(solution)/shard_map/ppermute | solution.py:463
  82.4 17.9 %collective-permute-start.22 = (bf16[2,8,128,128]{3,2,1,0:T(8,128)(2,1)S(1)}, bf16[2,8,128,128]{3,2,1,0:T(8,128)(2,1)S(1)}, u32[]{:S(2)}, u32[]{:S(2)}) collective-permute-start(bf16[2,8,128,128]{3,2,1,0:T(8,128)(2,1)S(1)} %get-tuple-element.141), channel_id=1, source_target_pairs={{1,2},{2,1},{5,6},{6,5},{9,10},{10,9},{13,14},{14,13},{17,18},{18,... | collective-permute-start | bytes 1572872 | tf_op jit(solution)/shard_map/ppermute | solution.py:463
  83.1 14.4 %collective-permute-start.15 = (bf16[2,4,128,128]{3,2,1,0:T(8,128)(2,1)S(1)}, bf16[2,4,128,128]{3,2,1,0:T(8,128)(2,1)S(1)}, u32[]{:S(2)}, u32[]{:S(2)}) collective-permute-start(bf16[2,4,128,128]{3,2,1,0:T(8,128)(2,1)S(1)} %get-tuple-element.128), channel_id=1, source_target_pairs={{0,1},{3,2},{1,0},{2,3},{4,5},{7,6},{5,4},{6,7},{8,9},{11,10},{9,8... | collective-permute-start | bytes 786440 | tf_op jit(solution)/shard_map/ppermute | solution.py:463
  87.5 5.5 %collective-permute-start.16 = (bf16[528,128]{1,0:T(8,128)(2,1)S(1)}, bf16[528,128]{1,0:T(8,128)(2,1)S(1)}, u32[]{:S(2)}, u32[]{:S(2)}) collective-permute-start(bf16[528,128]{1,0:T(8,128)(2,1)S(1)} %get-tuple-element.129), channel_id=1, source_target_pairs={{0,8},{8,0},{16,24},{24,16},{1,9},{9,1},{17,25},{25,17},{2,10},{10... | collective-permute-start | bytes 405512 | tf_op jit(solution)/shard_map/ppermute | solution.py:24
  88.8 5.0 %collective-permute-start.17 = (bf16[528,128]{1,0:T(8,128)(2,1)S(1)}, bf16[528,128]{1,0:T(8,128)(2,1)S(1)}, u32[]{:S(2)}, u32[]{:S(2)}) collective-permute-start(bf16[528,128]{1,0:T(8,128)(2,1)S(1)} %get-tuple-element.130), channel_id=1, source_target_pairs={{0,16},{8,24},{16,0},{24,8},{1,17},{9,25},{17,1},{25,9},{2,18},{10... | collective-permute-start | bytes 405512 | tf_op jit(solution)/shard_map/ppermute | solution.py:24
  89.6 5.9 %collective-permute-start.18 = (bf16[528,128]{1,0:T(8,128)(2,1)S(1)}, bf16[528,128]{1,0:T(8,128)(2,1)S(1)}, u32[]{:S(2)}, u32[]{:S(2)}) collective-permute-start(bf16[528,128]{1,0:T(8,128)(2,1)S(1)} %get-tuple-element.130), channel_id=1, source_target_pairs={{0,24},{8,16},{16,8},{24,0},{1,25},{9,17},{17,9},{25,1},{2,26},{10... | collective-permute-start | bytes 405512 | tf_op jit(solution)/shard_map/ppermute | solution.py:24
  100.9 22.9 %collective-permute-start.25 = (bf16[2,8,128,128]{3,2,1,0:T(8,128)(2,1)S(1)}, bf16[2,8,128,128]{3,2,1,0:T(8,128)(2,1)S(1)}, u32[]{:S(2)}, u32[]{:S(2)}) collective-permute-start(bf16[2,8,128,128]{3,2,1,0:T(8,128)(2,1)S(1)} %get-tuple-element.149), channel_id=1, source_target_pairs={{1,0},{2,3},{5,4},{6,7},{9,8},{10,11},{13,12},{14,15},{17,16},{18,... | collective-permute-start | bytes 1572872 | tf_op jit(solution)/shard_map/ppermute | solution.py:463
  102.2 16.2 %collective-permute-start.21 = (bf16[2,4,128,128]{3,2,1,0:T(8,128)(2,1)S(1)}, bf16[2,4,128,128]{3,2,1,0:T(8,128)(2,1)S(1)}, u32[]{:S(2)}, u32[]{:S(2)}) collective-permute-start(bf16[2,4,128,128]{3,2,1,0:T(8,128)(2,1)S(1)} %get-tuple-element.137), channel_id=1, source_target_pairs={{0,1},{3,2},{1,0},{2,3},{4,5},{7,6},{5,4},{6,7},{8,9},{11,10},{9,8... | collective-permute-start | bytes 786440 | tf_op jit(solution)/shard_map/ppermute | solution.py:463
  104.9 17.0 %collective-permute-start.20 = (bf16[2,4,128,128]{3,2,1,0:T(8,128)(2,1)S(1)}, bf16[2,4,128,128]{3,2,1,0:T(8,128)(2,1)S(1)}, u32[]{:S(2)}, u32[]{:S(2)}) collective-permute-start(bf16[2,4,128,128]{3,2,1,0:T(8,128)(2,1)S(1)} %get-tuple-element.136), channel_id=1, source_target_pairs={{1,2},{2,1},{5,6},{6,5},{9,10},{10,9},{13,14},{14,13},{17,18},{18,... | collective-permute-start | bytes 786440 | tf_op jit(solution)/shard_map/ppermute | solution.py:463
  105.6 18.2 %collective-permute-start.26 = (bf16[2,4,128,128]{3,2,1,0:T(8,128)(2,1)S(1)}, bf16[2,4,128,128]{3,2,1,0:T(8,128)(2,1)S(1)}, u32[]{:S(2)}, u32[]{:S(2)}) collective-permute-start(bf16[2,4,128,128]{3,2,1,0:T(8,128)(2,1)S(1)} %get-tuple-element.150), channel_id=1, source_target_pairs={{0,4},{4,0},{1,5},{5,1},{2,6},{6,2},{3,7},{7,3},{8,12},{12,8},{9,1... | collective-permute-start | bytes 786440 | tf_op jit(solution)/shard_map/ppermute | solution.py:24
  118.9 7.7 %collective-permute-start.24 = (bf16[2,4,128,128]{3,2,1,0:T(8,128)(2,1)S(1)}, bf16[2,4,128,128]{3,2,1,0:T(8,128)(2,1)S(1)}, u32[]{:S(2)}, u32[]{:S(2)}) collective-permute-start(bf16[2,4,128,128]{3,2,1,0:T(8,128)(2,1)S(1)} %get-tuple-element.148), channel_id=1, source_target_pairs={{1,2},{2,1},{5,6},{6,5},{9,10},{10,9},{13,14},{14,13},{17,18},{18,... | collective-permute-start | bytes 786440 | tf_op jit(solution)/shard_map/ppermute | solution.py:463
  122.5 10.3 %collective-permute-start.23 = (bf16[2,4,128,128]{3,2,1,0:T(8,128)(2,1)S(1)}, bf16[2,4,128,128]{3,2,1,0:T(8,128)(2,1)S(1)}, u32[]{:S(2)}, u32[]{:S(2)}) collective-permute-start(bf16[2,4,128,128]{3,2,1,0:T(8,128)(2,1)S(1)} %get-tuple-element.147), channel_id=1, source_target_pairs={{1,0},{2,3},{5,4},{6,7},{9,8},{10,11},{13,12},{14,15},{17,16},{18,... | collective-permute-start | bytes 786440 | tf_op jit(solution)/shard_map/ppermute | solution.py:463
  127.2 8.5 %collective-permute-start.27 = (bf16[2,4,128,128]{3,2,1,0:T(8,128)(2,1)S(1)}, bf16[2,4,128,128]{3,2,1,0:T(8,128)(2,1)S(1)}, u32[]{:S(2)}, u32[]{:S(2)}) collective-permute-start(bf16[2,4,128,128]{3,2,1,0:T(8,128)(2,1)S(1)} %get-tuple-element.159), channel_id=1, source_target_pairs={{1,0},{2,3},{5,4},{6,7},{9,8},{10,11},{13,12},{14,15},{17,16},{18,... | collective-permute-start | bytes 786440 | tf_op jit(solution)/shard_map/ppermute | solution.py:463

commit v6 on v5

--- a/solution.py
+++ b/solution.py
@@ -17,6 +17,7 @@
 SMEM = pl.BlockSpec(memory_space=pltpu.SMEM)
 HBM = pl.BlockSpec(memory_space=pltpu.HBM)
 LIMIT = 24 * 1024 * 1024
+COSTS = ()
 
 
 def pairs(array, axis, distance):
@@ -40,22 +41,22 @@
     return jnp.where(row, 1.0, 0.0).astype(F32)
 
 
-def call(token, kernel, operands, out_shape, scratch=(), aliases=None, specs=None, out_specs=None):
-    count, results = len(operands), len(out_shape)
+def call(token, kernel, operands, out_shape, cost=0, scratch=(), aliases=None, specs=None, out_specs=None, after=()):
+    count, results, behind = len(operands), len(out_shape), len(operands) + len(after)
 
     def ordered(*refs):
-        kernel(*refs[:count], *refs[count + 1 : count + 1 + results], *refs[count + 2 + results :])
+        kernel(*refs[:count], *refs[behind + 1 : behind + 1 + results], *refs[behind + 2 + results :])
 
     *outs, token = pl.pallas_call(
         ordered,
-        in_specs=list(specs or [SMEM] + [VMEM] * (count - 1)) + [VMEM],
+        in_specs=list(specs or [SMEM] + [VMEM] * (count - 1)) + [VMEM] * (len(after) + 1),
         out_specs=list(out_specs or [VMEM] * results) + [VMEM],
         out_shape=list(out_shape) + [jax.ShapeDtypeStruct(token.shape, token.dtype)],
         scratch_shapes=list(scratch),
-        input_output_aliases={**(aliases or {}), count: results},
+        input_output_aliases={**(aliases or {}), behind: results},
         compiler_params=pltpu.CompilerParams(vmem_limit_bytes=LIMIT),
-        cost_estimate=pl.CostEstimate(flops=0, bytes_accessed=0, transcendentals=0),
-    )(*operands, token)
+        cost_estimate=pl.CostEstimate(flops=int(cost * 1e9), bytes_accessed=0, transcendentals=0),
+    )(*operands, *after, token)
     return token, outs
 
 
@@ -107,11 +108,11 @@
     return pl.ds(group * unit * DH, unit * DH)
 
 
-def rest_terms(factor, unit, part, places, shift, total, ids, docs_ref, q_hbm, k_hbm, v_hbm, g_hbm, *refs):
+def rest_terms(factor, unit, part, places, mates, ids, docs_ref, q_hbm, k_hbm, v_hbm, g_hbm, *refs):
     outs, (q_ref, k_ref, v_ref, g_ref, sems) = refs[:-5], refs[-5:]
     waiting = []
-    for s, g in enumerate(places):
-        forward, backward = group_columns(g, unit), group_columns((g + shift) % total, unit)
+    for s, (g, mate) in enumerate(zip(places, mates)):
+        forward, backward = group_columns(g, unit), group_columns(mate, unit)
         waiting.append(fetch(
             [
                 (k_hbm.at[:, forward], k_ref.at[s]), (v_hbm.at[:, forward], v_ref.at[s]),
@@ -128,38 +129,49 @@
 
 
 def lead_terms(
-    factor, unit, part, shift, outer, inner, ids, docs_ref, labels, q_hbm, k_hbm, v_hbm, g_hbm, carry_hbm, cot_hbm, *refs,
+    factor, unit, part, places, mates, outer, inner, ids, docs_ref, labels, q_hbm, k_hbm, v_hbm, g_hbm, carry_hbm, cot_hbm,
+    *refs,
 ):
-    outs, sents, (q_ref, k_ref, v_ref, g_ref, carry_ref, cot_ref, sems) = refs[:inner], refs[inner : 2 * inner], refs[2 * inner :]
+    outs, (sent, carried), (q_ref, k_ref, v_ref, g_ref, carry_ref, cot_ref, sems) = refs[:inner], refs[inner : inner + 2], refs[inner + 2 :]
     o, c, z = ids[0], ids[1], ids[2]
-    held = carry_hbm.shape[0]
-    forward, backward = group_columns(0, unit), group_columns(shift, unit)
-    copies = fetch(
-        [
-            (k_hbm.at[:, forward], k_ref), (v_hbm.at[:, forward], v_ref),
-            (q_hbm.at[:, backward], q_ref), (g_hbm.at[:, backward], g_ref),
-            (carry_hbm.at[pl.ds(0, unit)], carry_ref), (cot_hbm.at[pl.ds(held - unit, unit)], cot_ref),
-        ],
-        sems,
-    )
-    for copy in copies:
+    waiting = [fetch([(carry_hbm, carry_ref), (cot_hbm, cot_ref)], sems.at[len(places)])]
+    for s, (g, mate) in enumerate(zip(places, mates)):
+        forward, backward = group_columns(g, unit), group_columns(mate, unit)
+        waiting.append(fetch(
+            [
+                (k_hbm.at[:, forward], k_ref.at[s]), (v_hbm.at[:, forward], v_ref.at[s]),
+                (q_hbm.at[:, backward], q_ref.at[s]), (g_hbm.at[:, backward], g_ref.at[s]),
+            ],
+            sems.at[s],
+        ))
+    for copy in waiting[0]:
         copy.wait()
     first, last = own_row(labels, z), own_row(labels, DEPTH + z)
-    opens = jnp.logical_and(jnp.logical_and(o == 0, c == 0), z == 0)
-    closes = jnp.logical_and(jnp.logical_and(o == outer - 1, c == inner - 1), z == DEPTH - 1)
-    open_f = flag(jnp.logical_and(opens, last == 0.0))
-    close_b = flag(jnp.logical_and(closes, first == last)) * factor
-
-    def extra(place):
-        return open_f * carry_ref[place], close_b * cot_ref[place]
-
-    add_terms(factor, part, docs_ref, c, q_ref, k_ref, v_ref, g_ref, outs, 0, extra)
+    newest = labels[2 * DEPTH - 1 : 2 * DEPTH, :]
+    opens, closes = jnp.logical_and(o == 0, c == 0), jnp.logical_and(o == outer - 1, c == inner - 1)
+    for s in range(len(places)):
+        for copy in waiting[1 + s]:
+            copy.wait()
+        open_f = flag(jnp.logical_and(jnp.logical_and(opens, z == s), last == 0.0))
+        close_b = flag(jnp.logical_and(jnp.logical_and(closes, z == DEPTH - 1 - s), first == newest)) * factor
+
+        def extra(place):
+            return open_f * carry_ref[place], close_b * cot_ref[place]
+
+        add_terms(
+            factor, part, docs_ref, c, q_ref.at[s], k_ref.at[s], v_ref.at[s], g_ref.at[s], outs, s * part, extra
+        )
     _, side, at_end = place_of(ids)
 
     @pl.when(at_end)
     def _():
-        for term, out in zip(outs, sents):
-            hop(side, edge_rows(z, labels, None), True, 0, part, term, None, None, 0, out, 0)
+        for t, term in enumerate(outs):
+            hop(side, edge_rows(z, labels, None), True, 0, part, term, None, None, 0, sent, t * part)
+
+    @pl.when(jnp.logical_not(at_end))
+    def _():
+        for i in range(unit):
+            carried[i] = jnp.where(side == 0, carry_ref[i], cot_ref[i] * factor).astype(BF16)
 
 
 def block_rows(labels, z, grouped):
@@ -189,7 +201,8 @@
         out[count * DH :, :] = marks.astype(BF16)
 
 
-def prefix_kernel(factor, unit, part, places, shift, total, inner, outer, grouped, ids, carry_ref, cot_ref, *refs):
+def prefix_kernel(factor, unit, part, places, mates, inner, outer, grouped, lacking, ids, carry_ref, cot_ref, *refs):
+    lacked, refs = (refs[0], refs[1:]) if lacking else (None, refs)
     labels, terms, fans = refs[:inner], refs[inner : 2 * inner], refs[2 * inner : 2 * inner + outer - 1]
     outs, edge_ref = refs[2 * inner + outer - 1 : -1], refs[-1]
     o, c, z = ids[0], ids[1], ids[2]
@@ -230,8 +243,8 @@
             take_b = jnp.logical_and(take_b, jnp.logical_and(o == outer - 1, (c ^ t) == inner - 1))
         priors.append(prior)
         laters.append(later)
-        plans.append((forward, backward, flag(take_f), flag(take_b) * factor))
-    for s, g in enumerate(places):
+        plans.append((forward, backward, flag(take_f), flag(take_b)))
+    for s, (g, mate) in enumerate(zip(places, mates)):
         for i in range(part):
             at = s * part + i
 
@@ -240,10 +253,14 @@
                 mine = jnp.logical_and(place >= 0, place < held)
                 return jnp.where(mine, ref[jnp.clip(place, 0, held - 1)], 0.0)
 
-            carries = (
+            carries = [
                 carried(g * unit + c * part + i, carry_ref),
-                carried((g + shift) % total * unit + c * part + i, cot_ref),
-            )
+                carried(mate * unit + c * part + i, cot_ref) * factor,
+            ]
+            if lacking:
+                more = lacked[c * part + i].astype(F32)
+                carries[0] = carries[0] + jnp.where(z == 0, more, 0.0)
+                carries[1] = carries[1] + jnp.where(z == DEPTH - 1, more, 0.0)
 
             def value(ref, side):
                 return (ref[at * DH : (at + 1) * DH, :] if side is None else ref[side, at]).astype(F32)
@@ -318,33 +335,33 @@
         pl.when(jnp.logical_not(at_end))(lambda: write(side if across else 1 - side, far))
 
 
-def lead_total_kernel(part, turns, ids, labels, *refs):
+def lead_total_kernel(part, plans, ids, labels, *refs):
     z, side, at_end = place_of(ids)
     rows = edge_rows(z, labels, None)
-    for t in range(turns):
+    for t, (off, near_off, middle_off, far_off) in enumerate(plans):
         term, near, middle, far = refs[4 * t : 4 * t + 4]
-        out = refs[4 * turns + t]
-
-        def total(which, over, rest):
+        out = refs[4 * len(plans) + t]
+
+        def total(which, over, over_off, rest, rest_off):
             own, neighbour, final, _, _ = pick(which, rows)
             counts, come = flag(own == final), flag(neighbour == final)
             for i in range(part):
-                value = counts * term[which, i].astype(F32)
+                value = counts * term[which, off + i].astype(F32)
                 if over is not None:
-                    value = value + come * over[0, i].astype(F32)
+                    value = value + come * over[0, over_off + i].astype(F32)
                 if rest is not None:
-                    value = value + rest[1, i].astype(F32)
+                    value = value + rest[1, rest_off + i].astype(F32)
                 out[which, i] = value.astype(BF16)
 
         @pl.when(at_end)
         def _():
-            total(side, None, far)
-            total(1 - side, far, None)
+            total(side, None, 0, far, far_off)
+            total(1 - side, far, far_off, None, 0)
 
         @pl.when(jnp.logical_not(at_end))
         def _():
-            total(side, near, middle)
-            total(1 - side, middle, near)
+            total(side, near, near_off, middle, middle_off)
+            total(1 - side, middle, middle_off, near, near_off)
 
 
 def local_kernel(factor, base, count, docs_ref, row_ref, q_ref, k_ref, v_ref, g_ref, out):
@@ -365,32 +382,30 @@
 
 def output_kernel(unit, part, plans, ids, labels, edges, docs_ref, q_ref, k_ref, v_ref, g_ref, *refs):
     count = len(plans)
-    sources, locals_ = refs[: 8 * count], refs[8 * count : 9 * count]
+    sources, locals_ = refs[: 4 * count], refs[4 * count : 5 * count]
     outs, (states, held, sems) = refs[-7:-3], refs[-3:]
     c = ids[1]
     z, side, at_end = place_of(ids)
     rows = edge_rows(z, labels, edges)
 
     def make_states(ends, side):
-        for n, (_, _, both) in enumerate(plans):
-            for which in range(2):
-                lead, off, near_off, middle_off, far_off = both[which]
-                prefix, near, middle, far = sources[8 * n + 4 * which : 8 * n + 4 * which + 4]
-                _, neighbour, _, target, prior = rows[which]
-                reach, come = flag(prior == target), flag(neighbour == target)
-                if ends:
-                    over, rest = (None, (far, far_off)) if side == which else ((far, far_off), None)
-                elif side == which:
-                    over, rest = (near, near_off), (middle, middle_off)
-                else:
-                    over, rest = (middle, middle_off), (near, near_off)
-                for i in range(part):
-                    value = reach * prefix[which, off + i].astype(F32)
-                    if over is not None:
-                        value = value + come * over[0][0, over[1] + i].astype(F32)
-                    if rest is not None and not lead:
-                        value = value + reach * rest[0][1, rest[1] + i].astype(F32)
-                    states[n, which, i] = value.astype(BF16)
+        for n, (which, _, _, lead, off, near_off, middle_off, far_off) in enumerate(plans):
+            prefix, near, middle, far = sources[4 * n : 4 * n + 4]
+            _, neighbour, _, target, prior = rows[which]
+            reach, come = flag(prior == target), flag(neighbour == target)
+            if ends:
+                over, rest = (None, (far, far_off)) if side == which else ((far, far_off), None)
+            elif side == which:
+                over, rest = (near, near_off), (middle, middle_off)
+            else:
+                over, rest = (middle, middle_off), (near, near_off)
+            for i in range(part):
+                value = reach * prefix[which, off + i].astype(F32)
+                if over is not None:
+                    value = value + come * over[0][0, over[1] + i].astype(F32)
+                if rest is not None and not lead:
+                    value = value + reach * rest[0][1, rest[1] + i].astype(F32)
+                states[n, i] = value.astype(BF16)
 
     for ends in (True, False):
         for which in range(2):
@@ -399,20 +414,24 @@
 
     in_first, in_last = document_masks(docs_ref[...])
     copies = []
-    for n, (group, turn, _) in enumerate(plans):
+    for n, (which, group, turn, *_) in enumerate(plans):
         place = (c ^ turn) * part
         for i in range(part):
             at = columns(group * unit + place + i)
-            before, after = states[n, 0, i], states[n, 1, i]
-            results = (
-                dot(jnp.where(in_first, q_ref[:, at], 0), before),
-                dot_transposed(jnp.where(in_first, g_ref[:, at], 0), before),
-                dot_transposed(jnp.where(in_last, v_ref[:, at], 0), after),
-                dot(jnp.where(in_last, k_ref[:, at], 0), after),
-            )
+            state = states[n, i]
+            if which == 0:
+                results = (
+                    dot(jnp.where(in_first, q_ref[:, at], 0), state),
+                    dot_transposed(jnp.where(in_first, g_ref[:, at], 0), state),
+                )
+            else:
+                results = (
+                    dot_transposed(jnp.where(in_last, v_ref[:, at], 0), state),
+                    dot(jnp.where(in_last, k_ref[:, at], 0), state),
+                )
             for m, result in enumerate(results):
-                held[n, m, i] = (locals_[n][m, place + i] + result).astype(BF16)
-                copy = pltpu.make_async_copy(held.at[n, m, i], outs[m].at[:, at], sems.at[n, m, i])
+                held[n, m, i] = (locals_[n][2 * which + m, place + i] + result).astype(BF16)
+                copy = pltpu.make_async_copy(held.at[n, m, i], outs[2 * which + m].at[:, at], sems.at[n, m, i])
                 copy.start()
                 copies.append(copy)
     for copy in copies:
@@ -429,8 +448,11 @@
     part = min(4, head_count // inner)
     unit = part * inner
     groups = head_count // unit
-    leads = held % unit == 0
-    shift = groups - 1 if leads else 0
+    leads = 2 if held == unit and groups == DEPTH and inner == 2 else 0
+    costs = iter(COSTS if leads else ())
+
+    def mate(g):
+        return groups - 1 - g if leads else g
 
     ids = jnp.stack([lax.axis_index(a) for a in ("outer", "inner", "heads")]).astype(jnp.int32)
     token, (own_labels, docs_column, docs_row) = call(
@@ -465,27 +487,32 @@
             kind[u] = (got, n * part)
         return got
 
+    def run(*args, **options):
+        nonlocal token
+        token, outs = call(token, *args, cost=next(costs, 0), **options)
+        return outs
+
     def make_lead_terms():
-        nonlocal token
-        block = pltpu.VMEM((SPAN, unit * DH), BF16)
+        places = tuple(range(leads))
+        block = pltpu.VMEM((leads, SPAN, unit * DH), BF16)
         carry = pltpu.VMEM((unit, DH, DH), F32)
-        token, own = call(
-            token,
-            functools.partial(lead_terms, factor, unit, part, shift, outer, inner),
+        own = run(
+            functools.partial(
+                lead_terms, factor, unit, part, places, tuple(mate(g) for g in places), outer, inner
+            ),
             (ids, docs_column, own_labels) + far_arrays + far_carries,
-            [state_pair(part)] * (2 * inner),
-            scratch=[block] * 4 + [carry] * 2 + [pltpu.SemaphoreType.DMA((6,))],
+            [state_pair(part * leads)] * inner + [state_pair(part * inner), jax.ShapeDtypeStruct((unit, DH, DH), BF16)],
+            scratch=[block] * 4 + [carry] * 2 + [pltpu.SemaphoreType.DMA((leads + 1, 4))],
             specs=[SMEM, VMEM, VMEM] + [HBM] * 6,
         )
-        terms[0] = [(a, 0) for a in own[:inner]]
-        for t in range(inner):
-            receive([(0, t)], near, own[inner + t], [(0, 1), (3, 2)])
+        for g in places:
+            terms[g] = [(a, g * part) for a in own[:inner]]
+        receive([(0, t) for t in range(inner)], near, own[inner], [(0, 1), (3, 2)])
+        return lax.ppermute(own[inner + 1], "heads", [(1, 0), (2, 3)])
 
     def make_terms(places):
-        nonlocal token
-        token, own = call(
-            token,
-            functools.partial(rest_terms, factor, unit, part, places, shift, groups),
+        own = run(
+            functools.partial(rest_terms, factor, unit, part, places, tuple(mate(g) for g in places)),
             (ids, docs_column) + far_arrays,
             [state_pair(part * len(places))] * inner,
             scratch=[pltpu.VMEM((len(places), SPAN, unit * DH), BF16)] * 4
@@ -499,23 +526,22 @@
     def make_sums(received, grouped):
         nonlocal token
         count = received[0].shape[1]
-        token, sums = call(
-            token,
+        sums = run(
             functools.partial(sum_kernel, inner, levels, grouped),
             (ids, *labels, *received),
             [jax.ShapeDtypeStruct((count * DH + LABELS, DH), BF16)] * levels,
         )
         return [pairs(sums[d.bit_length() - 1], "outer", d) for d in range(1, outer)]
 
-    def make_prefixes(places, received, fans, grouped):
-        nonlocal token, edge
+    def make_prefixes(places, received, fans, grouped, lacked=None):
+        nonlocal edge
         count = received[0].shape[1]
-        token, given = call(
-            token,
+        given = run(
             functools.partial(
-                prefix_kernel, factor, unit, part, places, shift, groups, inner, outer, grouped
+                prefix_kernel, factor, unit, part, places, tuple(mate(g) for g in places), inner, outer, grouped,
+                lacked is not None,
             ),
-            (ids, *carries, *labels, *received, *fans),
+            (ids, *carries, *([] if lacked is None else [lacked]), *labels, *received, *fans),
             [state_pair(count)] * inner + [jax.ShapeDtypeStruct((8, DH), F32)],
         )
         edge = given[-1] if edge is None else edge
@@ -523,17 +549,16 @@
         for s, g in enumerate(places):
             prefixes[g] = [(a, s * part) for a in given]
 
-    def move(near_units, far_units, across, perm):
-        nonlocal token
+    def move(near_units, far_units, across):
         units = list(near_units) + list(far_units)
-        use_edges = not all(leads and g == 0 for g, _ in units)
+        use_edges = not all(g < leads for g, _ in units)
         operands = [ids, own_labels] + ([edge] if use_edges else [])
 
         def plans_of(chosen, got):
             plans = []
             for u in chosen:
                 g, t = u
-                lead = leads and g == 0
+                lead = g < leads
                 array, off = terms[g][t]
                 operands.append(array)
                 if not lead:
@@ -545,8 +570,7 @@
 
         near_plans = plans_of(near_units, None)
         far_plans = plans_of(far_units, near if across else middle)
-        token, sent = call(
-            token,
+        sent = run(
             functools.partial(hop_kernel, part, near_plans, far_plans, across, use_edges),
             operands,
             [state_pair(part * max(len(near_units), len(far_units)))],
@@ -555,94 +579,99 @@
 
     def ends(near_units, far_units):
         perm = ([(0, 1), (3, 2)] if near_units else []) + ([(1, 0), (2, 3)] if far_units else [])
-        got = receive(near_units, near, move(near_units, far_units, False, perm), perm)
+        got = receive(near_units, near, move(near_units, far_units, False), perm)
         for n, u in enumerate(far_units):
             far[u] = (got, n * part)
 
     def across(units):
-        receive(units, middle, move([], units, True, None), [(1, 2), (2, 1)])
-
-    def make_local(g):
-        nonlocal token
-        token, out = call(
-            token,
+        receive(units, middle, move([], units, True), [(1, 2), (2, 1)])
+
+    def make_local(g, after=()):
+        out = run(
             functools.partial(local_kernel, factor, g * unit, unit),
             (docs_column, docs_row) + arrays,
             [jax.ShapeDtypeStruct((4, unit, SPAN, DH), F32)],
             specs=[VMEM] * 6,
+            after=after,
         )
         local[g] = out[0]
 
     out_shape = jax.ShapeDtypeStruct(queries.shape, BF16)
     results = ()
 
-    def make_outputs(units):
-        nonlocal token, results
+    def make_outputs(halves):
+        nonlocal results
         operands, plans = (ids, own_labels, edge, docs_column) + arrays, []
-        for g, t in units:
-            both = []
-            for u in ((g, t), ((g - shift) % groups, t)):
-                lead = leads and u[0] == 0
-                array, off = prefixes[u[0]][t]
-                both.append((lead, off, near[u][1], middle[u][1], far[u][1]))
-                operands += (array, near[u][0], middle[u][0], far[u][0])
-            plans.append((g, t, both))
-        operands += tuple(local[g] for g, _ in units)
-        count = len(units)
-        token, results = call(
-            token,
+        for which, g, t in halves:
+            array, off = prefixes[g][t]
+            kept = [kind[g, t] for kind in (near, middle, far)]
+            heads = mate(g) if which else g
+            plans.append((which, heads, t, g < leads, off) + tuple(at for _, at in kept))
+            operands += (array,) + tuple(a for a, _ in kept)
+        operands += tuple(local[mate(g) if which else g] for which, g, _ in halves)
+        count = len(halves)
+        results = run(
             functools.partial(output_kernel, unit, part, plans),
             operands + tuple(results),
             [out_shape] * 4,
             scratch=[
-                pltpu.VMEM((count, 2, part, DH, DH), BF16),
-                pltpu.VMEM((count, 4, part, SPAN, DH), BF16),
-                pltpu.SemaphoreType.DMA((count, 4, part)),
+                pltpu.VMEM((count, part, DH, DH), BF16),
+                pltpu.VMEM((count, 2, part, SPAN, DH), BF16),
+                pltpu.SemaphoreType.DMA((count, 2, part)),
             ],
             aliases={len(operands) + i: i for i in range(len(results))},
             specs=[SMEM] + [VMEM] * (len(operands) - 1) + [HBM] * len(results),
             out_specs=[HBM] * 4,
         )
 
-    if leads and groups == 4 and inner == 2:
-        make_lead_terms()
-        rest = tuple(range(1, groups))
-        got_rest = make_terms(rest)
-        across([(0, 0)])
+    def make_totals(g):
+        operands, plans = [ids, own_labels], []
+        for t in range(inner):
+            array, off = terms[g][t]
+            kept = [kind[g, t] for kind in (near, middle, far)]
+            operands += [array] + [a for a, _ in kept]
+            plans.append((off,) + tuple(at for _, at in kept))
+        totals = run(
+            functools.partial(lead_total_kernel, part, plans),
+            operands,
+            [state_pair(part)] * inner,
+        )
+        return exchange(totals)
+
+    def chunk(g):
+        return [(g, t) for t in range(inner)]
+
+    def halves_of(g):
+        return [(which, g, t) for which in range(2) for t in range(inner)]
+
+    if leads:
+        lacked = make_lead_terms()
+        got_rest = make_terms((2, 3))
         fans_rest = make_sums(got_rest, False)
-        across([(0, 1)])
+        ends(chunk(1), [])
+        across(chunk(0))
         make_local(0)
-        ends([], [(0, 0)])
         make_local(1)
-        ends([], [(0, 1)])
-        make_prefixes(rest, got_rest, fans_rest, False)
-        ends([(1, 0), (2, 0)], [])
-        token, totals = call(
-            token,
-            functools.partial(lead_total_kernel, part, inner),
-            [ids, own_labels]
-            + [a for t in range(inner) for a in (terms[0][t][0], near[0, t][0], middle[0, t][0], far[0, t][0])],
-            [state_pair(part)] * inner,
-        )
-        got_lead = exchange(totals)
-        ends([(3, 0), (1, 1)], [])
-        fans_lead = make_sums(got_lead, True)
-        across([(1, 0), (2, 0)])
+        make_prefixes((2, 3), got_rest, fans_rest, False)
+        across(chunk(1))
+        ends(chunk(2), chunk(0))
         make_local(2)
-        ends([(2, 1)], [(1, 0)])
-        across([(3, 0), (1, 1)])
-        make_prefixes((0,), got_lead, fans_lead, True)
-        ends([(3, 1)], [(2, 0)])
-        across([(2, 1)])
-        make_local(3)
-        ends([], [(3, 0), (1, 1)])
-        across([(3, 1)])
-        make_outputs([(1, 0), (0, 0)])
-        ends([], [(2, 1)])
-        make_outputs([(2, 0), (3, 0), (0, 1)])
-        ends([], [(3, 1)])
-        make_outputs([(1, 1)])
-        make_outputs([(2, 1), (3, 1)])
+        make_local(3, after=[lacked])
+        ends(chunk(3), chunk(1))
+        across(chunk(2))
+        got_first = make_totals(0)
+        fans_first = make_sums(got_first, True)
+        across(chunk(3))
+        ends([], chunk(2))
+        got_second = make_totals(1)
+        make_prefixes((0,), got_first, fans_first, True)
+        fans_second = make_sums(got_second, True)
+        ends([], chunk(3))
+        make_outputs(halves_of(0))
+        make_prefixes((1,), got_second, fans_second, True, lacked)
+        make_outputs(halves_of(1))
+        make_outputs(halves_of(2))
+        make_outputs(halves_of(3))
     else:
         assert not leads
         places = tuple(range(groups))
@@ -656,8 +685,8 @@
                 across([units[k]])
         for g in range(groups):
             make_local(g)
-        for u in units:
-            make_outputs([u])
+        for g, t in units:
+            make_outputs([(0, g, t), (1, g, t)])
     return tuple(results)
 
 

time: 139 us -> 117 us (0.84)
  starting transfers between devices: 43.4 us -> 30.5 us
  waiting for transfers between devices: 54.7 us -> 47.4 us
    ppermute x17 -> x10, waiting for transfers between devices: 40.1 us -> 20 us  [receive(): got = lax.ppermute(sent, 'heads', perm)]
    ppermute x17 -> x10, starting transfers between devices: 35.5 us -> 17.6 us  [receive(): got = lax.ppermute(sent, 'heads', perm)]
    ppermute x0 -> x1, waiting for transfers between devices: none -> 13.2 us  [make_lead_terms(): return lax.ppermute(own[inner + 1], 'heads', [(1, 0), (2, 3)])]
    ppermute x11 -> x16, starting transfers between devices: 7.92 us -> 11.7 us  [pairs(): return lax.ppermute(array, axis, [(i, i ^ distance) for i in range(count)])]
    pallas_call x31 -> x28, Pallas kernels: 37.9 us -> 36.8 us  [call(): pl.pallas_call(ordered, in_specs=list(specs or [SMEM] + [VMEM] * (count -...]
    ppermute x11 -> x16, waiting for transfers between devices: 14.6 us -> 14.2 us  [pairs(): return lax.ppermute(array, axis, [(i, i ^ distance) for i in range(count)])]
  transfers between devices with their start and end apart: 28 -> 27, of which waited for: 14 -> 14; matrix products, arithmetic and copies ran while one was open for 0% -> 0% of each run, Pallas kernels for 19% -> 24%
where the time goes in v6:
time: 117 us
  waiting for transfers between devices  47.4 us (41%)
  Pallas kernels  36.8 us (31%)
  starting transfers between devices  30.5 us (26%)
  between operations  1.21 us (1%)
    pallas_call x28, Pallas kernels, call(): pl.pallas_call(ordered, in_specs=list(specs or [SMEM] + [VMEM] * (count -...  36.8 us
    ppermute x10, waiting for transfers between devices, receive(): got = lax.ppermute(sent, 'heads', perm)  20 us
    ppermute x10, starting transfers between devices, receive(): got = lax.ppermute(sent, 'heads', perm)  17.6 us
    ppermute x16, waiting for transfers between devices, pairs(): return lax.ppermute(array, axis, [(i, i ^ distance) for i in range(count)])  14.2 us
    ppermute x1, waiting for transfers between devices, make_lead_terms(): return lax.ppermute(own[inner + 1], 'heads', [(1, 0), (2, 3)])  13.2 us
    ppermute x16, starting transfers between devices, pairs(): return lax.ppermute(array, axis, [(i, i ^ distance) for i in range(count)])  11.7 us
  transfers between devices with their start and end apart: 27, of which 14 were waited for; matrix products, arithmetic and copies ran while one was open for 0% of the time, Pallas kernels for 24%

profile of v6, /device:TPU:0, one launch (start us, length us, event | category | flops | bytes accessed | tf_op | source)
XLA Modules:
  0.0 116.7 jit_solution(6229621955528398583)
XLA Ops:
  0.7 0.7 copy-done.6
  2.0 3.1 %shard_map.103 = (bf16[2,8,128,128]{3,2,1,0:T(8,128)(2,1)S(1)}, bf16[2,8,128,128]{3,2,1,0:T(8,128)(2,1)S(1)}, bf16[2,8,128,128]{3,2,1,0:T(8,128)(2,1)S(1)}, bf16[8,128,128]{2,1,0:T(8,128)(2,1)S(1)}, f32[8,128]{1,0:T(8,128)S(1)}) custom-call(s32[3]{0:T(128)S(1)} %pad_add_fusion.refs_0_, ...), custom_call_target="tpu_custom_call", output_to_operand_aliasing={{4}: (9, {})} | custom-call | tf_op jit(solution)/shard_map/pallas_call | solution.py:50
  5.1 2.7 %shard_map.104 = (bf16[2,8,128,128]{3,2,1,0:T(8,128)(2,1)S(1)}, bf16[2,8,128,128]{3,2,1,0:T(8,128)(2,1)S(1)}, f32[8,128]{1,0:T(8,128)S(1)}) custom-call(s32[3]{0:T(128)S(1)} %pad_add_fusion.refs_0_, f32[128,128]{1,0:T(8,128)S(1)} %get-tuple-element.87.refs_1_.refs_0_.refs_3_, bf16[128,4096]{1,0:T(8,128)(2,1)} %refs_4_.19, ...), custom_call_target="tpu_custom_call", output_to_operand_aliasing={{2}: (6, {})} | custom-call | tf_op jit(solution)/shard_map/pallas_call | solution.py:50
  8.3 4.5 %collective-permute-start.5 = (bf16[2,8,128,128]{3,2,1,0:T(8,128)(2,1)S(1)}, bf16[2,8,128,128]{3,2,1,0:T(8,128)(2,1)S(1)}, u32[]{:S(2)}, u32[]{:S(2)}) collective-permute-start(bf16[2,8,128,128]{3,2,1,0:T(8,128)(2,1)S(1)} %get-tuple-element.97), channel_id=1, source_target_pairs={{0,1},{3,2},{4,5},{7,6},{8,9},{11,10},{12,13},{15,14},{16,17},{19,... | collective-permute-start | bytes 1572872 | tf_op jit(solution)/shard_map/ppermute | solution.py:485
  13.1 1.0 collective-permute-done.refs_2_.refs_4_.refs_5_
  14.1 0.8 shard_map.105
  14.9 1.6 %collective-permute-start.2 = (bf16[1040,128]{1,0:T(8,128)(2,1)S(1)}, bf16[1040,128]{1,0:T(8,128)(2,1)S(1)}, u32[]{:S(2)}, u32[]{:S(2)}) collective-permute-start(bf16[1040,128]{1,0:T(8,128)(2,1)S(1)} %get-tuple-element.93), channel_id=1, source_target_pairs={{0,8},{8,0},{16,24},{24,16},{1,9},{9,1},{17,25},{25,17},{2,10},{10... | collective-permute-start | bytes 798728 | tf_op jit(solution)/shard_map/ppermute | solution.py:25
  16.5 1.5 %collective-permute-start.4 = (bf16[1040,128]{1,0:T(8,128)(2,1)S(1)}, bf16[1040,128]{1,0:T(8,128)(2,1)S(1)}, u32[]{:S(2)}, u32[]{:S(2)}) collective-permute-start(bf16[1040,128]{1,0:T(8,128)(2,1)S(1)} %get-tuple-element.94), channel_id=1, source_target_pairs={{0,24},{8,16},{16,8},{24,0},{1,25},{9,17},{17,9},{25,1},{2,26},{10... | collective-permute-start | bytes 798728 | tf_op jit(solution)/shard_map/ppermute | solution.py:25
  19.1 1.4 %collective-permute-start.7 = (bf16[2,8,128,128]{3,2,1,0:T(8,128)(2,1)S(1)}, bf16[2,8,128,128]{3,2,1,0:T(8,128)(2,1)S(1)}, u32[]{:S(2)}, u32[]{:S(2)}) collective-permute-start(bf16[2,8,128,128]{3,2,1,0:T(8,128)(2,1)S(1)} %get-tuple-element.107), channel_id=1, source_target_pairs={{0,1},{3,2},{4,5},{7,6},{8,9},{11,10},{12,13},{15,14},{16,17},{19,... | collective-permute-start | bytes 1572872 | tf_op jit(solution)/shard_map/ppermute | solution.py:485
  20.4 4.6 %collective-permute-done.5.refs_3_.refs_5_.refs_7_.refs_9_.refs_13_.refs_17_.refs_21_ = bf16[2,8,128,128]{3,2,1,0:T(8,128)(2,1)S(1)} collective-permute-done((bf16[2,8,128,128]{3,2,1,0:T(8,128)(2,1)S(1)}, bf16[2,8,128,128]{3,2,1,0:T(8,128)(2,1)S(1)}, u32[]{:S(2)}, u32[]{:S(2)}) %collective-permute-start.5) | collective-permute-done | bytes 524320 | tf_op jit(solution)/shard_map/ppermute | solution.py:485
  25.6 0.7 collective-permute-start.10
  26.3 2.0 %shard_map.108 = (f32[4,8,128,128]{3,2,1,0:T(8,128)S(1)}, f32[8,128]{1,0:T(8,128)S(1)}) custom-call(f32[128,128]{1,0:T(8,128)S(1)} %get-tuple-element.87.refs_1_.refs_0_.refs_3_, f32[8,128]{1,0:T(8,128)S(1)} %get-tuple-element.95.refs_1_, bf16[128,4096]{1,0:T(8,128)(2,1)S(1)} %copy-done, ...), custom_call_target="tpu_custom_call", output_to_operand_aliasing={{1}: (6, {})} | custom-call | tf_op jit(solution)/shard_map/pallas_call | solution.py:50
  28.3 2.0 %shard_map.109 = (f32[4,8,128,128]{3,2,1,0:T(8,128)S(1)}, f32[8,128]{1,0:T(8,128)S(1)}) custom-call(f32[128,128]{1,0:T(8,128)S(1)} %get-tuple-element.87.refs_1_.refs_0_.refs_3_, f32[8,128]{1,0:T(8,128)S(1)} %get-tuple-element.95.refs_1_, bf16[128,4096]{1,0:T(8,128)(2,1)S(1)} %copy-done, ...), custom_call_target="tpu_custom_call", output_to_operand_aliasing={{1}: (6, {})} | custom-call | tf_op jit(solution)/shard_map/pallas_call | solution.py:50
  30.3 1.3 %collective-permute-done.3.refs_8_ = bf16[1040,128]{1,0:T(8,128)(2,1)S(1)} collective-permute-done((bf16[1040,128]{1,0:T(8,128)(2,1)S(1)}, bf16[1040,128]{1,0:T(8,128)(2,1)S(1)}, u32[]{:S(2)}, u32[]{:S(2)}) %collective-permute-start.3) | collective-permute-done | bytes 266272 | tf_op jit(solution)/shard_map/ppermute | solution.py:25
  31.6 1.5 %shard_map.110 = (bf16[2,8,128,128]{3,2,1,0:T(8,128)(2,1)S(1)}, bf16[2,8,128,128]{3,2,1,0:T(8,128)(2,1)S(1)}, f32[8,128]{1,0:T(8,128)S(1)}, f32[8,128]{1,0:T(8,128)S(1)}) custom-call(s32[3]{0:T(128)S(1)} %pad_add_fusion.refs_0_, f32[8,128,128]{2,1,0:T(8,128)S(1)} %copy-done.4, f32[8,128,128]{2,1,0:T(8,128)S(1)} %copy-done.5, ...), custom_call_target="tpu_custom_call", output_to_operand_aliasing={{3}: (10, {})} | custom-call | tf_op jit(solution)/shard_map/pallas_call | solution.py:50
  33.2 2.7 %collective-permute-done.7.refs_3_.refs_5_.refs_7_.refs_9_.refs_13_.refs_17_.refs_21_ = bf16[2,8,128,128]{3,2,1,0:T(8,128)(2,1)S(1)} collective-permute-done((bf16[2,8,128,128]{3,2,1,0:T(8,128)(2,1)S(1)}, bf16[2,8,128,128]{3,2,1,0:T(8,128)(2,1)S(1)}, u32[]{:S(2)}, u32[]{:S(2)}) %collective-permute-start.7) | collective-permute-done | bytes 524320 | tf_op jit(solution)/shard_map/ppermute | solution.py:485
  36.4 0.7 collective-permute-start.8
  37.8 6.2 %collective-permute-start.12 = (bf16[2,8,128,128]{3,2,1,0:T(8,128)(2,1)S(1)}, bf16[2,8,128,128]{3,2,1,0:T(8,128)(2,1)S(1)}, u32[]{:S(2)}, u32[]{:S(2)}) collective-permute-start(bf16[2,8,128,128]{3,2,1,0:T(8,128)(2,1)S(1)} %get-tuple-element.117), channel_id=1, source_target_pairs={{0,1},{3,2},{1,0},{2,3},{4,5},{7,6},{5,4},{6,7},{8,9},{11,10},{9,8... | collective-permute-start | bytes 1572872 | tf_op jit(solution)/shard_map/ppermute | solution.py:485
  44.0 1.3 %collective-permute-start.9 = (bf16[8,128,128]{2,1,0:T(8,128)(2,1)S(1)}, bf16[8,128,128]{2,1,0:T(8,128)(2,1)S(1)}, u32[]{:S(2)}, u32[]{:S(2)}) collective-permute-start(bf16[8,128,128]{2,1,0:T(8,128)(2,1)S(1)} %get-tuple-element.110), channel_id=1, source_target_pairs={{1,0},{2,3},{5,4},{6,7},{9,8},{10,11},{13,12},{14,15},{17,16},{18,... | collective-permute-start | bytes 786440 | tf_op jit(solution)/shard_map/ppermute | solution.py:511
  45.3 2.0 %shard_map.113 = (f32[4,8,128,128]{3,2,1,0:T(8,128)S(1)}, f32[8,128]{1,0:T(8,128)S(1)}) custom-call(f32[128,128]{1,0:T(8,128)S(1)} %get-tuple-element.87.refs_1_.refs_0_.refs_3_, f32[8,128]{1,0:T(8,128)S(1)} %get-tuple-element.95.refs_1_, bf16[128,4096]{1,0:T(8,128)(2,1)S(1)} %copy-done, ...), custom_call_target="tpu_custom_call", output_to_operand_aliasing={{1}: (6, {})} | custom-call | tf_op jit(solution)/shard_map/pallas_call | solution.py:50
  47.3 13.2 %collective-permute-done.9.refs_6_.refs_3_ = bf16[8,128,128]{2,1,0:T(8,128)(2,1)S(1)} collective-permute-done((bf16[8,128,128]{2,1,0:T(8,128)(2,1)S(1)}, bf16[8,128,128]{2,1,0:T(8,128)(2,1)S(1)}, u32[]{:S(2)}, u32[]{:S(2)}) %collective-permute-start.9) | collective-permute-done | bytes 262176 | tf_op jit(solution)/shard_map/ppermute | solution.py:511
  60.5 2.0 %shard_map.114 = (f32[4,8,128,128]{3,2,1,0:T(8,128)S(1)}, f32[8,128]{1,0:T(8,128)S(1)}) custom-call(f32[128,128]{1,0:T(8,128)S(1)} %get-tuple-element.87.refs_1_.refs_0_.refs_3_, f32[8,128]{1,0:T(8,128)S(1)} %get-tuple-element.95.refs_1_, bf16[128,4096]{1,0:T(8,128)(2,1)S(1)} %copy-done, ...), custom_call_target="tpu_custom_call", output_to_operand_aliasing={{1}: (7, {})} | custom-call | tf_op jit(solution)/shard_map/pallas_call | solution.py:50
  63.8 0.7 collective-permute-start.15
  64.5 0.7 shard_map.117
  65.3 1.5 %collective-permute-done.13.refs_4_.refs_6_ = bf16[2,4,128,128]{3,2,1,0:T(8,128)(2,1)S(1)} collective-permute-done((bf16[2,4,128,128]{3,2,1,0:T(8,128)(2,1)S(1)}, bf16[2,4,128,128]{3,2,1,0:T(8,128)(2,1)S(1)}, u32[]{:S(2)}, u32[]{:S(2)}) %collective-permute-start.13) | collective-permute-done | bytes 262176 | tf_op jit(solution)/shard_map/ppermute | solution.py:25
  67.5 7.6 %collective-permute-done.11.refs_5_.refs_8_.refs_9_.refs_11_.refs_15_.refs_19_.refs_23_.refs_13_.refs_17_.refs_21_ = bf16[2,8,128,128]{3,2,1,0:T(8,128)(2,1)S(1)} collective-permute-done((bf16[2,8,128,128]{3,2,1,0:T(8,128)(2,1)S(1)}, bf16[2,8,128,128]{3,2,1,0:T(8,128)(2,1)S(1)}, u32[]{:S(2)}, u32[]{:S(2)}) %collective-permute-start.11) | collective-permute-done | bytes 524320 | tf_op jit(solution)/shard_map/ppermute | solution.py:485
  75.7 0.7 collective-permute-start.14
  76.4 1.6 %collective-permute-start.17 = (bf16[528,128]{1,0:T(8,128)(2,1)S(1)}, bf16[528,128]{1,0:T(8,128)(2,1)S(1)}, u32[]{:S(2)}, u32[]{:S(2)}) collective-permute-start(bf16[528,128]{1,0:T(8,128)(2,1)S(1)} %get-tuple-element.130), channel_id=1, source_target_pairs={{0,8},{8,0},{16,24},{24,16},{1,9},{9,1},{17,25},{25,17},{2,10},{10... | collective-permute-start | bytes 405512 | tf_op jit(solution)/shard_map/ppermute | solution.py:25
  77.9 1.5 %collective-permute-start.19 = (bf16[528,128]{1,0:T(8,128)(2,1)S(1)}, bf16[528,128]{1,0:T(8,128)(2,1)S(1)}, u32[]{:S(2)}, u32[]{:S(2)}) collective-permute-start(bf16[528,128]{1,0:T(8,128)(2,1)S(1)} %get-tuple-element.131), channel_id=1, source_target_pairs={{0,24},{8,16},{16,8},{24,0},{1,25},{9,17},{17,9},{25,1},{2,26},{10... | collective-permute-start | bytes 405512 | tf_op jit(solution)/shard_map/ppermute | solution.py:25
  80.5 0.9 shard_map.121
  81.5 2.4 %collective-permute-done.19.refs_9_ = bf16[528,128]{1,0:T(8,128)(2,1)S(1)} collective-permute-done((bf16[528,128]{1,0:T(8,128)(2,1)S(1)}, bf16[528,128]{1,0:T(8,128)(2,1)S(1)}, u32[]{:S(2)}, u32[]{:S(2)}) %collective-permute-start.19) | collective-permute-done | bytes 135200 | tf_op jit(solution)/shard_map/ppermute | solution.py:25
  83.9 1.4 %collective-permute-done.18.refs_8_ = bf16[528,128]{1,0:T(8,128)(2,1)S(1)} collective-permute-done((bf16[528,128]{1,0:T(8,128)(2,1)S(1)}, bf16[528,128]{1,0:T(8,128)(2,1)S(1)}, u32[]{:S(2)}, u32[]{:S(2)}) %collective-permute-start.18) | collective-permute-done | bytes 135200 | tf_op jit(solution)/shard_map/ppermute | solution.py:25
  85.3 1.3 %shard_map.122 = (bf16[2,4,128,128]{3,2,1,0:T(8,128)(2,1)S(1)}, bf16[2,4,128,128]{3,2,1,0:T(8,128)(2,1)S(1)}, f32[8,128]{1,0:T(8,128)}, f32[8,128]{1,0:T(8,128)S(1)}) custom-call(s32[3]{0:T(128)S(1)} %pad_add_fusion.refs_0_, f32[8,128,128]{2,1,0:T(8,128)S(1)} %copy-done.4, f32[8,128,128]{2,1,0:T(8,128)S(1)} %copy-done.5, ...), custom_call_target="tpu_custom_call", output_to_operand_aliasing={{3}: (10, {})} | custom-call | tf_op jit(solution)/shard_map/pallas_call | solution.py:50
  86.6 1.3 %collective-permute-start.21 = (bf16[2,8,128,128]{3,2,1,0:T(8,128)(2,1)S(1)}, bf16[2,8,128,128]{3,2,1,0:T(8,128)(2,1)S(1)}, u32[]{:S(2)}, u32[]{:S(2)}) collective-permute-start(bf16[2,8,128,128]{3,2,1,0:T(8,128)(2,1)S(1)} %get-tuple-element.138), channel_id=1, source_target_pairs={{1,0},{2,3},{5,4},{6,7},{9,8},{10,11},{13,12},{14,15},{17,16},{18,... | collective-permute-start | bytes 1572872 | tf_op jit(solution)/shard_map/ppermute | solution.py:485
  87.9 0.7 shard_map.123
  89.2 1.3 %collective-permute-start.20 = (bf16[2,8,128,128]{3,2,1,0:T(8,128)(2,1)S(1)}, bf16[2,8,128,128]{3,2,1,0:T(8,128)(2,1)S(1)}, u32[]{:S(2)}, u32[]{:S(2)}) collective-permute-start(bf16[2,8,128,128]{3,2,1,0:T(8,128)(2,1)S(1)} %get-tuple-element.135), channel_id=1, source_target_pairs={{1,0},{2,3},{5,4},{6,7},{9,8},{10,11},{13,12},{14,15},{17,16},{18,... | collective-permute-start | bytes 1572872 | tf_op jit(solution)/shard_map/ppermute | solution.py:485
  90.5 1.6 %collective-permute-start.22 = (bf16[528,128]{1,0:T(8,128)(2,1)S(1)}, bf16[528,128]{1,0:T(8,128)(2,1)S(1)}, u32[]{:S(2)}, u32[]{:S(2)}) collective-permute-start(bf16[528,128]{1,0:T(8,128)(2,1)S(1)} %get-tuple-element.141), channel_id=1, source_target_pairs={{0,8},{8,0},{16,24},{24,16},{1,9},{9,1},{17,25},{25,17},{2,10},{10... | collective-permute-start | bytes 405512 | tf_op jit(solution)/shard_map/ppermute | solution.py:25
  92.0 1.1 collective-permute-start.24
  93.1 0.9 collective-permute-start.23
  94.0 2.2 %shard_map.125 = (bf16[128,4096]{1,0:T(8,128)(2,1)}, bf16[128,4096]{1,0:T(8,128)(2,1)}, bf16[128,4096]{1,0:T(8,128)(2,1)}, bf16[128,4096]{1,0:T(8,128)(2,1)}, f32[8,128]{1,0:T(8,128)S(1)}) custom-call(s32[3]{0:T(128)S(1)} %pad_add_fusion.refs_0_, f32[8,128]{1,0:T(8,128)S(1)} %get-tuple-element.86.refs_2_.refs_1_.refs_3_.refs_4_, ...), custom_call_target="tpu_custom_call", output_to_operand_aliasing={{4}: (28, {})} | custom-call | tf_op jit(solution)/shard_map/pallas_call | solution.py:50
  96.9 3.1 %collective-permute-done.24.refs_10_ = bf16[528,128]{1,0:T(8,128)(2,1)S(1)} collective-permute-done((bf16[528,128]{1,0:T(8,128)(2,1)S(1)}, bf16[528,128]{1,0:T(8,128)(2,1)S(1)}, u32[]{:S(2)}, u32[]{:S(2)}) %collective-permute-start.24) | collective-permute-done | bytes 135200 | tf_op jit(solution)/shard_map/ppermute | solution.py:25
  100.1 1.4 %collective-permute-done.23.refs_9_ = bf16[528,128]{1,0:T(8,128)(2,1)S(1)} collective-permute-done((bf16[528,128]{1,0:T(8,128)(2,1)S(1)}, bf16[528,128]{1,0:T(8,128)(2,1)S(1)}, u32[]{:S(2)}, u32[]{:S(2)}) %collective-permute-start.23) | collective-permute-done | bytes 135200 | tf_op jit(solution)/shard_map/ppermute | solution.py:25
  101.4 1.6 %shard_map.126 = (bf16[2,4,128,128]{3,2,1,0:T(8,128)(2,1)S(1)}, bf16[2,4,128,128]{3,2,1,0:T(8,128)(2,1)S(1)}, f32[8,128]{1,0:T(8,128)}, f32[8,128]{1,0:T(8,128)S(1)}) custom-call(s32[3]{0:T(128)S(1)} %pad_add_fusion.refs_0_, f32[8,128,128]{2,1,0:T(8,128)S(1)} %copy-done.4, f32[8,128,128]{2,1,0:T(8,128)S(1)} %copy-done.5, ...), custom_call_target="tpu_custom_call", output_to_operand_aliasing={{3}: (11, {})} | custom-call | tf_op jit(solution)/shard_map/pallas_call | solution.py:50
  103.0 1.5 %collective-permute-done.26.refs_12_.refs_20_ = bf16[2,4,128,128]{3,2,1,0:T(8,128)(2,1)S(1)} collective-permute-done((bf16[2,4,128,128]{3,2,1,0:T(8,128)(2,1)S(1)}, bf16[2,4,128,128]{3,2,1,0:T(8,128)(2,1)S(1)}, u32[]{:S(2)}, u32[]{:S(2)}) %collective-permute-start.26) | collective-permute-done | bytes 262176 | tf_op jit(solution)/shard_map/ppermute | solution.py:25
  104.6 2.2 %shard_map.127 = (bf16[128,4096]{1,0:T(8,128)(2,1)}, bf16[128,4096]{1,0:T(8,128)(2,1)}, bf16[128,4096]{1,0:T(8,128)(2,1)}, bf16[128,4096]{1,0:T(8,128)(2,1)}, f32[8,128]{1,0:T(8,128)S(1)}) custom-call(s32[3]{0:T(128)S(1)} %pad_add_fusion.refs_0_, ...), custom_call_target="tpu_custom_call", output_to_operand_aliasing={{0}: (28, {}), {1}: (29, {}), {2}: (30, {}), {3}: (31, {}),... | custom-call | tf_op jit(solution)/shard_map/pallas_call | solution.py:50
  106.8 2.3 %shard_map.128 = (bf16[128,4096]{1,0:T(8,128)(2,1)}, bf16[128,4096]{1,0:T(8,128)(2,1)}, bf16[128,4096]{1,0:T(8,128)(2,1)}, bf16[128,4096]{1,0:T(8,128)(2,1)}, f32[8,128]{1,0:T(8,128)S(1)}) custom-call(s32[3]{0:T(128)S(1)} %pad_add_fusion.refs_0_, ...), custom_call_target="tpu_custom_call", output_to_operand_aliasing={{0}: (28, {}), {1}: (29, {}), {2}: (30, {}), {3}: (31, {}),... | custom-call | tf_op jit(solution)/shard_map/pallas_call | solution.py:50
  109.2 5.1 %collective-permute-done.20.refs_11_.refs_15_.refs_19_.refs_23_ = bf16[2,8,128,128]{3,2,1,0:T(8,128)(2,1)S(1)} collective-permute-done((bf16[2,8,128,128]{3,2,1,0:T(8,128)(2,1)S(1)}, bf16[2,8,128,128]{3,2,1,0:T(8,128)(2,1)S(1)}, u32[]{:S(2)}, u32[]{:S(2)}) %collective-permute-start.20) | collective-permute-done | bytes 524320 | tf_op jit(solution)/shard_map/ppermute | solution.py:485
  114.3 2.3 %shard_map.129 = (bf16[128,4096]{1,0:T(8,128)(2,1)}, bf16[128,4096]{1,0:T(8,128)(2,1)}, bf16[128,4096]{1,0:T(8,128)(2,1)}, bf16[128,4096]{1,0:T(8,128)(2,1)}, f32[8,128]{1,0:T(8,128)S(1)}) custom-call(s32[3]{0:T(128)S(1)} %pad_add_fusion.refs_0_, ...), custom_call_target="tpu_custom_call", output_to_operand_aliasing={{0}: (28, {}), {1}: (29, {}), {2}: (30, {}), {3}: (31, {}),... | custom-call | tf_op jit(solution)/shard_map/pallas_call | solution.py:50
  (50 shorter events, 9.4 us)
Async XLA Ops:
  0.7 0.7 copy-start.6
  7.8 6.3 %collective-permute-start.1 = (bf16[2,8,128,128]{3,2,1,0:T(8,128)(2,1)S(1)}, bf16[2,8,128,128]{3,2,1,0:T(8,128)(2,1)S(1)}, u32[]{:S(2)}, u32[]{:S(2)}) collective-permute-start(bf16[2,8,128,128]{3,2,1,0:T(8,128)(2,1)S(1)} %get-tuple-element.91.refs_5_.refs_6_), channel_id=1, source_target_pairs={{0,4},{4,0},{1,5},{5,1},{2,6},{6,2},{3,7},{7,3},{8,12},{12,8},{9,1... | collective-permute-start | bytes 1572872 | tf_op jit(solution)/shard_map/ppermute | solution.py:25
  8.3 16.7 %collective-permute-start.5 = (bf16[2,8,128,128]{3,2,1,0:T(8,128)(2,1)S(1)}, bf16[2,8,128,128]{3,2,1,0:T(8,128)(2,1)S(1)}, u32[]{:S(2)}, u32[]{:S(2)}) collective-permute-start(bf16[2,8,128,128]{3,2,1,0:T(8,128)(2,1)S(1)} %get-tuple-element.97), channel_id=1, source_target_pairs={{0,1},{3,2},{4,5},{7,6},{8,9},{11,10},{12,13},{15,14},{16,17},{19,... | collective-permute-start | bytes 1572872 | tf_op jit(solution)/shard_map/ppermute | solution.py:485
  12.8 1.2 %collective-permute-start = (f32[8,128]{1,0:T(8,128)S(1)}, f32[8,128]{1,0:T(8,128)S(1)}, u32[]{:S(2)}, u32[]{:S(2)}) collective-permute-start(f32[8,128]{1,0:T(8,128)S(1)} %get-tuple-element.86.refs_2_.refs_1_.refs_3_.refs_4_), channel_id=1, source_target_pairs={{0,4},{4,0},{1,5},{5,1},{2,6},{6,2},{3,7},{7,3},{8,12},{12,8},{9,1... | collective-permute-start | bytes 12296 | tf_op jit(solution)/shard_map/ppermute | solution.py:25
  14.1 12.2 %copy-start = (bf16[128,4096]{1,0:T(8,128)(2,1)S(1)}, bf16[128,4096]{1,0:T(8,128)(2,1)}, u32[]{:S(2)}) copy-start(bf16[128,4096]{1,0:T(8,128)(2,1)} %refs_4_.19) | copy-start | bytes 3145732
  14.1 12.2 %copy-start.1 = (bf16[128,4096]{1,0:T(8,128)(2,1)S(1)}, bf16[128,4096]{1,0:T(8,128)(2,1)}, u32[]{:S(2)}) copy-start(bf16[128,4096]{1,0:T(8,128)(2,1)} %refs_5_.19) | copy-start | bytes 3145732
  14.1 12.2 %copy-start.2 = (bf16[128,4096]{1,0:T(8,128)(2,1)S(1)}, bf16[128,4096]{1,0:T(8,128)(2,1)}, u32[]{:S(2)}) copy-start(bf16[128,4096]{1,0:T(8,128)(2,1)} %refs_6_.9) | copy-start | bytes 3145732
  14.1 12.2 %copy-start.3 = (bf16[128,4096]{1,0:T(8,128)(2,1)S(1)}, bf16[128,4096]{1,0:T(8,128)(2,1)}, u32[]{:S(2)}) copy-start(bf16[128,4096]{1,0:T(8,128)(2,1)} %refs_7_.9) | copy-start | bytes 3145732
  14.9 15.4 %collective-permute-start.2 = (bf16[1040,128]{1,0:T(8,128)(2,1)S(1)}, bf16[1040,128]{1,0:T(8,128)(2,1)S(1)}, u32[]{:S(2)}, u32[]{:S(2)}) collective-permute-start(bf16[1040,128]{1,0:T(8,128)(2,1)S(1)} %get-tuple-element.93), channel_id=1, source_target_pairs={{0,8},{8,0},{16,24},{24,16},{1,9},{9,1},{17,25},{25,17},{2,10},{10... | collective-permute-start | bytes 798728 | tf_op jit(solution)/shard_map/ppermute | solution.py:25
  16.5 13.9 %collective-permute-start.4 = (bf16[1040,128]{1,0:T(8,128)(2,1)S(1)}, bf16[1040,128]{1,0:T(8,128)(2,1)S(1)}, u32[]{:S(2)}, u32[]{:S(2)}) collective-permute-start(bf16[1040,128]{1,0:T(8,128)(2,1)S(1)} %get-tuple-element.94), channel_id=1, source_target_pairs={{0,24},{8,16},{16,8},{24,0},{1,25},{9,17},{17,9},{25,1},{2,26},{10... | collective-permute-start | bytes 798728 | tf_op jit(solution)/shard_map/ppermute | solution.py:25
  17.9 13.6 %collective-permute-start.3 = (bf16[1040,128]{1,0:T(8,128)(2,1)S(1)}, bf16[1040,128]{1,0:T(8,128)(2,1)S(1)}, u32[]{:S(2)}, u32[]{:S(2)}) collective-permute-start(bf16[1040,128]{1,0:T(8,128)(2,1)S(1)} %get-tuple-element.94), channel_id=1, source_target_pairs={{0,16},{8,24},{16,0},{24,8},{1,17},{9,25},{17,1},{25,9},{2,18},{10... | collective-permute-start | bytes 798728 | tf_op jit(solution)/shard_map/ppermute | solution.py:25
  19.1 16.8 %collective-permute-start.7 = (bf16[2,8,128,128]{3,2,1,0:T(8,128)(2,1)S(1)}, bf16[2,8,128,128]{3,2,1,0:T(8,128)(2,1)S(1)}, u32[]{:S(2)}, u32[]{:S(2)}) collective-permute-start(bf16[2,8,128,128]{3,2,1,0:T(8,128)(2,1)S(1)} %get-tuple-element.107), channel_id=1, source_target_pairs={{0,1},{3,2},{4,5},{7,6},{8,9},{11,10},{12,13},{15,14},{16,17},{19,... | collective-permute-start | bytes 1572872 | tf_op jit(solution)/shard_map/ppermute | solution.py:485
  25.6 11.5 %collective-permute-start.10 = (bf16[2,8,128,128]{3,2,1,0:T(8,128)(2,1)S(1)}, bf16[2,8,128,128]{3,2,1,0:T(8,128)(2,1)S(1)}, u32[]{:S(2)}, u32[]{:S(2)}) collective-permute-start(bf16[2,8,128,128]{3,2,1,0:T(8,128)(2,1)S(1)} %get-tuple-element.111), channel_id=1, source_target_pairs={{1,2},{2,1},{5,6},{6,5},{9,10},{10,9},{13,14},{14,13},{17,18},{18,... | collective-permute-start | bytes 1572872 | tf_op jit(solution)/shard_map/ppermute | solution.py:485
  28.3 3.3 %copy-start.4 = (f32[8,128,128]{2,1,0:T(8,128)S(1)}, f32[8,128,128]{2,1,0:T(8,128)}, u32[]{:S(2)}) copy-start(f32[8,128,128]{2,1,0:T(8,128)} %refs_1_.5) | copy-start | bytes 1572868
  28.3 3.3 %copy-start.5 = (f32[8,128,128]{2,1,0:T(8,128)S(1)}, f32[8,128,128]{2,1,0:T(8,128)}, u32[]{:S(2)}) copy-start(f32[8,128,128]{2,1,0:T(8,128)} %refs_2_.15) | copy-start | bytes 1572868
  33.1 4.0 %collective-permute-start.6 = (bf16[2,8,128,128]{3,2,1,0:T(8,128)(2,1)S(1)}, bf16[2,8,128,128]{3,2,1,0:T(8,128)(2,1)S(1)}, u32[]{:S(2)}, u32[]{:S(2)}) collective-permute-start(bf16[2,8,128,128]{3,2,1,0:T(8,128)(2,1)S(1)} %get-tuple-element.106), channel_id=1, source_target_pairs={{0,4},{4,0},{1,5},{5,1},{2,6},{6,2},{3,7},{7,3},{8,12},{12,8},{9,1... | collective-permute-start | bytes 1572872 | tf_op jit(solution)/shard_map/ppermute | solution.py:25
  36.4 26.0 %collective-permute-start.8 = (bf16[2,8,128,128]{3,2,1,0:T(8,128)(2,1)S(1)}, bf16[2,8,128,128]{3,2,1,0:T(8,128)(2,1)S(1)}, u32[]{:S(2)}, u32[]{:S(2)}) collective-permute-start(bf16[2,8,128,128]{3,2,1,0:T(8,128)(2,1)S(1)} %get-tuple-element.109), channel_id=1, source_target_pairs={{1,2},{2,1},{5,6},{6,5},{9,10},{10,9},{13,14},{14,13},{17,18},{18,... | collective-permute-start | bytes 1572872 | tf_op jit(solution)/shard_map/ppermute | solution.py:485
  37.8 25.4 %collective-permute-start.12 = (bf16[2,8,128,128]{3,2,1,0:T(8,128)(2,1)S(1)}, bf16[2,8,128,128]{3,2,1,0:T(8,128)(2,1)S(1)}, u32[]{:S(2)}, u32[]{:S(2)}) collective-permute-start(bf16[2,8,128,128]{3,2,1,0:T(8,128)(2,1)S(1)} %get-tuple-element.117), channel_id=1, source_target_pairs={{0,1},{3,2},{1,0},{2,3},{4,5},{7,6},{5,4},{6,7},{8,9},{11,10},{9,8... | collective-permute-start | bytes 1572872 | tf_op jit(solution)/shard_map/ppermute | solution.py:485
  44.0 16.5 %collective-permute-start.9 = (bf16[8,128,128]{2,1,0:T(8,128)(2,1)S(1)}, bf16[8,128,128]{2,1,0:T(8,128)(2,1)S(1)}, u32[]{:S(2)}, u32[]{:S(2)}) collective-permute-start(bf16[8,128,128]{2,1,0:T(8,128)(2,1)S(1)} %get-tuple-element.110), channel_id=1, source_target_pairs={{1,0},{2,3},{5,4},{6,7},{9,8},{10,11},{13,12},{14,15},{17,16},{18,... | collective-permute-start | bytes 786440 | tf_op jit(solution)/shard_map/ppermute | solution.py:511
  63.1 12.0 %collective-permute-start.11 = (bf16[2,8,128,128]{3,2,1,0:T(8,128)(2,1)S(1)}, bf16[2,8,128,128]{3,2,1,0:T(8,128)(2,1)S(1)}, u32[]{:S(2)}, u32[]{:S(2)}) collective-permute-start(bf16[2,8,128,128]{3,2,1,0:T(8,128)(2,1)S(1)} %get-tuple-element.116), channel_id=1, source_target_pairs={{0,1},{3,2},{1,0},{2,3},{4,5},{7,6},{5,4},{6,7},{8,9},{11,10},{9,8... | collective-permute-start | bytes 1572872 | tf_op jit(solution)/shard_map/ppermute | solution.py:485
  63.8 16.2 %collective-permute-start.15 = (bf16[2,8,128,128]{3,2,1,0:T(8,128)(2,1)S(1)}, bf16[2,8,128,128]{3,2,1,0:T(8,128)(2,1)S(1)}, u32[]{:S(2)}, u32[]{:S(2)}) collective-permute-start(bf16[2,8,128,128]{3,2,1,0:T(8,128)(2,1)S(1)} %get-tuple-element.125), channel_id=1, source_target_pairs={{1,2},{2,1},{5,6},{6,5},{9,10},{10,9},{13,14},{14,13},{17,18},{18,... | collective-permute-start | bytes 1572872 | tf_op jit(solution)/shard_map/ppermute | solution.py:485
  65.2 1.6 %collective-permute-start.13 = (bf16[2,4,128,128]{3,2,1,0:T(8,128)(2,1)S(1)}, bf16[2,4,128,128]{3,2,1,0:T(8,128)(2,1)S(1)}, u32[]{:S(2)}, u32[]{:S(2)}) collective-permute-start(bf16[2,4,128,128]{3,2,1,0:T(8,128)(2,1)S(1)} %get-tuple-element.121), channel_id=1, source_target_pairs={{0,4},{4,0},{1,5},{5,1},{2,6},{6,2},{3,7},{7,3},{8,12},{12,8},{9,1... | collective-permute-start | bytes 786440 | tf_op jit(solution)/shard_map/ppermute | solution.py:25
  75.7 12.9 %collective-permute-start.14 = (bf16[2,8,128,128]{3,2,1,0:T(8,128)(2,1)S(1)}, bf16[2,8,128,128]{3,2,1,0:T(8,128)(2,1)S(1)}, u32[]{:S(2)}, u32[]{:S(2)}) collective-permute-start(bf16[2,8,128,128]{3,2,1,0:T(8,128)(2,1)S(1)} %get-tuple-element.124), channel_id=1, source_target_pairs={{1,2},{2,1},{5,6},{6,5},{9,10},{10,9},{13,14},{14,13},{17,18},{18,... | collective-permute-start | bytes 1572872 | tf_op jit(solution)/shard_map/ppermute | solution.py:485
  76.4 5.1 %collective-permute-start.17 = (bf16[528,128]{1,0:T(8,128)(2,1)S(1)}, bf16[528,128]{1,0:T(8,128)(2,1)S(1)}, u32[]{:S(2)}, u32[]{:S(2)}) collective-permute-start(bf16[528,128]{1,0:T(8,128)(2,1)S(1)} %get-tuple-element.130), channel_id=1, source_target_pairs={{0,8},{8,0},{16,24},{24,16},{1,9},{9,1},{17,25},{25,17},{2,10},{10... | collective-permute-start | bytes 405512 | tf_op jit(solution)/shard_map/ppermute | solution.py:25
  77.9 6.0 %collective-permute-start.19 = (bf16[528,128]{1,0:T(8,128)(2,1)S(1)}, bf16[528,128]{1,0:T(8,128)(2,1)S(1)}, u32[]{:S(2)}, u32[]{:S(2)}) collective-permute-start(bf16[528,128]{1,0:T(8,128)(2,1)S(1)} %get-tuple-element.131), channel_id=1, source_target_pairs={{0,24},{8,16},{16,8},{24,0},{1,25},{9,17},{17,9},{25,1},{2,26},{10... | collective-permute-start | bytes 405512 | tf_op jit(solution)/shard_map/ppermute | solution.py:25
  79.4 5.9 %collective-permute-start.18 = (bf16[528,128]{1,0:T(8,128)(2,1)S(1)}, bf16[528,128]{1,0:T(8,128)(2,1)S(1)}, u32[]{:S(2)}, u32[]{:S(2)}) collective-permute-start(bf16[528,128]{1,0:T(8,128)(2,1)S(1)} %get-tuple-element.131), channel_id=1, source_target_pairs={{0,16},{8,24},{16,0},{24,8},{1,17},{9,25},{17,1},{25,9},{2,18},{10... | collective-permute-start | bytes 405512 | tf_op jit(solution)/shard_map/ppermute | solution.py:25
  81.4 6.5 %collective-permute-start.16 = (bf16[2,4,128,128]{3,2,1,0:T(8,128)(2,1)S(1)}, bf16[2,4,128,128]{3,2,1,0:T(8,128)(2,1)S(1)}, u32[]{:S(2)}, u32[]{:S(2)}) collective-permute-start(bf16[2,4,128,128]{3,2,1,0:T(8,128)(2,1)S(1)} %get-tuple-element.129), channel_id=1, source_target_pairs={{0,4},{4,0},{1,5},{5,1},{2,6},{6,2},{3,7},{7,3},{8,12},{12,8},{9,1... | collective-permute-start | bytes 786440 | tf_op jit(solution)/shard_map/ppermute | solution.py:25
  86.6 6.5 %collective-permute-start.25 = (bf16[2,4,128,128]{3,2,1,0:T(8,128)(2,1)S(1)}, bf16[2,4,128,128]{3,2,1,0:T(8,128)(2,1)S(1)}, u32[]{:S(2)}, u32[]{:S(2)}) collective-permute-start(bf16[2,4,128,128]{3,2,1,0:T(8,128)(2,1)S(1)} %get-tuple-element.144), channel_id=1, source_target_pairs={{0,4},{4,0},{1,5},{5,1},{2,6},{6,2},{3,7},{7,3},{8,12},{12,8},{9,1... | collective-permute-start | bytes 786440 | tf_op jit(solution)/shard_map/ppermute | solution.py:25
  86.6 20.2 %collective-permute-start.21 = (bf16[2,8,128,128]{3,2,1,0:T(8,128)(2,1)S(1)}, bf16[2,8,128,128]{3,2,1,0:T(8,128)(2,1)S(1)}, u32[]{:S(2)}, u32[]{:S(2)}) collective-permute-start(bf16[2,8,128,128]{3,2,1,0:T(8,128)(2,1)S(1)} %get-tuple-element.138), channel_id=1, source_target_pairs={{1,0},{2,3},{5,4},{6,7},{9,8},{10,11},{13,12},{14,15},{17,16},{18,... | collective-permute-start | bytes 1572872 | tf_op jit(solution)/shard_map/ppermute | solution.py:485
  89.2 25.1 %collective-permute-start.20 = (bf16[2,8,128,128]{3,2,1,0:T(8,128)(2,1)S(1)}, bf16[2,8,128,128]{3,2,1,0:T(8,128)(2,1)S(1)}, u32[]{:S(2)}, u32[]{:S(2)}) collective-permute-start(bf16[2,8,128,128]{3,2,1,0:T(8,128)(2,1)S(1)} %get-tuple-element.135), channel_id=1, source_target_pairs={{1,0},{2,3},{5,4},{6,7},{9,8},{10,11},{13,12},{14,15},{17,16},{18,... | collective-permute-start | bytes 1572872 | tf_op jit(solution)/shard_map/ppermute | solution.py:485
  90.5 6.4 %collective-permute-start.22 = (bf16[528,128]{1,0:T(8,128)(2,1)S(1)}, bf16[528,128]{1,0:T(8,128)(2,1)S(1)}, u32[]{:S(2)}, u32[]{:S(2)}) collective-permute-start(bf16[528,128]{1,0:T(8,128)(2,1)S(1)} %get-tuple-element.141), channel_id=1, source_target_pairs={{0,8},{8,0},{16,24},{24,16},{1,9},{9,1},{17,25},{25,17},{2,10},{10... | collective-permute-start | bytes 405512 | tf_op jit(solution)/shard_map/ppermute | solution.py:25
  92.0 8.0 %collective-permute-start.24 = (bf16[528,128]{1,0:T(8,128)(2,1)S(1)}, bf16[528,128]{1,0:T(8,128)(2,1)S(1)}, u32[]{:S(2)}, u32[]{:S(2)}) collective-permute-start(bf16[528,128]{1,0:T(8,128)(2,1)S(1)} %get-tuple-element.142), channel_id=1, source_target_pairs={{0,24},{8,16},{16,8},{24,0},{1,25},{9,17},{17,9},{25,1},{2,26},{10... | collective-permute-start | bytes 405512 | tf_op jit(solution)/shard_map/ppermute | solution.py:25
  93.1 8.3 %collective-permute-start.23 = (bf16[528,128]{1,0:T(8,128)(2,1)S(1)}, bf16[528,128]{1,0:T(8,128)(2,1)S(1)}, u32[]{:S(2)}, u32[]{:S(2)}) collective-permute-start(bf16[528,128]{1,0:T(8,128)(2,1)S(1)} %get-tuple-element.142), channel_id=1, source_target_pairs={{0,16},{8,24},{16,0},{24,8},{1,17},{9,25},{17,1},{25,9},{2,18},{10... | collective-permute-start | bytes 405512 | tf_op jit(solution)/shard_map/ppermute | solution.py:25
  103.0 1.5 %collective-permute-start.26 = (bf16[2,4,128,128]{3,2,1,0:T(8,128)(2,1)S(1)}, bf16[2,4,128,128]{3,2,1,0:T(8,128)(2,1)S(1)}, u32[]{:S(2)}, u32[]{:S(2)}) collective-permute-start(bf16[2,4,128,128]{3,2,1,0:T(8,128)(2,1)S(1)} %get-tuple-element.148), channel_id=1, source_target_pairs={{0,4},{4,0},{1,5},{5,1},{2,6},{6,2},{3,7},{7,3},{8,12},{12,8},{9,1... | collective-permute-start | bytes 786440 | tf_op jit(solution)/shard_map/ppermute | solution.py:25

commit v7 on v6

--- a/solution.py
+++ b/solution.py
@@ -17,7 +17,16 @@
 SMEM = pl.BlockSpec(memory_space=pltpu.SMEM)
 HBM = pl.BlockSpec(memory_space=pltpu.HBM)
 LIMIT = 24 * 1024 * 1024
-COSTS = ()
+COSTS = (0, 0, 0, 0, 0, 0, 16, 0, 0, 0, 0, 0, 0, 0, 0, 0, 0, 8, 0, 0, 0, 0, 0, 0, 0, 0, 0, 0)
+ORDER = (
+    "K1 K0 L3 A0"
+    " E1 O0 B0 L0"
+    " O1 J2 L1 L2"
+    " J3 T0 O2 S0"
+    " O3 T1 F2 P0"
+    " S1 F3 W0 W2"
+    " P1 W1 W3"
+)
 
 
 def pairs(array, axis, distance):
@@ -41,22 +50,22 @@
     return jnp.where(row, 1.0, 0.0).astype(F32)
 
 
-def call(token, kernel, operands, out_shape, cost=0, scratch=(), aliases=None, specs=None, out_specs=None, after=()):
-    count, results, behind = len(operands), len(out_shape), len(operands) + len(after)
+def call(token, kernel, operands, out_shape, cost=0, scratch=(), aliases=None, specs=None, out_specs=None):
+    count, results = len(operands), len(out_shape)
 
     def ordered(*refs):
-        kernel(*refs[:count], *refs[behind + 1 : behind + 1 + results], *refs[behind + 2 + results :])
+        kernel(*refs[:count], *refs[count + 1 : count + 1 + results], *refs[count + 2 + results :])
 
     *outs, token = pl.pallas_call(
         ordered,
-        in_specs=list(specs or [SMEM] + [VMEM] * (count - 1)) + [VMEM] * (len(after) + 1),
+        in_specs=list(specs or [SMEM] + [VMEM] * (count - 1)) + [VMEM],
         out_specs=list(out_specs or [VMEM] * results) + [VMEM],
         out_shape=list(out_shape) + [jax.ShapeDtypeStruct(token.shape, token.dtype)],
         scratch_shapes=list(scratch),
-        input_output_aliases={**(aliases or {}), behind: results},
+        input_output_aliases={**(aliases or {}), count: results},
         compiler_params=pltpu.CompilerParams(vmem_limit_bytes=LIMIT),
         cost_estimate=pl.CostEstimate(flops=int(cost * 1e9), bytes_accessed=0, transcendentals=0),
-    )(*operands, *after, token)
+    )(*operands, token)
     return token, outs
 
 
@@ -132,7 +141,7 @@
     factor, unit, part, places, mates, outer, inner, ids, docs_ref, labels, q_hbm, k_hbm, v_hbm, g_hbm, carry_hbm, cot_hbm,
     *refs,
 ):
-    outs, (sent, carried), (q_ref, k_ref, v_ref, g_ref, carry_ref, cot_ref, sems) = refs[:inner], refs[inner : inner + 2], refs[inner + 2 :]
+    outs, sent, (q_ref, k_ref, v_ref, g_ref, carry_ref, cot_ref, sems) = refs[:inner], refs[inner], refs[inner + 1 :]
     o, c, z = ids[0], ids[1], ids[2]
     waiting = [fetch([(carry_hbm, carry_ref), (cot_hbm, cot_ref)], sems.at[len(places)])]
     for s, (g, mate) in enumerate(zip(places, mates)):
@@ -171,7 +180,7 @@
     @pl.when(jnp.logical_not(at_end))
     def _():
         for i in range(unit):
-            carried[i] = jnp.where(side == 0, carry_ref[i], cot_ref[i] * factor).astype(BF16)
+            sent[0, i] = jnp.where(side == 0, carry_ref[i], cot_ref[i] * factor).astype(BF16)
 
 
 def block_rows(labels, z, grouped):
@@ -258,7 +267,7 @@
                 carried(mate * unit + c * part + i, cot_ref) * factor,
             ]
             if lacking:
-                more = lacked[c * part + i].astype(F32)
+                more = lacked[0, c * part + i].astype(F32)
                 carries[0] = carries[0] + jnp.where(z == 0, more, 0.0)
                 carries[1] = carries[1] + jnp.where(z == DEPTH - 1, more, 0.0)
 
@@ -501,14 +510,13 @@
                 lead_terms, factor, unit, part, places, tuple(mate(g) for g in places), outer, inner
             ),
             (ids, docs_column, own_labels) + far_arrays + far_carries,
-            [state_pair(part * leads)] * inner + [state_pair(part * inner), jax.ShapeDtypeStruct((unit, DH, DH), BF16)],
+            [state_pair(part * leads)] * inner + [state_pair(unit)],
             scratch=[block] * 4 + [carry] * 2 + [pltpu.SemaphoreType.DMA((leads + 1, 4))],
             specs=[SMEM, VMEM, VMEM] + [HBM] * 6,
         )
         for g in places:
             terms[g] = [(a, g * part) for a in own[:inner]]
-        receive([(0, t) for t in range(inner)], near, own[inner], [(0, 1), (3, 2)])
-        return lax.ppermute(own[inner + 1], "heads", [(1, 0), (2, 3)])
+        return receive([(0, t) for t in range(inner)], near, own[inner], [(0, 1), (3, 2), (1, 0), (2, 3)])
 
     def make_terms(places):
         own = run(
@@ -586,13 +594,12 @@
     def across(units):
         receive(units, middle, move([], units, True), [(1, 2), (2, 1)])
 
-    def make_local(g, after=()):
+    def make_local(g):
         out = run(
             functools.partial(local_kernel, factor, g * unit, unit),
             (docs_column, docs_row) + arrays,
             [jax.ShapeDtypeStruct((4, unit, SPAN, DH), F32)],
             specs=[VMEM] * 6,
-            after=after,
         )
         local[g] = out[0]
 
@@ -638,40 +645,46 @@
         )
         return exchange(totals)
 
-    def chunk(g):
-        return [(g, t) for t in range(inner)]
-
-    def halves_of(g):
-        return [(which, g, t) for which in range(2) for t in range(inner)]
+    def chunk(n):
+        return [(n, t) for t in range(inner)] if n < leads else [(g, n - leads) for g in range(leads, groups)]
+
+    def halves_of(n):
+        return [(which, g, t) for which in range(2) for g, t in chunk(n)]
 
     if leads:
-        lacked = make_lead_terms()
-        got_rest = make_terms((2, 3))
-        fans_rest = make_sums(got_rest, False)
-        ends(chunk(1), [])
-        across(chunk(0))
-        make_local(0)
-        make_local(1)
-        make_prefixes((2, 3), got_rest, fans_rest, False)
-        across(chunk(1))
-        ends(chunk(2), chunk(0))
-        make_local(2)
-        make_local(3, after=[lacked])
-        ends(chunk(3), chunk(1))
-        across(chunk(2))
-        got_first = make_totals(0)
-        fans_first = make_sums(got_first, True)
-        across(chunk(3))
-        ends([], chunk(2))
-        got_second = make_totals(1)
-        make_prefixes((0,), got_first, fans_first, True)
-        fans_second = make_sums(got_second, True)
-        ends([], chunk(3))
-        make_outputs(halves_of(0))
-        make_prefixes((1,), got_second, fans_second, True, lacked)
-        make_outputs(halves_of(1))
-        make_outputs(halves_of(2))
-        make_outputs(halves_of(3))
+        kept = {}
+
+        def keep(name, make, *args):
+            kept[name] = make(*args)
+
+        def rest_sums():
+            kept["fans"] = make_sums(kept["got"], False)
+
+        def rest_prefixes():
+            make_prefixes((2, 3), kept["got"], kept["fans"], False)
+
+        def lead_sums(g):
+            kept["fans", g] = make_sums(kept["totals", g], True)
+
+        def lead_prefixes(g):
+            make_prefixes((g,), kept["totals", g], kept["fans", g], True, kept["lacked"] if g else None)
+
+        steps = {
+            "K": lambda g: keep("lacked", make_lead_terms) if g == 0 else keep("got", make_terms, (2, 3)),
+            "A": lambda g: rest_sums(),
+            "B": lambda g: rest_prefixes(),
+            "L": make_local,
+            "E": lambda g: ends(chunk(g), []),
+            "O": lambda g: across(chunk(g)),
+            "F": lambda g: ends([], chunk(g)),
+            "J": lambda g: ends(chunk(g), chunk(g - leads)),
+            "T": lambda g: keep(("totals", g), make_totals, g),
+            "S": lead_sums,
+            "P": lead_prefixes,
+            "W": lambda g: make_outputs(halves_of(g)),
+        }
+        for step in ORDER.split():
+            steps[step[0]](int(step[1]))
     else:
         assert not leads
         places = tuple(range(groups))

time: 117 us -> 101 us (0.86)
  waiting for transfers between devices: 47.4 us -> 26.2 us
  starting transfers between devices: 30.5 us -> 35.3 us
    ppermute x1 -> x0, waiting for transfers between devices: 13.2 us -> none  [make_lead_terms(): return lax.ppermute(own[inner + 1], 'heads', [(1, 0), (2, 3)])]
    ppermute x16, waiting for transfers between devices: 14.2 us -> 6.64 us  [pairs(): return lax.ppermute(array, axis, [(i, i ^ distance) for i in range(count)])]
    ppermute x10, starting transfers between devices: 17.6 us -> 23.3 us  [receive(): got = lax.ppermute(sent, 'heads', perm)]
    ppermute x1 -> x0, starting transfers between devices: 1.28 us -> none  [make_lead_terms(): return lax.ppermute(own[inner + 1], 'heads', [(1, 0), (2, 3)])]
  transfers between devices with their start and end apart: 27 -> 26, of which waited for: 14 -> 8; matrix products, arithmetic and copies ran while one was open for 0% -> 0% of each run, Pallas kernels for 24% -> 31%
where the time goes in v7:
time: 101 us; the launch traced here: 100 us
  Pallas kernels  36.8 us (36%)
  starting transfers between devices  35.3 us (35%)
  waiting for transfers between devices  26.2 us (26%)
  between operations  1.19 us (1%)
    pallas_call x28, Pallas kernels, call(): pl.pallas_call(ordered, in_specs=list(specs or [SMEM] + [VMEM] * (count -...  36.8 us
    ppermute x10, starting transfers between devices, receive(): got = lax.ppermute(sent, 'heads', perm)  23.3 us
    ppermute x10, waiting for transfers between devices, receive(): got = lax.ppermute(sent, 'heads', perm)  19.6 us
    ppermute x16, starting transfers between devices, pairs(): return lax.ppermute(array, axis, [(i, i ^ distance) for i in range(count)])  12 us
    ppermute x16, waiting for transfers between devices, pairs(): return lax.ppermute(array, axis, [(i, i ^ distance) for i in range(count)])  6.64 us
  transfers between devices with their start and end apart: 26, of which 8 were waited for; matrix products, arithmetic and copies ran while one was open for 0% of the time, Pallas kernels for 31%

profile of v7, /device:TPU:0, one launch (start us, length us, event | category | flops | bytes accessed | tf_op | source)
XLA Modules:
  0.0 100.4 jit_solution(9433678839949564993)
XLA Ops:
  0.7 0.7 copy-done.6
  1.4 0.6 shard_map.102
  2.0 2.7 %shard_map.103 = (bf16[2,8,128,128]{3,2,1,0:T(8,128)(2,1)S(1)}, bf16[2,8,128,128]{3,2,1,0:T(8,128)(2,1)S(1)}, f32[8,128]{1,0:T(8,128)S(1)}) custom-call(s32[3]{0:T(128)S(1)} %pad_add_fusion.refs_0_, f32[128,128]{1,0:T(8,128)S(1)} %get-tuple-element.86.refs_1_.refs_0_.refs_3_, bf16[128,4096]{1,0:T(8,128)(2,1)} %refs_4_.19, ...), custom_call_target="tpu_custom_call", output_to_operand_aliasing={{2}: (6, {})} | custom-call | tf_op jit(solution)/shard_map/pallas_call | solution.py:59
  5.3 3.3 %shard_map.104 = (bf16[2,8,128,128]{3,2,1,0:T(8,128)(2,1)S(1)}, bf16[2,8,128,128]{3,2,1,0:T(8,128)(2,1)S(1)}, bf16[2,8,128,128]{3,2,1,0:T(8,128)(2,1)S(1)}, f32[8,128]{1,0:T(8,128)S(1)}) custom-call(s32[3]{0:T(128)S(1)} %pad_add_fusion.refs_0_, f32[128,128]{1,0:T(8,128)S(1)} %get-tuple-element.86.refs_1_.refs_0_.refs_3_, ...), custom_call_target="tpu_custom_call", output_to_operand_aliasing={{3}: (9, {})} | custom-call | tf_op jit(solution)/shard_map/pallas_call | solution.py:59
  8.6 2.7 %collective-permute-start.5 = (bf16[2,8,128,128]{3,2,1,0:T(8,128)(2,1)S(1)}, bf16[2,8,128,128]{3,2,1,0:T(8,128)(2,1)S(1)}, u32[]{:S(2)}, u32[]{:S(2)}) collective-permute-start(bf16[2,8,128,128]{3,2,1,0:T(8,128)(2,1)S(1)} %get-tuple-element.97), channel_id=1, source_target_pairs={{0,1},{3,2},{1,0},{2,3},{4,5},{7,6},{5,4},{6,7},{8,9},{11,10},{9,8... | collective-permute-start | bytes 1572872 | tf_op jit(solution)/shard_map/ppermute | solution.py:494
  11.5 2.0 %shard_map.105 = (f32[4,8,128,128]{3,2,1,0:T(8,128)S(1)}, f32[8,128]{1,0:T(8,128)S(1)}) custom-call(f32[128,128]{1,0:T(8,128)S(1)} %get-tuple-element.86.refs_1_.refs_0_.refs_3_, f32[8,128]{1,0:T(8,128)S(1)} %get-tuple-element.90.refs_1_, bf16[128,4096]{1,0:T(8,128)(2,1)S(1)} %copy-done, ...), custom_call_target="tpu_custom_call", output_to_operand_aliasing={{1}: (6, {})} | custom-call | tf_op jit(solution)/shard_map/pallas_call | solution.py:59
  13.5 0.8 shard_map.106
  14.3 1.6 %collective-permute-start.2 = (bf16[1040,128]{1,0:T(8,128)(2,1)S(1)}, bf16[1040,128]{1,0:T(8,128)(2,1)S(1)}, u32[]{:S(2)}, u32[]{:S(2)}) collective-permute-start(bf16[1040,128]{1,0:T(8,128)(2,1)S(1)} %get-tuple-element.94), channel_id=1, source_target_pairs={{0,8},{8,0},{16,24},{24,16},{1,9},{9,1},{17,25},{25,17},{2,10},{10... | collective-permute-start | bytes 798728 | tf_op jit(solution)/shard_map/ppermute | solution.py:34
  15.8 1.5 %collective-permute-start.3 = (bf16[1040,128]{1,0:T(8,128)(2,1)S(1)}, bf16[1040,128]{1,0:T(8,128)(2,1)S(1)}, u32[]{:S(2)}, u32[]{:S(2)}) collective-permute-start(bf16[1040,128]{1,0:T(8,128)(2,1)S(1)} %get-tuple-element.95), channel_id=1, source_target_pairs={{0,16},{8,24},{16,0},{24,8},{1,17},{9,25},{17,1},{25,9},{2,18},{10... | collective-permute-start | bytes 798728 | tf_op jit(solution)/shard_map/ppermute | solution.py:34
  17.8 0.6 shard_map.107
  18.5 2.2 %collective-permute-start.7 = (bf16[2,8,128,128]{3,2,1,0:T(8,128)(2,1)S(1)}, bf16[2,8,128,128]{3,2,1,0:T(8,128)(2,1)S(1)}, u32[]{:S(2)}, u32[]{:S(2)}) collective-permute-start(bf16[2,8,128,128]{3,2,1,0:T(8,128)(2,1)S(1)} %get-tuple-element.104), channel_id=1, source_target_pairs={{0,1},{3,2},{4,5},{7,6},{8,9},{11,10},{12,13},{15,14},{16,17},{19,... | collective-permute-start | bytes 1572872 | tf_op jit(solution)/shard_map/ppermute | solution.py:494
  20.7 3.1 %collective-permute-done.5.refs_3_.refs_5_.refs_7_.refs_9_.refs_13_.refs_17_.refs_21_ = bf16[2,8,128,128]{3,2,1,0:T(8,128)(2,1)S(1)} collective-permute-done((bf16[2,8,128,128]{3,2,1,0:T(8,128)(2,1)S(1)}, bf16[2,8,128,128]{3,2,1,0:T(8,128)(2,1)S(1)}, u32[]{:S(2)}, u32[]{:S(2)}) %collective-permute-start.5) | collective-permute-done | bytes 524320 | tf_op jit(solution)/shard_map/ppermute | solution.py:494
  24.4 0.7 collective-permute-start.9
  25.1 4.8 %collective-permute-done.3.refs_8_ = bf16[1040,128]{1,0:T(8,128)(2,1)S(1)} collective-permute-done((bf16[1040,128]{1,0:T(8,128)(2,1)S(1)}, bf16[1040,128]{1,0:T(8,128)(2,1)S(1)}, u32[]{:S(2)}, u32[]{:S(2)}) %collective-permute-start.3) | collective-permute-done | bytes 266272 | tf_op jit(solution)/shard_map/ppermute | solution.py:34
  29.9 1.5 %shard_map.109 = (bf16[2,8,128,128]{3,2,1,0:T(8,128)(2,1)S(1)}, bf16[2,8,128,128]{3,2,1,0:T(8,128)(2,1)S(1)}, f32[8,128]{1,0:T(8,128)S(1)}, f32[8,128]{1,0:T(8,128)S(1)}) custom-call(s32[3]{0:T(128)S(1)} %pad_add_fusion.refs_0_, f32[8,128,128]{2,1,0:T(8,128)S(1)} %copy-done.4, f32[8,128,128]{2,1,0:T(8,128)S(1)} %copy-done.5, ...), custom_call_target="tpu_custom_call", output_to_operand_aliasing={{3}: (10, {})} | custom-call | flops 16000000000 | tf_op jit(solution)/shard_map/pallas_call | solution.py:59
  31.4 2.0 %shard_map.110 = (f32[4,8,128,128]{3,2,1,0:T(8,128)S(1)}, f32[8,128]{1,0:T(8,128)S(1)}) custom-call(f32[128,128]{1,0:T(8,128)S(1)} %get-tuple-element.86.refs_1_.refs_0_.refs_3_, f32[8,128]{1,0:T(8,128)S(1)} %get-tuple-element.90.refs_1_, bf16[128,4096]{1,0:T(8,128)(2,1)S(1)} %copy-done, ...), custom_call_target="tpu_custom_call", output_to_operand_aliasing={{1}: (6, {})} | custom-call | tf_op jit(solution)/shard_map/pallas_call | solution.py:59
  33.5 0.8 collective-permute-done.7.refs_3_.refs_5_.refs_7_.refs_9_.refs_13_.refs_17_.refs_21_
  34.9 0.7 collective-permute-start.8
  35.6 0.6 shard_map.112
  36.2 6.2 %collective-permute-start.11 = (bf16[2,8,128,128]{3,2,1,0:T(8,128)(2,1)S(1)}, bf16[2,8,128,128]{3,2,1,0:T(8,128)(2,1)S(1)}, u32[]{:S(2)}, u32[]{:S(2)}) collective-permute-start(bf16[2,8,128,128]{3,2,1,0:T(8,128)(2,1)S(1)} %get-tuple-element.115), channel_id=1, source_target_pairs={{0,1},{3,2},{1,0},{2,3},{4,5},{7,6},{5,4},{6,7},{8,9},{11,10},{9,8... | collective-permute-start | bytes 1572872 | tf_op jit(solution)/shard_map/ppermute | solution.py:494
  42.4 2.0 %shard_map.113 = (f32[4,8,128,128]{3,2,1,0:T(8,128)S(1)}, f32[8,128]{1,0:T(8,128)S(1)}) custom-call(f32[128,128]{1,0:T(8,128)S(1)} %get-tuple-element.86.refs_1_.refs_0_.refs_3_, f32[8,128]{1,0:T(8,128)S(1)} %get-tuple-element.90.refs_1_, bf16[128,4096]{1,0:T(8,128)(2,1)S(1)} %copy-done, ...), custom_call_target="tpu_custom_call", output_to_operand_aliasing={{1}: (6, {})} | custom-call | tf_op jit(solution)/shard_map/pallas_call | solution.py:59
  44.4 2.0 %shard_map.114 = (f32[4,8,128,128]{3,2,1,0:T(8,128)S(1)}, f32[8,128]{1,0:T(8,128)S(1)}) custom-call(f32[128,128]{1,0:T(8,128)S(1)} %get-tuple-element.86.refs_1_.refs_0_.refs_3_, f32[8,128]{1,0:T(8,128)S(1)} %get-tuple-element.90.refs_1_, bf16[128,4096]{1,0:T(8,128)(2,1)S(1)} %copy-done, ...), custom_call_target="tpu_custom_call", output_to_operand_aliasing={{1}: (6, {})} | custom-call | tf_op jit(solution)/shard_map/pallas_call | solution.py:59
  46.4 0.6 shard_map.115
  47.1 6.6 %collective-permute-start.10 = (bf16[2,8,128,128]{3,2,1,0:T(8,128)(2,1)S(1)}, bf16[2,8,128,128]{3,2,1,0:T(8,128)(2,1)S(1)}, u32[]{:S(2)}, u32[]{:S(2)}) collective-permute-start(bf16[2,8,128,128]{3,2,1,0:T(8,128)(2,1)S(1)} %get-tuple-element.114), channel_id=1, source_target_pairs={{0,1},{3,2},{1,0},{2,3},{4,5},{7,6},{5,4},{6,7},{8,9},{11,10},{9,8... | collective-permute-start | bytes 1572872 | tf_op jit(solution)/shard_map/ppermute | solution.py:494
  53.7 0.7 shard_map.116
  54.5 0.6 shard_map.117
  55.1 0.7 collective-permute-start.18
  56.0 0.7 shard_map.118
  56.7 1.6 %collective-permute-start.16 = (bf16[528,128]{1,0:T(8,128)(2,1)S(1)}, bf16[528,128]{1,0:T(8,128)(2,1)S(1)}, u32[]{:S(2)}, u32[]{:S(2)}) collective-permute-start(bf16[528,128]{1,0:T(8,128)(2,1)S(1)} %get-tuple-element.127), channel_id=1, source_target_pairs={{0,16},{8,24},{16,0},{24,8},{1,17},{9,25},{17,1},{25,9},{2,18},{10... | collective-permute-start | bytes 405512 | tf_op jit(solution)/shard_map/ppermute | solution.py:34
  58.3 1.4 %collective-permute-start.17 = (bf16[528,128]{1,0:T(8,128)(2,1)S(1)}, bf16[528,128]{1,0:T(8,128)(2,1)S(1)}, u32[]{:S(2)}, u32[]{:S(2)}) collective-permute-start(bf16[528,128]{1,0:T(8,128)(2,1)S(1)} %get-tuple-element.127), channel_id=1, source_target_pairs={{0,24},{8,16},{16,8},{24,0},{1,25},{9,17},{17,9},{25,1},{2,26},{10... | collective-permute-start | bytes 405512 | tf_op jit(solution)/shard_map/ppermute | solution.py:34
  60.2 4.3 %collective-permute-done.10.refs_5_.refs_8_.refs_9_.refs_11_.refs_15_.refs_19_.refs_23_.refs_13_.refs_17_.refs_21_ = bf16[2,8,128,128]{3,2,1,0:T(8,128)(2,1)S(1)} collective-permute-done((bf16[2,8,128,128]{3,2,1,0:T(8,128)(2,1)S(1)}, bf16[2,8,128,128]{3,2,1,0:T(8,128)(2,1)S(1)}, u32[]{:S(2)}, u32[]{:S(2)}) %collective-permute-start.10) | collective-permute-done | bytes 524320 | tf_op jit(solution)/shard_map/ppermute | solution.py:494
  65.1 0.7 collective-permute-start.13
  65.8 0.7 shard_map.120
  66.5 0.6 shard_map.121
  67.1 1.5 %collective-permute-start.23 = (bf16[2,8,128,128]{3,2,1,0:T(8,128)(2,1)S(1)}, bf16[2,8,128,128]{3,2,1,0:T(8,128)(2,1)S(1)}, u32[]{:S(2)}, u32[]{:S(2)}) collective-permute-start(bf16[2,8,128,128]{3,2,1,0:T(8,128)(2,1)S(1)} %get-tuple-element.140), channel_id=1, source_target_pairs={{1,0},{2,3},{5,4},{6,7},{9,8},{10,11},{13,12},{14,15},{17,16},{18,... | collective-permute-start | bytes 1572872 | tf_op jit(solution)/shard_map/ppermute | solution.py:494
  68.7 1.3 %shard_map.122 = (bf16[2,4,128,128]{3,2,1,0:T(8,128)(2,1)S(1)}, bf16[2,4,128,128]{3,2,1,0:T(8,128)(2,1)S(1)}, f32[8,128]{1,0:T(8,128)}, f32[8,128]{1,0:T(8,128)S(1)}) custom-call(s32[3]{0:T(128)S(1)} %pad_add_fusion.refs_0_, f32[8,128,128]{2,1,0:T(8,128)S(1)} %copy-done.4, f32[8,128,128]{2,1,0:T(8,128)S(1)} %copy-done.5, ...), custom_call_target="tpu_custom_call", output_to_operand_aliasing={{3}: (10, {})} | custom-call | tf_op jit(solution)/shard_map/pallas_call | solution.py:59
  70.5 0.7 shard_map.123
  71.8 1.3 %collective-permute-start.19 = (bf16[2,8,128,128]{3,2,1,0:T(8,128)(2,1)S(1)}, bf16[2,8,128,128]{3,2,1,0:T(8,128)(2,1)S(1)}, u32[]{:S(2)}, u32[]{:S(2)}) collective-permute-start(bf16[2,8,128,128]{3,2,1,0:T(8,128)(2,1)S(1)} %get-tuple-element.133), channel_id=1, source_target_pairs={{1,0},{2,3},{5,4},{6,7},{9,8},{10,11},{13,12},{14,15},{17,16},{18,... | collective-permute-start | bytes 1572872 | tf_op jit(solution)/shard_map/ppermute | solution.py:494
  73.1 1.6 %collective-permute-start.20 = (bf16[528,128]{1,0:T(8,128)(2,1)S(1)}, bf16[528,128]{1,0:T(8,128)(2,1)S(1)}, u32[]{:S(2)}, u32[]{:S(2)}) collective-permute-start(bf16[528,128]{1,0:T(8,128)(2,1)S(1)} %get-tuple-element.138), channel_id=1, source_target_pairs={{0,8},{8,0},{16,24},{24,16},{1,9},{9,1},{17,25},{25,17},{2,10},{10... | collective-permute-start | bytes 405512 | tf_op jit(solution)/shard_map/ppermute | solution.py:34
  74.6 1.5 %collective-permute-start.21 = (bf16[528,128]{1,0:T(8,128)(2,1)S(1)}, bf16[528,128]{1,0:T(8,128)(2,1)S(1)}, u32[]{:S(2)}, u32[]{:S(2)}) collective-permute-start(bf16[528,128]{1,0:T(8,128)(2,1)S(1)} %get-tuple-element.139), channel_id=1, source_target_pairs={{0,16},{8,24},{16,0},{24,8},{1,17},{9,25},{17,1},{25,9},{2,18},{10... | collective-permute-start | bytes 405512 | tf_op jit(solution)/shard_map/ppermute | solution.py:34
  76.6 2.2 %shard_map.125 = (bf16[128,4096]{1,0:T(8,128)(2,1)}, bf16[128,4096]{1,0:T(8,128)(2,1)}, bf16[128,4096]{1,0:T(8,128)(2,1)}, bf16[128,4096]{1,0:T(8,128)(2,1)}, f32[8,128]{1,0:T(8,128)S(1)}) custom-call(s32[3]{0:T(128)S(1)} %pad_add_fusion.refs_0_, f32[8,128]{1,0:T(8,128)S(1)} %get-tuple-element.85.refs_2_.refs_1_.refs_3_.refs_4_, ...), custom_call_target="tpu_custom_call", output_to_operand_aliasing={{4}: (28, {})} | custom-call | tf_op jit(solution)/shard_map/pallas_call | solution.py:59
  78.9 7.8 %collective-permute-done.23.refs_11_.refs_15_.refs_19_.refs_23_ = bf16[2,8,128,128]{3,2,1,0:T(8,128)(2,1)S(1)} collective-permute-done((bf16[2,8,128,128]{3,2,1,0:T(8,128)(2,1)S(1)}, bf16[2,8,128,128]{3,2,1,0:T(8,128)(2,1)S(1)}, u32[]{:S(2)}, u32[]{:S(2)}) %collective-permute-start.23) | collective-permute-done | bytes 524320 | tf_op jit(solution)/shard_map/ppermute | solution.py:494
  86.7 2.3 %shard_map.126 = (bf16[128,4096]{1,0:T(8,128)(2,1)}, bf16[128,4096]{1,0:T(8,128)(2,1)}, bf16[128,4096]{1,0:T(8,128)(2,1)}, bf16[128,4096]{1,0:T(8,128)(2,1)}, f32[8,128]{1,0:T(8,128)S(1)}) custom-call(s32[3]{0:T(128)S(1)} %pad_add_fusion.refs_0_, ...), custom_call_target="tpu_custom_call", output_to_operand_aliasing={{0}: (28, {}), {1}: (29, {}), {2}: (30, {}), {3}: (31, {}),... | custom-call | tf_op jit(solution)/shard_map/pallas_call | solution.py:59
  89.0 1.6 %shard_map.127 = (bf16[2,4,128,128]{3,2,1,0:T(8,128)(2,1)S(1)}, bf16[2,4,128,128]{3,2,1,0:T(8,128)(2,1)S(1)}, f32[8,128]{1,0:T(8,128)}, f32[8,128]{1,0:T(8,128)S(1)}) custom-call(s32[3]{0:T(128)S(1)} %pad_add_fusion.refs_0_, f32[8,128,128]{2,1,0:T(8,128)S(1)} %copy-done.4, f32[8,128,128]{2,1,0:T(8,128)S(1)} %copy-done.5, ...), custom_call_target="tpu_custom_call", output_to_operand_aliasing={{3}: (11, {})} | custom-call | tf_op jit(solution)/shard_map/pallas_call | solution.py:59
  90.6 1.5 %collective-permute-done.25.refs_12_.refs_20_ = bf16[2,4,128,128]{3,2,1,0:T(8,128)(2,1)S(1)} collective-permute-done((bf16[2,4,128,128]{3,2,1,0:T(8,128)(2,1)S(1)}, bf16[2,4,128,128]{3,2,1,0:T(8,128)(2,1)S(1)}, u32[]{:S(2)}, u32[]{:S(2)}) %collective-permute-start.25) | collective-permute-done | bytes 262176 | tf_op jit(solution)/shard_map/ppermute | solution.py:34
  92.1 2.2 %shard_map.128 = (bf16[128,4096]{1,0:T(8,128)(2,1)}, bf16[128,4096]{1,0:T(8,128)(2,1)}, bf16[128,4096]{1,0:T(8,128)(2,1)}, bf16[128,4096]{1,0:T(8,128)(2,1)}, f32[8,128]{1,0:T(8,128)S(1)}) custom-call(s32[3]{0:T(128)S(1)} %pad_add_fusion.refs_0_, ...), custom_call_target="tpu_custom_call", output_to_operand_aliasing={{0}: (28, {}), {1}: (29, {}), {2}: (30, {}), {3}: (31, {}),... | custom-call | tf_op jit(solution)/shard_map/pallas_call | solution.py:59
  94.4 3.5 %collective-permute-done.19.refs_11_.refs_15_.refs_19_.refs_23_ = bf16[2,8,128,128]{3,2,1,0:T(8,128)(2,1)S(1)} collective-permute-done((bf16[2,8,128,128]{3,2,1,0:T(8,128)(2,1)S(1)}, bf16[2,8,128,128]{3,2,1,0:T(8,128)(2,1)S(1)}, u32[]{:S(2)}, u32[]{:S(2)}) %collective-permute-start.19) | collective-permute-done | bytes 524320 | tf_op jit(solution)/shard_map/ppermute | solution.py:494
  97.9 2.3 %shard_map.129 = (bf16[128,4096]{1,0:T(8,128)(2,1)}, bf16[128,4096]{1,0:T(8,128)(2,1)}, bf16[128,4096]{1,0:T(8,128)(2,1)}, bf16[128,4096]{1,0:T(8,128)(2,1)}, f32[8,128]{1,0:T(8,128)S(1)}) custom-call(s32[3]{0:T(128)S(1)} %pad_add_fusion.refs_0_, ...), custom_call_target="tpu_custom_call", output_to_operand_aliasing={{0}: (28, {}), {1}: (29, {}), {2}: (30, {}), {3}: (31, {}),... | custom-call | tf_op jit(solution)/shard_map/pallas_call | solution.py:59
  (48 shorter events, 5.5 us)
Async XLA Ops:
  0.7 0.7 copy-start.6
  4.7 8.7 %collective-permute-start.1 = (bf16[2,8,128,128]{3,2,1,0:T(8,128)(2,1)S(1)}, bf16[2,8,128,128]{3,2,1,0:T(8,128)(2,1)S(1)}, u32[]{:S(2)}, u32[]{:S(2)}) collective-permute-start(bf16[2,8,128,128]{3,2,1,0:T(8,128)(2,1)S(1)} %get-tuple-element.89.refs_3_.refs_5_.refs_6_), channel_id=1, source_target_pairs={{0,4},{4,0},{1,5},{5,1},{2,6},{6,2},{3,7},{7,3},{8,12},{12,8},{9,1... | collective-permute-start | bytes 1572872 | tf_op jit(solution)/shard_map/ppermute | solution.py:34
  5.2 6.2 %copy-start = (bf16[128,4096]{1,0:T(8,128)(2,1)S(1)}, bf16[128,4096]{1,0:T(8,128)(2,1)}, u32[]{:S(2)}) copy-start(bf16[128,4096]{1,0:T(8,128)(2,1)} %refs_4_.19) | copy-start | bytes 3145732
  5.2 6.2 %copy-start.1 = (bf16[128,4096]{1,0:T(8,128)(2,1)S(1)}, bf16[128,4096]{1,0:T(8,128)(2,1)}, u32[]{:S(2)}) copy-start(bf16[128,4096]{1,0:T(8,128)(2,1)} %refs_5_.19) | copy-start | bytes 3145732
  5.2 6.2 %copy-start.2 = (bf16[128,4096]{1,0:T(8,128)(2,1)S(1)}, bf16[128,4096]{1,0:T(8,128)(2,1)}, u32[]{:S(2)}) copy-start(bf16[128,4096]{1,0:T(8,128)(2,1)} %refs_6_.9) | copy-start | bytes 3145732
  5.2 6.2 %copy-start.3 = (bf16[128,4096]{1,0:T(8,128)(2,1)S(1)}, bf16[128,4096]{1,0:T(8,128)(2,1)}, u32[]{:S(2)}) copy-start(bf16[128,4096]{1,0:T(8,128)(2,1)} %refs_7_.9) | copy-start | bytes 3145732
  8.6 15.2 %collective-permute-start.5 = (bf16[2,8,128,128]{3,2,1,0:T(8,128)(2,1)S(1)}, bf16[2,8,128,128]{3,2,1,0:T(8,128)(2,1)S(1)}, u32[]{:S(2)}, u32[]{:S(2)}) collective-permute-start(bf16[2,8,128,128]{3,2,1,0:T(8,128)(2,1)S(1)} %get-tuple-element.97), channel_id=1, source_target_pairs={{0,1},{3,2},{1,0},{2,3},{4,5},{7,6},{5,4},{6,7},{8,9},{11,10},{9,8... | collective-permute-start | bytes 1572872 | tf_op jit(solution)/shard_map/ppermute | solution.py:494
  11.3 2.2 %collective-permute-start = (f32[8,128]{1,0:T(8,128)S(1)}, f32[8,128]{1,0:T(8,128)S(1)}, u32[]{:S(2)}, u32[]{:S(2)}) collective-permute-start(f32[8,128]{1,0:T(8,128)S(1)} %get-tuple-element.85.refs_2_.refs_1_.refs_3_.refs_4_), channel_id=1, source_target_pairs={{0,4},{4,0},{1,5},{5,1},{2,6},{6,2},{3,7},{7,3},{8,12},{12,8},{9,1... | collective-permute-start | bytes 12296 | tf_op jit(solution)/shard_map/ppermute | solution.py:34
  13.5 16.4 %copy-start.4 = (f32[8,128,128]{2,1,0:T(8,128)S(1)}, f32[8,128,128]{2,1,0:T(8,128)}, u32[]{:S(2)}) copy-start(f32[8,128,128]{2,1,0:T(8,128)} %refs_1_.5) | copy-start | bytes 1572868
  13.5 16.4 %copy-start.5 = (f32[8,128,128]{2,1,0:T(8,128)S(1)}, f32[8,128,128]{2,1,0:T(8,128)}, u32[]{:S(2)}) copy-start(f32[8,128,128]{2,1,0:T(8,128)} %refs_2_.15) | copy-start | bytes 1572868
  14.3 10.8 %collective-permute-start.2 = (bf16[1040,128]{1,0:T(8,128)(2,1)S(1)}, bf16[1040,128]{1,0:T(8,128)(2,1)S(1)}, u32[]{:S(2)}, u32[]{:S(2)}) collective-permute-start(bf16[1040,128]{1,0:T(8,128)(2,1)S(1)} %get-tuple-element.94), channel_id=1, source_target_pairs={{0,8},{8,0},{16,24},{24,16},{1,9},{9,1},{17,25},{25,17},{2,10},{10... | collective-permute-start | bytes 798728 | tf_op jit(solution)/shard_map/ppermute | solution.py:34
  15.8 14.1 %collective-permute-start.3 = (bf16[1040,128]{1,0:T(8,128)(2,1)S(1)}, bf16[1040,128]{1,0:T(8,128)(2,1)S(1)}, u32[]{:S(2)}, u32[]{:S(2)}) collective-permute-start(bf16[1040,128]{1,0:T(8,128)(2,1)S(1)} %get-tuple-element.95), channel_id=1, source_target_pairs={{0,16},{8,24},{16,0},{24,8},{1,17},{9,25},{17,1},{25,9},{2,18},{10... | collective-permute-start | bytes 798728 | tf_op jit(solution)/shard_map/ppermute | solution.py:34
  17.4 12.6 %collective-permute-start.4 = (bf16[1040,128]{1,0:T(8,128)(2,1)S(1)}, bf16[1040,128]{1,0:T(8,128)(2,1)S(1)}, u32[]{:S(2)}, u32[]{:S(2)}) collective-permute-start(bf16[1040,128]{1,0:T(8,128)(2,1)S(1)} %get-tuple-element.95), channel_id=1, source_target_pairs={{0,24},{8,16},{16,8},{24,0},{1,25},{9,17},{17,9},{25,1},{2,26},{10... | collective-permute-start | bytes 798728 | tf_op jit(solution)/shard_map/ppermute | solution.py:34
  18.5 15.9 %collective-permute-start.7 = (bf16[2,8,128,128]{3,2,1,0:T(8,128)(2,1)S(1)}, bf16[2,8,128,128]{3,2,1,0:T(8,128)(2,1)S(1)}, u32[]{:S(2)}, u32[]{:S(2)}) collective-permute-start(bf16[2,8,128,128]{3,2,1,0:T(8,128)(2,1)S(1)} %get-tuple-element.104), channel_id=1, source_target_pairs={{0,1},{3,2},{4,5},{7,6},{8,9},{11,10},{12,13},{15,14},{16,17},{19,... | collective-permute-start | bytes 1572872 | tf_op jit(solution)/shard_map/ppermute | solution.py:494
  24.4 11.2 %collective-permute-start.9 = (bf16[2,8,128,128]{3,2,1,0:T(8,128)(2,1)S(1)}, bf16[2,8,128,128]{3,2,1,0:T(8,128)(2,1)S(1)}, u32[]{:S(2)}, u32[]{:S(2)}) collective-permute-start(bf16[2,8,128,128]{3,2,1,0:T(8,128)(2,1)S(1)} %get-tuple-element.109), channel_id=1, source_target_pairs={{1,2},{2,1},{5,6},{6,5},{9,10},{10,9},{13,14},{14,13},{17,18},{18,... | collective-permute-start | bytes 1572872 | tf_op jit(solution)/shard_map/ppermute | solution.py:494
  33.4 13.0 %collective-permute-start.6 = (bf16[2,8,128,128]{3,2,1,0:T(8,128)(2,1)S(1)}, bf16[2,8,128,128]{3,2,1,0:T(8,128)(2,1)S(1)}, u32[]{:S(2)}, u32[]{:S(2)}) collective-permute-start(bf16[2,8,128,128]{3,2,1,0:T(8,128)(2,1)S(1)} %get-tuple-element.103), channel_id=1, source_target_pairs={{0,4},{4,0},{1,5},{5,1},{2,6},{6,2},{3,7},{7,3},{8,12},{12,8},{9,1... | collective-permute-start | bytes 1572872 | tf_op jit(solution)/shard_map/ppermute | solution.py:34
  34.9 11.5 %collective-permute-start.8 = (bf16[2,8,128,128]{3,2,1,0:T(8,128)(2,1)S(1)}, bf16[2,8,128,128]{3,2,1,0:T(8,128)(2,1)S(1)}, u32[]{:S(2)}, u32[]{:S(2)}) collective-permute-start(bf16[2,8,128,128]{3,2,1,0:T(8,128)(2,1)S(1)} %get-tuple-element.107), channel_id=1, source_target_pairs={{1,2},{2,1},{5,6},{6,5},{9,10},{10,9},{13,14},{14,13},{17,18},{18,... | collective-permute-start | bytes 1572872 | tf_op jit(solution)/shard_map/ppermute | solution.py:494
  36.2 17.4 %collective-permute-start.11 = (bf16[2,8,128,128]{3,2,1,0:T(8,128)(2,1)S(1)}, bf16[2,8,128,128]{3,2,1,0:T(8,128)(2,1)S(1)}, u32[]{:S(2)}, u32[]{:S(2)}) collective-permute-start(bf16[2,8,128,128]{3,2,1,0:T(8,128)(2,1)S(1)} %get-tuple-element.115), channel_id=1, source_target_pairs={{0,1},{3,2},{1,0},{2,3},{4,5},{7,6},{5,4},{6,7},{8,9},{11,10},{9,8... | collective-permute-start | bytes 1572872 | tf_op jit(solution)/shard_map/ppermute | solution.py:494
  47.1 17.5 %collective-permute-start.10 = (bf16[2,8,128,128]{3,2,1,0:T(8,128)(2,1)S(1)}, bf16[2,8,128,128]{3,2,1,0:T(8,128)(2,1)S(1)}, u32[]{:S(2)}, u32[]{:S(2)}) collective-permute-start(bf16[2,8,128,128]{3,2,1,0:T(8,128)(2,1)S(1)} %get-tuple-element.114), channel_id=1, source_target_pairs={{0,1},{3,2},{1,0},{2,3},{4,5},{7,6},{5,4},{6,7},{8,9},{11,10},{9,8... | collective-permute-start | bytes 1572872 | tf_op jit(solution)/shard_map/ppermute | solution.py:494
  54.4 1.6 %collective-permute-start.12 = (bf16[2,4,128,128]{3,2,1,0:T(8,128)(2,1)S(1)}, bf16[2,4,128,128]{3,2,1,0:T(8,128)(2,1)S(1)}, u32[]{:S(2)}, u32[]{:S(2)}) collective-permute-start(bf16[2,4,128,128]{3,2,1,0:T(8,128)(2,1)S(1)} %get-tuple-element.118), channel_id=1, source_target_pairs={{0,4},{4,0},{1,5},{5,1},{2,6},{6,2},{3,7},{7,3},{8,12},{12,8},{9,1... | collective-permute-start | bytes 786440 | tf_op jit(solution)/shard_map/ppermute | solution.py:34
  55.1 11.5 %collective-permute-start.18 = (bf16[2,8,128,128]{3,2,1,0:T(8,128)(2,1)S(1)}, bf16[2,8,128,128]{3,2,1,0:T(8,128)(2,1)S(1)}, u32[]{:S(2)}, u32[]{:S(2)}) collective-permute-start(bf16[2,8,128,128]{3,2,1,0:T(8,128)(2,1)S(1)} %get-tuple-element.128), channel_id=1, source_target_pairs={{1,2},{2,1},{5,6},{6,5},{9,10},{10,9},{13,14},{14,13},{17,18},{18,... | collective-permute-start | bytes 1572872 | tf_op jit(solution)/shard_map/ppermute | solution.py:494
  56.7 12.0 %collective-permute-start.16 = (bf16[528,128]{1,0:T(8,128)(2,1)S(1)}, bf16[528,128]{1,0:T(8,128)(2,1)S(1)}, u32[]{:S(2)}, u32[]{:S(2)}) collective-permute-start(bf16[528,128]{1,0:T(8,128)(2,1)S(1)} %get-tuple-element.127), channel_id=1, source_target_pairs={{0,16},{8,24},{16,0},{24,8},{1,17},{9,25},{17,1},{25,9},{2,18},{10... | collective-permute-start | bytes 405512 | tf_op jit(solution)/shard_map/ppermute | solution.py:34
  58.3 10.4 %collective-permute-start.17 = (bf16[528,128]{1,0:T(8,128)(2,1)S(1)}, bf16[528,128]{1,0:T(8,128)(2,1)S(1)}, u32[]{:S(2)}, u32[]{:S(2)}) collective-permute-start(bf16[528,128]{1,0:T(8,128)(2,1)S(1)} %get-tuple-element.127), channel_id=1, source_target_pairs={{0,24},{8,16},{16,8},{24,0},{1,25},{9,17},{17,9},{25,1},{2,26},{10... | collective-permute-start | bytes 405512 | tf_op jit(solution)/shard_map/ppermute | solution.py:34
  59.7 8.9 %collective-permute-start.15 = (bf16[528,128]{1,0:T(8,128)(2,1)S(1)}, bf16[528,128]{1,0:T(8,128)(2,1)S(1)}, u32[]{:S(2)}, u32[]{:S(2)}) collective-permute-start(bf16[528,128]{1,0:T(8,128)(2,1)S(1)} %get-tuple-element.126), channel_id=1, source_target_pairs={{0,8},{8,0},{16,24},{24,16},{1,9},{9,1},{17,25},{25,17},{2,10},{10... | collective-permute-start | bytes 405512 | tf_op jit(solution)/shard_map/ppermute | solution.py:34
  65.1 6.1 %collective-permute-start.13 = (bf16[2,8,128,128]{3,2,1,0:T(8,128)(2,1)S(1)}, bf16[2,8,128,128]{3,2,1,0:T(8,128)(2,1)S(1)}, u32[]{:S(2)}, u32[]{:S(2)}) collective-permute-start(bf16[2,8,128,128]{3,2,1,0:T(8,128)(2,1)S(1)} %get-tuple-element.122), channel_id=1, source_target_pairs={{1,2},{2,1},{5,6},{6,5},{9,10},{10,9},{13,14},{14,13},{17,18},{18,... | collective-permute-start | bytes 1572872 | tf_op jit(solution)/shard_map/ppermute | solution.py:494
  67.1 19.6 %collective-permute-start.23 = (bf16[2,8,128,128]{3,2,1,0:T(8,128)(2,1)S(1)}, bf16[2,8,128,128]{3,2,1,0:T(8,128)(2,1)S(1)}, u32[]{:S(2)}, u32[]{:S(2)}) collective-permute-start(bf16[2,8,128,128]{3,2,1,0:T(8,128)(2,1)S(1)} %get-tuple-element.140), channel_id=1, source_target_pairs={{1,0},{2,3},{5,4},{6,7},{9,8},{10,11},{13,12},{14,15},{17,16},{18,... | collective-permute-start | bytes 1572872 | tf_op jit(solution)/shard_map/ppermute | solution.py:494
  68.6 1.9 %collective-permute-start.14 = (bf16[2,4,128,128]{3,2,1,0:T(8,128)(2,1)S(1)}, bf16[2,4,128,128]{3,2,1,0:T(8,128)(2,1)S(1)}, u32[]{:S(2)}, u32[]{:S(2)}) collective-permute-start(bf16[2,4,128,128]{3,2,1,0:T(8,128)(2,1)S(1)} %get-tuple-element.125), channel_id=1, source_target_pairs={{0,4},{4,0},{1,5},{5,1},{2,6},{6,2},{3,7},{7,3},{8,12},{12,8},{9,1... | collective-permute-start | bytes 786440 | tf_op jit(solution)/shard_map/ppermute | solution.py:34
  70.0 6.1 %collective-permute-start.24 = (bf16[2,4,128,128]{3,2,1,0:T(8,128)(2,1)S(1)}, bf16[2,4,128,128]{3,2,1,0:T(8,128)(2,1)S(1)}, u32[]{:S(2)}, u32[]{:S(2)}) collective-permute-start(bf16[2,4,128,128]{3,2,1,0:T(8,128)(2,1)S(1)} %get-tuple-element.142), channel_id=1, source_target_pairs={{0,4},{4,0},{1,5},{5,1},{2,6},{6,2},{3,7},{7,3},{8,12},{12,8},{9,1... | collective-permute-start | bytes 786440 | tf_op jit(solution)/shard_map/ppermute | solution.py:34
  71.8 26.2 %collective-permute-start.19 = (bf16[2,8,128,128]{3,2,1,0:T(8,128)(2,1)S(1)}, bf16[2,8,128,128]{3,2,1,0:T(8,128)(2,1)S(1)}, u32[]{:S(2)}, u32[]{:S(2)}) collective-permute-start(bf16[2,8,128,128]{3,2,1,0:T(8,128)(2,1)S(1)} %get-tuple-element.133), channel_id=1, source_target_pairs={{1,0},{2,3},{5,4},{6,7},{9,8},{10,11},{13,12},{14,15},{17,16},{18,... | collective-permute-start | bytes 1572872 | tf_op jit(solution)/shard_map/ppermute | solution.py:494
  73.1 15.9 %collective-permute-start.20 = (bf16[528,128]{1,0:T(8,128)(2,1)S(1)}, bf16[528,128]{1,0:T(8,128)(2,1)S(1)}, u32[]{:S(2)}, u32[]{:S(2)}) collective-permute-start(bf16[528,128]{1,0:T(8,128)(2,1)S(1)} %get-tuple-element.138), channel_id=1, source_target_pairs={{0,8},{8,0},{16,24},{24,16},{1,9},{9,1},{17,25},{25,17},{2,10},{10... | collective-permute-start | bytes 405512 | tf_op jit(solution)/shard_map/ppermute | solution.py:34
  74.6 14.4 %collective-permute-start.21 = (bf16[528,128]{1,0:T(8,128)(2,1)S(1)}, bf16[528,128]{1,0:T(8,128)(2,1)S(1)}, u32[]{:S(2)}, u32[]{:S(2)}) collective-permute-start(bf16[528,128]{1,0:T(8,128)(2,1)S(1)} %get-tuple-element.139), channel_id=1, source_target_pairs={{0,16},{8,24},{16,0},{24,8},{1,17},{9,25},{17,1},{25,9},{2,18},{10... | collective-permute-start | bytes 405512 | tf_op jit(solution)/shard_map/ppermute | solution.py:34
  76.1 12.9 %collective-permute-start.22 = (bf16[528,128]{1,0:T(8,128)(2,1)S(1)}, bf16[528,128]{1,0:T(8,128)(2,1)S(1)}, u32[]{:S(2)}, u32[]{:S(2)}) collective-permute-start(bf16[528,128]{1,0:T(8,128)(2,1)S(1)} %get-tuple-element.139), channel_id=1, source_target_pairs={{0,24},{8,16},{16,8},{24,0},{1,25},{9,17},{17,9},{25,1},{2,26},{10... | collective-permute-start | bytes 405512 | tf_op jit(solution)/shard_map/ppermute | solution.py:34
  90.6 1.5 %collective-permute-start.25 = (bf16[2,4,128,128]{3,2,1,0:T(8,128)(2,1)S(1)}, bf16[2,4,128,128]{3,2,1,0:T(8,128)(2,1)S(1)}, u32[]{:S(2)}, u32[]{:S(2)}) collective-permute-start(bf16[2,4,128,128]{3,2,1,0:T(8,128)(2,1)S(1)} %get-tuple-element.151), channel_id=1, source_target_pairs={{0,4},{4,0},{1,5},{5,1},{2,6},{6,2},{3,7},{7,3},{8,12},{12,8},{9,1... | collective-permute-start | bytes 786440 | tf_op jit(solution)/shard_map/ppermute | solution.py:34

commit v8 on v7

--- a/solution.py
+++ b/solution.py
@@ -17,12 +17,12 @@
 SMEM = pl.BlockSpec(memory_space=pltpu.SMEM)
 HBM = pl.BlockSpec(memory_space=pltpu.HBM)
 LIMIT = 24 * 1024 * 1024
-COSTS = (0, 0, 0, 0, 0, 0, 16, 0, 0, 0, 0, 0, 0, 0, 0, 0, 0, 8, 0, 0, 0, 0, 0, 0, 0, 0, 0, 0)
+COSTS = (0, 0, 0, 0, 0, 16, 0, 0, 0, 0, 0, 0, 0, 0, 0, 0, 8, 0, 0, 4, 0, 0, 0, 0, 0, 0, 0)
 ORDER = (
-    "K1 K0 L3 A0"
-    " E1 O0 B0 L0"
+    "K0 K1 A0 E1"
+    " L3 O0 B0 L0"
     " O1 J2 L1 L2"
-    " J3 T0 O2 S0"
+    " J3 O2 T0 S0"
     " O3 T1 F2 P0"
     " S1 F3 W0 W2"
     " P1 W1 W3"
@@ -77,11 +77,33 @@
     return pl.ds(pl.multiple_of(head * DH, DH), DH)
 
 
+class Pieces:
+    def __init__(self, refs):
+        self.refs, self.each = refs, refs[0].shape[1]
+        self.count = self.each * len(refs)
+
+    def __getitem__(self, at):
+        side, i = at
+        return self.refs[i // self.each][side, i % self.each]
+
+
+def in_pieces(refs, counts):
+    starts = [sum(counts[:n]) for n in range(len(counts))]
+    return [Pieces(refs[a : a + n]) for a, n in zip(starts, counts)]
+
+
 def own_row(ref, at):
     return ref[pl.ds(at, 1), :]
 
 
-def label_kernel(ids, docs_ref, labels_ref, column_ref, row_ref):
+def label_kernel(ids, docs_hbm, labels_ref, column_ref, row_ref, docs_ref, sem):
+    copy = pltpu.make_async_copy(docs_hbm, docs_ref, sem.at[0])
+    copy.start()
+    copy.wait()
+    write_labels(ids, docs_ref, labels_ref, column_ref, row_ref)
+
+
+def write_labels(ids, docs_ref, labels_ref, column_ref, row_ref):
     docs = docs_ref[...]
     for k in range(DEPTH):
         row = docs[k : k + 1, :].astype(F32)
@@ -99,9 +121,9 @@
     return copies
 
 
-def add_terms(factor, part, docs_ref, c, q_ref, k_ref, v_ref, g_ref, outs, off, extra=None):
+def add_terms(factor, part, docs_ref, c, q_ref, k_ref, v_ref, g_ref, outs, offs, extra=None):
     in_first, in_last = document_masks(docs_ref[...])
-    for t, out in enumerate(outs):
+    for t, (out, off) in enumerate(zip(outs, offs)):
         for i in range(part):
             at = columns((c ^ t) * part + i)
             forward = transposed_dot(jnp.where(in_last, k_ref[:, at], 0), v_ref[:, at]) * factor
@@ -133,17 +155,21 @@
         for copy in waiting[s]:
             copy.wait()
         add_terms(
-            factor, part, docs_ref, ids[1], q_ref.at[s], k_ref.at[s], v_ref.at[s], g_ref.at[s], outs, s * part
+            factor, part, docs_ref, ids[1], q_ref.at[s], k_ref.at[s], v_ref.at[s], g_ref.at[s],
+            [outs[0]] + list(outs[1 + s :: len(places)]), [s * part] + [0] * (len(outs) // len(places)),
         )
 
 
 def lead_terms(
-    factor, unit, part, places, mates, outer, inner, ids, docs_ref, labels, q_hbm, k_hbm, v_hbm, g_hbm, carry_hbm, cot_hbm,
-    *refs,
+    factor, unit, part, places, mates, outer, inner, ids, docs_hbm, q_hbm, k_hbm, v_hbm, g_hbm, carry_hbm, cot_hbm, *refs,
 ):
-    outs, sent, (q_ref, k_ref, v_ref, g_ref, carry_ref, cot_ref, sems) = refs[:inner], refs[inner], refs[inner + 1 :]
+    outs, sent, labels, docs_ref, row_ref = refs[:inner], refs[inner], *refs[inner + 1 : inner + 4]
+    blocks_ref, q_ref, k_ref, v_ref, g_ref, carry_ref, sems = refs[inner + 4 :]
     o, c, z = ids[0], ids[1], ids[2]
-    waiting = [fetch([(carry_hbm, carry_ref), (cot_hbm, cot_ref)], sems.at[len(places)])]
+    _, side, at_end = place_of(ids)
+    copy = pltpu.make_async_copy(docs_hbm, blocks_ref, sems.at[len(places), 0])
+    copy.start()
+    waiting = []
     for s, (g, mate) in enumerate(zip(places, mates)):
         forward, backward = group_columns(g, unit), group_columns(mate, unit)
         waiting.append(fetch(
@@ -153,34 +179,45 @@
             ],
             sems.at[s],
         ))
-    for copy in waiting[0]:
-        copy.wait()
+
+    def carries(act):
+        for which, source in enumerate((carry_hbm, cot_hbm)):
+
+            @pl.when(side == which)
+            def _():
+                act(pltpu.make_async_copy(source, carry_ref, sems.at[len(places), 1 + which]))
+
+    carries(lambda copy: copy.start())
+    copy.wait()
+    write_labels(ids, blocks_ref, labels, docs_ref, row_ref)
     first, last = own_row(labels, z), own_row(labels, DEPTH + z)
     newest = labels[2 * DEPTH - 1 : 2 * DEPTH, :]
     opens, closes = jnp.logical_and(o == 0, c == 0), jnp.logical_and(o == outer - 1, c == inner - 1)
     for s in range(len(places)):
-        for copy in waiting[1 + s]:
+        for copy in waiting[s]:
             copy.wait()
+        if s == 0:
+            carries(lambda copy: copy.wait())
         open_f = flag(jnp.logical_and(jnp.logical_and(opens, z == s), last == 0.0))
         close_b = flag(jnp.logical_and(jnp.logical_and(closes, z == DEPTH - 1 - s), first == newest)) * factor
 
         def extra(place):
-            return open_f * carry_ref[place], close_b * cot_ref[place]
+            return open_f * carry_ref[place], close_b * carry_ref[place]
 
         add_terms(
-            factor, part, docs_ref, c, q_ref.at[s], k_ref.at[s], v_ref.at[s], g_ref.at[s], outs, s * part, extra
-        )
-    _, side, at_end = place_of(ids)
+            factor, part, docs_ref, c, q_ref.at[s], k_ref.at[s], v_ref.at[s], g_ref.at[s], outs, [s * part] * inner, extra
+        )
 
     @pl.when(at_end)
     def _():
         for t, term in enumerate(outs):
-            hop(side, edge_rows(z, labels, None), True, 0, part, term, None, None, 0, sent, t * part)
+            hop(side, edge_rows(z, labels, None), True, 0, part, term, None, 0, None, 0, sent, t * part)
 
     @pl.when(jnp.logical_not(at_end))
     def _():
+        scale = jnp.where(side == 0, 1.0, factor)
         for i in range(unit):
-            sent[0, i] = jnp.where(side == 0, carry_ref[i], cot_ref[i] * factor).astype(BF16)
+            sent[0, i] = (carry_ref[i] * scale).astype(BF16)
 
 
 def block_rows(labels, z, grouped):
@@ -189,10 +226,11 @@
     return [own_row(l, z) for l in labels], [own_row(l, DEPTH + z) for l in labels]
 
 
-def sum_kernel(inner, levels, grouped, ids, *refs):
-    labels, terms, outs = refs[:inner], refs[inner : 2 * inner], refs[2 * inner :]
+def sum_kernel(counts, levels, grouped, ids, *refs):
+    inner, behind = len(counts), len(counts) + sum(counts)
+    labels, terms, outs = refs[:inner], in_pieces(refs[inner:behind], counts), refs[behind:]
     o, z = ids[0], ids[2]
-    count = terms[0].shape[1]
+    count = terms[0].count
     newest = functools.reduce(jnp.maximum, [l[2 * DEPTH - 1 : 2 * DEPTH, :] for l in labels])
     oldest = functools.reduce(jnp.minimum, [l[0:1, :] for l in labels])
     firsts, lasts = block_rows(labels, z, grouped)
@@ -210,13 +248,14 @@
         out[count * DH :, :] = marks.astype(BF16)
 
 
-def prefix_kernel(factor, unit, part, places, mates, inner, outer, grouped, lacking, ids, carry_ref, cot_ref, *refs):
+def prefix_kernel(factor, unit, part, places, mates, counts, outer, grouped, lacking, ids, carry_ref, cot_ref, *refs):
     lacked, refs = (refs[0], refs[1:]) if lacking else (None, refs)
-    labels, terms, fans = refs[:inner], refs[inner : 2 * inner], refs[2 * inner : 2 * inner + outer - 1]
-    outs, edge_ref = refs[2 * inner + outer - 1 : -1], refs[-1]
+    inner, behind = len(counts), len(counts) + sum(counts)
+    labels, terms, fans = refs[:inner], in_pieces(refs[inner:behind], counts), refs[behind : behind + outer - 1]
+    outs, edge_ref = refs[behind + outer - 1 : -1], refs[-1]
     o, c, z = ids[0], ids[1], ids[2]
     held = carry_ref.shape[0]
-    count = terms[0].shape[1]
+    count = terms[0].count
     group_first, group_last = block_rows(labels, z, True)
     block_first, block_last = block_rows(labels, z, grouped)
     marks = [r[count * DH : count * DH + LABELS, :].astype(F32) for r in fans]
@@ -306,7 +345,7 @@
     return [jnp.where(which == 0, a, b) for a, b in zip(*rows)]
 
 
-def hop(side, rows, lead, off, part, term_ref, prefix_ref, got_ref, got_off, out, out_off):
+def hop(side, rows, lead, off, part, term_ref, prefix_ref, prefix_off, got_ref, got_off, out, out_off):
     own, neighbour, _, _, prior = pick(side, rows)
     other, _, final, _, _ = pick(1 - side, rows)
     join, keep, counts = flag(prior == own), flag(neighbour == own), flag(other == final)
@@ -315,8 +354,8 @@
         if lead:
             rest = counts * term_ref[1 - side, off + i].astype(F32)
         else:
-            state = state + join * prefix_ref[side, off + i].astype(F32)
-            rest = prefix_ref[1 - side, off + i].astype(F32)
+            state = state + join * prefix_ref[side, prefix_off + i].astype(F32)
+            rest = prefix_ref[1 - side, prefix_off + i].astype(F32)
         if got_ref is not None:
             state = state + keep * got_ref[0, got_off + i].astype(F32)
             rest = rest + got_ref[1, got_off + i].astype(F32)
@@ -330,13 +369,13 @@
     rows = edge_rows(z, labels, refs.pop(0) if has_edges else None)
 
     def take(plans):
-        return [(plan, refs.pop(0), None if plan[0] else refs.pop(0), refs.pop(0) if plan[2] is not None else None) for plan in plans]
+        return [(plan, refs.pop(0), None if plan[0] else refs.pop(0), refs.pop(0) if plan[3] is not None else None) for plan in plans]
 
     near, far = take(near), take(far)
 
     def write(side, entries):
-        for n, ((lead, off, got_off), term, prefix, got) in enumerate(entries):
-            hop(side, rows, lead, off, part, term, prefix, got, got_off, out, n * part)
+        for n, ((lead, off, prefix_off, got_off), term, prefix, got) in enumerate(entries):
+            hop(side, rows, lead, off, part, term, prefix, prefix_off, got, got_off, out, n * part)
 
     if near:
         pl.when(at_end)(lambda: write(side, near))
@@ -464,17 +503,14 @@
         return groups - 1 - g if leads else g
 
     ids = jnp.stack([lax.axis_index(a) for a in ("outer", "inner", "heads")]).astype(jnp.int32)
-    token, (own_labels, docs_column, docs_row) = call(
-        jnp.zeros((8, DH), F32),
-        label_kernel,
-        (ids, doc_ids.reshape(depth, SPAN)),
-        [
-            jax.ShapeDtypeStruct((2 * depth, DH), F32),
-            jax.ShapeDtypeStruct((SPAN, SPAN), F32),
-            jax.ShapeDtypeStruct((8, SPAN), F32),
-        ],
-    )
-    labels = [own_labels] + [pairs(own_labels, "inner", d) for d in range(1, inner)]
+    token = jnp.zeros((8, DH), F32)
+    doc_blocks = pltpu.with_memory_space_constraint(doc_ids.reshape(depth, SPAN), pltpu.HBM)
+    label_shapes = [
+        jax.ShapeDtypeStruct((2 * depth, DH), F32),
+        jax.ShapeDtypeStruct((SPAN, SPAN), F32),
+        jax.ShapeDtypeStruct((8, SPAN), F32),
+    ]
+    own_labels = docs_column = docs_row = labels = None
 
     levels = (outer - 1).bit_length()
 
@@ -490,11 +526,28 @@
     def exchange(own):
         return [own[0]] + [pairs(own[d], "inner", d) for d in range(1, inner)]
 
+    def exchange_pieces(own):
+        return [own[0]] + [[pairs(a, "inner", d) for a in own[d]] for d in range(1, inner)]
+
     def receive(units, kind, sent, perm):
         got = lax.ppermute(sent, "heads", perm)
         for n, u in enumerate(units):
             kind[u] = (got, n * part)
         return got
+
+    def take_labels(arrays):
+        nonlocal own_labels, docs_column, docs_row, labels
+        own_labels, docs_column, docs_row = arrays
+        labels = [own_labels] + [pairs(own_labels, "inner", d) for d in range(1, inner)]
+
+    def make_labels():
+        take_labels(run(
+            label_kernel,
+            (ids, doc_blocks),
+            label_shapes,
+            scratch=[pltpu.VMEM((depth, SPAN), jnp.int32), pltpu.SemaphoreType.DMA((1,))],
+            specs=[SMEM, HBM],
+        ))
 
     def run(*args, **options):
         nonlocal token
@@ -509,11 +562,12 @@
             functools.partial(
                 lead_terms, factor, unit, part, places, tuple(mate(g) for g in places), outer, inner
             ),
-            (ids, docs_column, own_labels) + far_arrays + far_carries,
-            [state_pair(part * leads)] * inner + [state_pair(unit)],
-            scratch=[block] * 4 + [carry] * 2 + [pltpu.SemaphoreType.DMA((leads + 1, 4))],
-            specs=[SMEM, VMEM, VMEM] + [HBM] * 6,
-        )
+            (ids, doc_blocks) + far_arrays + far_carries,
+            [state_pair(part * leads)] * inner + [state_pair(unit)] + label_shapes,
+            scratch=[pltpu.VMEM((depth, SPAN), jnp.int32)] + [block] * 4 + [carry, pltpu.SemaphoreType.DMA((leads + 1, 4))],
+            specs=[SMEM] + [HBM] * 7,
+        )
+        take_labels(own[inner + 1 :])
         for g in places:
             terms[g] = [(a, g * part) for a in own[:inner]]
         return receive([(0, t) for t in range(inner)], near, own[inner], [(0, 1), (3, 2), (1, 0), (2, 3)])
@@ -522,34 +576,36 @@
         own = run(
             functools.partial(rest_terms, factor, unit, part, places, tuple(mate(g) for g in places)),
             (ids, docs_column) + far_arrays,
-            [state_pair(part * len(places))] * inner,
+            [state_pair(part * len(places))] + [state_pair(part)] * (len(places) * (inner - 1)),
             scratch=[pltpu.VMEM((len(places), SPAN, unit * DH), BF16)] * 4
             + [pltpu.SemaphoreType.DMA((len(places), 4))],
             specs=[SMEM, VMEM] + [HBM] * 4,
         )
+        own = [own[:1]] + [own[1 + d * len(places) :][: len(places)] for d in range(inner - 1)]
         for s, g in enumerate(places):
-            terms[g] = [(a, s * part) for a in own]
-        return exchange(own)
+            terms[g] = [(own[0][0], s * part)] + [(a[s], 0) for a in own[1:]]
+        return exchange_pieces(own)
 
     def make_sums(received, grouped):
         nonlocal token
-        count = received[0].shape[1]
+        count = sum(a.shape[1] for a in received[0])
         sums = run(
-            functools.partial(sum_kernel, inner, levels, grouped),
-            (ids, *labels, *received),
+            functools.partial(sum_kernel, tuple(len(a) for a in received), levels, grouped),
+            (ids, *labels, *(a for pieces in received for a in pieces)),
             [jax.ShapeDtypeStruct((count * DH + LABELS, DH), BF16)] * levels,
         )
         return [pairs(sums[d.bit_length() - 1], "outer", d) for d in range(1, outer)]
 
     def make_prefixes(places, received, fans, grouped, lacked=None):
         nonlocal edge
-        count = received[0].shape[1]
+        count = sum(a.shape[1] for a in received[0])
         given = run(
             functools.partial(
-                prefix_kernel, factor, unit, part, places, tuple(mate(g) for g in places), inner, outer, grouped,
+                prefix_kernel, factor, unit, part, places, tuple(mate(g) for g in places),
+                tuple(len(a) for a in received), outer, grouped,
                 lacked is not None,
             ),
-            (ids, *carries, *([] if lacked is None else [lacked]), *labels, *received, *fans),
+            (ids, *carries, *([] if lacked is None else [lacked]), *labels, *(a for pieces in received for a in pieces), *fans),
             [state_pair(count)] * inner + [jax.ShapeDtypeStruct((8, DH), F32)],
         )
         edge = given[-1] if edge is None else edge
@@ -573,7 +629,7 @@
                     operands.append(prefixes[g][t][0])
                 if got is not None:
                     operands.append(got[u][0])
-                plans.append((lead, off, None if got is None else got[u][1]))
+                plans.append((lead, off, 0 if lead else prefixes[g][t][1], None if got is None else got[u][1]))
             return plans
 
         near_plans = plans_of(near_units, None)
@@ -643,7 +699,7 @@
             operands,
             [state_pair(part)] * inner,
         )
-        return exchange(totals)
+        return exchange_pieces([[a] for a in totals])
 
     def chunk(n):
         return [(n, t) for t in range(inner)] if n < leads else [(g, n - leads) for g in range(leads, groups)]
@@ -678,6 +734,7 @@
             "O": lambda g: across(chunk(g)),
             "F": lambda g: ends([], chunk(g)),
             "J": lambda g: ends(chunk(g), chunk(g - leads)),
+            "M": lambda g: ends(chunk(g), chunk(0)),
             "T": lambda g: keep(("totals", g), make_totals, g),
             "S": lead_sums,
             "P": lead_prefixes,
@@ -687,6 +744,7 @@
             steps[step[0]](int(step[1]))
     else:
         assert not leads
+        make_labels()
         places = tuple(range(groups))
         got = make_terms(places)
         make_prefixes(places, got, make_sums(got, False), False)

time: 101 us -> 99.2 us (0.982)
    ppermute x10, waiting for transfers between devices: 19.6 us -> 16.5 us  [receive(): got = lax.ppermute(sent, 'heads', perm)]
    ppermute x16 -> x17, waiting for transfers between devices: 6.64 us -> 9.73 us  [pairs(): return lax.ppermute(array, axis, [(i, i ^ distance) for i in range(count)])]
    pallas_call x28 -> x27, Pallas kernels: 36.8 us -> 36.2 us  [call(): pl.pallas_call(ordered, in_specs=list(specs or [SMEM] + [VMEM] * (count -...]
    ppermute x16 -> x17, starting transfers between devices: 12 us -> 12 us  [pairs(): return lax.ppermute(array, axis, [(i, i ^ distance) for i in range(count)])]
  transfers between devices with their start and end apart: 26 -> 27, of which waited for: 8 -> 7; matrix products, arithmetic and copies ran while one was open for 0% -> 0% of each run, Pallas kernels for 31% -> 31%
where the time goes in v8:
time: 99.2 us; the launch traced here: 98.9 us
  Pallas kernels  36.2 us (36%)
  starting transfers between devices  35.1 us (35%)
  waiting for transfers between devices  26.2 us (26%)
  between operations  1.22 us (1%)
    pallas_call x27, Pallas kernels, call(): pl.pallas_call(ordered, in_specs=list(specs or [SMEM] + [VMEM] * (count -...  36.2 us
    ppermute x10, starting transfers between devices, receive(): got = lax.ppermute(sent, 'heads', perm)  23.1 us
    ppermute x10, waiting for transfers between devices, receive(): got = lax.ppermute(sent, 'heads', perm)  16.5 us
    ppermute x17, starting transfers between devices, pairs(): return lax.ppermute(array, axis, [(i, i ^ distance) for i in range(count)])  12 us
    ppermute x17, waiting for transfers between devices, pairs(): return lax.ppermute(array, axis, [(i, i ^ distance) for i in range(count)])  9.73 us
  transfers between devices with their start and end apart: 27, of which 7 were waited for; matrix products, arithmetic and copies ran while one was open for 0% of the time, Pallas kernels for 31%

profile of v8, /device:TPU:0, one launch (start us, length us, event | category | flops | bytes accessed | tf_op | source)
XLA Modules:
  0.0 98.9 jit_solution(3977900079753356165)
XLA Ops:
  0.7 3.3 %shard_map.102 = (bf16[2,8,128,128]{3,2,1,0:T(8,128)(2,1)S(1)}, bf16[2,8,128,128]{3,2,1,0:T(8,128)(2,1)S(1)}, bf16[2,8,128,128]{3,2,1,0:T(8,128)(2,1)S(1)}, f32[...) custom-call(s32[3]{0:T(128)S(1)} %pad_add_fusion.refs_0_, ...), custom_call_target="tpu_custom_call", output_to_operand_aliasing={{6}: (8, {})} | custom-call | tf_op jit(solution)/shard_map/pallas_call | solution.py:59
  4.0 3.1 %collective-permute-start.6 = (bf16[2,8,128,128]{3,2,1,0:T(8,128)(2,1)S(1)}, bf16[2,8,128,128]{3,2,1,0:T(8,128)(2,1)S(1)}, u32[]{:S(2)}, u32[]{:S(2)}) collective-permute-start(bf16[2,8,128,128]{3,2,1,0:T(8,128)(2,1)S(1)} %get-tuple-element.95), channel_id=1, source_target_pairs={{0,1},{3,2},{1,0},{2,3},{4,5},{7,6},{5,4},{6,7},{8,9},{11,10},{9,8... | collective-permute-start | bytes 1572872 | tf_op jit(solution)/shard_map/ppermute | solution.py:533
  7.0 2.8 %shard_map.103 = (bf16[2,8,128,128]{3,2,1,0:T(8,128)(2,1)S(1)}, bf16[2,4,128,128]{3,2,1,0:T(8,128)(2,1)S(1)}, bf16[2,4,128,128]{3,2,1,0:T(8,128)(2,1)S(1)}, f32[8,128]{1,0:T(8,128)S(1)}) custom-call(s32[3]{0:T(128)S(1)} %pad_add_fusion.refs_0_, f32[128,128]{1,0:T(8,128)S(1)} %get-tuple-element.86.refs_1_.refs_0_.refs_3_, ...), custom_call_target="tpu_custom_call", output_to_operand_aliasing={{3}: (6, {})} | custom-call | tf_op jit(solution)/shard_map/pallas_call | solution.py:59
  10.5 1.3 %collective-permute-done.refs_2_.refs_4_.refs_5_ = f32[8,128]{1,0:T(8,128)S(1)} collective-permute-done((f32[8,128]{1,0:T(8,128)S(1)}, f32[8,128]{1,0:T(8,128)S(1)}, u32[]{:S(2)}, u32[]{:S(2)}) %collective-permute-start) | collective-permute-done | bytes 4128 | tf_op jit(solution)/shard_map/ppermute | solution.py:34
  11.8 0.8 shard_map.104
  12.6 1.6 %collective-permute-start.4 = (bf16[1040,128]{1,0:T(8,128)(2,1)S(1)}, bf16[1040,128]{1,0:T(8,128)(2,1)S(1)}, u32[]{:S(2)}, u32[]{:S(2)}) collective-permute-start(bf16[1040,128]{1,0:T(8,128)(2,1)S(1)} %get-tuple-element.93), channel_id=1, source_target_pairs={{0,16},{8,24},{16,0},{24,8},{1,17},{9,25},{17,1},{25,9},{2,18},{10... | collective-permute-start | bytes 798728 | tf_op jit(solution)/shard_map/ppermute | solution.py:34
  14.2 1.4 %collective-permute-start.5 = (bf16[1040,128]{1,0:T(8,128)(2,1)S(1)}, bf16[1040,128]{1,0:T(8,128)(2,1)S(1)}, u32[]{:S(2)}, u32[]{:S(2)}) collective-permute-start(bf16[1040,128]{1,0:T(8,128)(2,1)S(1)} %get-tuple-element.93), channel_id=1, source_target_pairs={{0,24},{8,16},{16,8},{24,0},{1,25},{9,17},{17,9},{25,1},{2,26},{10... | collective-permute-start | bytes 798728 | tf_op jit(solution)/shard_map/ppermute | solution.py:34
  16.2 0.6 shard_map.105
  16.8 1.9 %collective-permute-start.8 = (bf16[2,8,128,128]{3,2,1,0:T(8,128)(2,1)S(1)}, bf16[2,8,128,128]{3,2,1,0:T(8,128)(2,1)S(1)}, u32[]{:S(2)}, u32[]{:S(2)}) collective-permute-start(bf16[2,8,128,128]{3,2,1,0:T(8,128)(2,1)S(1)} %get-tuple-element.104), channel_id=1, source_target_pairs={{0,1},{3,2},{4,5},{7,6},{8,9},{11,10},{12,13},{15,14},{16,17},{19,... | collective-permute-start | bytes 1572872 | tf_op jit(solution)/shard_map/ppermute | solution.py:533
  18.8 2.0 %shard_map.106 = (f32[4,8,128,128]{3,2,1,0:T(8,128)S(1)}, f32[8,128]{1,0:T(8,128)S(1)}) custom-call(f32[128,128]{1,0:T(8,128)S(1)} %get-tuple-element.86.refs_1_.refs_0_.refs_3_, f32[8,128]{1,0:T(8,128)S(1)} %get-tuple-element.97.refs_1_, bf16[128,4096]{1,0:T(8,128)(2,1)S(1)} %copy-done, ...), custom_call_target="tpu_custom_call", output_to_operand_aliasing={{1}: (6, {})} | custom-call | tf_op jit(solution)/shard_map/pallas_call | solution.py:59
  20.8 0.6 shard_map.107
  21.3 0.7 collective-permute-start.10
  22.0 6.0 %collective-permute-done.3.refs_8_ = bf16[1040,128]{1,0:T(8,128)(2,1)S(1)} collective-permute-done((bf16[1040,128]{1,0:T(8,128)(2,1)S(1)}, bf16[1040,128]{1,0:T(8,128)(2,1)S(1)}, u32[]{:S(2)}, u32[]{:S(2)}) %collective-permute-start.3) | collective-permute-done | bytes 266272 | tf_op jit(solution)/shard_map/ppermute | solution.py:34
  28.1 1.5 %shard_map.108 = (bf16[2,8,128,128]{3,2,1,0:T(8,128)(2,1)S(1)}, bf16[2,8,128,128]{3,2,1,0:T(8,128)(2,1)S(1)}, f32[8,128]{1,0:T(8,128)S(1)}, f32[8,128]{1,0:T(8,128)S(1)}) custom-call(s32[3]{0:T(128)S(1)} %pad_add_fusion.refs_0_, f32[8,128,128]{2,1,0:T(8,128)S(1)} %copy-done.4, f32[8,128,128]{2,1,0:T(8,128)S(1)} %copy-done.5, ...), custom_call_target="tpu_custom_call", output_to_operand_aliasing={{3}: (11, {})} | custom-call | tf_op jit(solution)/shard_map/pallas_call | solution.py:59
  29.6 2.0 %shard_map.109 = (f32[4,8,128,128]{3,2,1,0:T(8,128)S(1)}, f32[8,128]{1,0:T(8,128)S(1)}) custom-call(f32[128,128]{1,0:T(8,128)S(1)} %get-tuple-element.86.refs_1_.refs_0_.refs_3_, f32[8,128]{1,0:T(8,128)S(1)} %get-tuple-element.97.refs_1_, bf16[128,4096]{1,0:T(8,128)(2,1)S(1)} %copy-done, ...), custom_call_target="tpu_custom_call", output_to_operand_aliasing={{1}: (6, {})} | custom-call | tf_op jit(solution)/shard_map/pallas_call | solution.py:59
  31.7 0.6 shard_map.110
  32.2 0.7 collective-permute-start.9
  32.9 0.6 shard_map.111
  33.6 4.8 %collective-permute-start.12 = (bf16[2,8,128,128]{3,2,1,0:T(8,128)(2,1)S(1)}, bf16[2,8,128,128]{3,2,1,0:T(8,128)(2,1)S(1)}, u32[]{:S(2)}, u32[]{:S(2)}) collective-permute-start(bf16[2,8,128,128]{3,2,1,0:T(8,128)(2,1)S(1)} %get-tuple-element.115), channel_id=1, source_target_pairs={{0,1},{3,2},{1,0},{2,3},{4,5},{7,6},{5,4},{6,7},{8,9},{11,10},{9,8... | collective-permute-start | bytes 1572872 | tf_op jit(solution)/shard_map/ppermute | solution.py:533
  38.3 2.0 %shard_map.112 = (f32[4,8,128,128]{3,2,1,0:T(8,128)S(1)}, f32[8,128]{1,0:T(8,128)S(1)}) custom-call(f32[128,128]{1,0:T(8,128)S(1)} %get-tuple-element.86.refs_1_.refs_0_.refs_3_, f32[8,128]{1,0:T(8,128)S(1)} %get-tuple-element.97.refs_1_, bf16[128,4096]{1,0:T(8,128)(2,1)S(1)} %copy-done, ...), custom_call_target="tpu_custom_call", output_to_operand_aliasing={{1}: (6, {})} | custom-call | tf_op jit(solution)/shard_map/pallas_call | solution.py:59
  40.3 2.0 %shard_map.113 = (f32[4,8,128,128]{3,2,1,0:T(8,128)S(1)}, f32[8,128]{1,0:T(8,128)S(1)}) custom-call(f32[128,128]{1,0:T(8,128)S(1)} %get-tuple-element.86.refs_1_.refs_0_.refs_3_, f32[8,128]{1,0:T(8,128)S(1)} %get-tuple-element.97.refs_1_, bf16[128,4096]{1,0:T(8,128)(2,1)S(1)} %copy-done, ...), custom_call_target="tpu_custom_call", output_to_operand_aliasing={{1}: (6, {})} | custom-call | tf_op jit(solution)/shard_map/pallas_call | solution.py:59
  42.3 0.6 shard_map.114
  43.0 7.8 %collective-permute-start.11 = (bf16[2,8,128,128]{3,2,1,0:T(8,128)(2,1)S(1)}, bf16[2,8,128,128]{3,2,1,0:T(8,128)(2,1)S(1)}, u32[]{:S(2)}, u32[]{:S(2)}) collective-permute-start(bf16[2,8,128,128]{3,2,1,0:T(8,128)(2,1)S(1)} %get-tuple-element.114), channel_id=1, source_target_pairs={{0,1},{3,2},{1,0},{2,3},{4,5},{7,6},{5,4},{6,7},{8,9},{11,10},{9,8... | collective-permute-start | bytes 1572872 | tf_op jit(solution)/shard_map/ppermute | solution.py:533
  51.4 0.7 shard_map.116
  52.2 0.7 collective-permute-start.19
  52.9 0.8 collective-permute-done.13.refs_4_.refs_6_
  53.7 0.7 shard_map.117
  54.4 1.6 %collective-permute-start.17 = (bf16[528,128]{1,0:T(8,128)(2,1)S(1)}, bf16[528,128]{1,0:T(8,128)(2,1)S(1)}, u32[]{:S(2)}, u32[]{:S(2)}) collective-permute-start(bf16[528,128]{1,0:T(8,128)(2,1)S(1)} %get-tuple-element.127), channel_id=1, source_target_pairs={{0,16},{8,24},{16,0},{24,8},{1,17},{9,25},{17,1},{25,9},{2,18},{10... | collective-permute-start | bytes 405512 | tf_op jit(solution)/shard_map/ppermute | solution.py:34
  56.0 1.4 %collective-permute-start.18 = (bf16[528,128]{1,0:T(8,128)(2,1)S(1)}, bf16[528,128]{1,0:T(8,128)(2,1)S(1)}, u32[]{:S(2)}, u32[]{:S(2)}) collective-permute-start(bf16[528,128]{1,0:T(8,128)(2,1)S(1)} %get-tuple-element.127), channel_id=1, source_target_pairs={{0,24},{8,16},{16,8},{24,0},{1,25},{9,17},{17,9},{25,1},{2,26},{10... | collective-permute-start | bytes 405512 | tf_op jit(solution)/shard_map/ppermute | solution.py:34
  57.9 4.8 %collective-permute-done.11.refs_5_.refs_8_.refs_9_.refs_11_.refs_15_.refs_19_.refs_23_.refs_13_.refs_17_.refs_21_ = bf16[2,8,128,128]{3,2,1,0:T(8,128)(2,1)S(1)} collective-permute-done((bf16[2,8,128,128]{3,2,1,0:T(8,128)(2,1)S(1)}, bf16[2,8,128,128]{3,2,1,0:T(8,128)(2,1)S(1)}, u32[]{:S(2)}, u32[]{:S(2)}) %collective-permute-start.11) | collective-permute-done | bytes 524320 | tf_op jit(solution)/shard_map/ppermute | solution.py:533
  63.3 0.7 collective-permute-start.14
  64.0 0.7 shard_map.119
  64.8 0.6 shard_map.120
  65.4 1.5 %collective-permute-start.24 = (bf16[2,8,128,128]{3,2,1,0:T(8,128)(2,1)S(1)}, bf16[2,8,128,128]{3,2,1,0:T(8,128)(2,1)S(1)}, u32[]{:S(2)}, u32[]{:S(2)}) collective-permute-start(bf16[2,8,128,128]{3,2,1,0:T(8,128)(2,1)S(1)} %get-tuple-element.140), channel_id=1, source_target_pairs={{1,0},{2,3},{5,4},{6,7},{9,8},{10,11},{13,12},{14,15},{17,16},{18,... | collective-permute-start | bytes 1572872 | tf_op jit(solution)/shard_map/ppermute | solution.py:533
  66.9 1.3 %shard_map.121 = (bf16[2,4,128,128]{3,2,1,0:T(8,128)(2,1)S(1)}, bf16[2,4,128,128]{3,2,1,0:T(8,128)(2,1)S(1)}, f32[8,128]{1,0:T(8,128)}, f32[8,128]{1,0:T(8,128)S(1)}) custom-call(s32[3]{0:T(128)S(1)} %pad_add_fusion.refs_0_, f32[8,128,128]{2,1,0:T(8,128)S(1)} %copy-done.4, f32[8,128,128]{2,1,0:T(8,128)S(1)} %copy-done.5, ...), custom_call_target="tpu_custom_call", output_to_operand_aliasing={{3}: (10, {})} | custom-call | flops 4000000000 | tf_op jit(solution)/shard_map/pallas_call | solution.py:59
  68.7 0.7 shard_map.122
  69.4 0.6 shard_map.123
  70.0 1.3 %collective-permute-start.20 = (bf16[2,8,128,128]{3,2,1,0:T(8,128)(2,1)S(1)}, bf16[2,8,128,128]{3,2,1,0:T(8,128)(2,1)S(1)}, u32[]{:S(2)}, u32[]{:S(2)}) collective-permute-start(bf16[2,8,128,128]{3,2,1,0:T(8,128)(2,1)S(1)} %get-tuple-element.133), channel_id=1, source_target_pairs={{1,0},{2,3},{5,4},{6,7},{9,8},{10,11},{13,12},{14,15},{17,16},{18,... | collective-permute-start | bytes 1572872 | tf_op jit(solution)/shard_map/ppermute | solution.py:533
  71.3 1.6 %collective-permute-start.21 = (bf16[528,128]{1,0:T(8,128)(2,1)S(1)}, bf16[528,128]{1,0:T(8,128)(2,1)S(1)}, u32[]{:S(2)}, u32[]{:S(2)}) collective-permute-start(bf16[528,128]{1,0:T(8,128)(2,1)S(1)} %get-tuple-element.138), channel_id=1, source_target_pairs={{0,8},{8,0},{16,24},{24,16},{1,9},{9,1},{17,25},{25,17},{2,10},{10... | collective-permute-start | bytes 405512 | tf_op jit(solution)/shard_map/ppermute | solution.py:34
  72.8 1.5 %collective-permute-start.22 = (bf16[528,128]{1,0:T(8,128)(2,1)S(1)}, bf16[528,128]{1,0:T(8,128)(2,1)S(1)}, u32[]{:S(2)}, u32[]{:S(2)}) collective-permute-start(bf16[528,128]{1,0:T(8,128)(2,1)S(1)} %get-tuple-element.139), channel_id=1, source_target_pairs={{0,16},{8,24},{16,0},{24,8},{1,17},{9,25},{17,1},{25,9},{2,18},{10... | collective-permute-start | bytes 405512 | tf_op jit(solution)/shard_map/ppermute | solution.py:34
  74.8 2.2 %shard_map.124 = (bf16[128,4096]{1,0:T(8,128)(2,1)}, bf16[128,4096]{1,0:T(8,128)(2,1)}, bf16[128,4096]{1,0:T(8,128)(2,1)}, bf16[128,4096]{1,0:T(8,128)(2,1)}, f32[8,128]{1,0:T(8,128)S(1)}) custom-call(s32[3]{0:T(128)S(1)} %pad_add_fusion.refs_0_, f32[8,128]{1,0:T(8,128)S(1)} %get-tuple-element.85.refs_1_.refs_3_.refs_4_, ...), custom_call_target="tpu_custom_call", output_to_operand_aliasing={{4}: (28, {})} | custom-call | tf_op jit(solution)/shard_map/pallas_call | solution.py:59
  77.1 8.3 %collective-permute-done.24.refs_11_.refs_15_.refs_19_.refs_23_ = bf16[2,8,128,128]{3,2,1,0:T(8,128)(2,1)S(1)} collective-permute-done((bf16[2,8,128,128]{3,2,1,0:T(8,128)(2,1)S(1)}, bf16[2,8,128,128]{3,2,1,0:T(8,128)(2,1)S(1)}, u32[]{:S(2)}, u32[]{:S(2)}) %collective-permute-start.24) | collective-permute-done | bytes 524320 | tf_op jit(solution)/shard_map/ppermute | solution.py:533
  85.4 2.3 %shard_map.125 = (bf16[128,4096]{1,0:T(8,128)(2,1)}, bf16[128,4096]{1,0:T(8,128)(2,1)}, bf16[128,4096]{1,0:T(8,128)(2,1)}, bf16[128,4096]{1,0:T(8,128)(2,1)}, f32[8,128]{1,0:T(8,128)S(1)}) custom-call(s32[3]{0:T(128)S(1)} %pad_add_fusion.refs_0_, ...), custom_call_target="tpu_custom_call", output_to_operand_aliasing={{0}: (28, {}), {1}: (29, {}), {2}: (30, {}), {3}: (31, {}),... | custom-call | tf_op jit(solution)/shard_map/pallas_call | solution.py:59
  87.7 1.6 %shard_map.126 = (bf16[2,4,128,128]{3,2,1,0:T(8,128)(2,1)S(1)}, bf16[2,4,128,128]{3,2,1,0:T(8,128)(2,1)S(1)}, f32[8,128]{1,0:T(8,128)}, f32[8,128]{1,0:T(8,128)S(1)}) custom-call(s32[3]{0:T(128)S(1)} %pad_add_fusion.refs_0_, f32[8,128,128]{2,1,0:T(8,128)S(1)} %copy-done.4, f32[8,128,128]{2,1,0:T(8,128)S(1)} %copy-done.5, ...), custom_call_target="tpu_custom_call", output_to_operand_aliasing={{3}: (11, {})} | custom-call | tf_op jit(solution)/shard_map/pallas_call | solution.py:59
  89.3 1.5 %collective-permute-done.26.refs_12_.refs_20_ = bf16[2,4,128,128]{3,2,1,0:T(8,128)(2,1)S(1)} collective-permute-done((bf16[2,4,128,128]{3,2,1,0:T(8,128)(2,1)S(1)}, bf16[2,4,128,128]{3,2,1,0:T(8,128)(2,1)S(1)}, u32[]{:S(2)}, u32[]{:S(2)}) %collective-permute-start.26) | collective-permute-done | bytes 262176 | tf_op jit(solution)/shard_map/ppermute | solution.py:34
  90.8 2.2 %shard_map.127 = (bf16[128,4096]{1,0:T(8,128)(2,1)}, bf16[128,4096]{1,0:T(8,128)(2,1)}, bf16[128,4096]{1,0:T(8,128)(2,1)}, bf16[128,4096]{1,0:T(8,128)(2,1)}, f32[8,128]{1,0:T(8,128)S(1)}) custom-call(s32[3]{0:T(128)S(1)} %pad_add_fusion.refs_0_, ...), custom_call_target="tpu_custom_call", output_to_operand_aliasing={{0}: (28, {}), {1}: (29, {}), {2}: (30, {}), {3}: (31, {}),... | custom-call | tf_op jit(solution)/shard_map/pallas_call | solution.py:59
  93.1 3.4 %collective-permute-done.20.refs_11_.refs_15_.refs_19_.refs_23_ = bf16[2,8,128,128]{3,2,1,0:T(8,128)(2,1)S(1)} collective-permute-done((bf16[2,8,128,128]{3,2,1,0:T(8,128)(2,1)S(1)}, bf16[2,8,128,128]{3,2,1,0:T(8,128)(2,1)S(1)}, u32[]{:S(2)}, u32[]{:S(2)}) %collective-permute-start.20) | collective-permute-done | bytes 524320 | tf_op jit(solution)/shard_map/ppermute | solution.py:533
  96.5 2.3 %shard_map.128 = (bf16[128,4096]{1,0:T(8,128)(2,1)}, bf16[128,4096]{1,0:T(8,128)(2,1)}, bf16[128,4096]{1,0:T(8,128)(2,1)}, bf16[128,4096]{1,0:T(8,128)(2,1)}, f32[8,128]{1,0:T(8,128)S(1)}) custom-call(s32[3]{0:T(128)S(1)} %pad_add_fusion.refs_0_, ...), custom_call_target="tpu_custom_call", output_to_operand_aliasing={{0}: (28, {}), {1}: (29, {}), {2}: (30, {}), {3}: (31, {}),... | custom-call | tf_op jit(solution)/shard_map/pallas_call | solution.py:59
  (47 shorter events, 4.2 us)
Async XLA Ops:
  4.0 16.8 %collective-permute-start.6 = (bf16[2,8,128,128]{3,2,1,0:T(8,128)(2,1)S(1)}, bf16[2,8,128,128]{3,2,1,0:T(8,128)(2,1)S(1)}, u32[]{:S(2)}, u32[]{:S(2)}) collective-permute-start(bf16[2,8,128,128]{3,2,1,0:T(8,128)(2,1)S(1)} %get-tuple-element.95), channel_id=1, source_target_pairs={{0,1},{3,2},{1,0},{2,3},{4,5},{7,6},{5,4},{6,7},{8,9},{11,10},{9,8... | collective-permute-start | bytes 1572872 | tf_op jit(solution)/shard_map/ppermute | solution.py:533
  7.0 11.7 %copy-start.2 = (bf16[128,4096]{1,0:T(8,128)(2,1)S(1)}, bf16[128,4096]{1,0:T(8,128)(2,1)}, u32[]{:S(2)}) copy-start(bf16[128,4096]{1,0:T(8,128)(2,1)} %refs_6_.9) | copy-start | bytes 3145732
  7.0 11.7 %copy-start.3 = (bf16[128,4096]{1,0:T(8,128)(2,1)S(1)}, bf16[128,4096]{1,0:T(8,128)(2,1)}, u32[]{:S(2)}) copy-start(bf16[128,4096]{1,0:T(8,128)(2,1)} %refs_7_.9) | copy-start | bytes 3145732
  9.8 8.9 %copy-start = (bf16[128,4096]{1,0:T(8,128)(2,1)S(1)}, bf16[128,4096]{1,0:T(8,128)(2,1)}, u32[]{:S(2)}) copy-start(bf16[128,4096]{1,0:T(8,128)(2,1)} %refs_4_.19) | copy-start | bytes 3145732
  9.8 8.9 %copy-start.1 = (bf16[128,4096]{1,0:T(8,128)(2,1)S(1)}, bf16[128,4096]{1,0:T(8,128)(2,1)}, u32[]{:S(2)}) copy-start(bf16[128,4096]{1,0:T(8,128)(2,1)} %refs_5_.19) | copy-start | bytes 3145732
  9.8 2.0 %collective-permute-start.1 = (bf16[2,4,128,128]{3,2,1,0:T(8,128)(2,1)S(1)}, bf16[2,4,128,128]{3,2,1,0:T(8,128)(2,1)S(1)}, u32[]{:S(2)}, u32[]{:S(2)}) collective-permute-start(bf16[2,4,128,128]{3,2,1,0:T(8,128)(2,1)S(1)} %get-tuple-element.89.refs_3_), channel_id=1, source_target_pairs={{0,4},{4,0},{1,5},{5,1},{2,6},{6,2},{3,7},{7,3},{8,12},{12,8},{9,1... | collective-permute-start | bytes 786440 | tf_op jit(solution)/shard_map/ppermute | solution.py:34
  9.9 1.9 %collective-permute-start.2 = (bf16[2,4,128,128]{3,2,1,0:T(8,128)(2,1)S(1)}, bf16[2,4,128,128]{3,2,1,0:T(8,128)(2,1)S(1)}, u32[]{:S(2)}, u32[]{:S(2)}) collective-permute-start(bf16[2,4,128,128]{3,2,1,0:T(8,128)(2,1)S(1)} %get-tuple-element.90.refs_5_.refs_6_), channel_id=1, source_target_pairs={{0,4},{4,0},{1,5},{5,1},{2,6},{6,2},{3,7},{7,3},{8,12},{12,8},{9,1... | collective-permute-start | bytes 786440 | tf_op jit(solution)/shard_map/ppermute | solution.py:34
  10.4 1.4 %collective-permute-start = (f32[8,128]{1,0:T(8,128)S(1)}, f32[8,128]{1,0:T(8,128)S(1)}, u32[]{:S(2)}, u32[]{:S(2)}) collective-permute-start(f32[8,128]{1,0:T(8,128)S(1)} %get-tuple-element.85.refs_1_.refs_3_.refs_4_), channel_id=1, source_target_pairs={{0,4},{4,0},{1,5},{5,1},{2,6},{6,2},{3,7},{7,3},{8,12},{12,8},{9,1... | collective-permute-start | bytes 12296 | tf_op jit(solution)/shard_map/ppermute | solution.py:34
  12.6 15.4 %collective-permute-start.4 = (bf16[1040,128]{1,0:T(8,128)(2,1)S(1)}, bf16[1040,128]{1,0:T(8,128)(2,1)S(1)}, u32[]{:S(2)}, u32[]{:S(2)}) collective-permute-start(bf16[1040,128]{1,0:T(8,128)(2,1)S(1)} %get-tuple-element.93), channel_id=1, source_target_pairs={{0,16},{8,24},{16,0},{24,8},{1,17},{9,25},{17,1},{25,9},{2,18},{10... | collective-permute-start | bytes 798728 | tf_op jit(solution)/shard_map/ppermute | solution.py:34
  14.2 13.9 %collective-permute-start.5 = (bf16[1040,128]{1,0:T(8,128)(2,1)S(1)}, bf16[1040,128]{1,0:T(8,128)(2,1)S(1)}, u32[]{:S(2)}, u32[]{:S(2)}) collective-permute-start(bf16[1040,128]{1,0:T(8,128)(2,1)S(1)} %get-tuple-element.93), channel_id=1, source_target_pairs={{0,24},{8,16},{16,8},{24,0},{1,25},{9,17},{17,9},{25,1},{2,26},{10... | collective-permute-start | bytes 798728 | tf_op jit(solution)/shard_map/ppermute | solution.py:34
  15.6 12.4 %collective-permute-start.3 = (bf16[1040,128]{1,0:T(8,128)(2,1)S(1)}, bf16[1040,128]{1,0:T(8,128)(2,1)S(1)}, u32[]{:S(2)}, u32[]{:S(2)}) collective-permute-start(bf16[1040,128]{1,0:T(8,128)(2,1)S(1)} %get-tuple-element.92), channel_id=1, source_target_pairs={{0,8},{8,0},{16,24},{24,16},{1,9},{9,1},{17,25},{25,17},{2,10},{10... | collective-permute-start | bytes 798728 | tf_op jit(solution)/shard_map/ppermute | solution.py:34
  16.8 14.9 %collective-permute-start.8 = (bf16[2,8,128,128]{3,2,1,0:T(8,128)(2,1)S(1)}, bf16[2,8,128,128]{3,2,1,0:T(8,128)(2,1)S(1)}, u32[]{:S(2)}, u32[]{:S(2)}) collective-permute-start(bf16[2,8,128,128]{3,2,1,0:T(8,128)(2,1)S(1)} %get-tuple-element.104), channel_id=1, source_target_pairs={{0,1},{3,2},{4,5},{7,6},{8,9},{11,10},{12,13},{15,14},{16,17},{19,... | collective-permute-start | bytes 1572872 | tf_op jit(solution)/shard_map/ppermute | solution.py:533
  20.7 7.3 %copy-start.4 = (f32[8,128,128]{2,1,0:T(8,128)S(1)}, f32[8,128,128]{2,1,0:T(8,128)}, u32[]{:S(2)}) copy-start(f32[8,128,128]{2,1,0:T(8,128)} %refs_1_.5) | copy-start | bytes 1572868
  20.8 7.3 %copy-start.5 = (f32[8,128,128]{2,1,0:T(8,128)S(1)}, f32[8,128,128]{2,1,0:T(8,128)}, u32[]{:S(2)}) copy-start(f32[8,128,128]{2,1,0:T(8,128)} %refs_2_.17) | copy-start | bytes 1572868
  21.3 11.6 %collective-permute-start.10 = (bf16[2,8,128,128]{3,2,1,0:T(8,128)(2,1)S(1)}, bf16[2,8,128,128]{3,2,1,0:T(8,128)(2,1)S(1)}, u32[]{:S(2)}, u32[]{:S(2)}) collective-permute-start(bf16[2,8,128,128]{3,2,1,0:T(8,128)(2,1)S(1)} %get-tuple-element.109), channel_id=1, source_target_pairs={{1,2},{2,1},{5,6},{6,5},{9,10},{10,9},{13,14},{14,13},{17,18},{18,... | collective-permute-start | bytes 1572872 | tf_op jit(solution)/shard_map/ppermute | solution.py:533
  31.6 10.7 %collective-permute-start.7 = (bf16[2,8,128,128]{3,2,1,0:T(8,128)(2,1)S(1)}, bf16[2,8,128,128]{3,2,1,0:T(8,128)(2,1)S(1)}, u32[]{:S(2)}, u32[]{:S(2)}) collective-permute-start(bf16[2,8,128,128]{3,2,1,0:T(8,128)(2,1)S(1)} %get-tuple-element.103), channel_id=1, source_target_pairs={{0,4},{4,0},{1,5},{5,1},{2,6},{6,2},{3,7},{7,3},{8,12},{12,8},{9,1... | collective-permute-start | bytes 1572872 | tf_op jit(solution)/shard_map/ppermute | solution.py:34
  32.2 10.1 %collective-permute-start.9 = (bf16[2,8,128,128]{3,2,1,0:T(8,128)(2,1)S(1)}, bf16[2,8,128,128]{3,2,1,0:T(8,128)(2,1)S(1)}, u32[]{:S(2)}, u32[]{:S(2)}) collective-permute-start(bf16[2,8,128,128]{3,2,1,0:T(8,128)(2,1)S(1)} %get-tuple-element.107), channel_id=1, source_target_pairs={{1,2},{2,1},{5,6},{6,5},{9,10},{10,9},{13,14},{14,13},{17,18},{18,... | collective-permute-start | bytes 1572872 | tf_op jit(solution)/shard_map/ppermute | solution.py:533
  33.6 17.2 %collective-permute-start.12 = (bf16[2,8,128,128]{3,2,1,0:T(8,128)(2,1)S(1)}, bf16[2,8,128,128]{3,2,1,0:T(8,128)(2,1)S(1)}, u32[]{:S(2)}, u32[]{:S(2)}) collective-permute-start(bf16[2,8,128,128]{3,2,1,0:T(8,128)(2,1)S(1)} %get-tuple-element.115), channel_id=1, source_target_pairs={{0,1},{3,2},{1,0},{2,3},{4,5},{7,6},{5,4},{6,7},{8,9},{11,10},{9,8... | collective-permute-start | bytes 1572872 | tf_op jit(solution)/shard_map/ppermute | solution.py:533
  43.0 19.8 %collective-permute-start.11 = (bf16[2,8,128,128]{3,2,1,0:T(8,128)(2,1)S(1)}, bf16[2,8,128,128]{3,2,1,0:T(8,128)(2,1)S(1)}, u32[]{:S(2)}, u32[]{:S(2)}) collective-permute-start(bf16[2,8,128,128]{3,2,1,0:T(8,128)(2,1)S(1)} %get-tuple-element.114), channel_id=1, source_target_pairs={{0,1},{3,2},{1,0},{2,3},{4,5},{7,6},{5,4},{6,7},{8,9},{11,10},{9,8... | collective-permute-start | bytes 1572872 | tf_op jit(solution)/shard_map/ppermute | solution.py:533
  52.1 1.6 %collective-permute-start.13 = (bf16[2,4,128,128]{3,2,1,0:T(8,128)(2,1)S(1)}, bf16[2,4,128,128]{3,2,1,0:T(8,128)(2,1)S(1)}, u32[]{:S(2)}, u32[]{:S(2)}) collective-permute-start(bf16[2,4,128,128]{3,2,1,0:T(8,128)(2,1)S(1)} %get-tuple-element.119), channel_id=1, source_target_pairs={{0,4},{4,0},{1,5},{5,1},{2,6},{6,2},{3,7},{7,3},{8,12},{12,8},{9,1... | collective-permute-start | bytes 786440 | tf_op jit(solution)/shard_map/ppermute | solution.py:34
  52.2 12.5 %collective-permute-start.19 = (bf16[2,8,128,128]{3,2,1,0:T(8,128)(2,1)S(1)}, bf16[2,8,128,128]{3,2,1,0:T(8,128)(2,1)S(1)}, u32[]{:S(2)}, u32[]{:S(2)}) collective-permute-start(bf16[2,8,128,128]{3,2,1,0:T(8,128)(2,1)S(1)} %get-tuple-element.128), channel_id=1, source_target_pairs={{1,2},{2,1},{5,6},{6,5},{9,10},{10,9},{13,14},{14,13},{17,18},{18,... | collective-permute-start | bytes 1572872 | tf_op jit(solution)/shard_map/ppermute | solution.py:533
  54.4 12.5 %collective-permute-start.17 = (bf16[528,128]{1,0:T(8,128)(2,1)S(1)}, bf16[528,128]{1,0:T(8,128)(2,1)S(1)}, u32[]{:S(2)}, u32[]{:S(2)}) collective-permute-start(bf16[528,128]{1,0:T(8,128)(2,1)S(1)} %get-tuple-element.127), channel_id=1, source_target_pairs={{0,16},{8,24},{16,0},{24,8},{1,17},{9,25},{17,1},{25,9},{2,18},{10... | collective-permute-start | bytes 405512 | tf_op jit(solution)/shard_map/ppermute | solution.py:34
  56.0 10.9 %collective-permute-start.18 = (bf16[528,128]{1,0:T(8,128)(2,1)S(1)}, bf16[528,128]{1,0:T(8,128)(2,1)S(1)}, u32[]{:S(2)}, u32[]{:S(2)}) collective-permute-start(bf16[528,128]{1,0:T(8,128)(2,1)S(1)} %get-tuple-element.127), channel_id=1, source_target_pairs={{0,24},{8,16},{16,8},{24,0},{1,25},{9,17},{17,9},{25,1},{2,26},{10... | collective-permute-start | bytes 405512 | tf_op jit(solution)/shard_map/ppermute | solution.py:34
  57.4 8.0 %collective-permute-start.16 = (bf16[528,128]{1,0:T(8,128)(2,1)S(1)}, bf16[528,128]{1,0:T(8,128)(2,1)S(1)}, u32[]{:S(2)}, u32[]{:S(2)}) collective-permute-start(bf16[528,128]{1,0:T(8,128)(2,1)S(1)} %get-tuple-element.126), channel_id=1, source_target_pairs={{0,8},{8,0},{16,24},{24,16},{1,9},{9,1},{17,25},{25,17},{2,10},{10... | collective-permute-start | bytes 405512 | tf_op jit(solution)/shard_map/ppermute | solution.py:34
  63.3 6.1 %collective-permute-start.14 = (bf16[2,8,128,128]{3,2,1,0:T(8,128)(2,1)S(1)}, bf16[2,8,128,128]{3,2,1,0:T(8,128)(2,1)S(1)}, u32[]{:S(2)}, u32[]{:S(2)}) collective-permute-start(bf16[2,8,128,128]{3,2,1,0:T(8,128)(2,1)S(1)} %get-tuple-element.122), channel_id=1, source_target_pairs={{1,2},{2,1},{5,6},{6,5},{9,10},{10,9},{13,14},{14,13},{17,18},{18,... | collective-permute-start | bytes 1572872 | tf_op jit(solution)/shard_map/ppermute | solution.py:533
  64.7 4.0 %collective-permute-start.15 = (bf16[2,4,128,128]{3,2,1,0:T(8,128)(2,1)S(1)}, bf16[2,4,128,128]{3,2,1,0:T(8,128)(2,1)S(1)}, u32[]{:S(2)}, u32[]{:S(2)}) collective-permute-start(bf16[2,4,128,128]{3,2,1,0:T(8,128)(2,1)S(1)} %get-tuple-element.125), channel_id=1, source_target_pairs={{0,4},{4,0},{1,5},{5,1},{2,6},{6,2},{3,7},{7,3},{8,12},{12,8},{9,1... | collective-permute-start | bytes 786440 | tf_op jit(solution)/shard_map/ppermute | solution.py:34
  65.4 20.0 %collective-permute-start.24 = (bf16[2,8,128,128]{3,2,1,0:T(8,128)(2,1)S(1)}, bf16[2,8,128,128]{3,2,1,0:T(8,128)(2,1)S(1)}, u32[]{:S(2)}, u32[]{:S(2)}) collective-permute-start(bf16[2,8,128,128]{3,2,1,0:T(8,128)(2,1)S(1)} %get-tuple-element.140), channel_id=1, source_target_pairs={{1,0},{2,3},{5,4},{6,7},{9,8},{10,11},{13,12},{14,15},{17,16},{18,... | collective-permute-start | bytes 1572872 | tf_op jit(solution)/shard_map/ppermute | solution.py:533
  68.2 6.1 %collective-permute-start.25 = (bf16[2,4,128,128]{3,2,1,0:T(8,128)(2,1)S(1)}, bf16[2,4,128,128]{3,2,1,0:T(8,128)(2,1)S(1)}, u32[]{:S(2)}, u32[]{:S(2)}) collective-permute-start(bf16[2,4,128,128]{3,2,1,0:T(8,128)(2,1)S(1)} %get-tuple-element.142), channel_id=1, source_target_pairs={{0,4},{4,0},{1,5},{5,1},{2,6},{6,2},{3,7},{7,3},{8,12},{12,8},{9,1... | collective-permute-start | bytes 786440 | tf_op jit(solution)/shard_map/ppermute | solution.py:34
  70.0 26.5 %collective-permute-start.20 = (bf16[2,8,128,128]{3,2,1,0:T(8,128)(2,1)S(1)}, bf16[2,8,128,128]{3,2,1,0:T(8,128)(2,1)S(1)}, u32[]{:S(2)}, u32[]{:S(2)}) collective-permute-start(bf16[2,8,128,128]{3,2,1,0:T(8,128)(2,1)S(1)} %get-tuple-element.133), channel_id=1, source_target_pairs={{1,0},{2,3},{5,4},{6,7},{9,8},{10,11},{13,12},{14,15},{17,16},{18,... | collective-permute-start | bytes 1572872 | tf_op jit(solution)/shard_map/ppermute | solution.py:533
  71.3 16.4 %collective-permute-start.21 = (bf16[528,128]{1,0:T(8,128)(2,1)S(1)}, bf16[528,128]{1,0:T(8,128)(2,1)S(1)}, u32[]{:S(2)}, u32[]{:S(2)}) collective-permute-start(bf16[528,128]{1,0:T(8,128)(2,1)S(1)} %get-tuple-element.138), channel_id=1, source_target_pairs={{0,8},{8,0},{16,24},{24,16},{1,9},{9,1},{17,25},{25,17},{2,10},{10... | collective-permute-start | bytes 405512 | tf_op jit(solution)/shard_map/ppermute | solution.py:34
  72.8 14.9 %collective-permute-start.22 = (bf16[528,128]{1,0:T(8,128)(2,1)S(1)}, bf16[528,128]{1,0:T(8,128)(2,1)S(1)}, u32[]{:S(2)}, u32[]{:S(2)}) collective-permute-start(bf16[528,128]{1,0:T(8,128)(2,1)S(1)} %get-tuple-element.139), channel_id=1, source_target_pairs={{0,16},{8,24},{16,0},{24,8},{1,17},{9,25},{17,1},{25,9},{2,18},{10... | collective-permute-start | bytes 405512 | tf_op jit(solution)/shard_map/ppermute | solution.py:34
  74.3 13.4 %collective-permute-start.23 = (bf16[528,128]{1,0:T(8,128)(2,1)S(1)}, bf16[528,128]{1,0:T(8,128)(2,1)S(1)}, u32[]{:S(2)}, u32[]{:S(2)}) collective-permute-start(bf16[528,128]{1,0:T(8,128)(2,1)S(1)} %get-tuple-element.139), channel_id=1, source_target_pairs={{0,24},{8,16},{16,8},{24,0},{1,25},{9,17},{17,9},{25,1},{2,26},{10... | collective-permute-start | bytes 405512 | tf_op jit(solution)/shard_map/ppermute | solution.py:34
  89.3 1.5 %collective-permute-start.26 = (bf16[2,4,128,128]{3,2,1,0:T(8,128)(2,1)S(1)}, bf16[2,4,128,128]{3,2,1,0:T(8,128)(2,1)S(1)}, u32[]{:S(2)}, u32[]{:S(2)}) collective-permute-start(bf16[2,4,128,128]{3,2,1,0:T(8,128)(2,1)S(1)} %get-tuple-element.151), channel_id=1, source_target_pairs={{0,4},{4,0},{1,5},{5,1},{2,6},{6,2},{3,7},{7,3},{8,12},{12,8},{9,1... | collective-permute-start | bytes 786440 | tf_op jit(solution)/shard_map/ppermute | solution.py:34

commit v9 on v8

--- a/solution.py
+++ b/solution.py
@@ -17,15 +17,15 @@
 SMEM = pl.BlockSpec(memory_space=pltpu.SMEM)
 HBM = pl.BlockSpec(memory_space=pltpu.HBM)
 LIMIT = 24 * 1024 * 1024
-COSTS = (0, 0, 0, 0, 0, 16, 0, 0, 0, 0, 0, 0, 0, 0, 0, 0, 8, 0, 0, 4, 0, 0, 0, 0, 0, 0, 0)
+COSTS = (0, 0, 0, 0, 0, 16, 0, 0, 0, 0, 0, 0, 0, 0, 0, 0, 8, 0, 0, 4, 0, 0, 0, 0, 4, 16, 0)
 ORDER = (
     "K0 K1 A0 E1"
     " L3 O0 B0 L0"
     " O1 J2 L1 L2"
     " J3 O2 T0 S0"
     " O3 T1 F2 P0"
-    " S1 F3 W0 W2"
-    " P1 W1 W3"
+    " S1 W0 F3 P1"
+    " W2 W1 W3"
 )
 
 

time: 99.2 us -> 99.2 us (level)
  no operation moved by 1% of the time
where the time goes in v9:
time: 99.2 us; the launch traced here: 98.9 us
  Pallas kernels  36.3 us (37%)
  starting transfers between devices  35.2 us (35%)
  waiting for transfers between devices  26.2 us (26%)
  between operations  1.21 us (1%)
    pallas_call x27, Pallas kernels, call(): pl.pallas_call(ordered, in_specs=list(specs or [SMEM] + [VMEM] * (count -...  36.3 us
    ppermute x10, starting transfers between devices, receive(): got = lax.ppermute(sent, 'heads', perm)  23.1 us
    ppermute x10, waiting for transfers between devices, receive(): got = lax.ppermute(sent, 'heads', perm)  16 us
    ppermute x17, starting transfers between devices, pairs(): return lax.ppermute(array, axis, [(i, i ^ distance) for i in range(count)])  12 us
    ppermute x17, waiting for transfers between devices, pairs(): return lax.ppermute(array, axis, [(i, i ^ distance) for i in range(count)])  10.2 us
  transfers between devices with their start and end apart: 27, of which 7 were waited for; matrix products, arithmetic and copies ran while one was open for 0% of the time, Pallas kernels for 31%

profile of v9, /device:TPU:0, one launch (start us, length us, event | category | flops | bytes accessed | tf_op | source)
XLA Modules:
  0.0 98.9 jit_solution(18421031270739718252)
XLA Ops:
  0.7 3.3 %shard_map.102 = (bf16[2,8,128,128]{3,2,1,0:T(8,128)(2,1)S(1)}, bf16[2,8,128,128]{3,2,1,0:T(8,128)(2,1)S(1)}, bf16[2,8,128,128]{3,2,1,0:T(8,128)(2,1)S(1)}, f32[...) custom-call(s32[3]{0:T(128)S(1)} %pad_add_fusion.refs_0_, ...), custom_call_target="tpu_custom_call", output_to_operand_aliasing={{6}: (8, {})} | custom-call | tf_op jit(solution)/shard_map/pallas_call | solution.py:59
  4.0 3.1 %collective-permute-start.6 = (bf16[2,8,128,128]{3,2,1,0:T(8,128)(2,1)S(1)}, bf16[2,8,128,128]{3,2,1,0:T(8,128)(2,1)S(1)}, u32[]{:S(2)}, u32[]{:S(2)}) collective-permute-start(bf16[2,8,128,128]{3,2,1,0:T(8,128)(2,1)S(1)} %get-tuple-element.95), channel_id=1, source_target_pairs={{0,1},{3,2},{1,0},{2,3},{4,5},{7,6},{5,4},{6,7},{8,9},{11,10},{9,8... | collective-permute-start | bytes 1572872 | tf_op jit(solution)/shard_map/ppermute | solution.py:533
  7.0 2.8 %shard_map.103 = (bf16[2,8,128,128]{3,2,1,0:T(8,128)(2,1)S(1)}, bf16[2,4,128,128]{3,2,1,0:T(8,128)(2,1)S(1)}, bf16[2,4,128,128]{3,2,1,0:T(8,128)(2,1)S(1)}, f32[8,128]{1,0:T(8,128)S(1)}) custom-call(s32[3]{0:T(128)S(1)} %pad_add_fusion.refs_0_, f32[128,128]{1,0:T(8,128)S(1)} %get-tuple-element.86.refs_1_.refs_0_.refs_3_, ...), custom_call_target="tpu_custom_call", output_to_operand_aliasing={{3}: (6, {})} | custom-call | tf_op jit(solution)/shard_map/pallas_call | solution.py:59
  10.5 1.3 %collective-permute-done.refs_2_.refs_4_.refs_5_ = f32[8,128]{1,0:T(8,128)S(1)} collective-permute-done((f32[8,128]{1,0:T(8,128)S(1)}, f32[8,128]{1,0:T(8,128)S(1)}, u32[]{:S(2)}, u32[]{:S(2)}) %collective-permute-start) | collective-permute-done | bytes 4128 | tf_op jit(solution)/shard_map/ppermute | solution.py:34
  11.8 0.8 shard_map.104
  12.6 1.6 %collective-permute-start.4 = (bf16[1040,128]{1,0:T(8,128)(2,1)S(1)}, bf16[1040,128]{1,0:T(8,128)(2,1)S(1)}, u32[]{:S(2)}, u32[]{:S(2)}) collective-permute-start(bf16[1040,128]{1,0:T(8,128)(2,1)S(1)} %get-tuple-element.93), channel_id=1, source_target_pairs={{0,16},{8,24},{16,0},{24,8},{1,17},{9,25},{17,1},{25,9},{2,18},{10... | collective-permute-start | bytes 798728 | tf_op jit(solution)/shard_map/ppermute | solution.py:34
  14.2 1.4 %collective-permute-start.5 = (bf16[1040,128]{1,0:T(8,128)(2,1)S(1)}, bf16[1040,128]{1,0:T(8,128)(2,1)S(1)}, u32[]{:S(2)}, u32[]{:S(2)}) collective-permute-start(bf16[1040,128]{1,0:T(8,128)(2,1)S(1)} %get-tuple-element.93), channel_id=1, source_target_pairs={{0,24},{8,16},{16,8},{24,0},{1,25},{9,17},{17,9},{25,1},{2,26},{10... | collective-permute-start | bytes 798728 | tf_op jit(solution)/shard_map/ppermute | solution.py:34
  16.2 0.6 shard_map.105
  16.8 1.9 %collective-permute-start.8 = (bf16[2,8,128,128]{3,2,1,0:T(8,128)(2,1)S(1)}, bf16[2,8,128,128]{3,2,1,0:T(8,128)(2,1)S(1)}, u32[]{:S(2)}, u32[]{:S(2)}) collective-permute-start(bf16[2,8,128,128]{3,2,1,0:T(8,128)(2,1)S(1)} %get-tuple-element.104), channel_id=1, source_target_pairs={{0,1},{3,2},{4,5},{7,6},{8,9},{11,10},{12,13},{15,14},{16,17},{19,... | collective-permute-start | bytes 1572872 | tf_op jit(solution)/shard_map/ppermute | solution.py:533
  18.8 2.0 %shard_map.106 = (f32[4,8,128,128]{3,2,1,0:T(8,128)S(1)}, f32[8,128]{1,0:T(8,128)S(1)}) custom-call(f32[128,128]{1,0:T(8,128)S(1)} %get-tuple-element.86.refs_1_.refs_0_.refs_3_, f32[8,128]{1,0:T(8,128)S(1)} %get-tuple-element.97.refs_1_, bf16[128,4096]{1,0:T(8,128)(2,1)S(1)} %copy-done, ...), custom_call_target="tpu_custom_call", output_to_operand_aliasing={{1}: (6, {})} | custom-call | tf_op jit(solution)/shard_map/pallas_call | solution.py:59
  20.8 0.6 shard_map.107
  21.3 0.7 collective-permute-start.10
  22.0 6.0 %collective-permute-done.3.refs_8_ = bf16[1040,128]{1,0:T(8,128)(2,1)S(1)} collective-permute-done((bf16[1040,128]{1,0:T(8,128)(2,1)S(1)}, bf16[1040,128]{1,0:T(8,128)(2,1)S(1)}, u32[]{:S(2)}, u32[]{:S(2)}) %collective-permute-start.3) | collective-permute-done | bytes 266272 | tf_op jit(solution)/shard_map/ppermute | solution.py:34
  28.1 1.5 %shard_map.108 = (bf16[2,8,128,128]{3,2,1,0:T(8,128)(2,1)S(1)}, bf16[2,8,128,128]{3,2,1,0:T(8,128)(2,1)S(1)}, f32[8,128]{1,0:T(8,128)S(1)}, f32[8,128]{1,0:T(8,128)S(1)}) custom-call(s32[3]{0:T(128)S(1)} %pad_add_fusion.refs_0_, f32[8,128,128]{2,1,0:T(8,128)S(1)} %copy-done.4, f32[8,128,128]{2,1,0:T(8,128)S(1)} %copy-done.5, ...), custom_call_target="tpu_custom_call", output_to_operand_aliasing={{3}: (11, {})} | custom-call | tf_op jit(solution)/shard_map/pallas_call | solution.py:59
  29.7 2.0 %shard_map.109 = (f32[4,8,128,128]{3,2,1,0:T(8,128)S(1)}, f32[8,128]{1,0:T(8,128)S(1)}) custom-call(f32[128,128]{1,0:T(8,128)S(1)} %get-tuple-element.86.refs_1_.refs_0_.refs_3_, f32[8,128]{1,0:T(8,128)S(1)} %get-tuple-element.97.refs_1_, bf16[128,4096]{1,0:T(8,128)(2,1)S(1)} %copy-done, ...), custom_call_target="tpu_custom_call", output_to_operand_aliasing={{1}: (6, {})} | custom-call | tf_op jit(solution)/shard_map/pallas_call | solution.py:59
  31.7 0.6 shard_map.110
  32.2 0.7 collective-permute-start.9
  32.9 0.6 shard_map.111
  33.6 4.8 %collective-permute-start.12 = (bf16[2,8,128,128]{3,2,1,0:T(8,128)(2,1)S(1)}, bf16[2,8,128,128]{3,2,1,0:T(8,128)(2,1)S(1)}, u32[]{:S(2)}, u32[]{:S(2)}) collective-permute-start(bf16[2,8,128,128]{3,2,1,0:T(8,128)(2,1)S(1)} %get-tuple-element.115), channel_id=1, source_target_pairs={{0,1},{3,2},{1,0},{2,3},{4,5},{7,6},{5,4},{6,7},{8,9},{11,10},{9,8... | collective-permute-start | bytes 1572872 | tf_op jit(solution)/shard_map/ppermute | solution.py:533
  38.3 2.0 %shard_map.112 = (f32[4,8,128,128]{3,2,1,0:T(8,128)S(1)}, f32[8,128]{1,0:T(8,128)S(1)}) custom-call(f32[128,128]{1,0:T(8,128)S(1)} %get-tuple-element.86.refs_1_.refs_0_.refs_3_, f32[8,128]{1,0:T(8,128)S(1)} %get-tuple-element.97.refs_1_, bf16[128,4096]{1,0:T(8,128)(2,1)S(1)} %copy-done, ...), custom_call_target="tpu_custom_call", output_to_operand_aliasing={{1}: (6, {})} | custom-call | tf_op jit(solution)/shard_map/pallas_call | solution.py:59
  40.3 2.0 %shard_map.113 = (f32[4,8,128,128]{3,2,1,0:T(8,128)S(1)}, f32[8,128]{1,0:T(8,128)S(1)}) custom-call(f32[128,128]{1,0:T(8,128)S(1)} %get-tuple-element.86.refs_1_.refs_0_.refs_3_, f32[8,128]{1,0:T(8,128)S(1)} %get-tuple-element.97.refs_1_, bf16[128,4096]{1,0:T(8,128)(2,1)S(1)} %copy-done, ...), custom_call_target="tpu_custom_call", output_to_operand_aliasing={{1}: (6, {})} | custom-call | tf_op jit(solution)/shard_map/pallas_call | solution.py:59
  42.3 0.6 shard_map.114
  43.0 7.8 %collective-permute-start.11 = (bf16[2,8,128,128]{3,2,1,0:T(8,128)(2,1)S(1)}, bf16[2,8,128,128]{3,2,1,0:T(8,128)(2,1)S(1)}, u32[]{:S(2)}, u32[]{:S(2)}) collective-permute-start(bf16[2,8,128,128]{3,2,1,0:T(8,128)(2,1)S(1)} %get-tuple-element.114), channel_id=1, source_target_pairs={{0,1},{3,2},{1,0},{2,3},{4,5},{7,6},{5,4},{6,7},{8,9},{11,10},{9,8... | collective-permute-start | bytes 1572872 | tf_op jit(solution)/shard_map/ppermute | solution.py:533
  51.4 0.7 shard_map.116
  52.2 0.7 collective-permute-start.18
  52.9 0.8 collective-permute-done.13.refs_4_.refs_6_
  53.7 0.7 shard_map.117
  54.4 1.6 %collective-permute-start.16 = (bf16[528,128]{1,0:T(8,128)(2,1)S(1)}, bf16[528,128]{1,0:T(8,128)(2,1)S(1)}, u32[]{:S(2)}, u32[]{:S(2)}) collective-permute-start(bf16[528,128]{1,0:T(8,128)(2,1)S(1)} %get-tuple-element.124), channel_id=1, source_target_pairs={{0,16},{8,24},{16,0},{24,8},{1,17},{9,25},{17,1},{25,9},{2,18},{10... | collective-permute-start | bytes 405512 | tf_op jit(solution)/shard_map/ppermute | solution.py:34
  56.0 1.4 %collective-permute-start.17 = (bf16[528,128]{1,0:T(8,128)(2,1)S(1)}, bf16[528,128]{1,0:T(8,128)(2,1)S(1)}, u32[]{:S(2)}, u32[]{:S(2)}) collective-permute-start(bf16[528,128]{1,0:T(8,128)(2,1)S(1)} %get-tuple-element.124), channel_id=1, source_target_pairs={{0,24},{8,16},{16,8},{24,0},{1,25},{9,17},{17,9},{25,1},{2,26},{10... | collective-permute-start | bytes 405512 | tf_op jit(solution)/shard_map/ppermute | solution.py:34
  58.0 4.8 %collective-permute-done.11.refs_5_.refs_8_.refs_9_.refs_11_.refs_15_.refs_19_.refs_23_.refs_13_.refs_17_.refs_21_ = bf16[2,8,128,128]{3,2,1,0:T(8,128)(2,1)S(1)} collective-permute-done((bf16[2,8,128,128]{3,2,1,0:T(8,128)(2,1)S(1)}, bf16[2,8,128,128]{3,2,1,0:T(8,128)(2,1)S(1)}, u32[]{:S(2)}, u32[]{:S(2)}) %collective-permute-start.11) | collective-permute-done | bytes 524320 | tf_op jit(solution)/shard_map/ppermute | solution.py:533
  63.3 0.7 collective-permute-start.14
  64.0 0.7 shard_map.119
  64.8 0.6 shard_map.120
  65.4 1.5 %collective-permute-start.26 = (bf16[2,8,128,128]{3,2,1,0:T(8,128)(2,1)S(1)}, bf16[2,8,128,128]{3,2,1,0:T(8,128)(2,1)S(1)}, u32[]{:S(2)}, u32[]{:S(2)}) collective-permute-start(bf16[2,8,128,128]{3,2,1,0:T(8,128)(2,1)S(1)} %get-tuple-element.146), channel_id=1, source_target_pairs={{1,0},{2,3},{5,4},{6,7},{9,8},{10,11},{13,12},{14,15},{17,16},{18,... | collective-permute-start | bytes 1572872 | tf_op jit(solution)/shard_map/ppermute | solution.py:533
  66.9 1.3 %shard_map.121 = (bf16[2,4,128,128]{3,2,1,0:T(8,128)(2,1)S(1)}, bf16[2,4,128,128]{3,2,1,0:T(8,128)(2,1)S(1)}, f32[8,128]{1,0:T(8,128)}, f32[8,128]{1,0:T(8,128)S(1)}) custom-call(s32[3]{0:T(128)S(1)} %pad_add_fusion.refs_0_, f32[8,128,128]{2,1,0:T(8,128)S(1)} %copy-done.4, f32[8,128,128]{2,1,0:T(8,128)S(1)} %copy-done.5, ...), custom_call_target="tpu_custom_call", output_to_operand_aliasing={{3}: (10, {})} | custom-call | flops 4000000000 | tf_op jit(solution)/shard_map/pallas_call | solution.py:59
  68.7 0.7 shard_map.122
  69.4 1.5 %collective-permute-start.22 = (bf16[528,128]{1,0:T(8,128)(2,1)S(1)}, bf16[528,128]{1,0:T(8,128)(2,1)S(1)}, u32[]{:S(2)}, u32[]{:S(2)}) collective-permute-start(bf16[528,128]{1,0:T(8,128)(2,1)S(1)} %get-tuple-element.141), channel_id=1, source_target_pairs={{0,8},{8,0},{16,24},{24,16},{1,9},{9,1},{17,25},{25,17},{2,10},{10... | collective-permute-start | bytes 405512 | tf_op jit(solution)/shard_map/ppermute | solution.py:34
  71.0 1.5 %collective-permute-start.23 = (bf16[528,128]{1,0:T(8,128)(2,1)S(1)}, bf16[528,128]{1,0:T(8,128)(2,1)S(1)}, u32[]{:S(2)}, u32[]{:S(2)}) collective-permute-start(bf16[528,128]{1,0:T(8,128)(2,1)S(1)} %get-tuple-element.142), channel_id=1, source_target_pairs={{0,16},{8,24},{16,0},{24,8},{1,17},{9,25},{17,1},{25,9},{2,18},{10... | collective-permute-start | bytes 405512 | tf_op jit(solution)/shard_map/ppermute | solution.py:34
  73.0 2.2 %shard_map.123 = (bf16[128,4096]{1,0:T(8,128)(2,1)}, bf16[128,4096]{1,0:T(8,128)(2,1)}, bf16[128,4096]{1,0:T(8,128)(2,1)}, bf16[128,4096]{1,0:T(8,128)(2,1)}, f32[8,128]{1,0:T(8,128)S(1)}) custom-call(s32[3]{0:T(128)S(1)} %pad_add_fusion.refs_0_, f32[8,128]{1,0:T(8,128)S(1)} %get-tuple-element.85.refs_1_.refs_3_.refs_4_, ...), custom_call_target="tpu_custom_call", output_to_operand_aliasing={{4}: (28, {})} | custom-call | tf_op jit(solution)/shard_map/pallas_call | solution.py:59
  75.2 0.6 shard_map.124
  75.8 1.3 %collective-permute-start.21 = (bf16[2,8,128,128]{3,2,1,0:T(8,128)(2,1)S(1)}, bf16[2,8,128,128]{3,2,1,0:T(8,128)(2,1)S(1)}, u32[]{:S(2)}, u32[]{:S(2)}) collective-permute-start(bf16[2,8,128,128]{3,2,1,0:T(8,128)(2,1)S(1)} %get-tuple-element.138), channel_id=1, source_target_pairs={{1,0},{2,3},{5,4},{6,7},{9,8},{10,11},{13,12},{14,15},{17,16},{18,... | collective-permute-start | bytes 1572872 | tf_op jit(solution)/shard_map/ppermute | solution.py:533
  77.1 2.0 %collective-permute-done.23.refs_9_ = bf16[528,128]{1,0:T(8,128)(2,1)S(1)} collective-permute-done((bf16[528,128]{1,0:T(8,128)(2,1)S(1)}, bf16[528,128]{1,0:T(8,128)(2,1)S(1)}, u32[]{:S(2)}, u32[]{:S(2)}) %collective-permute-start.23) | collective-permute-done | bytes 135200 | tf_op jit(solution)/shard_map/ppermute | solution.py:34
  79.1 1.6 %shard_map.125 = (bf16[2,4,128,128]{3,2,1,0:T(8,128)(2,1)S(1)}, bf16[2,4,128,128]{3,2,1,0:T(8,128)(2,1)S(1)}, f32[8,128]{1,0:T(8,128)}, f32[8,128]{1,0:T(8,128)S(1)}) custom-call(s32[3]{0:T(128)S(1)} %pad_add_fusion.refs_0_, f32[8,128,128]{2,1,0:T(8,128)S(1)} %copy-done.4, f32[8,128,128]{2,1,0:T(8,128)S(1)} %copy-done.5, ...), custom_call_target="tpu_custom_call", output_to_operand_aliasing={{3}: (11, {})} | custom-call | tf_op jit(solution)/shard_map/pallas_call | solution.py:59
  80.7 4.7 %collective-permute-done.26.refs_11_.refs_15_.refs_19_.refs_23_ = bf16[2,8,128,128]{3,2,1,0:T(8,128)(2,1)S(1)} collective-permute-done((bf16[2,8,128,128]{3,2,1,0:T(8,128)(2,1)S(1)}, bf16[2,8,128,128]{3,2,1,0:T(8,128)(2,1)S(1)}, u32[]{:S(2)}, u32[]{:S(2)}) %collective-permute-start.26) | collective-permute-done | bytes 524320 | tf_op jit(solution)/shard_map/ppermute | solution.py:533
  85.4 2.3 %shard_map.126 = (bf16[128,4096]{1,0:T(8,128)(2,1)}, bf16[128,4096]{1,0:T(8,128)(2,1)}, bf16[128,4096]{1,0:T(8,128)(2,1)}, bf16[128,4096]{1,0:T(8,128)(2,1)}, f32[8,128]{1,0:T(8,128)S(1)}) custom-call(s32[3]{0:T(128)S(1)} %pad_add_fusion.refs_0_, ...), custom_call_target="tpu_custom_call", output_to_operand_aliasing={{0}: (28, {}), {1}: (29, {}), {2}: (30, {}), {3}: (31, {}),... | custom-call | flops 4000000000 | tf_op jit(solution)/shard_map/pallas_call | solution.py:59
  87.7 2.3 %shard_map.127 = (bf16[128,4096]{1,0:T(8,128)(2,1)}, bf16[128,4096]{1,0:T(8,128)(2,1)}, bf16[128,4096]{1,0:T(8,128)(2,1)}, bf16[128,4096]{1,0:T(8,128)(2,1)}, f32[8,128]{1,0:T(8,128)S(1)}) custom-call(s32[3]{0:T(128)S(1)} %pad_add_fusion.refs_0_, ...), custom_call_target="tpu_custom_call", output_to_operand_aliasing={{0}: (28, {}), {1}: (29, {}), {2}: (30, {}), {3}: (31, {}),... | custom-call | flops 16000000000 | tf_op jit(solution)/shard_map/pallas_call | solution.py:59
  90.0 6.4 %collective-permute-done.21.refs_11_.refs_15_.refs_19_.refs_23_ = bf16[2,8,128,128]{3,2,1,0:T(8,128)(2,1)S(1)} collective-permute-done((bf16[2,8,128,128]{3,2,1,0:T(8,128)(2,1)S(1)}, bf16[2,8,128,128]{3,2,1,0:T(8,128)(2,1)S(1)}, u32[]{:S(2)}, u32[]{:S(2)}) %collective-permute-start.21) | collective-permute-done | bytes 524320 | tf_op jit(solution)/shard_map/ppermute | solution.py:533
  96.5 2.3 %shard_map.128 = (bf16[128,4096]{1,0:T(8,128)(2,1)}, bf16[128,4096]{1,0:T(8,128)(2,1)}, bf16[128,4096]{1,0:T(8,128)(2,1)}, bf16[128,4096]{1,0:T(8,128)(2,1)}, f32[8,128]{1,0:T(8,128)S(1)}) custom-call(s32[3]{0:T(128)S(1)} %pad_add_fusion.refs_0_, ...), custom_call_target="tpu_custom_call", output_to_operand_aliasing={{0}: (28, {}), {1}: (29, {}), {2}: (30, {}), {3}: (31, {}),... | custom-call | tf_op jit(solution)/shard_map/pallas_call | solution.py:59
  (47 shorter events, 4.2 us)
Async XLA Ops:
  4.0 16.8 %collective-permute-start.6 = (bf16[2,8,128,128]{3,2,1,0:T(8,128)(2,1)S(1)}, bf16[2,8,128,128]{3,2,1,0:T(8,128)(2,1)S(1)}, u32[]{:S(2)}, u32[]{:S(2)}) collective-permute-start(bf16[2,8,128,128]{3,2,1,0:T(8,128)(2,1)S(1)} %get-tuple-element.95), channel_id=1, source_target_pairs={{0,1},{3,2},{1,0},{2,3},{4,5},{7,6},{5,4},{6,7},{8,9},{11,10},{9,8... | collective-permute-start | bytes 1572872 | tf_op jit(solution)/shard_map/ppermute | solution.py:533
  7.0 11.7 %copy-start.2 = (bf16[128,4096]{1,0:T(8,128)(2,1)S(1)}, bf16[128,4096]{1,0:T(8,128)(2,1)}, u32[]{:S(2)}) copy-start(bf16[128,4096]{1,0:T(8,128)(2,1)} %refs_6_.9) | copy-start | bytes 3145732
  7.0 11.7 %copy-start.3 = (bf16[128,4096]{1,0:T(8,128)(2,1)S(1)}, bf16[128,4096]{1,0:T(8,128)(2,1)}, u32[]{:S(2)}) copy-start(bf16[128,4096]{1,0:T(8,128)(2,1)} %refs_7_.9) | copy-start | bytes 3145732
  9.8 8.9 %copy-start = (bf16[128,4096]{1,0:T(8,128)(2,1)S(1)}, bf16[128,4096]{1,0:T(8,128)(2,1)}, u32[]{:S(2)}) copy-start(bf16[128,4096]{1,0:T(8,128)(2,1)} %refs_4_.19) | copy-start | bytes 3145732
  9.8 8.9 %copy-start.1 = (bf16[128,4096]{1,0:T(8,128)(2,1)S(1)}, bf16[128,4096]{1,0:T(8,128)(2,1)}, u32[]{:S(2)}) copy-start(bf16[128,4096]{1,0:T(8,128)(2,1)} %refs_5_.19) | copy-start | bytes 3145732
  9.8 2.0 %collective-permute-start.1 = (bf16[2,4,128,128]{3,2,1,0:T(8,128)(2,1)S(1)}, bf16[2,4,128,128]{3,2,1,0:T(8,128)(2,1)S(1)}, u32[]{:S(2)}, u32[]{:S(2)}) collective-permute-start(bf16[2,4,128,128]{3,2,1,0:T(8,128)(2,1)S(1)} %get-tuple-element.89.refs_3_), channel_id=1, source_target_pairs={{0,4},{4,0},{1,5},{5,1},{2,6},{6,2},{3,7},{7,3},{8,12},{12,8},{9,1... | collective-permute-start | bytes 786440 | tf_op jit(solution)/shard_map/ppermute | solution.py:34
  9.9 1.9 %collective-permute-start.2 = (bf16[2,4,128,128]{3,2,1,0:T(8,128)(2,1)S(1)}, bf16[2,4,128,128]{3,2,1,0:T(8,128)(2,1)S(1)}, u32[]{:S(2)}, u32[]{:S(2)}) collective-permute-start(bf16[2,4,128,128]{3,2,1,0:T(8,128)(2,1)S(1)} %get-tuple-element.90.refs_5_.refs_6_), channel_id=1, source_target_pairs={{0,4},{4,0},{1,5},{5,1},{2,6},{6,2},{3,7},{7,3},{8,12},{12,8},{9,1... | collective-permute-start | bytes 786440 | tf_op jit(solution)/shard_map/ppermute | solution.py:34
  10.4 1.4 %collective-permute-start = (f32[8,128]{1,0:T(8,128)S(1)}, f32[8,128]{1,0:T(8,128)S(1)}, u32[]{:S(2)}, u32[]{:S(2)}) collective-permute-start(f32[8,128]{1,0:T(8,128)S(1)} %get-tuple-element.85.refs_1_.refs_3_.refs_4_), channel_id=1, source_target_pairs={{0,4},{4,0},{1,5},{5,1},{2,6},{6,2},{3,7},{7,3},{8,12},{12,8},{9,1... | collective-permute-start | bytes 12296 | tf_op jit(solution)/shard_map/ppermute | solution.py:34
  12.6 15.4 %collective-permute-start.4 = (bf16[1040,128]{1,0:T(8,128)(2,1)S(1)}, bf16[1040,128]{1,0:T(8,128)(2,1)S(1)}, u32[]{:S(2)}, u32[]{:S(2)}) collective-permute-start(bf16[1040,128]{1,0:T(8,128)(2,1)S(1)} %get-tuple-element.93), channel_id=1, source_target_pairs={{0,16},{8,24},{16,0},{24,8},{1,17},{9,25},{17,1},{25,9},{2,18},{10... | collective-permute-start | bytes 798728 | tf_op jit(solution)/shard_map/ppermute | solution.py:34
  14.2 13.9 %collective-permute-start.5 = (bf16[1040,128]{1,0:T(8,128)(2,1)S(1)}, bf16[1040,128]{1,0:T(8,128)(2,1)S(1)}, u32[]{:S(2)}, u32[]{:S(2)}) collective-permute-start(bf16[1040,128]{1,0:T(8,128)(2,1)S(1)} %get-tuple-element.93), channel_id=1, source_target_pairs={{0,24},{8,16},{16,8},{24,0},{1,25},{9,17},{17,9},{25,1},{2,26},{10... | collective-permute-start | bytes 798728 | tf_op jit(solution)/shard_map/ppermute | solution.py:34
  15.6 12.4 %collective-permute-start.3 = (bf16[1040,128]{1,0:T(8,128)(2,1)S(1)}, bf16[1040,128]{1,0:T(8,128)(2,1)S(1)}, u32[]{:S(2)}, u32[]{:S(2)}) collective-permute-start(bf16[1040,128]{1,0:T(8,128)(2,1)S(1)} %get-tuple-element.92), channel_id=1, source_target_pairs={{0,8},{8,0},{16,24},{24,16},{1,9},{9,1},{17,25},{25,17},{2,10},{10... | collective-permute-start | bytes 798728 | tf_op jit(solution)/shard_map/ppermute | solution.py:34
  16.8 14.9 %collective-permute-start.8 = (bf16[2,8,128,128]{3,2,1,0:T(8,128)(2,1)S(1)}, bf16[2,8,128,128]{3,2,1,0:T(8,128)(2,1)S(1)}, u32[]{:S(2)}, u32[]{:S(2)}) collective-permute-start(bf16[2,8,128,128]{3,2,1,0:T(8,128)(2,1)S(1)} %get-tuple-element.104), channel_id=1, source_target_pairs={{0,1},{3,2},{4,5},{7,6},{8,9},{11,10},{12,13},{15,14},{16,17},{19,... | collective-permute-start | bytes 1572872 | tf_op jit(solution)/shard_map/ppermute | solution.py:533
  20.7 7.3 %copy-start.4 = (f32[8,128,128]{2,1,0:T(8,128)S(1)}, f32[8,128,128]{2,1,0:T(8,128)}, u32[]{:S(2)}) copy-start(f32[8,128,128]{2,1,0:T(8,128)} %refs_1_.5) | copy-start | bytes 1572868
  20.8 7.3 %copy-start.5 = (f32[8,128,128]{2,1,0:T(8,128)S(1)}, f32[8,128,128]{2,1,0:T(8,128)}, u32[]{:S(2)}) copy-start(f32[8,128,128]{2,1,0:T(8,128)} %refs_2_.17) | copy-start | bytes 1572868
  21.3 11.6 %collective-permute-start.10 = (bf16[2,8,128,128]{3,2,1,0:T(8,128)(2,1)S(1)}, bf16[2,8,128,128]{3,2,1,0:T(8,128)(2,1)S(1)}, u32[]{:S(2)}, u32[]{:S(2)}) collective-permute-start(bf16[2,8,128,128]{3,2,1,0:T(8,128)(2,1)S(1)} %get-tuple-element.109), channel_id=1, source_target_pairs={{1,2},{2,1},{5,6},{6,5},{9,10},{10,9},{13,14},{14,13},{17,18},{18,... | collective-permute-start | bytes 1572872 | tf_op jit(solution)/shard_map/ppermute | solution.py:533
  29.6 12.7 %collective-permute-start.7 = (bf16[2,8,128,128]{3,2,1,0:T(8,128)(2,1)S(1)}, bf16[2,8,128,128]{3,2,1,0:T(8,128)(2,1)S(1)}, u32[]{:S(2)}, u32[]{:S(2)}) collective-permute-start(bf16[2,8,128,128]{3,2,1,0:T(8,128)(2,1)S(1)} %get-tuple-element.103), channel_id=1, source_target_pairs={{0,4},{4,0},{1,5},{5,1},{2,6},{6,2},{3,7},{7,3},{8,12},{12,8},{9,1... | collective-permute-start | bytes 1572872 | tf_op jit(solution)/shard_map/ppermute | solution.py:34
  32.2 10.1 %collective-permute-start.9 = (bf16[2,8,128,128]{3,2,1,0:T(8,128)(2,1)S(1)}, bf16[2,8,128,128]{3,2,1,0:T(8,128)(2,1)S(1)}, u32[]{:S(2)}, u32[]{:S(2)}) collective-permute-start(bf16[2,8,128,128]{3,2,1,0:T(8,128)(2,1)S(1)} %get-tuple-element.107), channel_id=1, source_target_pairs={{1,2},{2,1},{5,6},{6,5},{9,10},{10,9},{13,14},{14,13},{17,18},{18,... | collective-permute-start | bytes 1572872 | tf_op jit(solution)/shard_map/ppermute | solution.py:533
  33.6 17.2 %collective-permute-start.12 = (bf16[2,8,128,128]{3,2,1,0:T(8,128)(2,1)S(1)}, bf16[2,8,128,128]{3,2,1,0:T(8,128)(2,1)S(1)}, u32[]{:S(2)}, u32[]{:S(2)}) collective-permute-start(bf16[2,8,128,128]{3,2,1,0:T(8,128)(2,1)S(1)} %get-tuple-element.115), channel_id=1, source_target_pairs={{0,1},{3,2},{1,0},{2,3},{4,5},{7,6},{5,4},{6,7},{8,9},{11,10},{9,8... | collective-permute-start | bytes 1572872 | tf_op jit(solution)/shard_map/ppermute | solution.py:533
  43.0 19.8 %collective-permute-start.11 = (bf16[2,8,128,128]{3,2,1,0:T(8,128)(2,1)S(1)}, bf16[2,8,128,128]{3,2,1,0:T(8,128)(2,1)S(1)}, u32[]{:S(2)}, u32[]{:S(2)}) collective-permute-start(bf16[2,8,128,128]{3,2,1,0:T(8,128)(2,1)S(1)} %get-tuple-element.114), channel_id=1, source_target_pairs={{0,1},{3,2},{1,0},{2,3},{4,5},{7,6},{5,4},{6,7},{8,9},{11,10},{9,8... | collective-permute-start | bytes 1572872 | tf_op jit(solution)/shard_map/ppermute | solution.py:533
  52.1 1.6 %collective-permute-start.13 = (bf16[2,4,128,128]{3,2,1,0:T(8,128)(2,1)S(1)}, bf16[2,4,128,128]{3,2,1,0:T(8,128)(2,1)S(1)}, u32[]{:S(2)}, u32[]{:S(2)}) collective-permute-start(bf16[2,4,128,128]{3,2,1,0:T(8,128)(2,1)S(1)} %get-tuple-element.119), channel_id=1, source_target_pairs={{0,4},{4,0},{1,5},{5,1},{2,6},{6,2},{3,7},{7,3},{8,12},{12,8},{9,1... | collective-permute-start | bytes 786440 | tf_op jit(solution)/shard_map/ppermute | solution.py:34
  52.2 12.6 %collective-permute-start.18 = (bf16[2,8,128,128]{3,2,1,0:T(8,128)(2,1)S(1)}, bf16[2,8,128,128]{3,2,1,0:T(8,128)(2,1)S(1)}, u32[]{:S(2)}, u32[]{:S(2)}) collective-permute-start(bf16[2,8,128,128]{3,2,1,0:T(8,128)(2,1)S(1)} %get-tuple-element.125), channel_id=1, source_target_pairs={{1,2},{2,1},{5,6},{6,5},{9,10},{10,9},{13,14},{14,13},{17,18},{18,... | collective-permute-start | bytes 1572872 | tf_op jit(solution)/shard_map/ppermute | solution.py:533
  54.4 12.5 %collective-permute-start.16 = (bf16[528,128]{1,0:T(8,128)(2,1)S(1)}, bf16[528,128]{1,0:T(8,128)(2,1)S(1)}, u32[]{:S(2)}, u32[]{:S(2)}) collective-permute-start(bf16[528,128]{1,0:T(8,128)(2,1)S(1)} %get-tuple-element.124), channel_id=1, source_target_pairs={{0,16},{8,24},{16,0},{24,8},{1,17},{9,25},{17,1},{25,9},{2,18},{10... | collective-permute-start | bytes 405512 | tf_op jit(solution)/shard_map/ppermute | solution.py:34
  56.0 10.9 %collective-permute-start.17 = (bf16[528,128]{1,0:T(8,128)(2,1)S(1)}, bf16[528,128]{1,0:T(8,128)(2,1)S(1)}, u32[]{:S(2)}, u32[]{:S(2)}) collective-permute-start(bf16[528,128]{1,0:T(8,128)(2,1)S(1)} %get-tuple-element.124), channel_id=1, source_target_pairs={{0,24},{8,16},{16,8},{24,0},{1,25},{9,17},{17,9},{25,1},{2,26},{10... | collective-permute-start | bytes 405512 | tf_op jit(solution)/shard_map/ppermute | solution.py:34
  57.4 8.0 %collective-permute-start.15 = (bf16[528,128]{1,0:T(8,128)(2,1)S(1)}, bf16[528,128]{1,0:T(8,128)(2,1)S(1)}, u32[]{:S(2)}, u32[]{:S(2)}) collective-permute-start(bf16[528,128]{1,0:T(8,128)(2,1)S(1)} %get-tuple-element.123), channel_id=1, source_target_pairs={{0,8},{8,0},{16,24},{24,16},{1,9},{9,1},{17,25},{25,17},{2,10},{10... | collective-permute-start | bytes 405512 | tf_op jit(solution)/shard_map/ppermute | solution.py:34
  63.3 11.9 %collective-permute-start.14 = (bf16[2,8,128,128]{3,2,1,0:T(8,128)(2,1)S(1)}, bf16[2,8,128,128]{3,2,1,0:T(8,128)(2,1)S(1)}, u32[]{:S(2)}, u32[]{:S(2)}) collective-permute-start(bf16[2,8,128,128]{3,2,1,0:T(8,128)(2,1)S(1)} %get-tuple-element.122), channel_id=1, source_target_pairs={{1,2},{2,1},{5,6},{6,5},{9,10},{10,9},{13,14},{14,13},{17,18},{18,... | collective-permute-start | bytes 1572872 | tf_op jit(solution)/shard_map/ppermute | solution.py:533
  64.8 4.0 %collective-permute-start.20 = (bf16[2,4,128,128]{3,2,1,0:T(8,128)(2,1)S(1)}, bf16[2,4,128,128]{3,2,1,0:T(8,128)(2,1)S(1)}, u32[]{:S(2)}, u32[]{:S(2)}) collective-permute-start(bf16[2,4,128,128]{3,2,1,0:T(8,128)(2,1)S(1)} %get-tuple-element.134), channel_id=1, source_target_pairs={{0,4},{4,0},{1,5},{5,1},{2,6},{6,2},{3,7},{7,3},{8,12},{12,8},{9,1... | collective-permute-start | bytes 786440 | tf_op jit(solution)/shard_map/ppermute | solution.py:34
  65.4 20.0 %collective-permute-start.26 = (bf16[2,8,128,128]{3,2,1,0:T(8,128)(2,1)S(1)}, bf16[2,8,128,128]{3,2,1,0:T(8,128)(2,1)S(1)}, u32[]{:S(2)}, u32[]{:S(2)}) collective-permute-start(bf16[2,8,128,128]{3,2,1,0:T(8,128)(2,1)S(1)} %get-tuple-element.146), channel_id=1, source_target_pairs={{1,0},{2,3},{5,4},{6,7},{9,8},{10,11},{13,12},{14,15},{17,16},{18,... | collective-permute-start | bytes 1572872 | tf_op jit(solution)/shard_map/ppermute | solution.py:533
  68.2 4.2 %collective-permute-start.19 = (bf16[2,4,128,128]{3,2,1,0:T(8,128)(2,1)S(1)}, bf16[2,4,128,128]{3,2,1,0:T(8,128)(2,1)S(1)}, u32[]{:S(2)}, u32[]{:S(2)}) collective-permute-start(bf16[2,4,128,128]{3,2,1,0:T(8,128)(2,1)S(1)} %get-tuple-element.130), channel_id=1, source_target_pairs={{0,4},{4,0},{1,5},{5,1},{2,6},{6,2},{3,7},{7,3},{8,12},{12,8},{9,1... | collective-permute-start | bytes 786440 | tf_op jit(solution)/shard_map/ppermute | solution.py:34
  69.4 7.7 %collective-permute-start.22 = (bf16[528,128]{1,0:T(8,128)(2,1)S(1)}, bf16[528,128]{1,0:T(8,128)(2,1)S(1)}, u32[]{:S(2)}, u32[]{:S(2)}) collective-permute-start(bf16[528,128]{1,0:T(8,128)(2,1)S(1)} %get-tuple-element.141), channel_id=1, source_target_pairs={{0,8},{8,0},{16,24},{24,16},{1,9},{9,1},{17,25},{25,17},{2,10},{10... | collective-permute-start | bytes 405512 | tf_op jit(solution)/shard_map/ppermute | solution.py:34
  71.0 8.1 %collective-permute-start.23 = (bf16[528,128]{1,0:T(8,128)(2,1)S(1)}, bf16[528,128]{1,0:T(8,128)(2,1)S(1)}, u32[]{:S(2)}, u32[]{:S(2)}) collective-permute-start(bf16[528,128]{1,0:T(8,128)(2,1)S(1)} %get-tuple-element.142), channel_id=1, source_target_pairs={{0,16},{8,24},{16,0},{24,8},{1,17},{9,25},{17,1},{25,9},{2,18},{10... | collective-permute-start | bytes 405512 | tf_op jit(solution)/shard_map/ppermute | solution.py:34
  72.5 6.6 %collective-permute-start.24 = (bf16[528,128]{1,0:T(8,128)(2,1)S(1)}, bf16[528,128]{1,0:T(8,128)(2,1)S(1)}, u32[]{:S(2)}, u32[]{:S(2)}) collective-permute-start(bf16[528,128]{1,0:T(8,128)(2,1)S(1)} %get-tuple-element.142), channel_id=1, source_target_pairs={{0,24},{8,16},{16,8},{24,0},{1,25},{9,17},{17,9},{25,1},{2,26},{10... | collective-permute-start | bytes 405512 | tf_op jit(solution)/shard_map/ppermute | solution.py:34
  75.8 20.7 %collective-permute-start.21 = (bf16[2,8,128,128]{3,2,1,0:T(8,128)(2,1)S(1)}, bf16[2,8,128,128]{3,2,1,0:T(8,128)(2,1)S(1)}, u32[]{:S(2)}, u32[]{:S(2)}) collective-permute-start(bf16[2,8,128,128]{3,2,1,0:T(8,128)(2,1)S(1)} %get-tuple-element.138), channel_id=1, source_target_pairs={{1,0},{2,3},{5,4},{6,7},{9,8},{10,11},{13,12},{14,15},{17,16},{18,... | collective-permute-start | bytes 1572872 | tf_op jit(solution)/shard_map/ppermute | solution.py:533
  80.7 7.0 %collective-permute-start.25 = (bf16[2,4,128,128]{3,2,1,0:T(8,128)(2,1)S(1)}, bf16[2,4,128,128]{3,2,1,0:T(8,128)(2,1)S(1)}, u32[]{:S(2)}, u32[]{:S(2)}) collective-permute-start(bf16[2,4,128,128]{3,2,1,0:T(8,128)(2,1)S(1)} %get-tuple-element.145), channel_id=1, source_target_pairs={{0,4},{4,0},{1,5},{5,1},{2,6},{6,2},{3,7},{7,3},{8,12},{12,8},{9,1... | collective-permute-start | bytes 786440 | tf_op jit(solution)/shard_map/ppermute | solution.py:34

commit v10 on v8

--- a/solution.py
+++ b/solution.py
@@ -19,13 +19,13 @@
 LIMIT = 24 * 1024 * 1024
 COSTS = (0, 0, 0, 0, 0, 16, 0, 0, 0, 0, 0, 0, 0, 0, 0, 0, 8, 0, 0, 4, 0, 0, 0, 0, 0, 0, 0)
 ORDER = (
-    "K0 K1 A0 E1"
-    " L3 O0 B0 L0"
-    " O1 J2 L1 L2"
-    " J3 O2 T0 S0"
-    " O3 T1 F2 P0"
-    " S1 F3 W0 W2"
-    " P1 W1 W3"
+    "K0 K1 A0 E1",
+    "L3 O0 B0 L0",
+    "O1 J2 L1 L2",
+    "J3 O2 T0 S0",
+    "O3 T1 F2 P0",
+    "S1 F3 W0 W2",
+    "P1 W1 W3",
 )
 
 
@@ -740,7 +740,7 @@
             "P": lead_prefixes,
             "W": lambda g: make_outputs(halves_of(g)),
         }
-        for step in ORDER.split():
+        for step in [step for line in ORDER for step in line.split()]:
             steps[step[0]](int(step[1]))
     else:
         assert not leads

time: 99.2 us -> 99.2 us (level)
  no operation moved by 1% of the time
where the time goes in v10:
time: 99.2 us; the launch traced here: 98.9 us
  Pallas kernels  36.2 us (36%)
  starting transfers between devices  35.1 us (35%)
  waiting for transfers between devices  26.2 us (26%)
  between operations  1.22 us (1%)
    pallas_call x27, Pallas kernels, call(): pl.pallas_call(ordered, in_specs=list(specs or [SMEM] + [VMEM] * (count -...  36.2 us
    ppermute x10, starting transfers between devices, receive(): got = lax.ppermute(sent, 'heads', perm)  23.1 us
    ppermute x10, waiting for transfers between devices, receive(): got = lax.ppermute(sent, 'heads', perm)  16.5 us
    ppermute x17, starting transfers between devices, pairs(): return lax.ppermute(array, axis, [(i, i ^ distance) for i in range(count)])  12 us
    ppermute x17, waiting for transfers between devices, pairs(): return lax.ppermute(array, axis, [(i, i ^ distance) for i in range(count)])  9.73 us
  transfers between devices with their start and end apart: 27, of which 7 were waited for; matrix products, arithmetic and copies ran while one was open for 0% of the time, Pallas kernels for 31%

profile of v10, /device:TPU:0, one launch (start us, length us, event | category | flops | bytes accessed | tf_op | source)
XLA Modules:
  0.0 98.9 jit_solution(3977900079753356165)
XLA Ops:
  0.7 3.3 %shard_map.102 = (bf16[2,8,128,128]{3,2,1,0:T(8,128)(2,1)S(1)}, bf16[2,8,128,128]{3,2,1,0:T(8,128)(2,1)S(1)}, bf16[2,8,128,128]{3,2,1,0:T(8,128)(2,1)S(1)}, f32[...) custom-call(s32[3]{0:T(128)S(1)} %pad_add_fusion.refs_0_, ...), custom_call_target="tpu_custom_call", output_to_operand_aliasing={{6}: (8, {})} | custom-call | tf_op jit(solution)/shard_map/pallas_call | solution.py:59
  4.0 3.1 %collective-permute-start.6 = (bf16[2,8,128,128]{3,2,1,0:T(8,128)(2,1)S(1)}, bf16[2,8,128,128]{3,2,1,0:T(8,128)(2,1)S(1)}, u32[]{:S(2)}, u32[]{:S(2)}) collective-permute-start(bf16[2,8,128,128]{3,2,1,0:T(8,128)(2,1)S(1)} %get-tuple-element.95), channel_id=1, source_target_pairs={{0,1},{3,2},{1,0},{2,3},{4,5},{7,6},{5,4},{6,7},{8,9},{11,10},{9,8... | collective-permute-start | bytes 1572872 | tf_op jit(solution)/shard_map/ppermute | solution.py:533
  7.0 2.8 %shard_map.103 = (bf16[2,8,128,128]{3,2,1,0:T(8,128)(2,1)S(1)}, bf16[2,4,128,128]{3,2,1,0:T(8,128)(2,1)S(1)}, bf16[2,4,128,128]{3,2,1,0:T(8,128)(2,1)S(1)}, f32[8,128]{1,0:T(8,128)S(1)}) custom-call(s32[3]{0:T(128)S(1)} %pad_add_fusion.refs_0_, f32[128,128]{1,0:T(8,128)S(1)} %get-tuple-element.86.refs_1_.refs_0_.refs_3_, ...), custom_call_target="tpu_custom_call", output_to_operand_aliasing={{3}: (6, {})} | custom-call | tf_op jit(solution)/shard_map/pallas_call | solution.py:59
  10.5 1.3 %collective-permute-done.refs_2_.refs_4_.refs_5_ = f32[8,128]{1,0:T(8,128)S(1)} collective-permute-done((f32[8,128]{1,0:T(8,128)S(1)}, f32[8,128]{1,0:T(8,128)S(1)}, u32[]{:S(2)}, u32[]{:S(2)}) %collective-permute-start) | collective-permute-done | bytes 4128 | tf_op jit(solution)/shard_map/ppermute | solution.py:34
  11.8 0.8 shard_map.104
  12.6 1.6 %collective-permute-start.4 = (bf16[1040,128]{1,0:T(8,128)(2,1)S(1)}, bf16[1040,128]{1,0:T(8,128)(2,1)S(1)}, u32[]{:S(2)}, u32[]{:S(2)}) collective-permute-start(bf16[1040,128]{1,0:T(8,128)(2,1)S(1)} %get-tuple-element.93), channel_id=1, source_target_pairs={{0,16},{8,24},{16,0},{24,8},{1,17},{9,25},{17,1},{25,9},{2,18},{10... | collective-permute-start | bytes 798728 | tf_op jit(solution)/shard_map/ppermute | solution.py:34
  14.2 1.4 %collective-permute-start.5 = (bf16[1040,128]{1,0:T(8,128)(2,1)S(1)}, bf16[1040,128]{1,0:T(8,128)(2,1)S(1)}, u32[]{:S(2)}, u32[]{:S(2)}) collective-permute-start(bf16[1040,128]{1,0:T(8,128)(2,1)S(1)} %get-tuple-element.93), channel_id=1, source_target_pairs={{0,24},{8,16},{16,8},{24,0},{1,25},{9,17},{17,9},{25,1},{2,26},{10... | collective-permute-start | bytes 798728 | tf_op jit(solution)/shard_map/ppermute | solution.py:34
  16.2 0.6 shard_map.105
  16.8 1.9 %collective-permute-start.8 = (bf16[2,8,128,128]{3,2,1,0:T(8,128)(2,1)S(1)}, bf16[2,8,128,128]{3,2,1,0:T(8,128)(2,1)S(1)}, u32[]{:S(2)}, u32[]{:S(2)}) collective-permute-start(bf16[2,8,128,128]{3,2,1,0:T(8,128)(2,1)S(1)} %get-tuple-element.104), channel_id=1, source_target_pairs={{0,1},{3,2},{4,5},{7,6},{8,9},{11,10},{12,13},{15,14},{16,17},{19,... | collective-permute-start | bytes 1572872 | tf_op jit(solution)/shard_map/ppermute | solution.py:533
  18.8 2.0 %shard_map.106 = (f32[4,8,128,128]{3,2,1,0:T(8,128)S(1)}, f32[8,128]{1,0:T(8,128)S(1)}) custom-call(f32[128,128]{1,0:T(8,128)S(1)} %get-tuple-element.86.refs_1_.refs_0_.refs_3_, f32[8,128]{1,0:T(8,128)S(1)} %get-tuple-element.97.refs_1_, bf16[128,4096]{1,0:T(8,128)(2,1)S(1)} %copy-done, ...), custom_call_target="tpu_custom_call", output_to_operand_aliasing={{1}: (6, {})} | custom-call | tf_op jit(solution)/shard_map/pallas_call | solution.py:59
  20.8 0.6 shard_map.107
  21.3 0.7 collective-permute-start.10
  22.0 6.0 %collective-permute-done.3.refs_8_ = bf16[1040,128]{1,0:T(8,128)(2,1)S(1)} collective-permute-done((bf16[1040,128]{1,0:T(8,128)(2,1)S(1)}, bf16[1040,128]{1,0:T(8,128)(2,1)S(1)}, u32[]{:S(2)}, u32[]{:S(2)}) %collective-permute-start.3) | collective-permute-done | bytes 266272 | tf_op jit(solution)/shard_map/ppermute | solution.py:34
  28.1 1.5 %shard_map.108 = (bf16[2,8,128,128]{3,2,1,0:T(8,128)(2,1)S(1)}, bf16[2,8,128,128]{3,2,1,0:T(8,128)(2,1)S(1)}, f32[8,128]{1,0:T(8,128)S(1)}, f32[8,128]{1,0:T(8,128)S(1)}) custom-call(s32[3]{0:T(128)S(1)} %pad_add_fusion.refs_0_, f32[8,128,128]{2,1,0:T(8,128)S(1)} %copy-done.4, f32[8,128,128]{2,1,0:T(8,128)S(1)} %copy-done.5, ...), custom_call_target="tpu_custom_call", output_to_operand_aliasing={{3}: (11, {})} | custom-call | tf_op jit(solution)/shard_map/pallas_call | solution.py:59
  29.6 2.0 %shard_map.109 = (f32[4,8,128,128]{3,2,1,0:T(8,128)S(1)}, f32[8,128]{1,0:T(8,128)S(1)}) custom-call(f32[128,128]{1,0:T(8,128)S(1)} %get-tuple-element.86.refs_1_.refs_0_.refs_3_, f32[8,128]{1,0:T(8,128)S(1)} %get-tuple-element.97.refs_1_, bf16[128,4096]{1,0:T(8,128)(2,1)S(1)} %copy-done, ...), custom_call_target="tpu_custom_call", output_to_operand_aliasing={{1}: (6, {})} | custom-call | tf_op jit(solution)/shard_map/pallas_call | solution.py:59
  31.7 0.6 shard_map.110
  32.2 0.7 collective-permute-start.9
  32.9 0.6 shard_map.111
  33.6 4.8 %collective-permute-start.12 = (bf16[2,8,128,128]{3,2,1,0:T(8,128)(2,1)S(1)}, bf16[2,8,128,128]{3,2,1,0:T(8,128)(2,1)S(1)}, u32[]{:S(2)}, u32[]{:S(2)}) collective-permute-start(bf16[2,8,128,128]{3,2,1,0:T(8,128)(2,1)S(1)} %get-tuple-element.115), channel_id=1, source_target_pairs={{0,1},{3,2},{1,0},{2,3},{4,5},{7,6},{5,4},{6,7},{8,9},{11,10},{9,8... | collective-permute-start | bytes 1572872 | tf_op jit(solution)/shard_map/ppermute | solution.py:533
  38.3 2.0 %shard_map.112 = (f32[4,8,128,128]{3,2,1,0:T(8,128)S(1)}, f32[8,128]{1,0:T(8,128)S(1)}) custom-call(f32[128,128]{1,0:T(8,128)S(1)} %get-tuple-element.86.refs_1_.refs_0_.refs_3_, f32[8,128]{1,0:T(8,128)S(1)} %get-tuple-element.97.refs_1_, bf16[128,4096]{1,0:T(8,128)(2,1)S(1)} %copy-done, ...), custom_call_target="tpu_custom_call", output_to_operand_aliasing={{1}: (6, {})} | custom-call | tf_op jit(solution)/shard_map/pallas_call | solution.py:59
  40.3 2.0 %shard_map.113 = (f32[4,8,128,128]{3,2,1,0:T(8,128)S(1)}, f32[8,128]{1,0:T(8,128)S(1)}) custom-call(f32[128,128]{1,0:T(8,128)S(1)} %get-tuple-element.86.refs_1_.refs_0_.refs_3_, f32[8,128]{1,0:T(8,128)S(1)} %get-tuple-element.97.refs_1_, bf16[128,4096]{1,0:T(8,128)(2,1)S(1)} %copy-done, ...), custom_call_target="tpu_custom_call", output_to_operand_aliasing={{1}: (6, {})} | custom-call | tf_op jit(solution)/shard_map/pallas_call | solution.py:59
  42.3 0.6 shard_map.114
  43.0 7.8 %collective-permute-start.11 = (bf16[2,8,128,128]{3,2,1,0:T(8,128)(2,1)S(1)}, bf16[2,8,128,128]{3,2,1,0:T(8,128)(2,1)S(1)}, u32[]{:S(2)}, u32[]{:S(2)}) collective-permute-start(bf16[2,8,128,128]{3,2,1,0:T(8,128)(2,1)S(1)} %get-tuple-element.114), channel_id=1, source_target_pairs={{0,1},{3,2},{1,0},{2,3},{4,5},{7,6},{5,4},{6,7},{8,9},{11,10},{9,8... | collective-permute-start | bytes 1572872 | tf_op jit(solution)/shard_map/ppermute | solution.py:533
  51.4 0.7 shard_map.116
  52.2 0.7 collective-permute-start.19
  52.9 0.8 collective-permute-done.13.refs_4_.refs_6_
  53.7 0.7 shard_map.117
  54.4 1.6 %collective-permute-start.17 = (bf16[528,128]{1,0:T(8,128)(2,1)S(1)}, bf16[528,128]{1,0:T(8,128)(2,1)S(1)}, u32[]{:S(2)}, u32[]{:S(2)}) collective-permute-start(bf16[528,128]{1,0:T(8,128)(2,1)S(1)} %get-tuple-element.127), channel_id=1, source_target_pairs={{0,16},{8,24},{16,0},{24,8},{1,17},{9,25},{17,1},{25,9},{2,18},{10... | collective-permute-start | bytes 405512 | tf_op jit(solution)/shard_map/ppermute | solution.py:34
  56.0 1.4 %collective-permute-start.18 = (bf16[528,128]{1,0:T(8,128)(2,1)S(1)}, bf16[528,128]{1,0:T(8,128)(2,1)S(1)}, u32[]{:S(2)}, u32[]{:S(2)}) collective-permute-start(bf16[528,128]{1,0:T(8,128)(2,1)S(1)} %get-tuple-element.127), channel_id=1, source_target_pairs={{0,24},{8,16},{16,8},{24,0},{1,25},{9,17},{17,9},{25,1},{2,26},{10... | collective-permute-start | bytes 405512 | tf_op jit(solution)/shard_map/ppermute | solution.py:34
  57.9 4.8 %collective-permute-done.11.refs_5_.refs_8_.refs_9_.refs_11_.refs_15_.refs_19_.refs_23_.refs_13_.refs_17_.refs_21_ = bf16[2,8,128,128]{3,2,1,0:T(8,128)(2,1)S(1)} collective-permute-done((bf16[2,8,128,128]{3,2,1,0:T(8,128)(2,1)S(1)}, bf16[2,8,128,128]{3,2,1,0:T(8,128)(2,1)S(1)}, u32[]{:S(2)}, u32[]{:S(2)}) %collective-permute-start.11) | collective-permute-done | bytes 524320 | tf_op jit(solution)/shard_map/ppermute | solution.py:533
  63.3 0.7 collective-permute-start.14
  64.0 0.7 shard_map.119
  64.8 0.6 shard_map.120
  65.4 1.5 %collective-permute-start.24 = (bf16[2,8,128,128]{3,2,1,0:T(8,128)(2,1)S(1)}, bf16[2,8,128,128]{3,2,1,0:T(8,128)(2,1)S(1)}, u32[]{:S(2)}, u32[]{:S(2)}) collective-permute-start(bf16[2,8,128,128]{3,2,1,0:T(8,128)(2,1)S(1)} %get-tuple-element.140), channel_id=1, source_target_pairs={{1,0},{2,3},{5,4},{6,7},{9,8},{10,11},{13,12},{14,15},{17,16},{18,... | collective-permute-start | bytes 1572872 | tf_op jit(solution)/shard_map/ppermute | solution.py:533
  66.9 1.3 %shard_map.121 = (bf16[2,4,128,128]{3,2,1,0:T(8,128)(2,1)S(1)}, bf16[2,4,128,128]{3,2,1,0:T(8,128)(2,1)S(1)}, f32[8,128]{1,0:T(8,128)}, f32[8,128]{1,0:T(8,128)S(1)}) custom-call(s32[3]{0:T(128)S(1)} %pad_add_fusion.refs_0_, f32[8,128,128]{2,1,0:T(8,128)S(1)} %copy-done.4, f32[8,128,128]{2,1,0:T(8,128)S(1)} %copy-done.5, ...), custom_call_target="tpu_custom_call", output_to_operand_aliasing={{3}: (10, {})} | custom-call | flops 4000000000 | tf_op jit(solution)/shard_map/pallas_call | solution.py:59
  68.7 0.7 shard_map.122
  69.4 0.6 shard_map.123
  70.0 1.3 %collective-permute-start.20 = (bf16[2,8,128,128]{3,2,1,0:T(8,128)(2,1)S(1)}, bf16[2,8,128,128]{3,2,1,0:T(8,128)(2,1)S(1)}, u32[]{:S(2)}, u32[]{:S(2)}) collective-permute-start(bf16[2,8,128,128]{3,2,1,0:T(8,128)(2,1)S(1)} %get-tuple-element.133), channel_id=1, source_target_pairs={{1,0},{2,3},{5,4},{6,7},{9,8},{10,11},{13,12},{14,15},{17,16},{18,... | collective-permute-start | bytes 1572872 | tf_op jit(solution)/shard_map/ppermute | solution.py:533
  71.3 1.6 %collective-permute-start.21 = (bf16[528,128]{1,0:T(8,128)(2,1)S(1)}, bf16[528,128]{1,0:T(8,128)(2,1)S(1)}, u32[]{:S(2)}, u32[]{:S(2)}) collective-permute-start(bf16[528,128]{1,0:T(8,128)(2,1)S(1)} %get-tuple-element.138), channel_id=1, source_target_pairs={{0,8},{8,0},{16,24},{24,16},{1,9},{9,1},{17,25},{25,17},{2,10},{10... | collective-permute-start | bytes 405512 | tf_op jit(solution)/shard_map/ppermute | solution.py:34
  72.8 1.5 %collective-permute-start.22 = (bf16[528,128]{1,0:T(8,128)(2,1)S(1)}, bf16[528,128]{1,0:T(8,128)(2,1)S(1)}, u32[]{:S(2)}, u32[]{:S(2)}) collective-permute-start(bf16[528,128]{1,0:T(8,128)(2,1)S(1)} %get-tuple-element.139), channel_id=1, source_target_pairs={{0,16},{8,24},{16,0},{24,8},{1,17},{9,25},{17,1},{25,9},{2,18},{10... | collective-permute-start | bytes 405512 | tf_op jit(solution)/shard_map/ppermute | solution.py:34
  74.8 2.2 %shard_map.124 = (bf16[128,4096]{1,0:T(8,128)(2,1)}, bf16[128,4096]{1,0:T(8,128)(2,1)}, bf16[128,4096]{1,0:T(8,128)(2,1)}, bf16[128,4096]{1,0:T(8,128)(2,1)}, f32[8,128]{1,0:T(8,128)S(1)}) custom-call(s32[3]{0:T(128)S(1)} %pad_add_fusion.refs_0_, f32[8,128]{1,0:T(8,128)S(1)} %get-tuple-element.85.refs_1_.refs_3_.refs_4_, ...), custom_call_target="tpu_custom_call", output_to_operand_aliasing={{4}: (28, {})} | custom-call | tf_op jit(solution)/shard_map/pallas_call | solution.py:59
  77.1 8.3 %collective-permute-done.24.refs_11_.refs_15_.refs_19_.refs_23_ = bf16[2,8,128,128]{3,2,1,0:T(8,128)(2,1)S(1)} collective-permute-done((bf16[2,8,128,128]{3,2,1,0:T(8,128)(2,1)S(1)}, bf16[2,8,128,128]{3,2,1,0:T(8,128)(2,1)S(1)}, u32[]{:S(2)}, u32[]{:S(2)}) %collective-permute-start.24) | collective-permute-done | bytes 524320 | tf_op jit(solution)/shard_map/ppermute | solution.py:533
  85.4 2.3 %shard_map.125 = (bf16[128,4096]{1,0:T(8,128)(2,1)}, bf16[128,4096]{1,0:T(8,128)(2,1)}, bf16[128,4096]{1,0:T(8,128)(2,1)}, bf16[128,4096]{1,0:T(8,128)(2,1)}, f32[8,128]{1,0:T(8,128)S(1)}) custom-call(s32[3]{0:T(128)S(1)} %pad_add_fusion.refs_0_, ...), custom_call_target="tpu_custom_call", output_to_operand_aliasing={{0}: (28, {}), {1}: (29, {}), {2}: (30, {}), {3}: (31, {}),... | custom-call | tf_op jit(solution)/shard_map/pallas_call | solution.py:59
  87.7 1.6 %shard_map.126 = (bf16[2,4,128,128]{3,2,1,0:T(8,128)(2,1)S(1)}, bf16[2,4,128,128]{3,2,1,0:T(8,128)(2,1)S(1)}, f32[8,128]{1,0:T(8,128)}, f32[8,128]{1,0:T(8,128)S(1)}) custom-call(s32[3]{0:T(128)S(1)} %pad_add_fusion.refs_0_, f32[8,128,128]{2,1,0:T(8,128)S(1)} %copy-done.4, f32[8,128,128]{2,1,0:T(8,128)S(1)} %copy-done.5, ...), custom_call_target="tpu_custom_call", output_to_operand_aliasing={{3}: (11, {})} | custom-call | tf_op jit(solution)/shard_map/pallas_call | solution.py:59
  89.3 1.5 %collective-permute-done.26.refs_12_.refs_20_ = bf16[2,4,128,128]{3,2,1,0:T(8,128)(2,1)S(1)} collective-permute-done((bf16[2,4,128,128]{3,2,1,0:T(8,128)(2,1)S(1)}, bf16[2,4,128,128]{3,2,1,0:T(8,128)(2,1)S(1)}, u32[]{:S(2)}, u32[]{:S(2)}) %collective-permute-start.26) | collective-permute-done | bytes 262176 | tf_op jit(solution)/shard_map/ppermute | solution.py:34
  90.8 2.2 %shard_map.127 = (bf16[128,4096]{1,0:T(8,128)(2,1)}, bf16[128,4096]{1,0:T(8,128)(2,1)}, bf16[128,4096]{1,0:T(8,128)(2,1)}, bf16[128,4096]{1,0:T(8,128)(2,1)}, f32[8,128]{1,0:T(8,128)S(1)}) custom-call(s32[3]{0:T(128)S(1)} %pad_add_fusion.refs_0_, ...), custom_call_target="tpu_custom_call", output_to_operand_aliasing={{0}: (28, {}), {1}: (29, {}), {2}: (30, {}), {3}: (31, {}),... | custom-call | tf_op jit(solution)/shard_map/pallas_call | solution.py:59
  93.1 3.4 %collective-permute-done.20.refs_11_.refs_15_.refs_19_.refs_23_ = bf16[2,8,128,128]{3,2,1,0:T(8,128)(2,1)S(1)} collective-permute-done((bf16[2,8,128,128]{3,2,1,0:T(8,128)(2,1)S(1)}, bf16[2,8,128,128]{3,2,1,0:T(8,128)(2,1)S(1)}, u32[]{:S(2)}, u32[]{:S(2)}) %collective-permute-start.20) | collective-permute-done | bytes 524320 | tf_op jit(solution)/shard_map/ppermute | solution.py:533
  96.5 2.3 %shard_map.128 = (bf16[128,4096]{1,0:T(8,128)(2,1)}, bf16[128,4096]{1,0:T(8,128)(2,1)}, bf16[128,4096]{1,0:T(8,128)(2,1)}, bf16[128,4096]{1,0:T(8,128)(2,1)}, f32[8,128]{1,0:T(8,128)S(1)}) custom-call(s32[3]{0:T(128)S(1)} %pad_add_fusion.refs_0_, ...), custom_call_target="tpu_custom_call", output_to_operand_aliasing={{0}: (28, {}), {1}: (29, {}), {2}: (30, {}), {3}: (31, {}),... | custom-call | tf_op jit(solution)/shard_map/pallas_call | solution.py:59
  (47 shorter events, 4.2 us)
Async XLA Ops:
  4.0 16.8 %collective-permute-start.6 = (bf16[2,8,128,128]{3,2,1,0:T(8,128)(2,1)S(1)}, bf16[2,8,128,128]{3,2,1,0:T(8,128)(2,1)S(1)}, u32[]{:S(2)}, u32[]{:S(2)}) collective-permute-start(bf16[2,8,128,128]{3,2,1,0:T(8,128)(2,1)S(1)} %get-tuple-element.95), channel_id=1, source_target_pairs={{0,1},{3,2},{1,0},{2,3},{4,5},{7,6},{5,4},{6,7},{8,9},{11,10},{9,8... | collective-permute-start | bytes 1572872 | tf_op jit(solution)/shard_map/ppermute | solution.py:533
  7.0 11.7 %copy-start.2 = (bf16[128,4096]{1,0:T(8,128)(2,1)S(1)}, bf16[128,4096]{1,0:T(8,128)(2,1)}, u32[]{:S(2)}) copy-start(bf16[128,4096]{1,0:T(8,128)(2,1)} %refs_6_.9) | copy-start | bytes 3145732
  7.0 11.7 %copy-start.3 = (bf16[128,4096]{1,0:T(8,128)(2,1)S(1)}, bf16[128,4096]{1,0:T(8,128)(2,1)}, u32[]{:S(2)}) copy-start(bf16[128,4096]{1,0:T(8,128)(2,1)} %refs_7_.9) | copy-start | bytes 3145732
  9.8 8.9 %copy-start = (bf16[128,4096]{1,0:T(8,128)(2,1)S(1)}, bf16[128,4096]{1,0:T(8,128)(2,1)}, u32[]{:S(2)}) copy-start(bf16[128,4096]{1,0:T(8,128)(2,1)} %refs_4_.19) | copy-start | bytes 3145732
  9.8 8.9 %copy-start.1 = (bf16[128,4096]{1,0:T(8,128)(2,1)S(1)}, bf16[128,4096]{1,0:T(8,128)(2,1)}, u32[]{:S(2)}) copy-start(bf16[128,4096]{1,0:T(8,128)(2,1)} %refs_5_.19) | copy-start | bytes 3145732
  9.8 2.0 %collective-permute-start.1 = (bf16[2,4,128,128]{3,2,1,0:T(8,128)(2,1)S(1)}, bf16[2,4,128,128]{3,2,1,0:T(8,128)(2,1)S(1)}, u32[]{:S(2)}, u32[]{:S(2)}) collective-permute-start(bf16[2,4,128,128]{3,2,1,0:T(8,128)(2,1)S(1)} %get-tuple-element.89.refs_3_), channel_id=1, source_target_pairs={{0,4},{4,0},{1,5},{5,1},{2,6},{6,2},{3,7},{7,3},{8,12},{12,8},{9,1... | collective-permute-start | bytes 786440 | tf_op jit(solution)/shard_map/ppermute | solution.py:34
  9.9 1.9 %collective-permute-start.2 = (bf16[2,4,128,128]{3,2,1,0:T(8,128)(2,1)S(1)}, bf16[2,4,128,128]{3,2,1,0:T(8,128)(2,1)S(1)}, u32[]{:S(2)}, u32[]{:S(2)}) collective-permute-start(bf16[2,4,128,128]{3,2,1,0:T(8,128)(2,1)S(1)} %get-tuple-element.90.refs_5_.refs_6_), channel_id=1, source_target_pairs={{0,4},{4,0},{1,5},{5,1},{2,6},{6,2},{3,7},{7,3},{8,12},{12,8},{9,1... | collective-permute-start | bytes 786440 | tf_op jit(solution)/shard_map/ppermute | solution.py:34
  10.4 1.4 %collective-permute-start = (f32[8,128]{1,0:T(8,128)S(1)}, f32[8,128]{1,0:T(8,128)S(1)}, u32[]{:S(2)}, u32[]{:S(2)}) collective-permute-start(f32[8,128]{1,0:T(8,128)S(1)} %get-tuple-element.85.refs_1_.refs_3_.refs_4_), channel_id=1, source_target_pairs={{0,4},{4,0},{1,5},{5,1},{2,6},{6,2},{3,7},{7,3},{8,12},{12,8},{9,1... | collective-permute-start | bytes 12296 | tf_op jit(solution)/shard_map/ppermute | solution.py:34
  12.6 15.4 %collective-permute-start.4 = (bf16[1040,128]{1,0:T(8,128)(2,1)S(1)}, bf16[1040,128]{1,0:T(8,128)(2,1)S(1)}, u32[]{:S(2)}, u32[]{:S(2)}) collective-permute-start(bf16[1040,128]{1,0:T(8,128)(2,1)S(1)} %get-tuple-element.93), channel_id=1, source_target_pairs={{0,16},{8,24},{16,0},{24,8},{1,17},{9,25},{17,1},{25,9},{2,18},{10... | collective-permute-start | bytes 798728 | tf_op jit(solution)/shard_map/ppermute | solution.py:34
  14.2 13.9 %collective-permute-start.5 = (bf16[1040,128]{1,0:T(8,128)(2,1)S(1)}, bf16[1040,128]{1,0:T(8,128)(2,1)S(1)}, u32[]{:S(2)}, u32[]{:S(2)}) collective-permute-start(bf16[1040,128]{1,0:T(8,128)(2,1)S(1)} %get-tuple-element.93), channel_id=1, source_target_pairs={{0,24},{8,16},{16,8},{24,0},{1,25},{9,17},{17,9},{25,1},{2,26},{10... | collective-permute-start | bytes 798728 | tf_op jit(solution)/shard_map/ppermute | solution.py:34
  15.6 12.4 %collective-permute-start.3 = (bf16[1040,128]{1,0:T(8,128)(2,1)S(1)}, bf16[1040,128]{1,0:T(8,128)(2,1)S(1)}, u32[]{:S(2)}, u32[]{:S(2)}) collective-permute-start(bf16[1040,128]{1,0:T(8,128)(2,1)S(1)} %get-tuple-element.92), channel_id=1, source_target_pairs={{0,8},{8,0},{16,24},{24,16},{1,9},{9,1},{17,25},{25,17},{2,10},{10... | collective-permute-start | bytes 798728 | tf_op jit(solution)/shard_map/ppermute | solution.py:34
  16.8 14.9 %collective-permute-start.8 = (bf16[2,8,128,128]{3,2,1,0:T(8,128)(2,1)S(1)}, bf16[2,8,128,128]{3,2,1,0:T(8,128)(2,1)S(1)}, u32[]{:S(2)}, u32[]{:S(2)}) collective-permute-start(bf16[2,8,128,128]{3,2,1,0:T(8,128)(2,1)S(1)} %get-tuple-element.104), channel_id=1, source_target_pairs={{0,1},{3,2},{4,5},{7,6},{8,9},{11,10},{12,13},{15,14},{16,17},{19,... | collective-permute-start | bytes 1572872 | tf_op jit(solution)/shard_map/ppermute | solution.py:533
  20.7 7.3 %copy-start.4 = (f32[8,128,128]{2,1,0:T(8,128)S(1)}, f32[8,128,128]{2,1,0:T(8,128)}, u32[]{:S(2)}) copy-start(f32[8,128,128]{2,1,0:T(8,128)} %refs_1_.5) | copy-start | bytes 1572868
  20.8 7.3 %copy-start.5 = (f32[8,128,128]{2,1,0:T(8,128)S(1)}, f32[8,128,128]{2,1,0:T(8,128)}, u32[]{:S(2)}) copy-start(f32[8,128,128]{2,1,0:T(8,128)} %refs_2_.17) | copy-start | bytes 1572868
  21.3 11.6 %collective-permute-start.10 = (bf16[2,8,128,128]{3,2,1,0:T(8,128)(2,1)S(1)}, bf16[2,8,128,128]{3,2,1,0:T(8,128)(2,1)S(1)}, u32[]{:S(2)}, u32[]{:S(2)}) collective-permute-start(bf16[2,8,128,128]{3,2,1,0:T(8,128)(2,1)S(1)} %get-tuple-element.109), channel_id=1, source_target_pairs={{1,2},{2,1},{5,6},{6,5},{9,10},{10,9},{13,14},{14,13},{17,18},{18,... | collective-permute-start | bytes 1572872 | tf_op jit(solution)/shard_map/ppermute | solution.py:533
  31.6 10.7 %collective-permute-start.7 = (bf16[2,8,128,128]{3,2,1,0:T(8,128)(2,1)S(1)}, bf16[2,8,128,128]{3,2,1,0:T(8,128)(2,1)S(1)}, u32[]{:S(2)}, u32[]{:S(2)}) collective-permute-start(bf16[2,8,128,128]{3,2,1,0:T(8,128)(2,1)S(1)} %get-tuple-element.103), channel_id=1, source_target_pairs={{0,4},{4,0},{1,5},{5,1},{2,6},{6,2},{3,7},{7,3},{8,12},{12,8},{9,1... | collective-permute-start | bytes 1572872 | tf_op jit(solution)/shard_map/ppermute | solution.py:34
  32.2 10.1 %collective-permute-start.9 = (bf16[2,8,128,128]{3,2,1,0:T(8,128)(2,1)S(1)}, bf16[2,8,128,128]{3,2,1,0:T(8,128)(2,1)S(1)}, u32[]{:S(2)}, u32[]{:S(2)}) collective-permute-start(bf16[2,8,128,128]{3,2,1,0:T(8,128)(2,1)S(1)} %get-tuple-element.107), channel_id=1, source_target_pairs={{1,2},{2,1},{5,6},{6,5},{9,10},{10,9},{13,14},{14,13},{17,18},{18,... | collective-permute-start | bytes 1572872 | tf_op jit(solution)/shard_map/ppermute | solution.py:533
  33.6 17.2 %collective-permute-start.12 = (bf16[2,8,128,128]{3,2,1,0:T(8,128)(2,1)S(1)}, bf16[2,8,128,128]{3,2,1,0:T(8,128)(2,1)S(1)}, u32[]{:S(2)}, u32[]{:S(2)}) collective-permute-start(bf16[2,8,128,128]{3,2,1,0:T(8,128)(2,1)S(1)} %get-tuple-element.115), channel_id=1, source_target_pairs={{0,1},{3,2},{1,0},{2,3},{4,5},{7,6},{5,4},{6,7},{8,9},{11,10},{9,8... | collective-permute-start | bytes 1572872 | tf_op jit(solution)/shard_map/ppermute | solution.py:533
  43.0 19.8 %collective-permute-start.11 = (bf16[2,8,128,128]{3,2,1,0:T(8,128)(2,1)S(1)}, bf16[2,8,128,128]{3,2,1,0:T(8,128)(2,1)S(1)}, u32[]{:S(2)}, u32[]{:S(2)}) collective-permute-start(bf16[2,8,128,128]{3,2,1,0:T(8,128)(2,1)S(1)} %get-tuple-element.114), channel_id=1, source_target_pairs={{0,1},{3,2},{1,0},{2,3},{4,5},{7,6},{5,4},{6,7},{8,9},{11,10},{9,8... | collective-permute-start | bytes 1572872 | tf_op jit(solution)/shard_map/ppermute | solution.py:533
  52.1 1.6 %collective-permute-start.13 = (bf16[2,4,128,128]{3,2,1,0:T(8,128)(2,1)S(1)}, bf16[2,4,128,128]{3,2,1,0:T(8,128)(2,1)S(1)}, u32[]{:S(2)}, u32[]{:S(2)}) collective-permute-start(bf16[2,4,128,128]{3,2,1,0:T(8,128)(2,1)S(1)} %get-tuple-element.119), channel_id=1, source_target_pairs={{0,4},{4,0},{1,5},{5,1},{2,6},{6,2},{3,7},{7,3},{8,12},{12,8},{9,1... | collective-permute-start | bytes 786440 | tf_op jit(solution)/shard_map/ppermute | solution.py:34
  52.2 12.5 %collective-permute-start.19 = (bf16[2,8,128,128]{3,2,1,0:T(8,128)(2,1)S(1)}, bf16[2,8,128,128]{3,2,1,0:T(8,128)(2,1)S(1)}, u32[]{:S(2)}, u32[]{:S(2)}) collective-permute-start(bf16[2,8,128,128]{3,2,1,0:T(8,128)(2,1)S(1)} %get-tuple-element.128), channel_id=1, source_target_pairs={{1,2},{2,1},{5,6},{6,5},{9,10},{10,9},{13,14},{14,13},{17,18},{18,... | collective-permute-start | bytes 1572872 | tf_op jit(solution)/shard_map/ppermute | solution.py:533
  54.4 12.5 %collective-permute-start.17 = (bf16[528,128]{1,0:T(8,128)(2,1)S(1)}, bf16[528,128]{1,0:T(8,128)(2,1)S(1)}, u32[]{:S(2)}, u32[]{:S(2)}) collective-permute-start(bf16[528,128]{1,0:T(8,128)(2,1)S(1)} %get-tuple-element.127), channel_id=1, source_target_pairs={{0,16},{8,24},{16,0},{24,8},{1,17},{9,25},{17,1},{25,9},{2,18},{10... | collective-permute-start | bytes 405512 | tf_op jit(solution)/shard_map/ppermute | solution.py:34
  56.0 10.9 %collective-permute-start.18 = (bf16[528,128]{1,0:T(8,128)(2,1)S(1)}, bf16[528,128]{1,0:T(8,128)(2,1)S(1)}, u32[]{:S(2)}, u32[]{:S(2)}) collective-permute-start(bf16[528,128]{1,0:T(8,128)(2,1)S(1)} %get-tuple-element.127), channel_id=1, source_target_pairs={{0,24},{8,16},{16,8},{24,0},{1,25},{9,17},{17,9},{25,1},{2,26},{10... | collective-permute-start | bytes 405512 | tf_op jit(solution)/shard_map/ppermute | solution.py:34
  57.4 8.0 %collective-permute-start.16 = (bf16[528,128]{1,0:T(8,128)(2,1)S(1)}, bf16[528,128]{1,0:T(8,128)(2,1)S(1)}, u32[]{:S(2)}, u32[]{:S(2)}) collective-permute-start(bf16[528,128]{1,0:T(8,128)(2,1)S(1)} %get-tuple-element.126), channel_id=1, source_target_pairs={{0,8},{8,0},{16,24},{24,16},{1,9},{9,1},{17,25},{25,17},{2,10},{10... | collective-permute-start | bytes 405512 | tf_op jit(solution)/shard_map/ppermute | solution.py:34
  63.3 6.1 %collective-permute-start.14 = (bf16[2,8,128,128]{3,2,1,0:T(8,128)(2,1)S(1)}, bf16[2,8,128,128]{3,2,1,0:T(8,128)(2,1)S(1)}, u32[]{:S(2)}, u32[]{:S(2)}) collective-permute-start(bf16[2,8,128,128]{3,2,1,0:T(8,128)(2,1)S(1)} %get-tuple-element.122), channel_id=1, source_target_pairs={{1,2},{2,1},{5,6},{6,5},{9,10},{10,9},{13,14},{14,13},{17,18},{18,... | collective-permute-start | bytes 1572872 | tf_op jit(solution)/shard_map/ppermute | solution.py:533
  64.7 4.0 %collective-permute-start.15 = (bf16[2,4,128,128]{3,2,1,0:T(8,128)(2,1)S(1)}, bf16[2,4,128,128]{3,2,1,0:T(8,128)(2,1)S(1)}, u32[]{:S(2)}, u32[]{:S(2)}) collective-permute-start(bf16[2,4,128,128]{3,2,1,0:T(8,128)(2,1)S(1)} %get-tuple-element.125), channel_id=1, source_target_pairs={{0,4},{4,0},{1,5},{5,1},{2,6},{6,2},{3,7},{7,3},{8,12},{12,8},{9,1... | collective-permute-start | bytes 786440 | tf_op jit(solution)/shard_map/ppermute | solution.py:34
  65.4 20.0 %collective-permute-start.24 = (bf16[2,8,128,128]{3,2,1,0:T(8,128)(2,1)S(1)}, bf16[2,8,128,128]{3,2,1,0:T(8,128)(2,1)S(1)}, u32[]{:S(2)}, u32[]{:S(2)}) collective-permute-start(bf16[2,8,128,128]{3,2,1,0:T(8,128)(2,1)S(1)} %get-tuple-element.140), channel_id=1, source_target_pairs={{1,0},{2,3},{5,4},{6,7},{9,8},{10,11},{13,12},{14,15},{17,16},{18,... | collective-permute-start | bytes 1572872 | tf_op jit(solution)/shard_map/ppermute | solution.py:533
  68.2 6.1 %collective-permute-start.25 = (bf16[2,4,128,128]{3,2,1,0:T(8,128)(2,1)S(1)}, bf16[2,4,128,128]{3,2,1,0:T(8,128)(2,1)S(1)}, u32[]{:S(2)}, u32[]{:S(2)}) collective-permute-start(bf16[2,4,128,128]{3,2,1,0:T(8,128)(2,1)S(1)} %get-tuple-element.142), channel_id=1, source_target_pairs={{0,4},{4,0},{1,5},{5,1},{2,6},{6,2},{3,7},{7,3},{8,12},{12,8},{9,1... | collective-permute-start | bytes 786440 | tf_op jit(solution)/shard_map/ppermute | solution.py:34
  70.0 26.5 %collective-permute-start.20 = (bf16[2,8,128,128]{3,2,1,0:T(8,128)(2,1)S(1)}, bf16[2,8,128,128]{3,2,1,0:T(8,128)(2,1)S(1)}, u32[]{:S(2)}, u32[]{:S(2)}) collective-permute-start(bf16[2,8,128,128]{3,2,1,0:T(8,128)(2,1)S(1)} %get-tuple-element.133), channel_id=1, source_target_pairs={{1,0},{2,3},{5,4},{6,7},{9,8},{10,11},{13,12},{14,15},{17,16},{18,... | collective-permute-start | bytes 1572872 | tf_op jit(solution)/shard_map/ppermute | solution.py:533
  71.3 16.4 %collective-permute-start.21 = (bf16[528,128]{1,0:T(8,128)(2,1)S(1)}, bf16[528,128]{1,0:T(8,128)(2,1)S(1)}, u32[]{:S(2)}, u32[]{:S(2)}) collective-permute-start(bf16[528,128]{1,0:T(8,128)(2,1)S(1)} %get-tuple-element.138), channel_id=1, source_target_pairs={{0,8},{8,0},{16,24},{24,16},{1,9},{9,1},{17,25},{25,17},{2,10},{10... | collective-permute-start | bytes 405512 | tf_op jit(solution)/shard_map/ppermute | solution.py:34
  72.8 14.9 %collective-permute-start.22 = (bf16[528,128]{1,0:T(8,128)(2,1)S(1)}, bf16[528,128]{1,0:T(8,128)(2,1)S(1)}, u32[]{:S(2)}, u32[]{:S(2)}) collective-permute-start(bf16[528,128]{1,0:T(8,128)(2,1)S(1)} %get-tuple-element.139), channel_id=1, source_target_pairs={{0,16},{8,24},{16,0},{24,8},{1,17},{9,25},{17,1},{25,9},{2,18},{10... | collective-permute-start | bytes 405512 | tf_op jit(solution)/shard_map/ppermute | solution.py:34
  74.3 13.4 %collective-permute-start.23 = (bf16[528,128]{1,0:T(8,128)(2,1)S(1)}, bf16[528,128]{1,0:T(8,128)(2,1)S(1)}, u32[]{:S(2)}, u32[]{:S(2)}) collective-permute-start(bf16[528,128]{1,0:T(8,128)(2,1)S(1)} %get-tuple-element.139), channel_id=1, source_target_pairs={{0,24},{8,16},{16,8},{24,0},{1,25},{9,17},{17,9},{25,1},{2,26},{10... | collective-permute-start | bytes 405512 | tf_op jit(solution)/shard_map/ppermute | solution.py:34
  89.3 1.5 %collective-permute-start.26 = (bf16[2,4,128,128]{3,2,1,0:T(8,128)(2,1)S(1)}, bf16[2,4,128,128]{3,2,1,0:T(8,128)(2,1)S(1)}, u32[]{:S(2)}, u32[]{:S(2)}) collective-permute-start(bf16[2,4,128,128]{3,2,1,0:T(8,128)(2,1)S(1)} %get-tuple-element.151), channel_id=1, source_target_pairs={{0,4},{4,0},{1,5},{5,1},{2,6},{6,2},{3,7},{7,3},{8,12},{12,8},{9,1... | collective-permute-start | bytes 786440 | tf_op jit(solution)/shard_map/ppermute | solution.py:34
